TPU v7x, 32 devices: a whole 2x2x4 slice. The times are simulated.
32 devices in a mesh: seq: 16 (over z, y, x), head: 2 (over core).
Axes of the slice: x: 2, y: 2, z: 4, core: 2. Of those that a mesh axis runs over, the one named last changes fastest.
Arguments:
- layer_input: float32 [4096, 2048], P('seq'), may hold values from -6 to 6
- doc_start: int32 [4096], P('seq'), may hold values from 0 to 4095, as said below
- mixer_gain: float32 [2048], replicated, may hold values from 0.5 to 1.5
- ffn_gain: float32 [2048], replicated, may hold values from 0.5 to 1.5
- z_weight: bfloat16 [2048, 3072], P('seq', 'head'), may hold values from -0.125 to 0.125
- x_weight: bfloat16 [2048, 3072], P('seq', 'head'), may hold values from -0.125 to 0.125
- bc_weight: bfloat16 [2048, 512], P('seq'), may hold values from -0.0068359375 to 0.0068359375
- dt_weight: bfloat16 [2048, 48], P('seq', 'head'), may hold values from -0.125 to 0.125
- q_weight: bfloat16 [2048, 1024], P('seq', 'head'), may hold values from -0.125 to 0.125
- k_weight: bfloat16 [2048, 256], P('seq', 'head'), may hold values from -0.125 to 0.125
- v_weight: bfloat16 [2048, 256], P('seq', 'head'), may hold values from -0.125 to 0.125
- o_weight: bfloat16 [2048, 1024], P('seq', 'head'), may hold values from -1.5 to 1.5
- out_weight: bfloat16 [2048, 3072], P('seq', 'head'), may hold values from -0.109375 to 0.109375
- gate_weight: bfloat16 [2048, 4096], P('seq', 'head'), may hold values from -0.125 to 0.125
- up_weight: bfloat16 [2048, 4096], P('seq', 'head'), may hold values from -0.125 to 0.125
- down_weight: bfloat16 [2048, 4096], P('seq', 'head'), may hold values from -0.09375 to 0.09375
- conv_inner: float32 [4, 3072], P(None, 'head'), may hold values from -3 to 3
- conv_state: float32 [4, 512], replicated, may hold values from -3 to 3
- decay_log: float32 [48], P('head'), may hold values from -16 to -2
- dt_bias: float32 [48], P('head'), may hold values from -1.5 to 0.5
- skip_coef: float32 [48], P('head'), may hold values from 0.5 to 1.5
- ssm_gain: float32 [3072], P('head'), may hold values from 0.5 to 1.5
- cotangent: float32 [4096, 2048], P('seq'), may hold values from -6 to 6
Outputs:
- layer_out: float32 [4096, 2048], P('seq')
- grad_input: float32 [4096, 2048], P('seq')
- grad_mixer_gain: float32 [2048], P('seq')
- grad_ffn_gain: float32 [2048], P('seq')
- grad_z_weight: float32 [2048, 3072], P('seq', 'head')
- grad_x_weight: float32 [2048, 3072], P('seq', 'head')
- grad_bc_weight: float32 [2048, 512], P('seq')
- grad_dt_weight: float32 [2048, 48], P('seq', 'head')
- grad_q_weight: float32 [2048, 1024], P('seq', 'head')
- grad_k_weight: float32 [2048, 256], P('seq', 'head')
- grad_v_weight: float32 [2048, 256], P('seq', 'head')
- grad_o_weight: float32 [2048, 1024], P('seq', 'head')
- grad_out_weight: float32 [2048, 3072], P('seq', 'head')
- grad_gate_weight: float32 [2048, 4096], P('seq', 'head')
- grad_up_weight: float32 [2048, 4096], P('seq', 'head')
- grad_down_weight: float32 [2048, 4096], P('seq', 'head')
- grad_conv_inner: float32 [4, 3072], P(None, 'head')
- grad_conv_state: float32 [4, 512], replicated
- grad_decay_log: float32 [48], P('head')
- grad_dt_bias: float32 [48], P('head')
- grad_skip_coef: float32 [48], P('head')
- grad_ssm_gain: float32 [3072], P('head')
Inputs may be any that keep to these rules, and one draw needn't show every extreme that they name: `doc_start`: documents are contiguous: entries never fall, each is at most its token's position, and a token whose entry equals its position begins a document; the first document begins at 0.
All inputs are finite; a program needn't handle non-finite values.
Results may differ from a plain program's by a relative error of at most 0.017.
Values may be sent and summed in bfloat16 or wider, within the bound.
A program may use at most 448 MiB of HBM per device.

v0:
```python
import jax
import jax.numpy as jnp
from jax import lax
from jax.sharding import PartitionSpec as P

P_SIZE = 64
N = 256
HD = 128
K = 4


highest = lax.Precision.HIGHEST
rope_base = 10000.0
norm_eps = 1e-05


def passed_along(block, axis, distance):
    devices = range(lax.axis_size(axis))
    route = [(i - distance, i) for i in devices if i - distance in devices]
    return lax.ppermute(block, axis, route)


def prefix(x, axis, combine, identity):
    count, mine = (lax.axis_size(axis), lax.axis_index(axis))
    everything = jax.tree.map(
        lambda part, kind: lax.all_gather(part.astype(kind), axis), x, (jnp.bfloat16, jnp.bfloat16)
    )
    start = jax.tree.map(
        lambda part, zero: jnp.broadcast_to(jnp.asarray(zero, part.dtype), part.shape), x, identity
    )

    def hop(k, before):
        reached = k < mine
        new = combine(
            before, jax.tree.map(lambda part, own: part[k].astype(own.dtype), everything, x)
        )
        return jax.tree.map(lambda a, b: jnp.where(reached, a, b), new, before)

    return lax.fori_loop(0, count, hop, start)


def entering(x, axis, join, neutral):
    count = lax.axis_size(axis)
    place = lax.axis_index(axis)
    ahead = count - 1 - place
    gathered = jax.tree.map(
        lambda a, kind: lax.all_gather(a.astype(kind), axis),
        x,
        jax.tree.map(lambda a: jnp.bfloat16 if a.dtype == jnp.float32 else a.dtype, x),
    )
    state = jax.tree.map(lambda a, e: jnp.zeros_like(a) + jnp.asarray(e, a.dtype), x, neutral)

    def one(hop, state):
        source = count - 1 - hop
        return join(
            state,
            jax.tree.map(
                lambda a, own: lax.dynamic_index_in_dim(a, source, 0, False).astype(own.dtype),
                gathered,
                x,
            ),
        )

    return lax.fori_loop(0, ahead, one, state)


def split_up(x, dim, count):
    before, after = (x.shape[:dim], x.shape[dim + 1 :])
    return jnp.moveaxis(x.reshape(*before, count, -1, *after), dim, 0)


def sum_at_owner(x, axis, dim):
    count = lax.axis_size(axis)
    blocks = lax.all_to_all(split_up(x, dim, count), axis, 0, 0, tiled=True)
    return jnp.sum(blocks.astype(jnp.float32), axis=0)


def side_by_side(arrays, axis, dim, along):
    widths = [a.shape[along] for a in arrays]
    both = jnp.concatenate(arrays, axis=along)
    result = sum_at_owner(both, axis, dim)
    return tuple(jnp.split(result, [sum(widths[:k]) for k in range(1, len(widths))], axis=along))


def rms_scale(values, gain):
    return values * lax.rsqrt(jnp.mean(values * values, axis=-1, keepdims=True) + norm_eps) * gain


def rotate(values, offsets):
    half = values.shape[-1] // 2
    freqs = rope_base ** (-2.0 * jnp.arange(half, dtype=values.dtype) / values.shape[-1])
    angles = offsets.astype(values.dtype)[:, None] * freqs[None, :]
    cosine = jnp.cos(angles)[:, None, :]
    sine = jnp.sin(angles)[:, None, :]
    first = values[..., :half]
    second = values[..., half:]
    return jnp.concatenate(
        [first * cosine - second * sine, second * cosine + first * sine], axis=-1
    )


def causal_conv(padded, taps, starts, places):
    width = taps.shape[0]
    length = starts.shape[0]
    total = jnp.zeros((length, padded.shape[1]), padded.dtype)
    for lag in range(width):
        valid = (places - (width - 1 - lag) >= starts)[:, None]
        total = total + jnp.where(valid, padded[lag : lag + length] * taps[lag][None, :], 0.0)
    return total


def ssd_block(state, block):
    inner, b_rows, c_rows, step_size, log_decay, starts, places = block
    cum_decay = jnp.cumsum(log_decay, axis=0)
    visible = (starts[:, None] <= places[None, :]) & (places[None, :] <= places[:, None])
    spans = cum_decay[:, None, :] - cum_decay[None, :, :]
    weights = jnp.where(
        visible[:, :, None], jnp.exp(jnp.where(visible[:, :, None], spans, 0.0)), 0.0
    )
    intersection = jnp.dot(c_rows, b_rows.T, precision=highest)
    driven = inner * step_size[:, :, None]
    mixed = jnp.einsum(
        "ijh,jhp->ihp", weights * intersection[:, :, None], driven, precision=highest
    )
    carried = (starts < places[0]).astype(inner.dtype)
    decay_in = jnp.exp(cum_decay) * carried[:, None]
    from_state = jnp.einsum("in,hpn->ihp", c_rows, state, precision=highest) * decay_in[:, :, None]
    closing = jnp.where(
        (starts[-1] <= places)[:, None], jnp.exp(cum_decay[-1][None, :] - cum_decay), 0.0
    )
    new_state = state * decay_in[-1][:, None, None] + jnp.einsum(
        "jh,jhp,jn->hpn", closing, driven, b_rows, precision=highest
    )
    return (new_state, mixed + from_state)


def project(left, weight):
    return jnp.dot(left, weight, preferred_element_type=jnp.float32)


def project_back(left, weight):
    return lax.dot_general(
        left, weight, (((1,), (1,)), ((), ())), preferred_element_type=jnp.float32
    )


def token_sum(left, right):
    return lax.dot_general(
        left, right, (((0,), (0,)), ((), ())), preferred_element_type=jnp.float32
    )


def head_sum(values):
    return lax.psum(values.astype(jnp.bfloat16), "head").astype(jnp.float32)


def chain_step(earlier, later):
    return (earlier[0] * later[0], earlier[1] * later[0][:, None, None] + later[1])


def on_device(
    layer_input,
    doc_start,
    mixer_gain,
    ffn_gain,
    z_weight,
    x_weight,
    bc_weight,
    dt_weight,
    q_weight,
    k_weight,
    v_weight,
    o_weight,
    out_weight,
    gate_weight,
    up_weight,
    down_weight,
    conv_inner,
    conv_state,
    decay_log,
    dt_bias,
    skip_coef,
    ssm_gain,
    cotangent,
):
    tokens = layer_input.shape[0]
    offset = lax.axis_index("seq") * tokens
    places = offset + jnp.arange(tokens, dtype=jnp.int32)
    total_tokens = tokens * lax.axis_size("seq")
    heads = decay_log.shape[0]
    kv_heads = k_weight.shape[1] // HD
    group = q_weight.shape[1] // HD // kv_heads
    block_len = min(128, tokens)
    key_len = min(512, total_tokens)
    edge = K - 1
    blocks = tokens // block_len
    shards = (
        z_weight,
        x_weight,
        bc_weight,
        dt_weight,
        q_weight,
        k_weight,
        v_weight,
        o_weight,
        out_weight,
        gate_weight,
        up_weight,
        down_weight,
    )
    gathered = (
        lax.all_gather(shards[0], "seq", axis=0, tiled=True),
        lax.all_gather(shards[1], "seq", axis=0, tiled=True),
        lax.all_gather(shards[2], "seq", axis=0, tiled=True),
        lax.all_gather(shards[3], "seq", axis=0, tiled=True),
        lax.all_gather(shards[4], "seq", axis=0, tiled=True),
        lax.all_gather(shards[5], "seq", axis=0, tiled=True),
        lax.all_gather(shards[6], "seq", axis=0, tiled=True),
        lax.all_gather(shards[7], "seq", axis=0, tiled=True),
        lax.all_gather(shards[8], "seq", axis=0, tiled=True),
        lax.all_gather(shards[9], "seq", axis=0, tiled=True),
        lax.all_gather(shards[10], "seq", axis=0, tiled=True),
        lax.all_gather(shards[11], "seq", axis=0, tiled=True),
    )
    (
        full_z,
        full_x,
        full_bc,
        full_dt,
        full_q,
        full_k,
        full_v,
        full_o,
        full_out,
        full_gate,
        full_up,
        full_down,
    ) = gathered
    normed_one, norm_one_back = jax.vjp(rms_scale, layer_input, mixer_gain)
    first_low = normed_one.astype(jnp.bfloat16)
    z_part = project(first_low, full_z)
    inner_pre = project(first_low, full_x)
    state_pre = project(first_low, full_bc)
    step_raw = project(first_low, full_dt)
    edge_inner, edge_state = passed_along(
        (inner_pre[tokens - edge :], state_pre[tokens - edge :]), "seq", 1
    )

    def conv_pair(inner, state, inner_rim, state_rim, taps_inner, taps_state):
        mixed_inner = jax.nn.silu(
            causal_conv(jnp.concatenate([inner_rim, inner], axis=0), taps_inner, doc_start, places)
        )
        mixed_state = jax.nn.silu(
            causal_conv(jnp.concatenate([state_rim, state], axis=0), taps_state, doc_start, places)
        )
        return (mixed_inner, mixed_state)

    (conv_x, conv_bc), conv_back = jax.vjp(
        conv_pair, inner_pre, state_pre, edge_inner, edge_state, conv_inner, conv_state
    )

    def gate_rates(raw, bias, logs):
        step = jax.nn.softplus(raw + bias)
        return (step, -jnp.exp(logs) * step)

    (step_size, log_decay), rates_back = jax.vjp(gate_rates, step_raw, dt_bias, decay_log)
    inner_heads = conv_x.reshape(tokens, heads, P_SIZE)
    b_rows = conv_bc[:, :N]
    c_rows = conv_bc[:, N:]

    def zero_part(inner, b_part, c_part, step, logs, skip):
        state_zero = jnp.zeros((heads, P_SIZE, N), jnp.float32)
        pieces = (
            inner.reshape(blocks, block_len, heads, P_SIZE),
            b_part.reshape(blocks, block_len, N),
            c_part.reshape(blocks, block_len, N),
            step.reshape(blocks, block_len, heads),
            logs.reshape(blocks, block_len, heads),
            doc_start.reshape(blocks, block_len),
            places.reshape(blocks, block_len),
        )
        final, outputs = lax.scan(ssd_block, state_zero, pieces)
        return (outputs.reshape(tokens, heads, P_SIZE) + skip[None, :, None] * inner, final)

    (ssm_zero, local_state), zero_back = jax.vjp(
        zero_part, inner_heads, b_rows, c_rows, step_size, log_decay, skip_coef
    )
    reset_free = (doc_start[tokens - 1] < offset).astype(jnp.float32)
    decay_total = jnp.exp(jnp.cumsum(log_decay, axis=0)[tokens - 1]) * reset_free
    identity = (jnp.ones((heads,), jnp.float32), jnp.zeros((heads, P_SIZE, N), jnp.float32))
    state_in = prefix((decay_total, local_state), "seq", chain_step, identity)[1]

    def edge_part(c_part, logs, incoming):
        cum_decay = jnp.cumsum(logs, axis=0)
        arrive = jnp.exp(cum_decay) * (doc_start < offset).astype(jnp.float32)[:, None]
        reach = jnp.einsum("tn,hpn->thp", c_part, incoming, precision=highest) * arrive[:, :, None]
        return (reach, incoming * (jnp.exp(cum_decay[tokens - 1]) * reset_free)[:, None, None])

    (reach, carry_out), edge_back = jax.vjp(edge_part, c_rows, log_decay, state_in)
    ssm_out = ssm_zero + reach

    def gated_norm(values, gate_in, gain):
        gated = values * jax.nn.silu(gate_in.reshape(tokens, heads, P_SIZE))
        scaled = gated * lax.rsqrt(jnp.mean(gated * gated, axis=-1, keepdims=True) + norm_eps)
        return (scaled * gain.reshape(heads, P_SIZE)).reshape(tokens, heads * P_SIZE)

    ssm_normed, tail_back = jax.vjp(gated_norm, ssm_out, z_part, ssm_gain)
    ssm_low = ssm_normed.astype(jnp.bfloat16)
    mamba_part = project_back(ssm_low, full_out)
    q_proj = project(first_low, full_q)
    k_proj = project(first_low, full_k)
    v_proj = project(first_low, full_v)
    offsets = places - doc_start

    def rope_pair(queries, keys):
        turned_q = rotate(queries.reshape(tokens, kv_heads * group, HD), offsets) * HD ** (-0.5)
        turned_k = rotate(keys.reshape(tokens, kv_heads, HD), offsets)
        return (turned_q, turned_k)

    (turned_q, turned_k), rope_back = jax.vjp(rope_pair, q_proj, k_proj)
    query_low = turned_q.reshape(tokens, kv_heads, group, HD).astype(jnp.bfloat16)
    key_low = turned_k.reshape(tokens, kv_heads * HD).astype(jnp.bfloat16)
    value_low = v_proj.astype(jnp.bfloat16)
    keys_all, values_all = (
        lax.all_gather(key_low, "seq", axis=0, tiled=True),
        lax.all_gather(value_low, "seq", axis=0, tiled=True),
    )
    last_block = (offset + tokens - 1) // key_len
    first_block = jnp.zeros((), jnp.int32)

    def key_block(index):
        begin = index * key_len
        keys_here = lax.dynamic_slice_in_dim(keys_all, begin, key_len, 0).reshape(
            key_len, kv_heads, HD
        )
        values_here = lax.dynamic_slice_in_dim(values_all, begin, key_len, 0).reshape(
            key_len, kv_heads, HD
        )
        key_places = begin + jnp.arange(key_len, dtype=jnp.int32)
        visible = (key_places[None, :] >= doc_start[:, None]) & (
            key_places[None, :] <= places[:, None]
        )
        scores = jnp.einsum(
            "tgcd,kgd->gctk", query_low, keys_here, preferred_element_type=jnp.float32
        )
        return (keys_here, values_here, visible, scores)

    def running_max(index, carry):
        peak, mass = carry
        _, _, visible, scores = key_block(index)
        masked = jnp.where(visible, scores, -1e30)
        new_peak = jnp.maximum(peak, jnp.max(masked, axis=-1))
        mass = mass * jnp.exp(peak - new_peak) + jnp.sum(
            jnp.where(visible, jnp.exp(scores - new_peak[..., None]), 0.0), axis=-1
        )
        return (new_peak, mass)

    start_carry = (
        jnp.full((kv_heads, group, tokens), -1e30, jnp.float32),
        jnp.zeros((kv_heads, group, tokens), jnp.float32),
    )
    peak, mass = lax.fori_loop(first_block, last_block + 1, running_max, start_carry)
    log_mass = peak + jnp.log(mass)

    def weighted(index, total):
        _, values_here, visible, scores = key_block(index)
        probs = jnp.where(visible, jnp.exp(scores - log_mass[..., None]), 0.0).astype(jnp.bfloat16)
        return total + jnp.einsum(
            "gctk,kgd->tgcd", probs, values_here, preferred_element_type=jnp.float32
        )

    attended = lax.fori_loop(
        first_block, last_block + 1, weighted, jnp.zeros((tokens, kv_heads, group, HD), jnp.float32)
    )
    attended_low = attended.reshape(tokens, kv_heads * group * HD).astype(jnp.bfloat16)
    attn_part = project_back(attended_low, full_o)
    hidden_state = layer_input + head_sum(mamba_part + attn_part)
    normed_two, norm_two_back = jax.vjp(rms_scale, hidden_state, ffn_gain)
    second_low = normed_two.astype(jnp.bfloat16)
    gate_pre = project(second_low, full_gate)
    up_pre = project(second_low, full_up)

    def swiglu(gate_in, up_in):
        return jax.nn.silu(gate_in) * up_in

    activated, swiglu_back = jax.vjp(swiglu, gate_pre, up_pre)
    activated_low = activated.astype(jnp.bfloat16)
    layer_out = hidden_state + head_sum(project_back(activated_low, full_down))
    again = (
        lax.all_gather(shards[0], "seq", axis=0, tiled=True),
        lax.all_gather(shards[1], "seq", axis=0, tiled=True),
        lax.all_gather(shards[2], "seq", axis=0, tiled=True),
        lax.all_gather(shards[3], "seq", axis=0, tiled=True),
        lax.all_gather(shards[4], "seq", axis=0, tiled=True),
        lax.all_gather(shards[5], "seq", axis=0, tiled=True),
        lax.all_gather(shards[6], "seq", axis=0, tiled=True),
        lax.all_gather(shards[7], "seq", axis=0, tiled=True),
        lax.all_gather(shards[8], "seq", axis=0, tiled=True),
        lax.all_gather(shards[9], "seq", axis=0, tiled=True),
        lax.all_gather(shards[10], "seq", axis=0, tiled=True),
        lax.all_gather(shards[11], "seq", axis=0, tiled=True),
    )
    (
        back_z,
        back_x,
        back_bc,
        back_dt,
        back_q,
        back_k,
        back_v,
        back_o,
        back_out,
        back_gate,
        back_up,
        back_down,
    ) = again
    out_low = cotangent.astype(jnp.bfloat16)
    grad_down = token_sum(out_low, activated_low)
    d_gate, d_up = swiglu_back(project(out_low, back_down))
    gate_low = d_gate.astype(jnp.bfloat16)
    up_low = d_up.astype(jnp.bfloat16)
    grad_gate = token_sum(second_low, gate_low)
    grad_up = token_sum(second_low, up_low)
    d_second = head_sum(project_back(gate_low, back_gate) + project_back(up_low, back_up))
    d_norm_two, grad_ffn_gain = norm_two_back(d_second)
    d_hidden = cotangent + d_norm_two
    branch_low = d_hidden.astype(jnp.bfloat16)
    grad_out = token_sum(branch_low, ssm_low)
    grad_o = token_sum(branch_low, attended_low)
    d_ssm_out, d_z, grad_ssm_gain = tail_back(project(branch_low, back_out))
    d_reach_c, d_reach_logs, from_here = edge_back((d_ssm_out, jnp.zeros_like(carry_out)))
    state_grad = entering((decay_total, from_here), "seq", chain_step, identity)[1]
    d_carry_c, d_carry_logs, _ = edge_back((jnp.zeros_like(reach), state_grad))
    d_inner, d_b_rows, d_c_rows, d_step, d_logs, grad_skip = zero_back((d_ssm_out, state_grad))
    d_raw, grad_dt_bias, grad_decay_log = rates_back((d_step, d_logs + d_reach_logs + d_carry_logs))
    d_conv_bc = lax.psum(
        jnp.concatenate([d_b_rows, d_c_rows + d_reach_c + d_carry_c], axis=1).astype(jnp.bfloat16),
        "head",
    ).astype(jnp.float32)
    d_inner_pre, d_state_pre, d_rim_inner, d_rim_state, grad_conv_inner, grad_conv_state = (
        conv_back((d_inner.reshape(tokens, heads * P_SIZE), d_conv_bc))
    )
    from_next_inner, from_next_state = passed_along((d_rim_inner, d_rim_state), "seq", -1)
    d_inner_pre = jnp.concatenate(
        [d_inner_pre[: tokens - edge], d_inner_pre[tokens - edge :] + from_next_inner], axis=0
    )
    d_state_pre = jnp.concatenate(
        [d_state_pre[: tokens - edge], d_state_pre[tokens - edge :] + from_next_state], axis=0
    )
    d_attended = (
        project(branch_low, back_o).astype(jnp.bfloat16).reshape(tokens, kv_heads, group, HD)
    )
    balance = jnp.einsum("tgcd,tgcd->gct", d_attended.astype(jnp.float32), attended)

    def attention_grads(index, carry):
        d_query, d_keys, d_values = carry
        keys_here, values_here, visible, scores = key_block(index)
        probs = jnp.where(visible, jnp.exp(scores - log_mass[..., None]), 0.0)
        probs_low = probs.astype(jnp.bfloat16)
        d_probs = jnp.einsum(
            "tgcd,kgd->gctk", d_attended, values_here, preferred_element_type=jnp.float32
        )
        d_scores = (probs * (d_probs - balance[..., None])).astype(jnp.bfloat16)
        d_query = d_query + jnp.einsum(
            "gctk,kgd->tgcd", d_scores, keys_here, preferred_element_type=jnp.float32
        )
        key_piece = jnp.einsum(
            "gctk,tgcd->kgd", d_scores, query_low, preferred_element_type=jnp.float32
        ).reshape(key_len, kv_heads * HD)
        value_piece = jnp.einsum(
            "gctk,tgcd->kgd", probs_low, d_attended, preferred_element_type=jnp.float32
        ).reshape(key_len, kv_heads * HD)
        d_keys = lax.dynamic_update_slice_in_dim(d_keys, key_piece, index * key_len, 0)
        d_values = lax.dynamic_update_slice_in_dim(d_values, value_piece, index * key_len, 0)
        return (d_query, d_keys, d_values)

    zero_rows = jnp.zeros((total_tokens, kv_heads * HD), jnp.float32)
    d_query, d_keys, d_values = lax.fori_loop(
        first_block,
        last_block + 1,
        attention_grads,
        (jnp.zeros((tokens, kv_heads, group, HD), jnp.float32), zero_rows, zero_rows),
    )
    d_key_own, d_value_own = side_by_side(
        (d_keys.astype(jnp.bfloat16), d_values.astype(jnp.bfloat16)), "seq", 0, 1
    )
    d_q_proj, d_k_proj = rope_back(
        (d_query.reshape(tokens, kv_heads * group, HD), d_key_own.reshape(tokens, kv_heads, HD))
    )
    q_low = d_q_proj.astype(jnp.bfloat16)
    k_low = d_k_proj.astype(jnp.bfloat16)
    v_low = d_value_own.astype(jnp.bfloat16)
    z_low = d_z.astype(jnp.bfloat16)
    inner_low = d_inner_pre.astype(jnp.bfloat16)
    raw_low = d_raw.astype(jnp.bfloat16)
    state_low = d_state_pre.astype(jnp.bfloat16)
    d_first = head_sum(
        project_back(z_low, back_z)
        + project_back(inner_low, back_x)
        + project_back(raw_low, back_dt)
        + project_back(q_low, back_q)
        + project_back(k_low, back_k)
        + project_back(v_low, back_v)
    )
    d_first = d_first + project_back(state_low, back_bc)
    d_norm_one, grad_mixer_gain = norm_one_back(d_first)
    grad_input = d_hidden + d_norm_one
    grads = (
        lax.psum_scatter(token_sum(first_low, z_low), "seq", scatter_dimension=0, tiled=True),
        lax.psum_scatter(token_sum(first_low, inner_low), "seq", scatter_dimension=0, tiled=True),
        lax.psum_scatter(token_sum(first_low, state_low), "seq", scatter_dimension=0, tiled=True),
        lax.psum_scatter(token_sum(first_low, raw_low), "seq", scatter_dimension=0, tiled=True),
        lax.psum_scatter(token_sum(first_low, q_low), "seq", scatter_dimension=0, tiled=True),
        lax.psum_scatter(token_sum(first_low, k_low), "seq", scatter_dimension=0, tiled=True),
        lax.psum_scatter(token_sum(first_low, v_low), "seq", scatter_dimension=0, tiled=True),
        lax.psum_scatter(grad_o, "seq", scatter_dimension=0, tiled=True),
        lax.psum_scatter(grad_out, "seq", scatter_dimension=0, tiled=True),
        lax.psum_scatter(grad_gate, "seq", scatter_dimension=0, tiled=True),
        lax.psum_scatter(grad_up, "seq", scatter_dimension=0, tiled=True),
        lax.psum_scatter(grad_down, "seq", scatter_dimension=0, tiled=True),
        lax.psum_scatter(grad_mixer_gain, "seq", scatter_dimension=0, tiled=True),
        lax.psum_scatter(grad_ffn_gain, "seq", scatter_dimension=0, tiled=True),
    )
    small = lax.psum(
        (grad_conv_inner, grad_conv_state, grad_decay_log, grad_dt_bias, grad_skip, grad_ssm_gain),
        "seq",
    )
    return (
        layer_out,
        grad_input,
        grads[12],
        grads[13],
        grads[0],
        grads[1],
        grads[2],
        grads[3],
        grads[4],
        grads[5],
        grads[6],
        grads[7],
        grads[8],
        grads[9],
        grads[10],
        grads[11],
        small[0],
        small[1],
        small[2],
        small[3],
        small[4],
        small[5],
    )


def solution(mesh):
    placed = (
        P("seq", None),
        P("seq"),
        P(),
        P(),
        P("seq", "head"),
        P("seq", "head"),
        P("seq", None),
        P("seq", "head"),
        P("seq", "head"),
        P("seq", "head"),
        P("seq", "head"),
        P("seq", "head"),
        P("seq", "head"),
        P("seq", "head"),
        P("seq", "head"),
        P("seq", "head"),
        P(None, "head"),
        P(),
        P("head"),
        P("head"),
        P("head"),
        P("head"),
        P("seq", None),
    )
    return jax.shard_map(
        on_device,
        mesh=mesh,
        in_specs=placed,
        out_specs=(
            P("seq", None),
            P("seq", None),
            P("seq"),
            P("seq"),
            P("seq", "head"),
            P("seq", "head"),
            P("seq", None),
            P("seq", "head"),
            P("seq", "head"),
            P("seq", "head"),
            P("seq", "head"),
            P("seq", "head"),
            P("seq", "head"),
            P("seq", "head"),
            P("seq", "head"),
            P("seq", "head"),
            P(None, "head"),
            P(),
            P("head"),
            P("head"),
            P("head"),
            P("head"),
        ),
        check_vma=False,
    )
```

profile of v0, /device:TPU:0, one launch (start us, length us, event | category | flops | bytes accessed | tf_op | source)
XLA Modules:
  0.0 3796.7 jit_solution(16633805908835643696)
XLA Ops:
  11.2 46.5 %all_gather.82 = bf16[2048,128]{1,0:T(8,128)(2,1)S(1)} all-gather(bf16[128,128]{1,0:T(8,128)(2,1)S(1)} %copy-done.150), channel_id=1, replica_groups=mesh['seq'=16,'head'=2] {'seq'}, dimensions={0}, use_global_device_ids=true | all-gather | bytes 557056 | tf_op jit(solution)/shard_map/all_gather | solution.py:217
  60.8 41.0 %all_gather.80 = bf16[2048,128]{1,0:T(8,128)(2,1)S(1)} all-gather(bf16[128,128]{1,0:T(8,128)(2,1)S(1)} %copy-done.151), channel_id=1, replica_groups=mesh['seq'=16,'head'=2] {'seq'}, dimensions={0}, use_global_device_ids=true | all-gather | bytes 557056 | tf_op jit(solution)/shard_map/all_gather | solution.py:218
  105.0 38.0 %all_gather.72 = bf16[2048,24]{0,1:T(8,128)(2,1)S(1)} all-gather(bf16[128,24]{0,1:T(8,128)(2,1)S(1)} %copy-done.189), channel_id=1, replica_groups=mesh['seq'=16,'head'=2] {'seq'}, dimensions={0}, use_global_device_ids=true | all-gather | bytes 104448 | tf_op jit(solution)/shard_map/all_gather | solution.py:215
  153.3 22.8 all-gather.18.cloned.1.call-done
  198.9 100.0 %while.150 = (s32[]{:T(128)}, f32[24,64,256]{2,1,0:T(8,128)S(1)}, f32[2,128,24,64]{1,0,3,2:T(2,128)}, pred[2,128,128,24]{2,3,1,0:T(8,128)(4,1)}, f32[2,128,128,2...) while((s32[]{:T(128)}, f32[24,64,256]{2,1,0:T(8,128)S(1)}, ...), condition=%wide.region_3.4_spmd.clone, body=%wide.region_1.3_spmd.clone.sunk | while | flops 1567424128 | bytes 38250876 | solution.py:282
  220.1 19.0 dynamic_update_slice.290
  270.2 19.0 dynamic_update_slice.290
  305.0 39.2 %all-gather.3 = bf16[16,1,24]{2,1,0:T(2,128)(2,1)S(1)} all-gather(bf16[1,1,24]{2,1,0:T(2,128)(2,1)S(1)} %bitcast.944), channel_id=1, replica_groups=mesh['seq'=16,'head'=2] {'seq'}, dimensions={0}, use_global_device_ids=true | all-gather | bytes 816 | tf_op jit(solution)/shard_map/all_gather | solution.py:26
  357.8 90.3 %all-gather.22.cloned.1.call-done = bf16[2048,1536]{1,0:T(8,128)(2,1)} async-done(((bf16[128,1536]{1,0:T(8,128)(2,1)}), bf16[2048,1536]{1,0:T(8,128)(2,1)}) %all-gather.22.cloned.1.call-update) | async-done | bytes 6291472 | tf_op jit(solution)/shard_map/all_gather | solution.py:212
  448.1 6.5 fusion.293
  458.0 143.8 %all-gather.38.cloned.1.call-done = bf16[384,64,256]{2,1,0:T(8,128)(2,1)} async-done(((bf16[24,64,256]{2,1,0:T(8,128)(2,1)}), bf16[384,64,256]{2,1,0:T(8,128)(2,1)}) %all-gather.38.cloned.1.call-update) | async-done | bytes 12582928 | tf_op jit(solution)/shard_map/all_gather | solution.py:26
  601.8 41.3 %while.151 = (s32[]{:T(128)}, f32[24,64,256]{2,1,0:T(8,128)S(1)}, s32[]{:T(128)}, bf16[16,24]{1,0:T(8,128)(2,1)}, bf16[16,24,64,256]{3,2,1,0:T(8,128)(2,1)}, /*index=5*/s32[]{:T(128)}, s32[]{:T(128)}) while((s32[]{:T(128)}, f32[24,64,256]{2,1,0:T(8,128)S(1)}, s32[]{:T(128)}, bf16[16,24]{1,0:T(8,128)(2,1)}, ...), condition=%wide.region_7.8_spmd.clone, body=%wide.region_6.7_spmd.clone.sunk | while | flops 1966108 | bytes 3932513 | solution.py:39
  643.1 6.7 multiply_reduce_fusion.15
  651.3 45.6 %all-gather.24.cloned.1.call-done = bf16[2048,1536]{1,0:T(8,128)(2,1)} async-done(((bf16[128,1536]{1,0:T(8,128)(2,1)}), bf16[2048,1536]{1,0:T(8,128)(2,1)}) %all-gather.24.cloned.1.call-update) | async-done | bytes 6291472 | tf_op jit(solution)/shard_map/all_gather | solution.py:220
  702.9 55.8 %all-gather.30.cloned.1.call-done = bf16[2048,512]{1,0:T(8,128)(2,1)} async-done(((bf16[128,512]{1,0:T(8,128)(2,1)}), bf16[2048,512]{1,0:T(8,128)(2,1)}) %all-gather.30.cloned.1.call-update) | async-done | bytes 2097168 | tf_op jit(solution)/shard_map/all_gather | solution.py:219
  765.0 16.1 all-reduce.32.cloned.1.call-done
  784.2 114.2 %all-gather.32.cloned.1.call-done = bf16[2048,2048]{1,0:T(8,128)(2,1)} async-done(((bf16[128,2048]{1,0:T(8,128)(2,1)}), bf16[2048,2048]{1,0:T(8,128)(2,1)}) %all-gather.32.cloned.1.call-update) | async-done | bytes 8388624 | tf_op jit(solution)/shard_map/all_gather | solution.py:221
  898.3 7.4 fusion.296
  905.7 106.7 %all-gather.34.cloned.1.call-done = bf16[2048,2048]{1,0:T(8,128)(2,1)} async-done(((bf16[128,2048]{1,0:T(8,128)(2,1)}), bf16[2048,2048]{1,0:T(8,128)(2,1)}) %all-gather.34.cloned.1.call-update) | async-done | bytes 8388624 | tf_op jit(solution)/shard_map/all_gather | solution.py:222
  1012.4 7.4 fusion.297
  1019.7 106.8 %all-gather.36.cloned.1.call-done = bf16[2048,2048]{1,0:T(8,128)(2,1)} async-done(((bf16[128,2048]{1,0:T(8,128)(2,1)}), bf16[2048,2048]{1,0:T(8,128)(2,1)}) %all-gather.36.cloned.1.call-update) | async-done | bytes 8388624 | tf_op jit(solution)/shard_map/all_gather | solution.py:223
  1126.6 9.2 multiply_convert_fusion
  1135.8 6.6 fusion.298
  1146.2 17.5 all-reduce.34.cloned.1.call-done
  1195.5 49.1 %all-to-all-start = ((bf16[16,256,256]{2,1,0:T(8,128)(2,1)}), bf16[16,256,256]{2,1,0:T(8,128)(2,1)}, u32[]{:S(2)}, u32[]{:S(2)}) async-start(bf16[16,256,256]{2,1,0:T(8,128)(2,1)} %bitcast.887), calls=%async_computation | async-start | bytes 4194304 | tf_op jit(solution)/shard_map/all_to_all | solution.py:74
  1249.8 6.8 convolution_convert_fusion
  1265.8 48.1 %all-to-all-done = bf16[16,256,256]{2,1,0:T(8,128)(2,1)} async-done(((bf16[16,256,256]{2,1,0:T(8,128)(2,1)}), bf16[16,256,256]{2,1,0:T(8,128)(2,1)}, u32[]{:S(2)}, u32[]{:S(2)}) %all-to-all-start) | async-done | bytes 2097184 | tf_op jit(solution)/shard_map/all_to_all | solution.py:74
  1319.8 50.8 %all-gather.42.cloned.1.call-done = bf16[384,64,256]{2,1,0:T(8,128)(2,1)} async-done(((bf16[24,64,256]{2,1,0:T(8,128)(2,1)}), bf16[384,64,256]{2,1,0:T(8,128)(2,1)}) %all-gather.42.cloned.1.call-update) | async-done | bytes 12582928 | tf_op jit(solution)/shard_map/all_gather | solution.py:47
  1370.8 32.7 while.145
  1408.6 93.6 %while.146 = (s32[]{:T(128)}, f32[24,64,256]{2,1,0:T(8,128)S(1)}, f32[2,128,24,64]{1,0,3,2:T(2,128)}, bf16[2,128,256]{2,1,0:T(8,128)(2,1)}, f32[2,128,256]{2,1,0...) while((s32[]{:T(128)}, f32[24,64,256]{2,1,0:T(8,128)S(1)}, ...), condition=%wide.region_32.33_spmd, body=%wide.region_23.32_spmd.sunk | while | flops 3127910400 | bytes 107504608 | solution.py:282
  1421.8 18.9 dynamic_update_slice.273
  1468.4 18.9 dynamic_update_slice.273
  1549.7 8.7 convolution_bitcast_fusion.5
  1586.8 8.1 fusion.305
  1596.2 8.2 fusion.306
  1630.5 77.2 %all-reduce.26 = (f32[2048]{0:T(1024)S(1)}, f32[2048]{0:T(1024)S(1)}, f32[4,1536]{1,0:T(4,128)}, f32[4,512]{1,0:T(4,128)}, f32[24]{0:T(128)}, /*index=5*/f32[24]{0:T(128)}, f32[24]{0:T(128)}, f32[1536]{0:T(1024)}) all-reduce(f32[2048]{0:T(1024)S(1)} %get-tuple-element.1927, ...), channel_id=5, replica_groups=mesh['seq'=16,'head'=2] {'seq'}, use_global_device_ids=true, to_apply=%region_48.49.clone | all-reduce | flops 13896 | bytes 111168
  1715.0 206.2 %reduce-scatter.35.cloned.1.call-done = f32[128,2048]{0,1:T(8,128)} async-done(((f32[2048,2048]{0,1:T(8,128)}), f32[128,2048]{0,1:T(8,128)}) %reduce-scatter.35.cloned.1.call-update) | async-done | bytes 1048592 | tf_op jit(solution)/shard_map/reduce_scatter | solution.py:520
  1923.7 83.6 %reduce-scatter.23.cloned.1.call-done = f32[128,128]{1,0:T(8,128)} async-done(((f32[2048,128]{1,0:T(8,128)}), f32[128,128]{1,0:T(8,128)}) %reduce-scatter.23.cloned.1.call-update) | async-done | bytes 65552 | tf_op jit(solution)/shard_map/reduce_scatter | solution.py:514
  2007.3 77.2 %reduce-scatter.25.cloned.1.call-done = f32[128,128]{1,0:T(8,128)} async-done(((f32[2048,128]{1,0:T(8,128)}), f32[128,128]{1,0:T(8,128)}) %reduce-scatter.25.cloned.1.call-update) | async-done | bytes 65552 | tf_op jit(solution)/shard_map/reduce_scatter | solution.py:515
  2084.5 94.3 %reduce-scatter.21.cloned.1.call-done = f32[128,512]{1,0:T(8,128)} async-done(((f32[2048,512]{1,0:T(8,128)}), f32[128,512]{1,0:T(8,128)}) %reduce-scatter.21.cloned.1.call-update) | async-done | bytes 262160 | tf_op jit(solution)/shard_map/reduce_scatter | solution.py:513
  2178.8 97.7 %reduce-scatter.27.cloned.1.call-done = f32[128,512]{1,0:T(8,128)} async-done(((f32[2048,512]{1,0:T(8,128)}), f32[128,512]{1,0:T(8,128)}) %reduce-scatter.27.cloned.1.call-update) | async-done | bytes 262160 | tf_op jit(solution)/shard_map/reduce_scatter | solution.py:516
  2276.5 78.7 %reduce-scatter.19.cloned.1.call-done = f32[128,24]{0,1:T(8,128)} async-done(((f32[2048,24]{0,1:T(8,128)}), f32[128,24]{0,1:T(8,128)}) %reduce-scatter.19.cloned.1.call-update) | async-done | bytes 12304 | tf_op jit(solution)/shard_map/reduce_scatter | solution.py:512
  2355.2 206.6 %reduce-scatter.13.cloned.1.call-done = f32[128,1536]{1,0:T(8,128)} async-done(((f32[2048,1536]{1,0:T(8,128)}), f32[128,1536]{1,0:T(8,128)}) %reduce-scatter.13.cloned.1.call-update) | async-done | bytes 786448 | tf_op jit(solution)/shard_map/reduce_scatter | solution.py:509
  2561.9 210.7 %reduce-scatter.29.cloned.1.call-done = f32[128,1536]{1,0:T(8,128)} async-done(((f32[2048,1536]{1,0:T(8,128)}), f32[128,1536]{1,0:T(8,128)}) %reduce-scatter.29.cloned.1.call-update) | async-done | bytes 786448 | tf_op jit(solution)/shard_map/reduce_scatter | solution.py:517
  2772.6 348.9 %reduce-scatter.31.cloned.1.call-done = f32[128,2048]{1,0:T(8,128)} async-done(((f32[2048,2048]{1,0:T(8,128)}), f32[128,2048]{1,0:T(8,128)}) %reduce-scatter.31.cloned.1.call-update) | async-done | bytes 1048592 | tf_op jit(solution)/shard_map/reduce_scatter | solution.py:518
  3121.4 354.8 %reduce-scatter.33.cloned.1.call-done = f32[128,2048]{1,0:T(8,128)} async-done(((f32[2048,2048]{1,0:T(8,128)}), f32[128,2048]{1,0:T(8,128)}) %reduce-scatter.33.cloned.1.call-update) | async-done | bytes 1048592 | tf_op jit(solution)/shard_map/reduce_scatter | solution.py:519
  3476.2 103.5 %reduce-scatter.17.cloned.1.call-done = f32[128,512]{1,0:T(8,128)} async-done(((f32[2048,512]{1,0:T(8,128)}), f32[128,512]{1,0:T(8,128)}) %reduce-scatter.17.cloned.1.call-update) | async-done | bytes 262160 | tf_op jit(solution)/shard_map/reduce_scatter | solution.py:511
  3579.7 209.9 %reduce-scatter.15.cloned.1.call-done = f32[128,1536]{1,0:T(8,128)} async-done(((f32[2048,1536]{1,0:T(8,128)}), f32[128,1536]{1,0:T(8,128)}) %reduce-scatter.15.cloned.1.call-update) | async-done | bytes 786448 | tf_op jit(solution)/shard_map/reduce_scatter | solution.py:510
  (935 shorter events, 454.2 us)
Async XLA Ops:
  7.2 137.5 %all-gather.20.cloned.1.call-start = ((), (), s32[]{:S(2)}) async-start(), calls=%async_computation.14 | async-start | bytes 2228224 | tf_op jit(solution)/shard_map/all_gather | solution.py:214
  8.0 168.1 %all-gather.18.cloned.1.call-start = ((), (), s32[]{:S(2)}) async-start(), calls=%async_computation.13 | async-start | bytes 6684672 | tf_op jit(solution)/shard_map/all_gather | solution.py:213
  8.7 336.1 %all-gather.40.cloned.1.call-start = ((), (), s32[]{:S(2)}) async-start(), calls=%async_computation.38 | async-start | bytes 1114112 | tf_op jit(solution)/shard_map/all_gather | solution.py:325
  58.4 389.7 %copy-start = (bf16[256,2048]{1,0:T(8,128)(2,1)}, bf16[256,2048]{1,0:T(8,128)(2,1)S(1)}, u32[]{:S(2)}) copy-start(bf16[256,2048]{1,0:T(8,128)(2,1)S(1)} %multiply_convert_fusion.3) | copy-start | bytes 3145732
  59.5 83.5 %copy-start.165 = (f32[4,1536]{1,0:T(4,128)S(1)}, f32[4,1536]{1,0:T(4,128)}, u32[]{:S(2)}) copy-start(f32[4,1536]{1,0:T(4,128)} %param.53) | copy-start | bytes 73732
  59.5 84.1 %copy-start.199 = (f32[24]{0:T(128)S(1)}, f32[24]{0:T(128)}, u32[]{:S(2)}) copy-start(f32[24]{0:T(128)} %param.56) | copy-start | bytes 292
  60.2 286.9 %all-gather.28.cloned.1.call-start = ((), (), s32[]{:S(2)}) async-start(), calls=%async_computation.18 | async-start | bytes 2228224 | tf_op jit(solution)/shard_map/all_gather | solution.py:216
  60.8 291.7 %all-gather.26.cloned.1.call-start = ((), (), s32[]{:S(2)}) async-start(), calls=%async_computation.17 | async-start | bytes 1114112 | tf_op jit(solution)/shard_map/all_gather | solution.py:326
  103.7 344.4 %all-gather.22.cloned.1.call-start = ((), (), s32[]{:S(2)}) async-start(), calls=%async_computation.15 | async-start | bytes 6684672 | tf_op jit(solution)/shard_map/all_gather | solution.py:212
  104.3 497.5 %all-gather.38.cloned.1.call-start = ((), (), s32[]{:S(2)}) async-start(), calls=%async_computation.37 | async-start | bytes 13369344 | tf_op jit(solution)/shard_map/all_gather | solution.py:26
  104.9 80.6 %copy-start.154 = (pred[256]{0:T(512)(128)(4,1)}, pred[256]{0:T(512)(128)(4,1)S(1)}, u32[]{:S(2)}) copy-start(pred[256]{0:T(512)(128)(4,1)S(1)} %get-tuple-element.2235) | copy-start | bytes 772
  104.9 80.6 %copy-start.156 = (pred[256]{0:T(512)(128)(4,1)}, pred[256]{0:T(512)(128)(4,1)S(1)}, u32[]{:S(2)}) copy-start(pred[256]{0:T(512)(128)(4,1)S(1)} %get-tuple-element.2236) | copy-start | bytes 772
  104.9 80.6 %copy-start.159 = (pred[256]{0:T(512)(128)(4,1)}, pred[256]{0:T(512)(128)(4,1)S(1)}, u32[]{:S(2)}) copy-start(pred[256]{0:T(512)(128)(4,1)S(1)} %get-tuple-element.2237) | copy-start | bytes 772
  104.9 80.6 %copy-start.162 = (pred[256]{0:T(512)(128)(4,1)}, pred[256]{0:T(512)(128)(4,1)S(1)}, u32[]{:S(2)}) copy-start(pred[256]{0:T(512)(128)(4,1)S(1)} %get-tuple-element.2238) | copy-start | bytes 772
  147.0 4.8 collective-permute-start.1
  180.8 4.8 collective-permute-start
  300.0 396.9 %all-gather.24.cloned.1.call-start = ((), (), s32[]{:S(2)}) async-start(), calls=%async_computation.16 | async-start | bytes 6684672 | tf_op jit(solution)/shard_map/all_gather | solution.py:220
  300.8 457.9 %all-gather.30.cloned.1.call-start = ((), (), s32[]{:S(2)}) async-start(), calls=%async_computation.19 | async-start | bytes 2228224 | tf_op jit(solution)/shard_map/all_gather | solution.py:219
  301.5 479.6 %all-reduce.32.cloned.1.call-start = ((), (), s32[]{:S(2)}) async-start(), calls=%async_computation.20 | async-start | bytes 2097152 | tf_op jit(solution)/shard_map/psum | solution.py:154
  357.8 400.9 %copy-start.71 = (bf16[256,1,4,128]{0,3,2,1:T(8,128)(2,1)}, bf16[256,1,4,128]{0,3,2,1:T(8,128)(2,1)S(1)}, u32[]{:S(2)}) copy-start(bf16[256,1,4,128]{0,3,2,1:T(8,128)(2,1)S(1)} %convert_element_type.231) | copy-start | bytes 786436
  651.3 51.6 %copy-start.64 = (bf16[256,24,64]{0,2,1:T(8,128)(2,1)}, bf16[256,24,64]{0,2,1:T(8,128)(2,1)S(1)}, u32[]{:S(2)}) copy-start(bf16[256,24,64]{0,2,1:T(8,128)(2,1)S(1)} %multiply_convert_fusion.4) | copy-start | bytes 2359300
  762.7 135.6 %all-gather.32.cloned.1.call-start = ((), (), s32[]{:S(2)}) async-start(), calls=%async_computation.21 | async-start | bytes 8912896 | tf_op jit(solution)/shard_map/all_gather | solution.py:221
  763.4 248.9 %all-gather.34.cloned.1.call-start = ((), (), s32[]{:S(2)}) async-start(), calls=%async_computation.22 | async-start | bytes 8912896 | tf_op jit(solution)/shard_map/all_gather | solution.py:222
  764.0 362.6 %all-gather.36.cloned.1.call-start = ((), (), s32[]{:S(2)}) async-start(), calls=%async_computation.23 | async-start | bytes 8912896 | tf_op jit(solution)/shard_map/all_gather | solution.py:223
  764.8 398.9 %all-reduce.34.cloned.1.call-start = ((), (), s32[]{:S(2)}) async-start(), calls=%async_computation.24 | async-start | bytes 2097152 | tf_op jit(solution)/shard_map/psum | solution.py:154
  782.8 384.0 %copy-start.152 = (f32[256]{0:T(256)}, f32[256]{0:T(256)S(1)}, u32[]{:S(2)}) copy-start(f32[256]{0:T(256)S(1)} %fusion.272) | copy-start | bytes 3076
  1145.7 224.9 %all-gather.42.cloned.1.call-start = ((), (), s32[]{:S(2)}) async-start(), calls=%async_computation.39 | async-start | bytes 13369344 | tf_op jit(solution)/shard_map/all_gather | solution.py:47
  1195.5 118.4 %all-to-all-start = ((bf16[16,256,256]{2,1,0:T(8,128)(2,1)}), bf16[16,256,256]{2,1,0:T(8,128)(2,1)}, u32[]{:S(2)}, u32[]{:S(2)}) async-start(bf16[16,256,256]{2,1,0:T(8,128)(2,1)} %bitcast.887), calls=%async_computation | async-start | bytes 4194304 | tf_op jit(solution)/shard_map/all_to_all | solution.py:74
  1244.6 360.0 %all-reduce.36.cloned.1.call-start = ((), (), s32[]{:S(2)}) async-start(), calls=%async_computation.40 | async-start | bytes 4718592 | tf_op jit(solution)/shard_map/psum | solution.py:154
  1519.3 18.2 collective-permute-start.2
  1548.2 373.0 %reduce-scatter.35.cloned.1.call-start = ((), (), s32[]{:S(2)}) async-start(), calls=%async_computation.36 | async-start | bytes 17825792 | tf_op jit(solution)/shard_map/reduce_scatter | solution.py:520
  1558.5 448.8 %reduce-scatter.23.cloned.1.call-start = ((), (), s32[]{:S(2)}) async-start(), calls=%async_computation.30 | async-start | bytes 1114112 | tf_op jit(solution)/shard_map/reduce_scatter | solution.py:514
  1561.2 523.3 %reduce-scatter.25.cloned.1.call-start = ((), (), s32[]{:S(2)}) async-start(), calls=%async_computation.31 | async-start | bytes 1114112 | tf_op jit(solution)/shard_map/reduce_scatter | solution.py:515
  1562.8 616.0 %reduce-scatter.21.cloned.1.call-start = ((), (), s32[]{:S(2)}) async-start(), calls=%async_computation.29 | async-start | bytes 4456448 | tf_op jit(solution)/shard_map/reduce_scatter | solution.py:513
  1565.6 710.9 %reduce-scatter.27.cloned.1.call-start = ((), (), s32[]{:S(2)}) async-start(), calls=%async_computation.32 | async-start | bytes 4456448 | tf_op jit(solution)/shard_map/reduce_scatter | solution.py:516
  1569.9 785.3 %reduce-scatter.19.cloned.1.call-start = ((), (), s32[]{:S(2)}) async-start(), calls=%async_computation.28 | async-start | bytes 208896 | tf_op jit(solution)/shard_map/reduce_scatter | solution.py:512
  1570.9 990.9 %reduce-scatter.13.cloned.1.call-start = ((), (), s32[]{:S(2)}) async-start(), calls=%async_computation.25 | async-start | bytes 13369344 | tf_op jit(solution)/shard_map/reduce_scatter | solution.py:509
  1577.5 1195.0 %reduce-scatter.29.cloned.1.call-start = ((), (), s32[]{:S(2)}) async-start(), calls=%async_computation.33 | async-start | bytes 13369344 | tf_op jit(solution)/shard_map/reduce_scatter | solution.py:517
  1585.3 1536.1 %reduce-scatter.31.cloned.1.call-start = ((), (), s32[]{:S(2)}) async-start(), calls=%async_computation.34 | async-start | bytes 17825792 | tf_op jit(solution)/shard_map/reduce_scatter | solution.py:518
  1595.0 1881.2 %reduce-scatter.33.cloned.1.call-start = ((), (), s32[]{:S(2)}) async-start(), calls=%async_computation.35 | async-start | bytes 17825792 | tf_op jit(solution)/shard_map/reduce_scatter | solution.py:519
  1604.5 1975.2 %reduce-scatter.17.cloned.1.call-start = ((), (), s32[]{:S(2)}) async-start(), calls=%async_computation.27 | async-start | bytes 4456448 | tf_op jit(solution)/shard_map/reduce_scatter | solution.py:511
  1607.5 6.3 collective-permute-start.3
  1616.5 2173.1 %reduce-scatter.15.cloned.1.call-start = ((), (), s32[]{:S(2)}) async-start(), calls=%async_computation.26 | async-start | bytes 13369344 | tf_op jit(solution)/shard_map/reduce_scatter | solution.py:510
  1626.3 82.6 %copy-start.186 = (f32[256]{0:T(256)S(1)}, f32[256]{0:T(256)}, u32[]{:S(2)}) copy-start(f32[256]{0:T(256)} %copy-done.185) | copy-start | bytes 3076
  1626.3 82.6 %copy-start.20 = (bf16[256,2048]{1,0:T(8,128)(2,1)S(1)}, bf16[256,2048]{1,0:T(8,128)(2,1)}, u32[]{:S(2)}) copy-start(bf16[256,2048]{1,0:T(8,128)(2,1)} %all-reduce.32.cloned.1.call-done) | copy-start | bytes 3145732
  1626.3 82.6 %copy-start.123 = (f32[2048]{0:T(1024)S(1)}, f32[2048]{0:T(1024)}, u32[]{:S(2)}) copy-start(f32[2048]{0:T(1024)} %param.40) | copy-start | bytes 24580
  1626.3 82.6 %copy-start.153 = (f32[256]{0:T(256)S(1)}, f32[256]{0:T(256)}, u32[]{:S(2)}) copy-start(f32[256]{0:T(256)} %copy-done.152) | copy-start | bytes 3076
  1626.3 82.6 %copy-start.182 = (f32[256]{0:T(256)S(1)}, f32[256]{0:T(256)}, u32[]{:S(2)}) copy-start(f32[256]{0:T(256)} %copy-done.181) | copy-start | bytes 3076
  (222 other events, 1885.0 us)
Sparse Core Ops, SparseCore 0:
  10.8 69.2 all-gather.19
  82.9 93.1 all-gather.17
  179.4 53.4 all-gather.39
  235.5 59.5 all-gather.27
  298.3 54.0 all-gather.25
  355.1 92.9 all-gather.21
  451.5 150.2 all-gather.37
  604.6 92.3 all-gather.23
  699.7 58.9 all-gather.29
  762.8 18.2 all-reduce.31
  784.3 114.0 all-gather.31
  901.3 111.0 all-gather.33
  1015.5 111.0 all-gather.35
  1145.8 17.7 all-reduce.33
  1182.1 188.5 all-gather.41
  1548.3 20.1 all-reduce.35
  1570.8 350.3 reduce-scatter.34
  1924.0 83.3 reduce-scatter.22
  2010.1 74.2 reduce-scatter.24
  2087.3 91.4 reduce-scatter.20
  2181.8 94.7 reduce-scatter.26
  2279.4 75.7 reduce-scatter.18
  2361.5 200.3 reduce-scatter.12
  2568.9 203.6 reduce-scatter.28
  2775.4 345.9 reduce-scatter.30
  3124.2 352.0 reduce-scatter.32
  3478.9 100.6 reduce-scatter.16
  3585.9 203.6 reduce-scatter.14
where the time goes:
time: 3810 us; the launch traced here: 3800 us
  waiting for transfers between devices  2900 us (76%)
  blocking collectives  242 us (6%)
  matrix products  233 us (6%)
  local copies, waits for them, and re-layouts  180 us (5%)
  other arithmetic  159 us (4%)
  starting transfers between devices  60.2 us (2%)
    reduce_scatter x1, waiting for transfers between devices, on_device(): lax.psum_scatter(grad_up, 'seq', scatter_dimension=0, tiled=True)  355 us
    reduce_scatter x1, waiting for transfers between devices, on_device(): lax.psum_scatter(grad_gate, 'seq', scatter_dimension=0, tiled=True)  349 us
    reduce_scatter x1, waiting for transfers between devices, on_device(): lax.psum_scatter(grad_out, 'seq', scatter_dimension=0, tiled=True)  211 us
    reduce_scatter x1, waiting for transfers between devices, on_device(): lax.psum_scatter(token_sum(first_low, inner_low), 'seq', scatter_dimensio...  210 us
    reduce_scatter x1, waiting for transfers between devices, on_device(): lax.psum_scatter(token_sum(first_low, z_low), 'seq', scatter_dimension=0,...  207 us
    reduce_scatter x1, waiting for transfers between devices, on_device(): lax.psum_scatter(grad_down, 'seq', scatter_dimension=0, tiled=True)  206 us
    all_gather x1, waiting for transfers between devices, prefix(): lax.all_gather(part.astype(kind), axis)  144 us
    all_gather x1, waiting for transfers between devices, on_device(): lax.all_gather(shards[9], 'seq', axis=0, tiled=True)  114 us
  transfers between devices with their start and end apart: 33, of which 27 were waited for; matrix products, arithmetic and copies ran while one was open for 9% of the time, Pallas kernels for 0%

commit v1 on v0

v1 whole, which is shorter than its diff:
```python
import jax
import jax.numpy as jnp
from jax import lax
from jax.sharding import Mesh, PartitionSpec as P

P_SIZE = 64
N = 256
HD = 128
K = 4
G = 4
CHUNK = 128

highest = lax.Precision.HIGHEST
rope_base = 10000.0
norm_eps = 1e-05
bf16 = jnp.bfloat16
f32 = jnp.float32


def dot(a, b, ca, cb):
    return lax.dot_general(a, b, (((ca,), (cb,)), ((), ())), preferred_element_type=f32)


def exact(text, *operands):
    return jnp.einsum(text, *operands, precision=highest, preferred_element_type=f32)


def d_silu(v):
    s = jax.nn.sigmoid(v)
    return s * (1.0 + v * (1.0 - s))


def shifted(block, axis, distance):
    count = lax.axis_size(axis)
    route = [(i - distance, i) for i in range(count) if 0 <= i - distance < count]
    return lax.ppermute(block, axis, route)


def rope_tables(offsets, first, count):
    half = HD // 2
    index = (first + jnp.arange(count)).astype(f32)
    freqs = rope_base ** (-2.0 * index / HD)
    angles = offsets.astype(f32)[:, None] * freqs[None, :]
    return jnp.cos(angles), jnp.sin(angles)


def turn(v, cosine, sine):
    half = v.shape[-1] // 2
    a, b = v[:, :half], v[:, half:]
    return jnp.concatenate([a * cosine - b * sine, b * cosine + a * sine], axis=-1)


def conv_parts(padded, starts, places):
    length = starts.shape[0]
    parts = []
    for lag in range(K):
        valid = (places - (K - 1 - lag) >= starts)[:, None]
        parts.append(jnp.where(valid, padded[lag : lag + length], 0.0))
    return parts


def conv_back(grad, padded, taps, starts, places):
    length = starts.shape[0]
    total = jnp.zeros_like(padded)
    tap_grads = []
    for lag in range(K):
        valid = (places - (K - 1 - lag) >= starts)[:, None]
        g = jnp.where(valid, grad, 0.0)
        total = total + jnp.pad(g * taps[lag][None, :], ((lag, K - 1 - lag), (0, 0)))
        tap_grads.append(jnp.sum(g * padded[lag : lag + length], axis=0))
    return total, jnp.stack(tap_grads)


def on_device(
    layer_input, doc_start, mixer_gain, ffn_gain,
    z_weight, x_weight, bc_weight, dt_weight, q_weight, k_weight, v_weight,
    o_weight, out_weight, gate_weight, up_weight, down_weight,
    conv_inner, conv_state, decay_log, dt_bias, skip_coef, ssm_gain, cotangent,
):
    tokens, width = layer_input.shape
    rows = z_weight.shape[0]
    planes = lax.axis_size("z")
    cores = lax.axis_size("head")
    zi, pi, hi = (lax.axis_index(a) for a in ("z", "p", "head"))
    T = tokens * G
    total_tokens = T * planes
    offset = zi * T
    places = offset + jnp.arange(T, dtype=jnp.int32)
    starts = lax.all_gather(doc_start, "p", axis=0, tiled=True)
    heads = decay_log.shape[0] // G
    chan = heads * P_SIZE
    bcs = 2 * N // cores // G
    quarter_half = HD // 2 // G

    def my_slice(v, size, index, axis):
        return lax.dynamic_slice_in_dim(v, index * size, size, axis)

    taps_inner = my_slice(conv_inner, chan, pi, 1)
    taps_state = my_slice(conv_state, bcs, hi * G + pi, 1)
    rates = my_slice(decay_log, heads, pi, 0)
    bias = my_slice(dt_bias, heads, pi, 0)
    skip = my_slice(skip_coef, heads, pi, 0)
    gain_s = my_slice(ssm_gain, chan, pi, 0)

    def cut(w):
        return w.reshape(rows, G, -1)

    bc_mine = lax.dynamic_slice_in_dim(bc_weight, hi * (2 * N // cores), 2 * N // cores, 1)
    k_cut = jnp.moveaxis(k_weight.reshape(rows, 2, G, quarter_half), 2, 1).reshape(rows, G, -1)
    a_parts = [cut(z_weight), cut(x_weight), cut(q_weight), cut(bc_mine), k_cut, cut(v_weight), cut(dt_weight)]
    a_sizes = [a.shape[-1] for a in a_parts]
    a_cols = sum(a_sizes)
    pad = -a_cols % 128
    a_parts.append(jnp.zeros((rows, G, pad), bf16))
    a_at = [sum(a_sizes[:i]) for i in range(len(a_sizes))]

    def gather(parts):
        w = jnp.moveaxis(jnp.concatenate(parts, axis=2), 1, 0)
        w = lax.all_to_all(w, "p", 0, 0, tiled=True)
        return lax.all_gather(w.reshape(G * rows, -1), "z", axis=0, tiled=True)

    def scatter(grad):
        g = lax.psum_scatter(grad.astype(bf16), "z", scatter_dimension=0, tiled=True)
        g = lax.all_to_all(g.reshape(G, rows, -1), "p", 0, 0, tiled=True)
        return jnp.moveaxis(g, 0, 1).astype(f32)

    wa = gather(a_parts)
    wb = gather([cut(out_weight), cut(o_weight)])
    wc = gather([cut(gate_weight), cut(up_weight)])
    wd = gather([cut(down_weight)])

    r1 = lax.rsqrt(jnp.mean(layer_input * layer_input, axis=-1, keepdims=True) + norm_eps)
    first_own = (layer_input * r1 * mixer_gain).astype(bf16)
    first = lax.all_gather(first_own, "p", axis=0, tiled=True)
    out_low = lax.all_gather(cotangent.astype(bf16), "p", axis=0, tiled=True)
    pa = dot(first, wa, 1, 0)
    z_part, inner_pre, q_proj, bc_pre, k_proj, v_proj, step_raw = (
        pa[:, a : a + s] for a, s in zip(a_at, a_sizes)
    )
    edge = K - 1
    rim_inner, rim_bc = shifted((inner_pre[T - edge :], bc_pre[T - edge :]), "z", 1)
    pad_inner = jnp.concatenate([rim_inner, inner_pre], axis=0)
    pad_bc = jnp.concatenate([rim_bc, bc_pre], axis=0)
    cv_x = sum(p * t[None, :] for p, t in zip(conv_parts(pad_inner, starts, places), taps_inner))
    cv_bc = sum(p * t[None, :] for p, t in zip(conv_parts(pad_bc, starts, places), taps_state))
    conv_x = jax.nn.silu(cv_x)
    bc_low = jax.nn.silu(cv_bc).astype(bf16)
    bc_all = lax.all_gather(bc_low, ("head", "p"), axis=1, tiled=True)
    step = jax.nn.softplus(step_raw + bias)
    log_decay = -jnp.exp(rates) * step

    L = CHUNK
    nc = T // L
    lower = (jnp.arange(L)[:, None] >= jnp.arange(L)[None, :]).astype(f32)
    b_rows = bc_all[:, :N].astype(f32).reshape(nc, L, N)
    c_rows = bc_all[:, N:].astype(f32).reshape(nc, L, N)

    def by_head(v):
        return v.reshape(nc, L, heads, P_SIZE).transpose(0, 2, 1, 3)

    def by_token(v):
        return v.transpose(0, 2, 1, 3).reshape(T, chan)

    xh = by_head(conv_x)
    step_h = step.reshape(nc, L, heads).transpose(0, 2, 1)
    la_h = log_decay.reshape(nc, L, heads).transpose(0, 2, 1)
    cs = exact("ij,chj->chi", lower, la_h)
    st = starts.reshape(nc, L)
    pl_ = places.reshape(nc, L)
    visible = (st[:, :, None] <= pl_[:, None, :]) & (pl_[:, None, :] <= pl_[:, :, None])
    span = cs[:, :, :, None] - cs[:, :, None, :]
    weights = jnp.where(visible[:, None], jnp.exp(jnp.where(visible[:, None], span, 0.0)), 0.0)
    inter = exact("cin,cjn->cij", c_rows, b_rows)
    mix = weights * inter[:, None]
    driven = xh * step_h[..., None]
    carried = (st < pl_[:, :1]).astype(f32)
    decay_in = jnp.exp(cs) * carried[:, None, :]
    closing = jnp.where((st[:, -1:] <= pl_)[:, None, :], jnp.exp(cs[:, :, -1:] - cs), 0.0)
    dtot = decay_in[:, :, -1]
    local = exact("chjp,cjn->chpn", driven * closing[..., None], b_rows)
    entering = []
    state = jnp.zeros((heads, P_SIZE, N), f32)
    through = jnp.ones((heads,), f32)
    reach = []
    for c in range(nc):
        entering.append(state)
        reach.append(through)
        state = state * dtot[c][:, None, None] + local[c]
        through = through * dtot[c]
    everyone = lax.all_gather(state.astype(bf16), "z", axis=0)
    factors = lax.all_gather(through, "z", axis=0)
    before = jnp.zeros((heads, P_SIZE, N), f32)
    for k in range(planes - 1):
        new = before * factors[k][:, None, None] + everyone[k].astype(f32)
        before = jnp.where(k < zi, new, before)
    state_in = jnp.stack([s + before * r[:, None, None] for s, r in zip(entering, reach)])
    y_off = exact("cin,chpn->chip", c_rows, state_in) * decay_in[..., None]
    y_scan = exact("chij,chjp->chip", mix, driven) + y_off
    y_h = y_scan + skip[None, :, None, None] * xh

    ssm = by_token(y_h)
    same_head = (jnp.arange(chan)[:, None] // P_SIZE == jnp.arange(heads)[None, :]).astype(f32)

    def head_mean(v):
        return jnp.repeat(jnp.mean(v.reshape(T, heads, P_SIZE), axis=-1), P_SIZE, axis=1)

    sz = jax.nn.silu(z_part)
    gated = ssm * sz
    r_s = lax.rsqrt(head_mean(gated * gated) + norm_eps)
    ssm_low = (gated * r_s * gain_s).astype(bf16)

    offsets = places - starts
    cos_q, sin_q = rope_tables(offsets, 0, HD // 2)
    cos_k, sin_k = rope_tables(offsets, pi * quarter_half, quarter_half)
    scale = HD ** (-0.5)
    query = (turn(q_proj, cos_q, sin_q) * scale).astype(bf16)
    kv_own = jnp.concatenate([turn(k_proj, cos_k, sin_k).astype(bf16), v_proj.astype(bf16)], axis=1)
    kv_all = lax.all_gather(kv_own, ("z", "p"), axis=0)
    kv_all = kv_all.reshape(planes, G, T, 4, quarter_half)
    keys = kv_all[:, :, :, :2].transpose(0, 2, 3, 1, 4).reshape(total_tokens, HD)
    values = kv_all[:, :, :, 2:].reshape(planes, G, T, 2 * quarter_half).transpose(0, 2, 1, 3).reshape(total_tokens, HD)
    key_len = min(512, total_tokens)
    first_block = starts[0] // key_len
    last_block = (offset + T - 1) // key_len

    def key_block(index):
        begin = index * key_len
        kb = lax.dynamic_slice_in_dim(keys, begin, key_len, 0)
        vb = lax.dynamic_slice_in_dim(values, begin, key_len, 0)
        at = begin + jnp.arange(key_len, dtype=jnp.int32)
        seen = (at[None, :] >= starts[:, None]) & (at[None, :] <= places[:, None])
        return kb, vb, seen, dot(query, kb, 1, 1)

    def running(index, carry):
        peak, mass = carry
        _, _, seen, scores = key_block(index)
        new = jnp.maximum(peak, jnp.max(jnp.where(seen, scores, -1e30), axis=-1))
        mass = mass * jnp.exp(peak - new) + jnp.sum(jnp.where(seen, jnp.exp(scores - new[:, None]), 0.0), axis=-1)
        return new, mass

    peak, mass = lax.fori_loop(
        first_block, last_block + 1, running, (jnp.full((T,), -1e30, f32), jnp.zeros((T,), f32))
    )
    log_mass = peak + jnp.log(mass)

    def weighted(index, total):
        _, vb, seen, scores = key_block(index)
        probs = jnp.where(seen, jnp.exp(scores - log_mass[:, None]), 0.0).astype(bf16)
        return total + dot(probs, vb, 1, 0)

    attended = lax.fori_loop(first_block, last_block + 1, weighted, jnp.zeros((T, HD), f32))
    att_low = attended.astype(bf16)

    def plane_sum(part):
        mine = lax.psum_scatter(part.astype(bf16), "p", scatter_dimension=0, tiled=True)
        return lax.psum(mine, "head").astype(f32)

    both_low = jnp.concatenate([ssm_low, att_low], axis=1)
    hidden = layer_input + plane_sum(dot(both_low, wb, 1, 1))
    r2 = lax.rsqrt(jnp.mean(hidden * hidden, axis=-1, keepdims=True) + norm_eps)
    second = lax.all_gather((hidden * r2 * ffn_gain).astype(bf16), "p", axis=0, tiled=True)
    pc = dot(second, wc, 1, 0)
    ff = pc.shape[1] // 2
    gate_pre, up_pre = pc[:, :ff], pc[:, ff:]
    s_gate = jax.nn.silu(gate_pre)
    act_low = (s_gate * up_pre).astype(bf16)
    layer_out = hidden + plane_sum(dot(act_low, wd, 1, 1))

    grad_d = dot(out_low, act_low, 0, 0)
    d_act = dot(out_low, wd, 1, 0)
    gu_low = jnp.concatenate([d_act * up_pre * d_silu(gate_pre), d_act * s_gate], axis=1).astype(bf16)
    grad_c = dot(second, gu_low, 0, 0)
    d_second = plane_sum(dot(gu_low, wc, 1, 1))
    u2 = d_second * ffn_gain
    d_hidden = cotangent + r2 * u2 - hidden * r2**3 * jnp.mean(u2 * hidden, axis=-1, keepdims=True)
    grad_ffn = jnp.sum(d_second * hidden * r2, axis=0)
    branch = lax.all_gather(d_hidden.astype(bf16), "p", axis=0, tiled=True)
    grad_b = dot(branch, both_low, 0, 0)
    d_both = dot(branch, wb, 1, 0)
    d_norm_s, d_att = d_both[:, :chan], d_both[:, chan:].astype(bf16)

    grad_gain_s = jnp.sum(d_norm_s * gated * r_s, axis=0)
    u_s = d_norm_s * gain_s
    d_gated = r_s * u_s - gated * r_s**3 * head_mean(u_s * gated)
    d_z = d_gated * ssm * d_silu(z_part)
    dy = by_head(d_gated * sz)
    dy_in = dy * decay_in[..., None]
    from_chunk = exact("chip,cin->chpn", dy_in, c_rows)
    zero_state = jnp.zeros((heads, P_SIZE, N), f32)
    g = zero_state
    leaving = [None] * nc
    for c in reversed(range(nc)):
        leaving[c] = g
        g = g * dtot[c][:, None, None] + from_chunk[c]
    every_grad = lax.all_gather(g.astype(bf16), "z", axis=0)
    after = zero_state
    for k in reversed(range(1, planes)):
        new = after * factors[k][:, None, None] + every_grad[k].astype(f32)
        after = jnp.where(k > zi, new, after)
    scale_c = jnp.ones((heads,), f32)
    d_state = [None] * nc
    for c in reversed(range(nc)):
        d_state[c] = leaving[c] + after * scale_c[:, None, None]
        scale_c = scale_c * dtot[c]
    d_state = jnp.stack(d_state)
    d_mix = exact("chip,chjp->chij", dy, driven)
    d_inter = jnp.sum(weights * d_mix, axis=1)
    d_c = exact("cij,cjn->cin", d_inter, b_rows) + exact("chip,chpn->cin", dy_in, state_in)
    closed = driven * closing[..., None]
    d_b = exact("cij,cin->cjn", d_inter, c_rows) + exact("chpn,chjp->cjn", d_state, closed)
    d_driven = exact("chij,chip->chjp", mix, dy) + closing[..., None] * exact("chpn,cjn->chjp", d_state, b_rows)
    d_closing = jnp.sum(closed * exact("chpn,cjn->chjp", d_state, b_rows), axis=-1)
    d_cs = jnp.sum(dy * y_scan, axis=-1) - jnp.sum(driven * d_driven, axis=-1)
    d_total = jnp.sum(d_closing, axis=-1) + dtot * jnp.sum(d_state * state_in, axis=(2, 3))
    d_la = exact("ji,chj->chi", lower, d_cs) + d_total[:, :, None]
    d_step = jnp.sum(d_driven * xh, axis=-1)
    dx = by_token(d_driven * step_h[..., None] + skip[None, :, None, None] * dy)
    grad_skip = jnp.sum(dy * xh, axis=(0, 2, 3))
    d_raw = (d_step - jnp.exp(rates)[None, :, None] * d_la).transpose(0, 2, 1).reshape(T, heads)
    d_raw = d_raw * jax.nn.sigmoid(step_raw + bias)
    grad_bias = jnp.sum(d_raw, axis=0)
    grad_rates = jnp.sum(d_la * la_h, axis=(0, 2))
    d_bc_all = jnp.concatenate([d_b.reshape(T, N), d_c.reshape(T, N)], axis=1).astype(bf16)
    d_bc = lax.psum_scatter(d_bc_all, ("head", "p"), scatter_dimension=1, tiled=True).astype(f32)
    pad_g, grad_conv_inner = conv_back(dx * d_silu(cv_x), pad_inner, taps_inner, starts, places)
    pad_h, grad_conv_state = conv_back(d_bc * d_silu(cv_bc), pad_bc, taps_state, starts, places)
    next_g, next_h = shifted((pad_g[:edge], pad_h[:edge]), "z", -1)
    d_inner_pre = pad_g[edge:] + jnp.pad(next_g, ((T - edge, 0), (0, 0)))
    d_bc_pre = pad_h[edge:] + jnp.pad(next_h, ((T - edge, 0), (0, 0)))

    balance = jnp.sum(d_att.astype(f32) * attended, axis=-1, keepdims=True)

    def grads(index, carry):
        d_query, d_keys, d_values = carry
        kb, vb, seen, scores = key_block(index)
        probs = jnp.where(seen, jnp.exp(scores - log_mass[:, None]), 0.0)
        d_scores = (probs * (dot(d_att, vb, 1, 1) - balance)).astype(bf16)
        d_query = d_query + dot(d_scores, kb, 1, 0)
        d_keys = lax.dynamic_update_slice_in_dim(d_keys, dot(d_scores, query, 0, 0), index * key_len, 0)
        d_values = lax.dynamic_update_slice_in_dim(d_values, dot(probs.astype(bf16), d_att, 0, 0), index * key_len, 0)
        return d_query, d_keys, d_values

    zero_keys = jnp.zeros((total_tokens, HD), f32)
    d_query, d_keys, d_values = lax.fori_loop(
        first_block, last_block + 1, grads, (jnp.zeros((T, HD), f32), zero_keys, zero_keys)
    )
    dk_cut = d_keys.astype(bf16).reshape(planes, T, 2, G, quarter_half).transpose(0, 3, 1, 2, 4)
    dv_cut = d_values.astype(bf16).reshape(planes, T, G, 2 * quarter_half).transpose(0, 2, 1, 3)
    dkv = jnp.concatenate([dk_cut.reshape(planes, G, T, -1), dv_cut], axis=-1).reshape(planes * G, T, -1)
    dkv = jnp.sum(lax.all_to_all(dkv, ("z", "p"), 0, 0, tiled=True).astype(f32), axis=0)
    d_q = turn(d_query, cos_q, -sin_q) * scale
    d_k = turn(dkv[:, : 2 * quarter_half], cos_k, -sin_k)
    d_v = dkv[:, 2 * quarter_half :]

    da_low = jnp.concatenate(
        [d_z, d_inner_pre, d_q, d_bc_pre, d_k, d_v, d_raw, jnp.zeros((T, pad), f32)], axis=1
    ).astype(bf16)
    grad_a = dot(first, da_low, 0, 0)
    d_first = plane_sum(dot(da_low, wa, 1, 1))
    u1 = d_first * mixer_gain
    grad_input = d_hidden + r1 * u1 - layer_input * r1**3 * jnp.mean(u1 * layer_input, axis=-1, keepdims=True)
    grad_mixer = jnp.sum(d_first * layer_input * r1, axis=0)

    ga, gb, gc, gd = (scatter(g) for g in (grad_a, grad_b, grad_c, grad_d))
    g_z, g_x, g_q, g_bc, g_k, g_v, g_dt = (ga[:, :, a : a + s] for a, s in zip(a_at, a_sizes))
    g_k = jnp.moveaxis(g_k.reshape(rows, G, 2, quarter_half), 1, 2)
    g_bc = lax.all_gather(g_bc.reshape(rows, -1).astype(bf16), "head", axis=1, tiled=True).astype(f32)

    small = [grad_conv_inner, grad_conv_state, grad_rates, grad_bias, grad_skip, grad_gain_s]
    flat = jnp.concatenate([s.reshape(-1) for s in small])
    every = jnp.sum(lax.all_gather(flat, ("z", "p", "head")).reshape(planes, G, cores, -1), axis=0)
    mine = lax.dynamic_index_in_dim(every, hi, 1, False)
    at = [0]
    for s in small:
        at.append(at[-1] + s.size)
    pieces = [mine[:, a:b] for a, b in zip(at, at[1:])]
    o_conv_inner = jnp.moveaxis(pieces[0].reshape(G, K, chan), 0, 1).reshape(K, G * chan)
    o_conv_state = every[:, :, at[1] : at[2]].reshape(G, cores, K, bcs).transpose(2, 1, 0, 3).reshape(K, 2 * N)
    gains = lax.psum_scatter(jnp.stack([grad_mixer, grad_ffn]), ("z", "p"), scatter_dimension=1, tiled=True)

    def whole(g):
        return g.reshape(rows, -1)

    return (
        layer_out, grad_input, gains[0], gains[1],
        whole(g_z), whole(g_x), g_bc, whole(g_dt), whole(g_q), whole(g_k), whole(g_v),
        whole(gb[:, :, chan:]), whole(gb[:, :, :chan]),
        whole(gc[:, :, :ff]), whole(gc[:, :, ff:]), whole(gd),
        o_conv_inner, o_conv_state,
        pieces[2].reshape(-1), pieces[3].reshape(-1), pieces[4].reshape(-1), pieces[5].reshape(-1),
    )


def solution(mesh):
    seq, cores = mesh.shape["seq"], mesh.shape["head"]
    planes = Mesh(mesh.devices.reshape(seq // G, G, cores), ("z", "p", "head"))
    s = ("z", "p")
    both, row, head, whole = P(s, "head"), P(s, None), P("head"), P()
    placed = (
        row, P(s), whole, whole, both, both, row, both, both, both, both, both, both, both, both, both,
        P(None, "head"), whole, head, head, head, head, row,
    )
    return jax.shard_map(
        on_device,
        mesh=planes,
        in_specs=placed,
        out_specs=(
            row, row, P(s), P(s), both, both, row, both, both, both, both, both, both, both, both, both,
            P(None, "head"), whole, head, head, head, head,
        ),
        check_vma=False,
    )
```

time: 3810 us -> 1600 us (0.42)
  waiting for transfers between devices: 2900 us -> 1000 us
  blocking collectives: 242 us -> 126 us
  matrix products: 233 us -> 150 us
  other arithmetic: 159 us -> 94.9 us
    reduce_scatter x12 -> x8, waiting for transfers between devices: 2070 us -> 302 us  [the longest x4 214 us: plane_sum(): lax.psum_scatter(part.astype(bf16), 'p', scatter_dimension=0, tiled=True)]
    all_gather x13 -> x10, waiting for transfers between devices: 737 us -> 385 us  [the longest x4 206 us: gather(): return lax.all_gather(w.reshape(G * rows, -1), 'z', axis=0, tiled=True)]
    unnamed x28 -> x27, waiting for transfers between devices: 6.01 us -> 183 us
    all_gather x4 -> x5, blocking collectives: 165 us -> 59.8 us  [the longest x1 22.6 us: on_device(): everyone = lax.all_gather(state.astype(bf16), 'z', axis=0)]
    dynamic_update_slice x30 -> x0, local copies, waits for them, and re-layouts: 84.4 us -> none  [zero_part(): final, outputs = lax.scan(ssd_block, state_zero, pieces)]
    dot_general x70 -> x40, matrix products: 230 us -> 150 us  [the longest x26 108 us: dot(): lax.dot_general(a, b, (((ca,), (cb,)), ((), ())), preferred_element_type=...]
    ppermute x4, waiting for transfers between devices: 5.89 us -> 85.2 us  [shifted(): return lax.ppermute(block, axis, route)]
    unnamed x1 -> x0, blocking collectives: 77.2 us -> none
  transfers between devices with their start and end apart: 33 -> 33, of which waited for: 27 -> 21; matrix products, arithmetic and copies ran while one was open for 9% -> 18% of each run, Pallas kernels for 0% -> 0%
where the time goes in v1:
time: 1600 us; the launch traced here: 1590 us
  waiting for transfers between devices  1000 us (62%)
  local copies, waits for them, and re-layouts  155 us (10%)
  matrix products  150 us (9%)
  blocking collectives  126 us (8%)
  other arithmetic  94.9 us (6%)
  starting transfers between devices  43.1 us (3%)
  between operations  20 us (1%)
    reduce_scatter x4, waiting for transfers between devices, plane_sum(): lax.psum_scatter(part.astype(bf16), 'p', scatter_dimension=0, tiled=True)  214 us
    all_gather x4, waiting for transfers between devices, gather(): return lax.all_gather(w.reshape(G * rows, -1), 'z', axis=0, tiled=True)  206 us
    unnamed x27, waiting for transfers between devices  183 us
    dot_general x26, matrix products, dot(): lax.dot_general(a, b, (((ca,), (cb,)), ((), ())), preferred_element_type=...  108 us
    reduce_scatter x4, waiting for transfers between devices, scatter(): lax.psum_scatter(grad.astype(bf16), 'z', scatter_dimension=0, tiled=True)  87.6 us
    ppermute x4, waiting for transfers between devices, shifted(): return lax.ppermute(block, axis, route)  85.2 us
    all_to_all x3, blocking collectives, gather(): w = lax.all_to_all(w, 'p', 0, 0, tiled=True)  56.1 us
    all_gather x1, waiting for transfers between devices, on_device(): branch = lax.all_gather(d_hidden.astype(bf16), 'p', axis=0, tiled=True)  53.8 us
  transfers between devices with their start and end apart: 33, of which 21 were waited for; matrix products, arithmetic and copies ran while one was open for 18% of the time, Pallas kernels for 0%

profile of v1, /device:TPU:0, one launch (start us, length us, event | category | flops | bytes accessed | tf_op | source)
XLA Modules:
  0.0 1589.0 jit_solution(10721748335333225015)
XLA Ops:
  16.2 6.6 concatenate.53
  22.8 27.0 %all_to_all.45 = bf16[4,128,1152]{1,2,0:T(8,128)(2,1)} all-to-all(bf16[4,128,1152]{1,2,0:T(8,128)(2,1)S(1)} %bitcast.411), channel_id=1, replica_groups=mesh['z'=4,'p'=4,'head'=2] {'p'}, dimensions={0} | all-to-all | bytes 2359296 | tf_op jit(solution)/shard_map/all_to_all | solution.py:119
  52.2 8.0 all-gather.3
  61.1 18.8 %all-gather.15.cloned.1.call-done = bf16[1024,2048]{1,0:T(8,128)(2,1)} async-done(((bf16[256,2048]{1,0:T(8,128)(2,1)}), bf16[1024,2048]{1,0:T(8,128)(2,1)}) %all-gather.15.cloned.1.call-update) | async-done | bytes 4194320 | tf_op jit(solution)/shard_map/all_gather | solution.py:134
  79.9 91.6 %all-gather.17.cloned.1.call-done = bf16[2048,1152]{1,0:T(8,128)(2,1)} async-done(((bf16[512,1152]{1,0:T(8,128)(2,1)}), bf16[2048,1152]{1,0:T(8,128)(2,1)}) %all-gather.17.cloned.1.call-update) | async-done | bytes 4718608 | tf_op jit(solution)/shard_map/all_gather | solution.py:120
  171.5 8.7 fusion.183
  218.6 7.7 all-gather
  247.1 22.6 %all_gather.62 = bf16[4,6,64,256]{3,2,1,0:T(8,128)(2,1)S(1)} all-gather(bf16[1,6,64,256]{3,2,1,0:T(8,128)(2,1)S(1)} %get-tuple-element.817), channel_id=1, replica_groups=mesh['z'=4,'p'=4,'head'=2] {'z'}, dimensions={0}, use_global_device_ids=true | all-gather | bytes 983040 | tf_op jit(solution)/shard_map/all_gather | solution.py:190
  270.1 6.5 fusion.38
  302.6 5.3 copy.718
  331.5 12.1 all-gather.21.cloned.1.call-done
  343.6 6.2 convolution_convert_fusion.3
  349.9 51.5 %reduce-scatter.15.cloned.1.call-done = bf16[256,2048]{1,0:T(8,128)(2,1)} async-done(((bf16[1024,2048]{1,0:T(8,128)(2,1)}), bf16[256,2048]{1,0:T(8,128)(2,1)}) %reduce-scatter.15.cloned.1.call-update) | async-done | bytes 1048592 | tf_op jit(solution)/shard_map/reduce_scatter | solution.py:255
  404.8 17.6 %all_to_all.46 = bf16[4,128,1024]{1,2,0:T(8,128)(2,1)} all-to-all(bf16[4,128,1024]{1,2,0:T(8,128)(2,1)S(1)} %maximum_bitcast_fusion), channel_id=1, replica_groups=mesh['z'=4,'p'=4,'head'=2] {'p'}, dimensions={0} | all-to-all | bytes 2097152 | tf_op jit(solution)/shard_map/all_to_all | solution.py:119
  429.2 11.6 all_to_all.47
  443.3 64.3 %all-gather.25.cloned.1.call-done = bf16[2048,1024]{1,0:T(8,128)(2,1)} async-done(((bf16[512,1024]{1,0:T(8,128)(2,1)}), bf16[2048,1024]{1,0:T(8,128)(2,1)}) %all-gather.25.cloned.1.call-update) | async-done | bytes 4194320 | tf_op jit(solution)/shard_map/all_gather | solution.py:120
  507.6 53.7 %all-gather.23.cloned.1.call-done = bf16[1024,2048]{1,0:T(8,128)(2,1)} async-done(((bf16[256,2048]{1,0:T(8,128)(2,1)}), bf16[1024,2048]{1,0:T(8,128)(2,1)}) %all-gather.23.cloned.1.call-update) | async-done | bytes 4194320 | tf_op jit(solution)/shard_map/all_gather | solution.py:261
  561.3 10.1 fusion.185
  571.3 37.9 %all-gather.27.cloned.1.call-done = bf16[2048,512]{1,0:T(8,128)(2,1)} async-done(((bf16[512,512]{1,0:T(8,128)(2,1)}), bf16[2048,512]{1,0:T(8,128)(2,1)}) %all-gather.27.cloned.1.call-update) | async-done | bytes 2097168 | tf_op jit(solution)/shard_map/all_gather | solution.py:120
  609.2 53.3 %all-gather.29.cloned.1.call-done = bf16[1024,2048]{1,0:T(8,128)(2,1)} async-done(((bf16[256,2048]{1,0:T(8,128)(2,1)}), bf16[1024,2048]{1,0:T(8,128)(2,1)}) %all-gather.29.cloned.1.call-update) | async-done | bytes 4194320 | tf_op jit(solution)/shard_map/all_gather | solution.py:135
  662.5 8.2 multiply_convert_fusion.1
  672.1 6.2 convolution_convert_fusion.5
  678.4 52.8 %reduce-scatter.19.cloned.1.call-done = bf16[256,2048]{1,0:T(8,128)(2,1)} async-done(((bf16[1024,2048]{1,0:T(8,128)(2,1)}), bf16[256,2048]{1,0:T(8,128)(2,1)}) %reduce-scatter.19.cloned.1.call-update) | async-done | bytes 1048592 | tf_op jit(solution)/shard_map/reduce_scatter | solution.py:255
  731.2 22.0 %all-reduce.19.cloned.1.call-done = bf16[256,2048]{1,0:T(8,128)(2,1)} async-done(((bf16[256,2048]{1,0:T(8,128)(2,1)}), bf16[256,2048]{1,0:T(8,128)(2,1)}) %all-reduce.19.cloned.1.call-update) | async-done | bytes 1048592 | tf_op jit(solution)/shard_map/psum | solution.py:256
  758.0 53.8 %all-gather.31.cloned.1.call-done = bf16[1024,2048]{1,0:T(8,128)(2,1)} async-done(((bf16[256,2048]{1,0:T(8,128)(2,1)}), bf16[1024,2048]{1,0:T(8,128)(2,1)}) %all-gather.31.cloned.1.call-update) | async-done | bytes 4194320 | tf_op jit(solution)/shard_map/all_gather | solution.py:277
  811.8 5.2 fusion.186
  832.4 6.0 fusion.126
  843.4 6.4 multiply_reduce_fusion.1
  854.9 19.6 %all_gather.71 = bf16[4,6,64,256]{3,2,1,0:T(8,128)(2,1)S(1)} all-gather(bf16[1,6,64,256]{3,2,1,0:T(8,128)(2,1)S(1)} %get-tuple-element.799), channel_id=1, replica_groups=mesh['z'=4,'p'=4,'head'=2] {'z'}, dimensions={0}, use_global_device_ids=true | all-gather | bytes 983040 | tf_op jit(solution)/shard_map/all_gather | solution.py:295
  884.0 6.2 fusion.40
  890.2 9.5 convolution_convert_fusion.4
  899.9 6.2 convolution_convert_fusion.7
  917.3 6.6 fusion.70
  946.5 6.1 convolution_convert_fusion.2
  955.2 10.8 while.41
  974.9 19.3 %all-to-all-start.4 = ((bf16[16,1024,64]{1,2,0:T(8,128)(2,1)}), bf16[16,1024,64]{1,2,0:T(8,128)(2,1)S(1)}, u32[]{:S(2)}, u32[]{:S(2)}) async-start(bf16[16,1024,64]{1,2,0:T(8,128)(2,1)} %pad_maximum_fusion.1), calls=%async_computation.7 | async-start | bytes 4194304 | tf_op jit(solution)/shard_map/all_to_all | solution.py:350
  1004.2 45.4 %collective-permute-done.2 = f32[3,384]{1,0:T(4,128)S(1)} collective-permute-done((f32[3,384]{1,0:T(4,128)S(1)}, f32[3,384]{1,0:T(4,128)S(1)}, u32[]{:S(2)}, u32[]{:S(2)}) %collective-permute-start.2) | collective-permute-done | bytes 4640 | tf_op jit(solution)/shard_map/ppermute | solution.py:36
  1053.8 39.9 %collective-permute-done.3 = f32[3,64]{1,0:T(4,128)S(1)} collective-permute-done((f32[3,64]{1,0:T(4,128)S(1)}, f32[3,64]{1,0:T(4,128)S(1)}, u32[]{:S(2)}, u32[]{:S(2)}) %collective-permute-start.3) | collective-permute-done | bytes 800 | tf_op jit(solution)/shard_map/ppermute | solution.py:36
  1102.0 9.5 convolution_convert_fusion.1
  1111.6 10.6 convolution_convert_fusion
  1123.4 10.6 all_to_all.48
  1138.9 9.0 all-to-all-done.7
  1154.0 110.1 %all-reduce.21.cloned.1.call-done = f32[70208]{0:T(1024)} async-done(((f32[70208]{0:T(1024)}), f32[70208]{0:T(1024)}) %all-reduce.21.cloned.1.call-update) | async-done | bytes 280848
  1266.9 53.7 %reduce-scatter.17.cloned.1.call-done = bf16[256,2048]{1,0:T(8,128)(2,1)} async-done(((bf16[1024,2048]{1,0:T(8,128)(2,1)}), bf16[256,2048]{1,0:T(8,128)(2,1)}) %reduce-scatter.17.cloned.1.call-update) | async-done | bytes 1048592 | tf_op jit(solution)/shard_map/reduce_scatter | solution.py:255
  1320.5 56.0 %reduce-scatter.21.cloned.1.call-done = bf16[256,2048]{1,0:T(8,128)(2,1)} async-done(((bf16[1024,2048]{1,0:T(8,128)(2,1)}), bf16[256,2048]{1,0:T(8,128)(2,1)}) %reduce-scatter.21.cloned.1.call-update) | async-done | bytes 1048592 | tf_op jit(solution)/shard_map/reduce_scatter | solution.py:255
  1376.5 87.6 %reduce-scatter.23.cloned.1.call-done = bf16[512,1152]{1,0:T(8,128)(2,1)} async-done(((bf16[2048,1152]{1,0:T(8,128)(2,1)}), bf16[512,1152]{1,0:T(8,128)(2,1)}) %reduce-scatter.23.cloned.1.call-update) | async-done | bytes 1179664 | tf_op jit(solution)/shard_map/reduce_scatter | solution.py:123
  1475.4 10.8 all-to-all-done.5
  1507.4 72.3 %reduce-scatter.33.cloned.1.call-done = f32[128,2]{1,0:T(8,128)} async-done(((f32[2048,2]{1,0:T(8,128)}), f32[128,2]{1,0:T(8,128)}) %reduce-scatter.33.cloned.1.call-update) | async-done | bytes 1040
  (689 shorter events, 304.7 us)
Async XLA Ops:
  7.2 72.7 %all-gather.15.cloned.1.call-start = ((), (), s32[]{:S(2)}) async-start(), calls=%async_computation.19 | async-start | bytes 5242880 | tf_op jit(solution)/shard_map/all_gather | solution.py:134
  11.9 159.6 %all-gather.17.cloned.1.call-start = ((), (), s32[]{:S(2)}) async-start(), calls=%async_computation.20 | async-start | bytes 5898240 | tf_op jit(solution)/shard_map/all_gather | solution.py:120
  52.1 187.6 %all-gather.19.cloned.1.call-start = ((), (), s32[]{:S(2)}) async-start(), calls=%async_computation.21 | async-start | bytes 1179648 | tf_op jit(solution)/shard_map/all_gather | solution.py:148
  60.2 121.3 %copy-start.152 = (f32[64]{0:T(128)}, f32[64]{0:T(128)S(1)}, u32[]{:S(2)}) copy-start(f32[64]{0:T(128)S(1)} %multiply_power_fusion) | copy-start | bytes 772
  61.0 124.7 %copy-start.116 = (f32[64]{0:T(128)}, f32[64]{0:T(128)S(1)}, u32[]{:S(2)}) copy-start(f32[64]{0:T(128)S(1)} %get-tuple-element.891) | copy-start | bytes 772
  61.0 124.7 %copy-start.118 = (f32[64]{0:T(128)}, f32[64]{0:T(128)S(1)}, u32[]{:S(2)}) copy-start(f32[64]{0:T(128)S(1)} %get-tuple-element.892) | copy-start | bytes 772
  61.0 124.7 %copy-start.120 = (f32[64]{0:T(128)}, f32[64]{0:T(128)S(1)}, u32[]{:S(2)}) copy-start(f32[64]{0:T(128)S(1)} %get-tuple-element.893) | copy-start | bytes 772
  61.0 124.7 %copy-start.122 = (f32[64]{0:T(128)}, f32[64]{0:T(128)S(1)}, u32[]{:S(2)}) copy-start(f32[64]{0:T(128)S(1)} %get-tuple-element.894) | copy-start | bytes 772
  61.0 132.2 %copy-start.61 = (f32[1024]{0:T(1024)}, f32[1024]{0:T(1024)S(1)}, u32[]{:S(2)}) copy-start(f32[1024]{0:T(1024)S(1)} %subtract_convert_fusion) | copy-start | bytes 12292
  61.1 124.7 %copy-start.69 = (pred[1024]{0:T(1024)(128)(4,1)}, pred[1024]{0:T(1024)(128)(4,1)S(1)}, u32[]{:S(2)}) copy-start(pred[1024]{0:T(1024)(128)(4,1)S(1)} %get-tuple-element.879) | copy-start | bytes 3076
  61.1 124.7 %copy-start.72 = (pred[1024]{0:T(1024)(128)(4,1)}, pred[1024]{0:T(1024)(128)(4,1)S(1)}, u32[]{:S(2)}) copy-start(pred[1024]{0:T(1024)(128)(4,1)S(1)} %get-tuple-element.880) | copy-start | bytes 3076
  61.1 169.5 %copy-start.65 = (pred[1024]{0:T(1024)(128)(4,1)}, pred[1024]{0:T(1024)(128)(4,1)S(1)}, u32[]{:S(2)}) copy-start(pred[1024]{0:T(1024)(128)(4,1)S(1)} %get-tuple-element.877) | copy-start | bytes 3076
  61.1 169.5 %copy-start.67 = (pred[1024]{0:T(1024)(128)(4,1)}, pred[1024]{0:T(1024)(128)(4,1)S(1)}, u32[]{:S(2)}) copy-start(pred[1024]{0:T(1024)(128)(4,1)S(1)} %get-tuple-element.878) | copy-start | bytes 3076
  180.3 5.4 collective-permute-start
  189.4 113.2 %all-gather.33.cloned.1.call-start = ((), (), s32[]{:S(2)}) async-start(), calls=%async_computation.38 | async-start | bytes 4456448 | tf_op jit(solution)/shard_map/all_gather | solution.py:218
  197.6 14.8 all-to-all-start.1
  201.4 142.2 %all-gather.21.cloned.1.call-start = ((), (), s32[]{:S(2)}) async-start(), calls=%async_computation.22 | async-start | bytes 2621440 | tf_op jit(solution)/shard_map/all_gather | solution.py:120
  206.4 93.3 %copy-start.77 = (f32[384]{0:T(512)}, f32[384]{0:T(512)S(1)}, u32[]{:S(2)}) copy-start(f32[384]{0:T(512)S(1)} %dynamic_slice.46) | copy-start | bytes 4612
  213.4 188.0 %reduce-scatter.15.cloned.1.call-start = ((), (), s32[]{:S(2)}) async-start(), calls=%async_computation.23 | async-start | bytes 5242880 | tf_op jit(solution)/shard_map/reduce_scatter | solution.py:255
  216.2 14.4 collective-permute-start.1
  349.8 52.7 %copy-start.45 = (bf16[128,2048]{1,0:T(8,128)(2,1)S(1)}, bf16[128,2048]{1,0:T(8,128)(2,1)}, u32[]{:S(2)}) copy-start(bf16[128,2048]{1,0:T(8,128)(2,1)} %param.43) | copy-start | bytes 1572868
  349.8 74.9 %all-reduce.17.cloned.1.call-start = ((), (), s32[]{:S(2)}) async-start(), calls=%async_computation.24 | async-start | bytes 2097152 | tf_op jit(solution)/shard_map/psum | solution.py:256
  401.4 106.2 %all-gather.25.cloned.1.call-start = ((), (), s32[]{:S(2)}) async-start(), calls=%async_computation.26 | async-start | bytes 5242880 | tf_op jit(solution)/shard_map/all_gather | solution.py:120
  424.6 136.7 %all-gather.23.cloned.1.call-start = ((), (), s32[]{:S(2)}) async-start(), calls=%async_computation.25 | async-start | bytes 5242880 | tf_op jit(solution)/shard_map/all_gather | solution.py:261
  428.9 180.4 %all-gather.27.cloned.1.call-start = ((), (), s32[]{:S(2)}) async-start(), calls=%async_computation.27 | async-start | bytes 2621440 | tf_op jit(solution)/shard_map/all_gather | solution.py:120
  441.8 220.7 %all-gather.29.cloned.1.call-start = ((), (), s32[]{:S(2)}) async-start(), calls=%async_computation.29 | async-start | bytes 5242880 | tf_op jit(solution)/shard_map/all_gather | solution.py:135
  443.1 288.1 %reduce-scatter.19.cloned.1.call-start = ((), (), s32[]{:S(2)}) async-start(), calls=%async_computation.30 | async-start | bytes 5242880 | tf_op jit(solution)/shard_map/reduce_scatter | solution.py:255
  678.3 74.9 %copy-start.5 = (f32[256,2048]{1,0:T(8,128)S(1)}, f32[256,2048]{1,0:T(8,128)}, u32[]{:S(2)}) copy-start(f32[256,2048]{1,0:T(8,128)} %copy-done.4) | copy-start | bytes 6291460
  678.3 74.9 %all-reduce.19.cloned.1.call-start = ((), (), s32[]{:S(2)}) async-start(), calls=%async_computation.31 | async-start | bytes 2097152 | tf_op jit(solution)/shard_map/psum | solution.py:256
  731.2 80.6 %all-gather.31.cloned.1.call-start = ((), (), s32[]{:S(2)}) async-start(), calls=%async_computation.32 | async-start | bytes 5242880 | tf_op jit(solution)/shard_map/all_gather | solution.py:277
  757.7 182.1 %reduce-scatter.31.cloned.1.call-start = ((), (), s32[]{:S(2)}) async-start(), calls=%async_computation.40 | async-start | bytes 1179648
  883.8 238.5 %reduce-scatter.29.cloned.1.call-start = ((), (), s32[]{:S(2)}) async-start(), calls=%async_computation.37 | async-start | bytes 2621440 | tf_op jit(solution)/shard_map/reduce_scatter | solution.py:123
  890.2 243.8 %reduce-scatter.27.cloned.1.call-start = ((), (), s32[]{:S(2)}) async-start(), calls=%async_computation.36 | async-start | bytes 5242880 | tf_op jit(solution)/shard_map/reduce_scatter | solution.py:123
  899.8 248.3 %reduce-scatter.25.cloned.1.call-start = ((), (), s32[]{:S(2)}) async-start(), calls=%async_computation.35 | async-start | bytes 2621440 | tf_op jit(solution)/shard_map/reduce_scatter | solution.py:123
  906.1 358.0 %all-reduce.21.cloned.1.call-start = ((), (), s32[]{:S(2)}) async-start(), calls=%async_computation.39 | async-start | bytes 565248
  946.0 374.5 %reduce-scatter.17.cloned.1.call-start = ((), (), s32[]{:S(2)}) async-start(), calls=%async_computation.28 | async-start | bytes 5242880 | tf_op jit(solution)/shard_map/reduce_scatter | solution.py:255
  974.9 119.6 %all-to-all-start.4 = ((bf16[16,1024,64]{1,2,0:T(8,128)(2,1)}), bf16[16,1024,64]{1,2,0:T(8,128)(2,1)S(1)}, u32[]{:S(2)}, u32[]{:S(2)}) async-start(bf16[16,1024,64]{1,2,0:T(8,128)(2,1)} %pad_maximum_fusion.1), calls=%async_computation.7 | async-start | bytes 4194304 | tf_op jit(solution)/shard_map/all_to_all | solution.py:350
  994.2 382.2 %reduce-scatter.21.cloned.1.call-start = ((), (), s32[]{:S(2)}) async-start(), calls=%async_computation.33 | async-start | bytes 5242880 | tf_op jit(solution)/shard_map/reduce_scatter | solution.py:255
  997.1 52.4 %collective-permute-start.2 = (f32[3,384]{1,0:T(4,128)S(1)}, f32[3,384]{1,0:T(4,128)S(1)}, u32[]{:S(2)}, u32[]{:S(2)}) collective-permute-start(f32[3,384]{1,0:T(4,128)S(1)} %pad_add_fusion.2), channel_id=1, source_target_pairs={{8,0},{16,8},{24,16},{9,1},{17,9},{25,17},{10,2},{18,10},{26,18},{... | collective-permute-start | bytes 13832 | tf_op jit(solution)/shard_map/ppermute | solution.py:36
  1052.1 41.6 %collective-permute-start.3 = (f32[3,64]{1,0:T(4,128)S(1)}, f32[3,64]{1,0:T(4,128)S(1)}, u32[]{:S(2)}, u32[]{:S(2)}) collective-permute-start(f32[3,64]{1,0:T(4,128)S(1)} %pad_add_fusion.3), channel_id=1, source_target_pairs={{8,0},{16,8},{24,16},{9,1},{17,9},{25,17},{10,2},{18,10},{26,18},{... | collective-permute-start | bytes 2312 | tf_op jit(solution)/shard_map/ppermute | solution.py:36
  1111.5 352.6 %reduce-scatter.23.cloned.1.call-start = ((), (), s32[]{:S(2)}) async-start(), calls=%async_computation.34 | async-start | bytes 5898240 | tf_op jit(solution)/shard_map/reduce_scatter | solution.py:123
  1133.9 13.9 all-to-all-start.7
  1148.1 318.4 %all-to-all-start.6 = ((bf16[4,128,512]{2,1,0:T(8,128)(2,1)}), bf16[4,128,512]{2,1,0:T(8,128)(2,1)S(1)}, u32[]{:S(2)}, u32[]{:S(2)}) async-start(bf16[4,128,512]{2,1,0:T(8,128)(2,1)} %bitcast.446), calls=%async_computation.12 | async-start | bytes 1048576 | tf_op jit(solution)/shard_map/all_to_all | solution.py:124
  1151.6 347.2 %all-reduce.23.cloned.1.call-start = ((), (), s32[]{:S(2)}) async-start(), calls=%async_computation.42 | async-start | bytes 4194304 | tf_op jit(solution)/shard_map/psum | solution.py:256
  1265.5 201.0 %copy-start.57 = (f32[4,2,2194]{2,1,0:T(2,128)}, f32[4,2,2194]{2,1,0:T(2,128)S(1)}, u32[]{:S(2)}) copy-start(f32[4,2,2194]{2,1,0:T(2,128)S(1)} %reduce_sum.308) | copy-start | bytes 210628
  1466.5 19.7 %all-to-all-start.5 = ((bf16[4,128,1152]{1,2,0:T(8,128)(2,1)}), bf16[4,128,1152]{1,2,0:T(8,128)(2,1)}, u32[]{:S(2)}, u32[]{:S(2)}) async-start(bf16[4,128,1152]{1,2,0:T(8,128)(2,1)} %copy.765), calls=%async_computation.10 | async-start | bytes 2359296 | tf_op jit(solution)/shard_map/all_to_all | solution.py:124
  1470.8 109.0 %reduce-scatter.33.cloned.1.call-start = ((), (), s32[]{:S(2)}) async-start(), calls=%async_computation.41 | async-start | bytes 1114112
  1505.8 76.1 %copy-start.1 = (bf16[128,512]{1,0:T(8,128)(2,1)S(1)}, bf16[128,512]{1,0:T(8,128)(2,1)}, u32[]{:S(2)}) copy-start(bf16[128,512]{1,0:T(8,128)(2,1)} %param.35) | copy-start | bytes 393220
  (151 other events, 1277.4 us)
Sparse Core Ops, SparseCore 0:
  12.0 67.8 all-gather.14
  82.1 89.4 all-gather.16
  189.6 24.2 all-gather.18
  217.1 79.8 all-gather.32
  299.0 44.5 all-gather.20
  349.9 51.4 reduce-scatter.14
  403.9 19.5 all-reduce.16
  425.6 81.9 all-gather.24
  510.0 51.2 all-gather.22
  563.3 45.9 all-gather.26
  611.1 51.4 all-gather.28
  678.4 52.6 reduce-scatter.18
  733.6 19.5 all-reduce.18
  757.8 53.8 all-gather.30
  883.9 34.3 reduce-scatter.30
  920.5 43.8 reduce-scatter.28
  966.6 109.5 reduce-scatter.26
  1078.4 54.3 reduce-scatter.24
  1139.1 124.9 all-reduce.20
  1266.9 53.6 reduce-scatter.16
  1323.8 52.6 reduce-scatter.20
  1378.8 85.2 reduce-scatter.22
  1466.5 21.7 all-reduce.22
  1502.3 77.4 reduce-scatter.32

commit v2 on v1

--- a/solution.py
+++ b/solution.py
@@ -1,6 +1,10 @@
+import functools
+
 import jax
 import jax.numpy as jnp
 from jax import lax
+from jax.experimental import pallas as pl
+from jax.experimental.pallas import tpu as pltpu
 from jax.sharding import Mesh, PartitionSpec as P
 
 P_SIZE = 64
@@ -9,12 +13,455 @@
 K = 4
 G = 4
 CHUNK = 128
+RIM = 16
 
 highest = lax.Precision.HIGHEST
 rope_base = 10000.0
 norm_eps = 1e-05
 bf16 = jnp.bfloat16
 f32 = jnp.float32
+MESH = pl.DeviceIdType.MESH
+HBM = pl.BlockSpec(memory_space=pl.ANY)
+VMEM = pl.BlockSpec(memory_space=pltpu.VMEM)
+DMA = pltpu.SemaphoreType.DMA
+
+
+def rcopy(src, dst, send, recv, **where):
+    return pltpu.make_async_remote_copy(
+        src_ref=src, dst_ref=dst, send_sem=send, recv_sem=recv, device_id=where, device_id_type=MESH
+    )
+
+
+def here():
+    return lax.axis_index("z"), lax.axis_index("p"), lax.axis_index("head")
+
+
+def ring(p, d):
+    return lax.rem(p + d + G, G)
+
+
+def greet(*partners):
+    barrier = pltpu.get_barrier_semaphore()
+    for where in partners:
+        pl.semaphore_signal(barrier, inc=1, device_id=where, device_id_type=MESH)
+    pl.semaphore_wait(barrier, len(partners))
+
+
+def plane_partners(p, c):
+    return [{"p": ring(p, d)} for d in range(1, G)] + [{"head": 1 - c}]
+
+
+def line_partners(z, planes):
+    return [{"z": lax.rem(z + d, planes)} for d in range(1, planes)]
+
+
+def slot_at(p, c, rows, base=0):
+    return pl.ds(pl.multiple_of(base + (p * 2 + c) * rows, 16), rows)
+
+
+class Spread:
+    sems = [DMA((3,)), DMA((3,)), DMA((4,)), DMA((4,)), DMA(())]
+
+    def __init__(self, block, out, at, sems):
+        self.block, self.out, self.at = block, out, at
+        self.s1, self.r1, self.s2, self.r2, self.keep = sems
+        _, self.p, self.c = here()
+
+    def over(self, d):
+        spot = self.out.at[self.at(self.p, self.c)]
+        return rcopy(self.block, spot, self.s1.at[d - 1], self.r1.at[d - 1], p=ring(self.p, d))
+
+    def across(self, d):
+        spot = self.out.at[self.at(ring(self.p, -d), self.c)]
+        return rcopy(spot if d else self.block, spot, self.s2.at[d], self.r2.at[d], head=1 - self.c)
+
+    def mine(self):
+        return pltpu.make_async_copy(self.block, self.out.at[self.at(self.p, self.c)], self.keep)
+
+    def start(self):
+        for d in (1, 2, 3):
+            self.over(d).start()
+        self.across(0).start()
+        self.mine().start()
+
+    def pass_on(self):
+        for d in (1, 3, 2):
+            self.over(d).wait_recv()
+            self.across(d).start()
+
+    def finish(self):
+        self.mine().wait()
+        for d in (1, 2, 3):
+            self.over(d).wait_send()
+        for d in (0, 1, 2, 3):
+            self.across(d).wait()
+
+
+class Collect:
+    @staticmethod
+    def scratch(rows, width):
+        return [
+            pltpu.VMEM((4, rows, width), bf16), pltpu.VMEM((3, rows, width), bf16), pltpu.VMEM((3, rows, width), bf16),
+            pltpu.VMEM((rows, width), f32), DMA((4,)), DMA((4,)), DMA((3,)), DMA((3,)),
+        ]
+
+    def __init__(self, part, at, scratch, strip=16):
+        self.part, self.at = part, at
+        self.cx, self.out, self.rx, self.total, self.s1, self.r1, self.s2, self.r2 = scratch
+        self.strip = strip
+        _, self.p, self.c = here()
+
+    def across(self, d):
+        spot = self.part.at[self.at(ring(self.p, d), 1 - self.c)]
+        return rcopy(spot, self.cx.at[d], self.s1.at[d], self.r1.at[d], head=1 - self.c)
+
+    def over(self, d):
+        return rcopy(self.out.at[d - 1], self.rx.at[d - 1], self.s2.at[d - 1], self.r2.at[d - 1], p=ring(self.p, d))
+
+    def strips(self, body):
+        def one(i, carry):
+            body(pl.ds(pl.multiple_of(i * self.strip, self.strip), self.strip), i * self.strip)
+            return carry
+
+        lax.fori_loop(0, self.total.shape[0] // self.strip, one, 0)
+
+    def start(self):
+        for d in (2, 1, 3, 0):
+            self.across(d).start()
+
+    def middle(self):
+        for d in (2, 1, 3, 0):
+            self.across(d).wait_recv()
+            first = self.at(ring(self.p, d), self.c).start
+
+            def add(rows, at, d=d, first=first):
+                own = self.part[pl.ds(pl.multiple_of(first + at, self.strip), self.strip)].astype(f32)
+                both = own + self.cx[d, rows].astype(f32)
+                if d:
+                    self.out[d - 1, rows] = both.astype(bf16)
+                else:
+                    self.total[rows] = both
+
+            self.strips(add)
+            if d:
+                self.over(d).start()
+
+    def arrive(self):
+        for d in (1, 3, 2):
+            self.over(d).wait_recv()
+
+    def sum_of(self, rows):
+        return self.total[rows] + self.rx[0, rows].astype(f32) + self.rx[1, rows].astype(f32) + self.rx[2, rows].astype(f32)
+
+    def finish(self):
+        for d in range(4):
+            self.across(d).wait_send()
+        for d in (1, 2, 3):
+            self.over(d).wait_send()
+
+
+def call(body, name_id, outs, out_specs, ins, in_specs, scratch, cost=20_000_000):
+    return pl.pallas_call(
+        body,
+        out_shape=outs,
+        in_specs=in_specs,
+        out_specs=out_specs,
+        scratch_shapes=scratch,
+        cost_estimate=pl.CostEstimate(flops=0, bytes_accessed=cost, transcendentals=0),
+        compiler_params=pltpu.CompilerParams(
+            collective_id=name_id, has_side_effects=True, vmem_limit_bytes=48 * 2**20
+        ),
+    )(*ins)
+
+
+def shape(dims, kind):
+    return jax.ShapeDtypeStruct(dims, kind)
+
+
+def exchange_copies(pieces, sems, keep):
+    _, p, _ = here()
+    away, own = [], []
+    for i, (source, width, target, first, led) in enumerate(pieces):
+        rows = source.shape[-2]
+        spot = target.at[pl.ds(pl.multiple_of(p * rows, 16), rows), pl.ds(first, width)]
+        for d in range(G):
+            q = ring(p, d)
+            taken = source.at[q] if led else source.at[:, pl.ds(pl.multiple_of(q * width, 128), width)]
+            if d:
+                away.append(rcopy(taken, spot, sems[0].at[d - 1, i], sems[1].at[d - 1, i], p=q))
+            else:
+                own.append(pltpu.make_async_copy(taken, spot, keep.at[i]))
+    return away, own
+
+
+def exchange_a_body(z_ref, x_ref, q_ref, small_ref, out_ref, send, recv, keep):
+    _, p, c = here()
+    greet(*[{"p": ring(p, d)} for d in range(1, G)])
+    zw, xw, qw, sw = (r.shape[1] // G for r in (z_ref, x_ref, q_ref, q_ref))
+    pieces = [
+        (z_ref, zw, out_ref, 0, False), (x_ref, xw, out_ref, zw, False),
+        (q_ref, qw, out_ref, zw + xw, False), (small_ref, small_ref.shape[2], out_ref, zw + xw + qw, True),
+    ]
+    away, own = exchange_copies(pieces, (send, recv), keep)
+    for copy in away + own:
+        copy.start()
+    for copy in own + away:
+        copy.wait()
+
+
+def start_body(planes, out_w, o_w, gate_w, up_w, down_w, first, low, wb, wc, wd, n1, ol, *sems):
+    z, p, c = here()
+    greet(*plane_partners(p, c), *line_partners(z, planes))
+    send, recv, keep, rim_s, rim_r = sems[:5]
+    rows = first.shape[0]
+    a = Spread(first, n1, lambda q, k: slot_at(q, k, rows, RIM), sems[5:10])
+    b = Spread(low, ol, lambda q, k: slot_at(q, k, rows), sems[10:15])
+    ow, aw, gw, uw, dw = (r.shape[1] // G for r in (out_w, o_w, gate_w, up_w, down_w))
+    pieces = [
+        (out_w, ow, wb, 0, False), (o_w, aw, wb, ow, False),
+        (gate_w, gw, wc, 0, False), (up_w, uw, wc, gw, False), (down_w, dw, wd, 0, False),
+    ]
+    away, own = exchange_copies(pieces, (send, recv), keep)
+    a.start()
+    for copy in away + own:
+        copy.start()
+    b.start()
+    a.pass_on()
+    a.finish()
+    last = n1.at[pl.ds(n1.shape[0] - RIM, RIM)]
+    rim = rcopy(last, n1.at[pl.ds(0, RIM)], rim_s, rim_r, z=lax.rem(z + 1, planes))
+    rim.start()
+    for copy in own + away:
+        copy.wait()
+    b.pass_on()
+    b.finish()
+    rim.wait()
+
+
+def spread_body(block, out, *sems):
+    _, p, c = here()
+    greet(*plane_partners(p, c))
+    rows = block.shape[0]
+    s = Spread(block, out, lambda q, k: pl.ds(pl.multiple_of((k * G + q) * rows, 16), rows), sems)
+    s.start()
+    s.pass_on()
+    s.finish()
+
+
+def line_body(planes, upward, state, factor, states, factors, s1, r1, s2, r2):
+    z, _, _ = here()
+    greet(*line_partners(z, planes))
+    way = 1 if upward else -1
+
+    def pair(d):
+        to = lax.rem(z + way * d + planes, planes)
+        return (
+            rcopy(state, states.at[d - 1], s1.at[d - 1], r1.at[d - 1], z=to),
+            rcopy(factor, factors.at[d - 1], s2.at[d - 1], r2.at[d - 1], z=to),
+        )
+
+    for d in range(1, planes):
+        @pl.when((z + d < planes) if upward else (z - d >= 0))
+        def _():
+            for copy in pair(d):
+                copy.start()
+
+    for d in range(1, planes):
+        @pl.when((z - d >= 0) if upward else (z + d < planes))
+        def _():
+            for copy in pair(d):
+                copy.wait_recv()
+
+        @pl.when((z + d < planes) if upward else (z - d >= 0))
+        def _():
+            for copy in pair(d):
+                copy.wait_send()
+
+
+def hidden_body(part, x_ref, gain, hidden, second, *scratch):
+    _, p, c = here()
+    greet(*plane_partners(p, c))
+    rows = x_ref.shape[0]
+    at = lambda q, k: slot_at(q, k, rows)
+    s = Collect(part, at, scratch[:8])
+    stage = scratch[8]
+    s.start()
+    s.middle()
+    s.arrive()
+
+    def one(r, _):
+        h = x_ref[r] + s.sum_of(r)
+        hidden[r] = h
+        scale = lax.rsqrt(jnp.mean(h * h, axis=-1, keepdims=True) + norm_eps)
+        stage[r] = (h * scale * gain[...]).astype(bf16)
+
+    s.strips(one)
+    g = Spread(stage, second, at, scratch[9:14])
+    g.start()
+    g.pass_on()
+    s.finish()
+    g.finish()
+
+
+def branch_body(part, hidden, cot, gain, d_hidden, gain_grad, branch, *scratch):
+    _, p, c = here()
+    greet(*plane_partners(p, c))
+    rows = hidden.shape[0]
+    at = lambda q, k: slot_at(q, k, rows)
+    s = Collect(part, at, scratch[:8])
+    stage = scratch[8]
+    gain_grad[...] = jnp.zeros_like(gain_grad)
+    s.start()
+    s.middle()
+    s.arrive()
+
+    def one(r, _):
+        h = hidden[r]
+        scale = lax.rsqrt(jnp.mean(h * h, axis=-1, keepdims=True) + norm_eps)
+        grad = s.sum_of(r)
+        gain_grad[pl.ds(0, 1)] += jnp.sum(grad * h * scale, axis=0, keepdims=True)
+        u = grad * gain[...]
+        d = cot[r] + scale * u - h * (scale * scale * scale * jnp.mean(u * h, axis=-1, keepdims=True))
+        d_hidden[r] = d
+        stage[r] = d.astype(bf16)
+
+    s.strips(one)
+    g = Spread(stage, branch, at, scratch[9:14])
+    g.start()
+    g.pass_on()
+    s.finish()
+    g.finish()
+
+
+def final_body(planes, part, x_ref, d_hidden, layer, gain, small, grad_in, layer_out, sums, *scratch):
+    z, p, c = here()
+    greet(*plane_partners(p, c), *line_partners(z, planes))
+    rows = x_ref.shape[0]
+    at = lambda q, k: slot_at(q, k, rows)
+    s = Collect(part, at, scratch[:8])
+    stage, mine, others, zs, zr, es, er, ek = scratch[8:16]
+    half = pl.ds(pl.multiple_of(c * rows, 16), rows)
+
+    def halves(i, source, target):
+        return (
+            rcopy(source, target.at[half], es.at[i], er.at[i], head=1 - c),
+            pltpu.make_async_copy(source, target.at[half], ek.at[i]),
+        )
+
+    s.start()
+    first = halves(0, layer, layer_out)
+    for copy in first:
+        copy.start()
+    mine[...] = small[...]
+    s.middle()
+    s.arrive()
+
+    def one(r, _):
+        v = x_ref[r]
+        scale = lax.rsqrt(jnp.mean(v * v, axis=-1, keepdims=True) + norm_eps)
+        grad = s.sum_of(r)
+        mine[pl.ds(3, 1)] += jnp.sum(grad * v * scale, axis=0, keepdims=True)
+        u = grad * gain[...]
+        stage[r] = d_hidden[r] + scale * u - v * (scale * scale * scale * jnp.mean(u * v, axis=-1, keepdims=True))
+
+    s.strips(one)
+    second = halves(1, stage, grad_in)
+    for copy in second:
+        copy.start()
+    lines = [
+        rcopy(mine, others.at[d - 1], zs.at[d - 1], zr.at[d - 1], z=lax.rem(z + d, planes)) for d in range(1, planes)
+    ]
+    for copy in lines:
+        copy.start()
+    for copy in lines:
+        copy.wait()
+    total = mine[...]
+    for d in range(1, planes):
+        total = total + others[d - 1]
+    mine[...] = total
+    g = Spread(mine, sums, lambda q, k: q * 2 + k, scratch[16:21])
+    g.start()
+    g.pass_on()
+    s.finish()
+    for copy in first + second:
+        copy.wait()
+    g.finish()
+
+
+def back_body(planes, dbc, dkv, d_silu_bc, gx, g_bc, rim_bc, rim_x, kv_out, *scratch):
+    z, p, c = here()
+    greet(*plane_partners(p, c), *line_partners(z, planes))
+    (cx, bx, rbc, skv, rkv, zkv, acc, xs, xr, bs, br, ks, kr, zs, zr, ms, mr) = scratch
+    rows = rbc.shape[1]
+    across = rcopy(
+        dbc.at[pl.ds(pl.multiple_of((1 - c) * G * rows, 16), G * rows)], cx, xs, xr, head=1 - c
+    )
+    across.start()
+    kv_over = [rcopy(dkv.at[ring(p, d)], rkv.at[d - 1], ks.at[d - 1], kr.at[d - 1], p=ring(p, d)) for d in (1, 2, 3)]
+    for copy in kv_over:
+        copy.start()
+    across.wait_recv()
+    bc_over = []
+    for d in (1, 2, 3, 0):
+        q = ring(p, d)
+        own = dbc[pl.ds(pl.multiple_of((c * G + q) * rows, 16), rows)].astype(f32)
+        own = own + cx[pl.ds(pl.multiple_of(q * rows, 16), rows)].astype(f32)
+        if d:
+            bx[d - 1] = own.astype(bf16)
+            bc_over.append(rcopy(bx.at[d - 1], rbc.at[d - 1], bs.at[d - 1], br.at[d - 1], p=q))
+            bc_over[-1].start()
+        else:
+            acc[...] = own
+    for copy in kv_over:
+        copy.wait_recv()
+
+    def add_kv(i, carry):
+        v = dkv[p, i].astype(f32)
+        for d in range(3):
+            v = v + rkv[d, i].astype(f32)
+        skv[i] = v.astype(bf16)
+        return carry
+
+    lax.fori_loop(0, planes, add_kv, 0)
+
+    def kv_down(d):
+        to = lax.rem(z - d + planes, planes)
+        return rcopy(skv.at[to], zkv.at[d - 1], zs.at[d - 1], zr.at[d - 1], z=to)
+
+    for d in range(1, planes):
+        @pl.when(z - d >= 0)
+        def _():
+            kv_down(d).start()
+
+    for copy in bc_over:
+        copy.wait_recv()
+    g = acc[...]
+    for d in range(3):
+        g = g + rbc[d].astype(f32)
+    g_bc[...] = g * d_silu_bc[...]
+    before = lax.rem(z - 1 + planes, planes)
+    rims = [
+        rcopy(g_bc.at[:, pl.ds(0, 128)], rim_bc, ms.at[0], mr.at[0], z=before),
+        rcopy(gx, rim_x, ms.at[1], mr.at[1], z=before),
+    ]
+    for copy in rims:
+        copy.start()
+    kv_out[...] = skv[z].astype(f32)
+    for d in range(1, planes):
+        @pl.when(z + d < planes)
+        def _():
+            kv_down(d).wait_recv()
+            kv_out[...] += zkv[d - 1].astype(f32)
+
+        @pl.when(z - d >= 0)
+        def _():
+            kv_down(d).wait_send()
+
+    for copy in rims:
+        copy.wait()
+    across.wait_send()
+    for copy in kv_over + bc_over:
+        copy.wait_send()
 
 
 def dot(a, b, ca, cb):
@@ -59,16 +506,24 @@
     return parts
 
 
-def conv_back(grad, padded, taps, starts, places):
+def conv_back(grad, grad_next, padded, taps, starts, places, starts_next):
     length = starts.shape[0]
-    total = jnp.zeros_like(padded)
+    edge = K - 1
+    longer = jnp.concatenate([grad, grad_next], axis=0)
+    starts_long = jnp.concatenate([starts, starts_next])
+    total = jnp.zeros_like(grad)
     tap_grads = []
     for lag in range(K):
-        valid = (places - (K - 1 - lag) >= starts)[:, None]
-        g = jnp.where(valid, grad, 0.0)
-        total = total + jnp.pad(g * taps[lag][None, :], ((lag, K - 1 - lag), (0, 0)))
-        tap_grads.append(jnp.sum(g * padded[lag : lag + length], axis=0))
+        ahead = edge - lag
+        seen = (places >= starts_long[ahead : ahead + length])[:, None]
+        total = total + jnp.where(seen, longer[ahead : ahead + length], 0.0) * taps[lag][None, :]
+        valid = (places - ahead >= starts)[:, None]
+        tap_grads.append(jnp.sum(jnp.where(valid, grad, 0.0) * padded[lag : lag + length], axis=0))
     return total, jnp.stack(tap_grads)
+
+
+def mixer_row(v):
+    return v.reshape(1, -1)
 
 
 def on_device(
@@ -86,7 +541,9 @@
     total_tokens = T * planes
     offset = zi * T
     places = offset + jnp.arange(T, dtype=jnp.int32)
-    starts = lax.all_gather(doc_start, "p", axis=0, tiled=True)
+    all_starts = lax.all_gather(doc_start, ("z", "p"), axis=0, tiled=True)
+    starts = lax.dynamic_slice_in_dim(all_starts, offset, T, 0)
+    own = tokens // cores
     heads = decay_log.shape[0] // G
     chan = heads * P_SIZE
     bcs = 2 * N // cores // G
@@ -107,45 +564,61 @@
 
     bc_mine = lax.dynamic_slice_in_dim(bc_weight, hi * (2 * N // cores), 2 * N // cores, 1)
     k_cut = jnp.moveaxis(k_weight.reshape(rows, 2, G, quarter_half), 2, 1).reshape(rows, G, -1)
-    a_parts = [cut(z_weight), cut(x_weight), cut(q_weight), cut(bc_mine), k_cut, cut(v_weight), cut(dt_weight)]
-    a_sizes = [a.shape[-1] for a in a_parts]
-    a_cols = sum(a_sizes)
-    pad = -a_cols % 128
-    a_parts.append(jnp.zeros((rows, G, pad), bf16))
+    a_sizes = [chan, chan, HD, bcs, 2 * quarter_half, 2 * quarter_half, heads]
     a_at = [sum(a_sizes[:i]) for i in range(len(a_sizes))]
-
-    def gather(parts):
-        w = jnp.moveaxis(jnp.concatenate(parts, axis=2), 1, 0)
-        w = lax.all_to_all(w, "p", 0, 0, tiled=True)
-        return lax.all_gather(w.reshape(G * rows, -1), "z", axis=0, tiled=True)
+    pad = -sum(a_sizes) % 128
+    small_w = jnp.concatenate(
+        [cut(bc_mine), k_cut, cut(v_weight), cut(dt_weight), jnp.zeros((rows, G, pad), bf16)], axis=2
+    )
+    small_w = jnp.moveaxis(small_w, 1, 0)
+    a_cols = sum(a_sizes) + pad
+
+    def gather(w):
+        return lax.all_gather(w, "z", axis=0, tiled=True)
+
+    exchange_sems = lambda n: [DMA((3, n)), DMA((3, n)), DMA((n,))]
+    wa = gather(call(
+        exchange_a_body, 0, shape((G * rows, a_cols), bf16), HBM,
+        (z_weight, x_weight, q_weight, small_w), [HBM] * 4, exchange_sems(4),
+    ))
+
+    def half(v):
+        return lax.dynamic_slice_in_dim(v, hi * own, own, 0)
+
+    x_own, cot_own = half(layer_input), half(cotangent)
+    r1 = lax.rsqrt(jnp.mean(x_own * x_own, axis=-1, keepdims=True) + norm_eps)
+    first_own = (x_own * r1 * mixer_gain).astype(bf16)
+    wb, wc, wd, first_rim, out_low = call(
+        functools.partial(start_body, planes), 1,
+        (shape((G * rows, chan + HD), bf16), shape((G * rows, gate_weight.shape[1] * 2 // G), bf16),
+         shape((G * rows, down_weight.shape[1] // G), bf16), shape((RIM + T, width), bf16), shape((T, width), bf16)),
+        (HBM,) * 5,
+        (out_weight, o_weight, gate_weight, up_weight, down_weight, first_own, cot_own.astype(bf16)),
+        [HBM] * 5 + [VMEM] * 2,
+        exchange_sems(5) + [DMA(()), DMA(())] + Spread.sems * 2, cost=150_000_000,
+    )
+    wb, wc, wd = gather(wb), gather(wc), gather(wd)
+    first = first_rim[RIM:]
 
     def scatter(grad):
         g = lax.psum_scatter(grad.astype(bf16), "z", scatter_dimension=0, tiled=True)
         g = lax.all_to_all(g.reshape(G, rows, -1), "p", 0, 0, tiled=True)
         return jnp.moveaxis(g, 0, 1).astype(f32)
 
-    wa = gather(a_parts)
-    wb = gather([cut(out_weight), cut(o_weight)])
-    wc = gather([cut(gate_weight), cut(up_weight)])
-    wd = gather([cut(down_weight)])
-
-    r1 = lax.rsqrt(jnp.mean(layer_input * layer_input, axis=-1, keepdims=True) + norm_eps)
-    first_own = (layer_input * r1 * mixer_gain).astype(bf16)
-    first = lax.all_gather(first_own, "p", axis=0, tiled=True)
-    out_low = lax.all_gather(cotangent.astype(bf16), "p", axis=0, tiled=True)
-    pa = dot(first, wa, 1, 0)
+    edge = K - 1
+    pa = dot(first_rim, wa, 1, 0)
+    rim_seen = jnp.where(zi > 0, pa[RIM - edge : RIM], 0.0)
     z_part, inner_pre, q_proj, bc_pre, k_proj, v_proj, step_raw = (
-        pa[:, a : a + s] for a, s in zip(a_at, a_sizes)
-    )
-    edge = K - 1
-    rim_inner, rim_bc = shifted((inner_pre[T - edge :], bc_pre[T - edge :]), "z", 1)
-    pad_inner = jnp.concatenate([rim_inner, inner_pre], axis=0)
-    pad_bc = jnp.concatenate([rim_bc, bc_pre], axis=0)
+        pa[RIM:, a : a + s] for a, s in zip(a_at, a_sizes)
+    )
+    pad_inner = jnp.concatenate([rim_seen[:, a_at[1] : a_at[1] + chan], inner_pre], axis=0)
+    pad_bc = jnp.concatenate([rim_seen[:, a_at[3] : a_at[3] + bcs], bc_pre], axis=0)
     cv_x = sum(p * t[None, :] for p, t in zip(conv_parts(pad_inner, starts, places), taps_inner))
     cv_bc = sum(p * t[None, :] for p, t in zip(conv_parts(pad_bc, starts, places), taps_state))
     conv_x = jax.nn.silu(cv_x)
     bc_low = jax.nn.silu(cv_bc).astype(bf16)
-    bc_all = lax.all_gather(bc_low, ("head", "p"), axis=1, tiled=True)
+    bc_t = call(spread_body, 2, shape((2 * N, T), bf16), HBM, (bc_low.T,), [HBM], Spread.sems)
+    bc_all = bc_t.T
     step = jax.nn.softplus(step_raw + bias)
     log_decay = -jnp.exp(rates) * step
 
@@ -187,12 +660,23 @@
         reach.append(through)
         state = state * dtot[c][:, None, None] + local[c]
         through = through * dtot[c]
-    everyone = lax.all_gather(state.astype(bf16), "z", axis=0)
-    factors = lax.all_gather(through, "z", axis=0)
-    before = jnp.zeros((heads, P_SIZE, N), f32)
-    for k in range(planes - 1):
-        new = before * factors[k][:, None, None] + everyone[k].astype(f32)
-        before = jnp.where(k < zi, new, before)
+
+    def line(upward, state, name_id):
+        flat = jnp.broadcast_to(jnp.pad(through, (0, 8 - heads))[:, None], (8, 128))
+        states, factors = call(
+            functools.partial(line_body, planes, upward), name_id,
+            (shape((planes - 1, chan, N), bf16), shape((planes - 1, 8, 128), f32)), (HBM, HBM),
+            (state.reshape(chan, N).astype(bf16), flat), [HBM, HBM],
+            [DMA((planes - 1,)) for _ in range(4)],
+        )
+        total = jnp.zeros((heads, P_SIZE, N), f32)
+        for d in reversed(range(1, planes)):
+            there = (zi - d >= 0) if upward else (zi + d < planes)
+            new = total * factors[d - 1, :heads, :1][:, :, None] + states[d - 1].reshape(heads, P_SIZE, N).astype(f32)
+            total = jnp.where(there, new, total)
+        return total
+
+    before = line(True, state, 3)
     state_in = jnp.stack([s + before * r[:, None, None] for s, r in zip(entering, reach)])
     y_off = exact("cin,chpn->chip", c_rows, state_in) * decay_in[..., None]
     y_scan = exact("chij,chjp->chip", mix, driven) + y_off
@@ -215,10 +699,9 @@
     scale = HD ** (-0.5)
     query = (turn(q_proj, cos_q, sin_q) * scale).astype(bf16)
     kv_own = jnp.concatenate([turn(k_proj, cos_k, sin_k).astype(bf16), v_proj.astype(bf16)], axis=1)
-    kv_all = lax.all_gather(kv_own, ("z", "p"), axis=0)
-    kv_all = kv_all.reshape(planes, G, T, 4, quarter_half)
-    keys = kv_all[:, :, :, :2].transpose(0, 2, 3, 1, 4).reshape(total_tokens, HD)
-    values = kv_all[:, :, :, 2:].reshape(planes, G, T, 2 * quarter_half).transpose(0, 2, 1, 3).reshape(total_tokens, HD)
+    kv_all = lax.all_gather(kv_own.T, ("z", "p"), axis=0).reshape(planes, G, 4, quarter_half, T)
+    keys = kv_all[:, :, :2].transpose(0, 4, 2, 1, 3).reshape(total_tokens, HD)
+    values = kv_all[:, :, 2:].transpose(0, 4, 1, 2, 3).reshape(total_tokens, HD)
     key_len = min(512, total_tokens)
     first_block = starts[0] // key_len
     last_block = (offset + T - 1) // key_len
@@ -251,30 +734,29 @@
     attended = lax.fori_loop(first_block, last_block + 1, weighted, jnp.zeros((T, HD), f32))
     att_low = attended.astype(bf16)
 
-    def plane_sum(part):
-        mine = lax.psum_scatter(part.astype(bf16), "p", scatter_dimension=0, tiled=True)
-        return lax.psum(mine, "head").astype(f32)
-
     both_low = jnp.concatenate([ssm_low, att_low], axis=1)
-    hidden = layer_input + plane_sum(dot(both_low, wb, 1, 1))
-    r2 = lax.rsqrt(jnp.mean(hidden * hidden, axis=-1, keepdims=True) + norm_eps)
-    second = lax.all_gather((hidden * r2 * ffn_gain).astype(bf16), "p", axis=0, tiled=True)
+    collect = Collect.scratch(own, width) + [pltpu.VMEM((own, width), bf16)] + Spread.sems
+    hidden, second = call(
+        hidden_body, 4, (shape((own, width), f32), shape((T, width), bf16)), (VMEM, HBM),
+        (dot(both_low, wb, 1, 1).astype(bf16), x_own, mixer_row(ffn_gain)), [VMEM] * 3, collect,
+    )
     pc = dot(second, wc, 1, 0)
     ff = pc.shape[1] // 2
     gate_pre, up_pre = pc[:, :ff], pc[:, ff:]
     s_gate = jax.nn.silu(gate_pre)
     act_low = (s_gate * up_pre).astype(bf16)
-    layer_out = hidden + plane_sum(dot(act_low, wd, 1, 1))
+    layer_own = hidden + lax.psum_scatter(
+        dot(act_low, wd, 1, 1).astype(bf16), ("p", "head"), scatter_dimension=0, tiled=True
+    ).astype(f32)
 
     grad_d = dot(out_low, act_low, 0, 0)
     d_act = dot(out_low, wd, 1, 0)
     gu_low = jnp.concatenate([d_act * up_pre * d_silu(gate_pre), d_act * s_gate], axis=1).astype(bf16)
     grad_c = dot(second, gu_low, 0, 0)
-    d_second = plane_sum(dot(gu_low, wc, 1, 1))
-    u2 = d_second * ffn_gain
-    d_hidden = cotangent + r2 * u2 - hidden * r2**3 * jnp.mean(u2 * hidden, axis=-1, keepdims=True)
-    grad_ffn = jnp.sum(d_second * hidden * r2, axis=0)
-    branch = lax.all_gather(d_hidden.astype(bf16), "p", axis=0, tiled=True)
+    d_hidden, grad_ffn, branch = call(
+        branch_body, 5, (shape((own, width), f32), shape((8, width), f32), shape((T, width), bf16)), (VMEM, VMEM, HBM),
+        (dot(gu_low, wc, 1, 1).astype(bf16), hidden, cot_own, mixer_row(ffn_gain)), [VMEM] * 4, collect,
+    )
     grad_b = dot(branch, both_low, 0, 0)
     d_both = dot(branch, wb, 1, 0)
     d_norm_s, d_att = d_both[:, :chan], d_both[:, chan:].astype(bf16)
@@ -292,11 +774,7 @@
     for c in reversed(range(nc)):
         leaving[c] = g
         g = g * dtot[c][:, None, None] + from_chunk[c]
-    every_grad = lax.all_gather(g.astype(bf16), "z", axis=0)
-    after = zero_state
-    for k in reversed(range(1, planes)):
-        new = after * factors[k][:, None, None] + every_grad[k].astype(f32)
-        after = jnp.where(k > zi, new, after)
+    after = line(False, g, 6)
     scale_c = jnp.ones((heads,), f32)
     d_state = [None] * nc
     for c in reversed(range(nc)):
@@ -321,13 +799,7 @@
     grad_bias = jnp.sum(d_raw, axis=0)
     grad_rates = jnp.sum(d_la * la_h, axis=(0, 2))
     d_bc_all = jnp.concatenate([d_b.reshape(T, N), d_c.reshape(T, N)], axis=1).astype(bf16)
-    d_bc = lax.psum_scatter(d_bc_all, ("head", "p"), scatter_dimension=1, tiled=True).astype(f32)
-    pad_g, grad_conv_inner = conv_back(dx * d_silu(cv_x), pad_inner, taps_inner, starts, places)
-    pad_h, grad_conv_state = conv_back(d_bc * d_silu(cv_bc), pad_bc, taps_state, starts, places)
-    next_g, next_h = shifted((pad_g[:edge], pad_h[:edge]), "z", -1)
-    d_inner_pre = pad_g[edge:] + jnp.pad(next_g, ((T - edge, 0), (0, 0)))
-    d_bc_pre = pad_h[edge:] + jnp.pad(next_h, ((T - edge, 0), (0, 0)))
-
+    gx = dx * d_silu(cv_x)
     balance = jnp.sum(d_att.astype(f32) * attended, axis=-1, keepdims=True)
 
     def grads(index, carry):
@@ -344,10 +816,28 @@
     d_query, d_keys, d_values = lax.fori_loop(
         first_block, last_block + 1, grads, (jnp.zeros((T, HD), f32), zero_keys, zero_keys)
     )
-    dk_cut = d_keys.astype(bf16).reshape(planes, T, 2, G, quarter_half).transpose(0, 3, 1, 2, 4)
-    dv_cut = d_values.astype(bf16).reshape(planes, T, G, 2 * quarter_half).transpose(0, 2, 1, 3)
-    dkv = jnp.concatenate([dk_cut.reshape(planes, G, T, -1), dv_cut], axis=-1).reshape(planes * G, T, -1)
-    dkv = jnp.sum(lax.all_to_all(dkv, ("z", "p"), 0, 0, tiled=True).astype(f32), axis=0)
+    dk_cut = d_keys.astype(bf16).reshape(planes, T, 2, G, quarter_half).transpose(3, 0, 2, 4, 1)
+    dv_cut = d_values.astype(bf16).reshape(planes, T, G, 2, quarter_half).transpose(2, 0, 3, 4, 1)
+    dkv = jnp.concatenate([dk_cut, dv_cut], axis=2).reshape(G, planes, 4 * quarter_half, T)
+    kvr = 4 * quarter_half
+    gx_first = gx[:RIM]
+    g_bc, rim_bc, rim_x, dkv = call(
+        functools.partial(back_body, planes), 7,
+        (shape((bcs, T), f32), shape((bcs, 128), f32), shape((RIM, chan), f32), shape((kvr, T), f32)), (VMEM,) * 4,
+        (d_bc_all.T, dkv, d_silu(cv_bc).T, gx_first), [VMEM] * 4,
+        [pltpu.VMEM((G * bcs, T), bf16), pltpu.VMEM((3, bcs, T), bf16), pltpu.VMEM((3, bcs, T), bf16),
+         pltpu.VMEM((planes, kvr, T), bf16), pltpu.VMEM((3, planes, kvr, T), bf16), pltpu.VMEM((planes - 1, kvr, T), bf16),
+         pltpu.VMEM((bcs, T), f32), DMA(()), DMA(()), DMA((3,)), DMA((3,)), DMA((3,)), DMA((3,)),
+         DMA((planes - 1,)), DMA((planes - 1,)), DMA((2,)), DMA((2,))],
+    )
+    dkv = dkv.T
+    later = zi < planes - 1
+    gx_next = jnp.where(later, rim_x[:edge], 0.0)
+    gb_next = jnp.where(later, rim_bc[:, :edge].T, 0.0)
+    ends = jnp.minimum(offset + T + jnp.arange(edge), total_tokens - 1)
+    starts_next = jnp.where(later, all_starts[ends], total_tokens)
+    d_inner_pre, grad_conv_inner = conv_back(gx, gx_next, pad_inner, taps_inner, starts, places, starts_next)
+    d_bc_pre, grad_conv_state = conv_back(g_bc.T, gb_next, pad_bc, taps_state, starts, places, starts_next)
     d_q = turn(d_query, cos_q, -sin_q) * scale
     d_k = turn(dkv[:, : 2 * quarter_half], cos_k, -sin_k)
     d_v = dkv[:, 2 * quarter_half :]
@@ -356,27 +846,36 @@
         [d_z, d_inner_pre, d_q, d_bc_pre, d_k, d_v, d_raw, jnp.zeros((T, pad), f32)], axis=1
     ).astype(bf16)
     grad_a = dot(first, da_low, 0, 0)
-    d_first = plane_sum(dot(da_low, wa, 1, 1))
-    u1 = d_first * mixer_gain
-    grad_input = d_hidden + r1 * u1 - layer_input * r1**3 * jnp.mean(u1 * layer_input, axis=-1, keepdims=True)
-    grad_mixer = jnp.sum(d_first * layer_input * r1, axis=0)
+    small = [grad_conv_inner, grad_conv_state, grad_rates, grad_bias, grad_skip, grad_gain_s]
+    at = [0]
+    for s in small:
+        at.append(at[-1] + s.size)
+    flat = jnp.concatenate([s.reshape(-1) for s in small] + [jnp.zeros((2 * width - at[-1],), f32)]).reshape(2, width)
+    flat = jnp.concatenate([flat, grad_ffn[:1], jnp.zeros((5, width), f32)], axis=0)
+    grad_input, layer_out, sums = call(
+        functools.partial(final_body, planes), 8,
+        (shape((tokens, width), f32), shape((tokens, width), f32), shape((2 * G, 8, width), f32)), (HBM, HBM, VMEM),
+        (dot(da_low, wa, 1, 1).astype(bf16), x_own, d_hidden, layer_own, mixer_row(mixer_gain), flat), [VMEM] * 6,
+        Collect.scratch(own, width)
+        + [pltpu.VMEM((own, width), f32), pltpu.VMEM((8, width), f32), pltpu.VMEM((planes - 1, 8, width), f32),
+           DMA((planes - 1,)), DMA((planes - 1,)), DMA((2,)), DMA((2,)), DMA((2,))]
+        + Spread.sems,
+    )
 
     ga, gb, gc, gd = (scatter(g) for g in (grad_a, grad_b, grad_c, grad_d))
     g_z, g_x, g_q, g_bc, g_k, g_v, g_dt = (ga[:, :, a : a + s] for a, s in zip(a_at, a_sizes))
     g_k = jnp.moveaxis(g_k.reshape(rows, G, 2, quarter_half), 1, 2)
     g_bc = lax.all_gather(g_bc.reshape(rows, -1).astype(bf16), "head", axis=1, tiled=True).astype(f32)
 
-    small = [grad_conv_inner, grad_conv_state, grad_rates, grad_bias, grad_skip, grad_gain_s]
-    flat = jnp.concatenate([s.reshape(-1) for s in small])
-    every = jnp.sum(lax.all_gather(flat, ("z", "p", "head")).reshape(planes, G, cores, -1), axis=0)
+    sums = sums.reshape(G, cores, 8, width)
+    every = sums[:, :, :2].reshape(G, cores, 2 * width)
     mine = lax.dynamic_index_in_dim(every, hi, 1, False)
-    at = [0]
-    for s in small:
-        at.append(at[-1] + s.size)
     pieces = [mine[:, a:b] for a, b in zip(at, at[1:])]
     o_conv_inner = jnp.moveaxis(pieces[0].reshape(G, K, chan), 0, 1).reshape(K, G * chan)
     o_conv_state = every[:, :, at[1] : at[2]].reshape(G, cores, K, bcs).transpose(2, 1, 0, 3).reshape(K, 2 * N)
-    gains = lax.psum_scatter(jnp.stack([grad_mixer, grad_ffn]), ("z", "p"), scatter_dimension=1, tiled=True)
+    per = width // (planes * G)
+    gains = lax.dynamic_slice_in_dim(jnp.sum(sums[:, :, 2:4], axis=(0, 1)), (zi * G + pi) * per, per, 1)
+    gains = (gains[1], gains[0])
 
     def whole(g):
         return g.reshape(rows, -1)

time: 1600 us -> 953 us (0.60)
  waiting for transfers between devices: 1000 us -> 46.6 us
  Pallas kernels: 0 us -> 404 us
  blocking collectives: 126 us -> 41.1 us
  starting transfers between devices: 43.1 us -> 19.4 us
    pallas_call x0 -> x9, Pallas kernels: none -> 404 us  [call(): pl.pallas_call(body, out_shape=outs, in_specs=in_specs, out_specs=out_spe...]
    all_gather x10 -> x5, waiting for transfers between devices: 385 us -> 14.2 us  [the longest x4 14.2 us: gather(): return lax.all_gather(w, 'z', axis=0, tiled=True)]
    reduce_scatter x4 -> x1, waiting for transfers between devices: 214 us -> 0.01 us  [on_device(): lax.psum_scatter(dot(act_low, wd, 1, 1).astype(bf16), ('p', 'head'), scat...]
    unnamed x27 -> x10, waiting for transfers between devices: 183 us -> 1.85 us
    reduce_scatter x4, waiting for transfers between devices: 87.6 us -> 0.01 us  [scatter(): lax.psum_scatter(grad.astype(bf16), 'z', scatter_dimension=0, tiled=True)]
    ppermute x4 -> x0, waiting for transfers between devices: 85.2 us -> none  [shifted(): return lax.ppermute(block, axis, route)]
    all_to_all x4 -> x0, blocking collectives: 66.7 us -> none  [the longest x3 56.1 us: gather(): w = lax.all_to_all(w, 'p', 0, 0, tiled=True)]
    all_to_all x2 -> x0, starting transfers between devices: 23.2 us -> none  [the longest x1 19.3 us: on_device(): lax.all_to_all(dkv, ('z', 'p'), 0, 0, tiled=True).astype(f32)]
  transfers between devices with their start and end apart: 33 -> 14, of which waited for: 21 -> 5; matrix products, arithmetic and copies ran while one was open for 18% -> 36% of each run, Pallas kernels for 0% -> 35%
where the time goes in v2:
time: 953 us; the launch traced here: 938 us
  Pallas kernels  404 us (42%)
  local copies, waits for them, and re-layouts  159 us (17%)
  matrix products  152 us (16%)
  other arithmetic  95.2 us (10%)
  waiting for transfers between devices  46.6 us (5%)
  blocking collectives  41.1 us (4%)
  between operations  20.1 us (2%)
  starting transfers between devices  19.4 us (2%)
    pallas_call x9, Pallas kernels, call(): pl.pallas_call(body, out_shape=outs, in_specs=in_specs, out_specs=out_spe...  404 us
    dot_general x26, matrix products, dot(): lax.dot_general(a, b, (((ca,), (cb,)), ((), ())), preferred_element_type=...  110 us
    unnamed x426, local copies, waits for them, and re-layouts  54.3 us
    dot_general x14, matrix products, exact(): jnp.einsum(text, *operands, precision=highest, preferred_element_type=f32)  41.8 us
    all_gather x1, blocking collectives, on_device(): all_starts = lax.all_gather(doc_start, ('z', 'p'), axis=0, tiled=True)  39.2 us
    all_to_all x4, waiting for transfers between devices, scatter(): g = lax.all_to_all(g.reshape(G, rows, -1), 'p', 0, 0, tiled=True)  30.5 us
  transfers between devices with their start and end apart: 14, of which 5 were waited for; matrix products, arithmetic and copies ran while one was open for 36% of the time, Pallas kernels for 35%

profile of v2, /device:TPU:0, one launch (start us, length us, event | category | flops | bytes accessed | tf_op | source)
XLA Modules:
  0.0 938.4 jit_solution(18397988010021945440)
XLA Ops:
  11.6 17.9 %shard_map.391 = bf16[512,1152]{1,0:T(8,128)(2,1)} custom-call(bf16[128,1536]{1,0:T(8,128)(2,1)S(1)} %copy-done.9, bf16[128,1536]{1,0:T(8,128)(2,1)S(1)} %copy-done.10, bf16[128,512]{1,0:T(8,128)(2,1)S(1)} %copy-done.14, bf16[4,128,256]{2,1,0:T(8,128)(2,1)S(1)} %bitcast.470), custom_call_target="tpu_custom_call" | custom-call | bytes 20000000 | tf_op jit(solution)/shard_map/pallas_call | solution.py:164
  32.9 75.2 %shard_map.390 = (bf16[512,512]{1,0:T(8,128)(2,1)}, bf16[512,1024]{1,0:T(8,128)(2,1)}, bf16[512,512]{1,0:T(8,128)(2,1)}, bf16[1040,2048]{1,0:T(8,128)(2,1)}, bf16[1024,2048]{1,0:T(8,128)(2,1)}) custom-call(bf16[128,1536]{1,0:T(8,128)(2,1)S(1)} %copy-done.11, bf16[128,512]{1,0:T(8,128)(2,1)S(1)} %copy-done.15, bf16[128,2048]{1,0:T(8,128)(2,1)S(1)} %copy-done.6, ...), custom_call_target="tpu_custom_call" | custom-call | bytes 150000000 | tf_op jit(solution)/shard_map/pallas_call | solution.py:164
  108.1 39.2 %all-gather.1 = s32[16,1,256]{2,1,0:T(1,128)S(1)} all-gather(s32[1,1,256]{2,1,0:T(1,128)S(1)} %bitcast.562), channel_id=1, replica_groups=mesh['z'=4,'p'=4,'head'=2] {'z','p'}, dimensions={0}, use_global_device_ids=true | all-gather | bytes 17408 | tf_op jit(solution)/shard_map/all_gather | solution.py:544
  147.4 8.9 fusion.220
  181.9 6.9 fusion.72
  194.7 4.7 fusion.131
  202.0 13.8 %shard_map.392 = bf16[512,1024]{1,0:T(8,128)(2,1)S(1)} custom-call(bf16[64,1024]{1,0:T(8,128)(2,1)S(1)} %copy.558.block), custom_call_target="tpu_custom_call" | custom-call | bytes 20000000 | tf_op jit(solution)/shard_map/pallas_call | solution.py:164
  228.1 25.3 %shard_map.393 = (bf16[3,384,256]{2,1,0:T(8,128)(2,1)S(1)}, f32[3,8,128]{2,1,0:T(8,128)S(1)}) custom-call(bf16[384,256]{1,0:T(8,128)(2,1)S(1)} %fusion.165.state, f32[8,128]{1,0:T(8,128)S(1)} %broadcast_in_dim.332.factor), custom_call_target="tpu_custom_call" | custom-call | bytes 20000000 | tf_op jit(solution)/shard_map/pallas_call | solution.py:164
  265.3 6.5 fusion.39
  280.7 4.0 fusion.202
  290.7 3.2 copy.579
  305.3 4.2 while.39
  315.2 4.1 while.40
  320.0 6.3 convolution_convert_fusion.3.part
  326.3 60.4 %shard_map.394 = (f32[128,2048]{1,0:T(8,128)S(1)}, bf16[1024,2048]{1,0:T(8,128)(2,1)}) custom-call(bf16[1024,2048]{1,0:T(8,128)(2,1)} %convolution_convert_fusion.3.part, f32[128,2048]{1,0:T(8,128)S(1)} %get-tuple-element.769.x_ref, f32[1,2048]{1,0:T(1,128)S(1)} %bitcast.472), custom_call_target="tpu_custom_call" | custom-call | bytes 20000000 | tf_op jit(solution)/shard_map/pallas_call | solution.py:164
  386.8 10.5 %fusion.222 = f32[1024,1024]{0,1:T(8,128)} fusion(bf16[1024,2048]{1,0:T(8,128)(2,1)} %get-tuple-element.214, bf16[2048,1024]{1,0:T(8,128)(2,1)} %all-gather.14.cloned.1.call-done), kind=kOutput, calls=%fused_computation.441 | convolution fusion | flops 4294967296 | bytes 12582912 | tf_op jit(solution)/shard_map/dot_general | solution.py:468
  397.2 14.2 %all-gather.10.cloned.1.call-done = bf16[2048,512]{1,0:T(8,128)(2,1)} async-done(((bf16[512,512]{1,0:T(8,128)(2,1)}), bf16[2048,512]{1,0:T(8,128)(2,1)}) %all-gather.10.cloned.1.call-update) | async-done | bytes 2097168 | tf_op jit(solution)/shard_map/all_gather | solution.py:577
  411.4 8.2 multiply_convert_fusion.2
  419.7 6.2 convolution_convert_fusion.5.part
  425.9 59.9 %shard_map.395 = (f32[128,2048]{1,0:T(8,128)S(1)}, f32[8,2048]{1,0:T(8,128)S(1)}, bf16[1024,2048]{1,0:T(8,128)(2,1)}) custom-call(bf16[1024,2048]{1,0:T(8,128)(2,1)} %convolution_convert_fusion.5.part, f32[128,2048]{1,0:T(8,128)S(1)} %get-tuple-element.216.hidden, f32[128,2048]{1,0:T(8,128)S(1)} %get-tuple-element.767.cot, f32[1,2048]{1,0:T(1,128)S(1)} %bitcast.473), custom_call_target="tpu_custom_call" | custom-call | bytes 20000000 | tf_op jit(solution)/shard_map/pallas_call | solution.py:164
  486.8 5.9 convolution_convert_fusion.7
  493.9 5.9 convolution_convert_fusion.6
  504.2 5.2 fusion.223
  512.1 3.1 copy.654
  527.1 6.4 fusion.174
  542.1 48.9 %shard_map.396 = (bf16[3,384,256]{2,1,0:T(8,128)(2,1)S(1)}, f32[3,8,128]{2,1,0:T(8,128)S(1)}) custom-call(bf16[384,256]{1,0:T(8,128)(2,1)S(1)} %fusion.157.state, f32[8,128]{1,0:T(8,128)S(1)} %broadcast_in_dim.332.factor), custom_call_target="tpu_custom_call" | custom-call | bytes 20000000 | tf_op jit(solution)/shard_map/pallas_call | solution.py:164
  591.1 4.4 convolution_convert_fusion.1
  604.9 3.6 fusion.224
  608.6 5.2 fusion.64
  625.9 5.1 multiply_reduce_fusion.6
  632.7 9.6 %convolution_convert_fusion.4 = bf16[2048,1024]{1,0:T(8,128)(2,1)} fusion(bf16[1024,2048]{1,0:T(8,128)(2,1)} %get-tuple-element.214, bf16[1024,512]{0,1:T(8,128)(2,1)} %copy-done.198, bf16[1024,512]{0,1:T(8,128)(2,1)} %copy-done.197), kind=kOutput, calls=%fused_computation.52 | convolution fusion | flops 4301258752 | bytes 10485760 | tf_op jit(solution)/shard_map/dot_general | solution.py:468
  644.5 13.3 %while.41 = (s32[]{:T(128)}, f32[1024,128]{1,0:T(8,128)S(1)}, bf16[4096,128]{1,0:T(8,128)(2,1)}, bf16[4096,128]{1,0:T(8,128)(2,1)}, s32[]{:T(128)}, /*index=5*/s...) while((s32[]{:T(128)}, f32[1024,128]{1,0:T(8,128)S(1)}, ...), condition=%wide.region_12.13_spmd.clone, body=%wide.region_11.12_spmd.clone.sunk | while | flops 675939840 | bytes 12476647 | solution.py:816
  675.3 6.0 multiply_reduce_fusion.1
  684.8 5.5 fusion.92
  695.0 53.7 %shard_map.397 = (f32[64,1024]{1,0:T(8,128)S(1)}, f32[64,128]{1,0:T(8,128)S(1)}, f32[16,384]{1,0:T(8,128)S(1)}, f32[64,1024]{1,0:T(8,128)S(1)}) custom-call(bf16[512,1024]{1,0:T(8,128)(2,1)S(1)} %maximum_bitcast_fusion.dbc, bf16[4,4,64,1024]{3,2,1,0:T(8,128)(2,1)S(1)} %bitcast.468, f32[64,1024]{1,0:T(8,128)S(1)} %copy.607.d_silu_bc, f32[16,384]{1,0:T(8,128)S(1)} %slice.554.gx), custom_call_target="tpu_custom_call" | custom-call | bytes 20000000 | tf_op jit(solution)/shard_map/pallas_call | solution.py:164
  767.4 5.3 concatenate.68
  772.7 9.5 %convolution_convert_fusion = bf16[2048,1152]{1,0:T(8,128)(2,1)} fusion(bf16[1024,1152]{1,0:T(8,128)(2,1)} %concatenate.68, bf16[1040,2048]{1,0:T(8,128)(2,1)} %get-tuple-element.205), kind=kOutput, calls=%fused_computation.47 | convolution fusion | flops 4834197504 | bytes 11272192 | tf_op jit(solution)/shard_map/dot_general | solution.py:468
  786.2 9.8 %convolution_convert_fusion.2.part = bf16[1024,2048]{1,0:T(8,128)(2,1)} fusion(bf16[1024,1152]{1,0:T(8,128)(2,1)} %concatenate.68, bf16[2048,1152]{1,0:T(8,128)(2,1)} %all-gather.8.cloned.1.call-done), kind=kOutput, calls=%fused_computation.50 | convolution fusion | flops 4833935360 | bytes 11272192 | tf_op jit(solution)/shard_map/dot_general | solution.py:468
  795.9 5.7 all-to-all-start.1
  801.7 6.5 all-to-all-done.1
  808.2 4.1 all-to-all-start.3
  813.5 5.5 all-to-all-done.3
  824.3 48.8 %shard_map.398 = (f32[256,2048]{1,0:T(8,128)S(1)}, f32[256,2048]{1,0:T(8,128)}, f32[8,8,2048]{2,1,0:T(8,128)S(1)}) custom-call(bf16[1024,2048]{1,0:T(8,128)(2,1)} %convolution_convert_fusion.2.part, f32[128,2048]{1,0:T(8,128)S(1)} %get-tuple-element.769.x_ref, f32[128,2048]{1,0:T(8,128)S(1)} %copy-done.5, f32[128,2048]{1,0:T(8,128)S(1)} %convert_add_fusion.layer, ...), custom_call_target="tpu_custom_call" | custom-call | bytes 20000000 | tf_op jit(solution)/shard_map/pallas_call | solution.py:164
  874.0 4.4 all-to-all-start.2
  881.2 11.6 %all-to-all-done.2 = bf16[4,128,1024]{2,1,0:T(8,128)(2,1)} async-done(((bf16[4,128,1024]{2,1,0:T(8,128)(2,1)}), bf16[4,128,1024]{2,1,0:T(8,128)(2,1)}, u32[]{:S(2)}, u32[]{:S(2)}) %all-to-all-start.2) | async-done | bytes 1048608 | tf_op jit(solution)/shard_map/all_to_all | solution.py:605
  892.9 4.3 all-to-all-start
  905.3 6.9 all-to-all-done
  926.7 3.2 copy.770
  (716 shorter events, 252.6 us)
Async XLA Ops:
  7.2 140.1 %all-gather.8.cloned.1.call-start = ((), (), s32[]{:S(2)}) async-start(), calls=%async_computation.9 | async-start | bytes 5898240 | tf_op jit(solution)/shard_map/all_gather | solution.py:577
  29.6 268.5 %all-gather.16.cloned.1.call-start = ((), (), s32[]{:S(2)}) async-start(), calls=%async_computation.18 | async-start | bytes 2228224 | tf_op jit(solution)/shard_map/all_gather | solution.py:702
  32.8 75.3 %copy-start.186 = (s32[256]{0:T(256)S(1)}, s32[256]{0:T(256)}, u32[]{:S(2)}) copy-start(s32[256]{0:T(256)} %param.30) | copy-start | bytes 3076
  147.3 9.1 copy-start.165
  147.3 47.4 %copy-start.93 = (f32[1024]{0:T(1024)}, f32[1024]{0:T(1024)S(1)}, u32[]{:S(2)}) copy-start(f32[1024]{0:T(1024)S(1)} %get-tuple-element.743) | copy-start | bytes 12292
  160.9 10.3 %copy-start.194 = (f32[24]{0:T(128)S(1)}, f32[24]{0:T(128)}, u32[]{:S(2)}) copy-start(f32[24]{0:T(128)} %param.49) | copy-start | bytes 292
  162.0 158.0 %all-gather.12.cloned.1.call-start = ((), (), s32[]{:S(2)}) async-start(), calls=%async_computation.11 | async-start | bytes 2621440 | tf_op jit(solution)/shard_map/all_gather | solution.py:577
  162.7 224.1 %all-gather.14.cloned.1.call-start = ((), (), s32[]{:S(2)}) async-start(), calls=%async_computation.12 | async-start | bytes 5242880 | tf_op jit(solution)/shard_map/all_gather | solution.py:577
  163.3 248.1 %all-gather.10.cloned.1.call-start = ((), (), s32[]{:S(2)}) async-start(), calls=%async_computation.10 | async-start | bytes 2621440 | tf_op jit(solution)/shard_map/all_gather | solution.py:577
  163.9 632.1 %reduce-scatter.10.cloned.1.call-start = ((), (), s32[]{:S(2)}) async-start(), calls=%async_computation.15 | async-start | bytes 2621440 | tf_op jit(solution)/shard_map/reduce_scatter | solution.py:604
  163.9 30.8 %copy-start.183 = (f32[64]{0:T(128)}, f32[64]{0:T(128)S(1)}, u32[]{:S(2)}) copy-start(f32[64]{0:T(128)S(1)} %multiply_power_fusion) | copy-start | bytes 772
  169.1 9.4 %copy-start.167 = (f32[6]{0:T(128)}, f32[6]{0:T(128)S(1)}, u32[]{:S(2)}) copy-start(f32[6]{0:T(128)S(1)} %dynamic_slice.57) | copy-start | bytes 76
  170.4 29.0 %copy-start.97 = (pred[1024]{0:T(1024)(128)(4,1)}, pred[1024]{0:T(1024)(128)(4,1)S(1)}, u32[]{:S(2)}) copy-start(pred[1024]{0:T(1024)(128)(4,1)S(1)} %get-tuple-element.831) | copy-start | bytes 3076
  170.4 29.0 %copy-start.103 = (pred[1024]{0:T(1024)(128)(4,1)}, pred[1024]{0:T(1024)(128)(4,1)S(1)}, u32[]{:S(2)}) copy-start(pred[1024]{0:T(1024)(128)(4,1)S(1)} %get-tuple-element.832) | copy-start | bytes 3076
  170.4 29.0 %copy-start.106 = (pred[1024]{0:T(1024)(128)(4,1)}, pred[1024]{0:T(1024)(128)(4,1)S(1)}, u32[]{:S(2)}) copy-start(pred[1024]{0:T(1024)(128)(4,1)S(1)} %get-tuple-element.833) | copy-start | bytes 3076
  170.4 29.0 %copy-start.109 = (pred[1024]{0:T(1024)(128)(4,1)}, pred[1024]{0:T(1024)(128)(4,1)S(1)}, u32[]{:S(2)}) copy-start(pred[1024]{0:T(1024)(128)(4,1)S(1)} %get-tuple-element.834) | copy-start | bytes 3076
  171.2 28.2 %copy-start.155 = (f32[64]{0:T(128)}, f32[64]{0:T(128)S(1)}, u32[]{:S(2)}) copy-start(f32[64]{0:T(128)S(1)} %get-tuple-element.842) | copy-start | bytes 772
  171.2 28.2 %copy-start.157 = (f32[64]{0:T(128)}, f32[64]{0:T(128)S(1)}, u32[]{:S(2)}) copy-start(f32[64]{0:T(128)S(1)} %get-tuple-element.843) | copy-start | bytes 772
  171.2 28.3 %copy-start.159 = (f32[64]{0:T(128)}, f32[64]{0:T(128)S(1)}, u32[]{:S(2)}) copy-start(f32[64]{0:T(128)S(1)} %get-tuple-element.844) | copy-start | bytes 772
  171.2 28.3 %copy-start.161 = (f32[64]{0:T(128)}, f32[64]{0:T(128)S(1)}, u32[]{:S(2)}) copy-start(f32[64]{0:T(128)S(1)} %get-tuple-element.845) | copy-start | bytes 772
  172.7 122.5 %copy-start.101 = (f32[384]{0:T(512)}, f32[384]{0:T(512)S(1)}, u32[]{:S(2)}) copy-start(f32[384]{0:T(512)S(1)} %dynamic_slice.61) | copy-start | bytes 4612
  177.1 11.7 %copy-start.95 = (f32[3,384]{1,0:T(4,128)}, f32[3,384]{1,0:T(4,128)S(1)}, u32[]{:S(2)}) copy-start(f32[3,384]{1,0:T(4,128)S(1)} %slice.509) | copy-start | bytes 13828
  177.1 22.3 %copy-start.122 = (f32[3,64]{1,0:T(4,128)}, f32[3,64]{1,0:T(4,128)S(1)}, u32[]{:S(2)}) copy-start(f32[3,64]{1,0:T(4,128)S(1)} %slice.501) | copy-start | bytes 2308
  178.5 39.4 %copy-start.61 = (f32[1024,6]{1,0:T(8,128)}, f32[1024,6]{1,0:T(8,128)S(1)}, u32[]{:S(2)}) copy-start(f32[1024,6]{1,0:T(8,128)S(1)} %get-tuple-element.763) | copy-start | bytes 73732
  179.9 84.9 %copy-start.86 = (f32[8,6,128]{2,1,0:T(8,128)}, f32[8,6,128]{2,1,0:T(8,128)S(1)}, u32[]{:S(2)}) copy-start(f32[8,6,128]{2,1,0:T(8,128)S(1)} %fusion.178) | copy-start | bytes 73732
  180.1 38.0 %copy-start.81 = (f32[8,6,128]{2,1,0:T(8,128)}, f32[8,6,128]{2,1,0:T(8,128)S(1)}, u32[]{:S(2)}) copy-start(f32[8,6,128]{2,1,0:T(8,128)S(1)} %get-tuple-element.825) | copy-start | bytes 73732
  180.4 8.4 copy-start.141
  180.4 82.8 %copy-start.116 = (f32[6]{0:T(128)}, f32[6]{0:T(128)S(1)}, u32[]{:S(2)}) copy-start(f32[6]{0:T(128)S(1)} %get-tuple-element.650) | copy-start | bytes 76
  180.4 82.8 %copy-start.120 = (f32[6]{0:T(128)}, f32[6]{0:T(128)S(1)}, u32[]{:S(2)}) copy-start(f32[6]{0:T(128)S(1)} %get-tuple-element.651) | copy-start | bytes 76
  180.5 83.4 %copy-start.114 = (f32[6]{0:T(128)}, f32[6]{0:T(128)S(1)}, u32[]{:S(2)}) copy-start(f32[6]{0:T(128)S(1)} %get-tuple-element.648) | copy-start | bytes 76
  180.5 83.4 %copy-start.118 = (f32[6]{0:T(128)}, f32[6]{0:T(128)S(1)}, u32[]{:S(2)}) copy-start(f32[6]{0:T(128)S(1)} %get-tuple-element.649) | copy-start | bytes 76
  180.5 91.3 %copy-start.132 = (f32[6]{0:T(128)}, f32[6]{0:T(128)S(1)}, u32[]{:S(2)}) copy-start(f32[6]{0:T(128)S(1)} %get-tuple-element.647) | copy-start | bytes 76
  218.1 46.7 %copy-start.78 = (f32[8,6,128]{2,1,0:T(8,128)}, f32[8,6,128]{2,1,0:T(8,128)S(1)}, u32[]{:S(2)}) copy-start(f32[8,6,128]{2,1,0:T(8,128)S(1)} %copy.563) | copy-start | bytes 73732
  225.5 28.7 %copy-start.112 = (f32[384]{0:T(512)}, f32[384]{0:T(512)S(1)}, u32[]{:S(2)}) copy-start(f32[384]{0:T(512)S(1)} %mul.1481) | copy-start | bytes 4612
  225.6 28.7 %copy-start.72 = (bf16[32,8,8,128]{3,1,2,0:T(8,128)(2,1)S(1)}, bf16[32,8,8,128]{3,1,2,0:T(8,128)(2,1)}, u32[]{:S(2)}) copy-start(bf16[32,8,8,128]{3,1,2,0:T(8,128)(2,1)} %get-tuple-element.807) | copy-start | bytes 1572868
  386.7 39.1 %copy-start.2 = (f32[128,2048]{1,0:T(8,128)}, f32[128,2048]{1,0:T(8,128)S(1)}, u32[]{:S(2)}) copy-start(f32[128,2048]{1,0:T(8,128)S(1)} %get-tuple-element.216.hidden) | copy-start | bytes 3145732
  425.9 60.9 %copy-start.75 = (bf16[1024,384]{1,0:T(8,128)(2,1)S(1)}, bf16[1024,384]{1,0:T(8,128)(2,1)}, u32[]{:S(2)}) copy-start(bf16[1024,384]{1,0:T(8,128)(2,1)} %multiply_convert_fusion.4) | copy-start | bytes 2359300
  492.7 309.0 %reduce-scatter.14.cloned.1.call-start = ((), (), s32[]{:S(2)}) async-start(), calls=%async_computation.17 | async-start | bytes 2621440 | tf_op jit(solution)/shard_map/reduce_scatter | solution.py:604
  499.9 322.1 %reduce-scatter.6.cloned.1.call-start = ((), (), s32[]{:S(2)}) async-start(), calls=%async_computation.13 | async-start | bytes 4718592 | tf_op jit(solution)/shard_map/reduce_scatter | solution.py:748
  540.4 50.7 %copy-start.192 = (bf16[2048,512]{1,0:T(8,128)(2,1)S(1)}, bf16[2048,512]{1,0:T(8,128)(2,1)}, u32[]{:S(2)}) copy-start(bf16[2048,512]{1,0:T(8,128)(2,1)} %all-gather.10.cloned.1.call-done) | copy-start | bytes 6291460
  540.4 50.7 %copy-start.196 = (bf16[1024,512]{0,1:T(8,128)(2,1)S(1)}, bf16[1024,512]{0,1:T(8,128)(2,1)}, u32[]{:S(2)}) copy-start(bf16[1024,512]{0,1:T(8,128)(2,1)} %get-tuple-element.782) | copy-start | bytes 3145732
  595.5 278.5 %reduce-scatter.12.cloned.1.call-start = ((), (), s32[]{:S(2)}) async-start(), calls=%async_computation.16 | async-start | bytes 5242880 | tf_op jit(solution)/shard_map/reduce_scatter | solution.py:604
  642.4 236.5 %reduce-scatter.8.cloned.1.call-start = ((), (), s32[]{:S(2)}) async-start(), calls=%async_computation.14 | async-start | bytes 5898240 | tf_op jit(solution)/shard_map/reduce_scatter | solution.py:604
  795.9 12.2 %all-to-all-start.1 = ((bf16[4,128,512]{2,1,0:T(8,128)(2,1)}), bf16[4,128,512]{2,1,0:T(8,128)(2,1)S(1)}, u32[]{:S(2)}, u32[]{:S(2)}) async-start(bf16[4,128,512]{2,1,0:T(8,128)(2,1)} %bitcast.535), calls=%async_computation.4 | async-start | bytes 1048576 | tf_op jit(solution)/shard_map/all_to_all | solution.py:605
  808.2 10.8 %all-to-all-start.3 = ((bf16[4,128,512]{2,1,0:T(8,128)(2,1)}), bf16[4,128,512]{2,1,0:T(8,128)(2,1)}, u32[]{:S(2)}, u32[]{:S(2)}) async-start(bf16[4,128,512]{2,1,0:T(8,128)(2,1)} %bitcast.534), calls=%async_computation.8 | async-start | bytes 1048576 | tf_op jit(solution)/shard_map/all_to_all | solution.py:605
  813.5 8.4 copy-start.3
  874.0 18.9 %all-to-all-start.2 = ((bf16[4,128,1024]{2,1,0:T(8,128)(2,1)}), bf16[4,128,1024]{2,1,0:T(8,128)(2,1)}, u32[]{:S(2)}, u32[]{:S(2)}) async-start(bf16[4,128,1024]{2,1,0:T(8,128)(2,1)} %bitcast.523), calls=%async_computation.6 | async-start | bytes 2097152 | tf_op jit(solution)/shard_map/all_to_all | solution.py:605
  892.9 19.4 %all-to-all-start = ((bf16[4,128,1152]{1,2,0:T(8,128)(2,1)}), bf16[4,128,1152]{1,2,0:T(8,128)(2,1)}, u32[]{:S(2)}, u32[]{:S(2)}) async-start(bf16[4,128,1152]{1,2,0:T(8,128)(2,1)} %copy.618), calls=%async_computation.2 | async-start | bytes 2359296 | tf_op jit(solution)/shard_map/all_to_all | solution.py:605
  (167 other events, 589.1 us)
Sparse Core Ops, SparseCore 0:
  29.7 92.0 all-gather.7
  162.1 58.3 all-gather.15
  222.1 53.7 all-gather.11
  277.3 88.0 all-gather.13
  366.9 44.4 all-gather.9
  492.8 47.2 reduce-scatter.9
  542.6 56.3 reduce-scatter.13
  602.3 51.8 reduce-scatter.5
  656.7 76.7 reduce-scatter.11
  782.5 89.4 reduce-scatter.7

commit v3 on v2

v3 whole, which is shorter than its diff:
```python
import functools

import jax
import jax.numpy as jnp
from jax import lax
from jax.experimental import pallas as pl
from jax.experimental.pallas import tpu as pltpu
from jax.sharding import Mesh, PartitionSpec as P

P_SIZE = 64
N = 256
HD = 128
K = 4
G = 4
CHUNK = 128
RIM = 16

highest = lax.Precision.HIGHEST
rope_base = 10000.0
norm_eps = 1e-05
bf16 = jnp.bfloat16
f32 = jnp.float32
MESH = pl.DeviceIdType.MESH
HBM = pl.BlockSpec(memory_space=pl.ANY)
VMEM = pl.BlockSpec(memory_space=pltpu.VMEM)
DMA = pltpu.SemaphoreType.DMA


def rcopy(src, dst, send, recv, **where):
    return pltpu.make_async_remote_copy(
        src_ref=src, dst_ref=dst, send_sem=send, recv_sem=recv, device_id=where, device_id_type=MESH
    )


def here():
    return lax.axis_index("z"), lax.axis_index("p"), lax.axis_index("head")


def ring(p, d):
    return lax.rem(p + d + G, G)


def greet(*partners):
    barrier = pltpu.get_barrier_semaphore()
    for where in partners:
        pl.semaphore_signal(barrier, inc=1, device_id=where, device_id_type=MESH)
    pl.semaphore_wait(barrier, len(partners))


def plane_partners(p, c):
    return [{"p": ring(p, d)} for d in range(1, G)] + [{"head": 1 - c}]


def line_partners(z, planes):
    return [{"z": lax.rem(z + d, planes)} for d in range(1, planes)]


def beside(p):
    return p + 1 - 2 * lax.rem(p, 2), lax.rem(p + 2, G), G - 1 - p


class Spread:
    sems = [DMA((2,)), DMA((2,)), DMA((2,)), DMA((2,)), DMA((4,)), DMA((4,)), DMA(())]

    def __init__(self, block, out, start, rows, sems, cores=True):
        self.block, self.out, self.first, self.rows, self.cores = block, out, start, rows, cores
        self.s1, self.r1, self.s2, self.r2, self.s3, self.r3, self.keep = sems
        _, self.p, self.c = here()
        self.around = beside(self.p)

    def spot(self, q, half=None):
        first, rows = self.first(q, self.c), self.rows
        if half is not None:
            first, rows = first + half * (rows // 2), rows // 2
        return self.out.at[pl.ds(first, rows)]

    def over(self, i):
        return rcopy(self.block, self.spot(self.p), self.s1.at[i], self.r1.at[i], p=self.around[i])

    def relay(self, i):
        spot = self.spot(self.around[i], i)
        return rcopy(spot, spot, self.s2.at[i], self.r2.at[i], p=self.around[1 - i])

    def relayed(self, i):
        spot = self.spot(self.around[2], 1 - i)
        return rcopy(spot, spot, self.s2.at[1 - i], self.r2.at[1 - i], p=self.around[i])

    def across(self, i):
        spot = self.spot(self.p if i == 3 else self.around[i])
        return rcopy(self.block if i == 3 else spot, spot, self.s3.at[i], self.r3.at[i], head=1 - self.c)

    def mine(self):
        return pltpu.make_async_copy(self.block, self.spot(self.p), self.keep)

    def start(self):
        for i in (0, 1):
            self.over(i).start()
        if self.cores:
            self.across(3).start()
        self.mine().start()

    def pass_on(self):
        for i in (0, 1):
            self.over(i).wait_recv()
            self.relay(i).start()
            if self.cores:
                self.across(i).start()
        for i in (0, 1):
            self.relayed(i).wait_recv()
        if self.cores:
            self.across(2).start()

    def finish(self):
        self.mine().wait()
        for i in (0, 1):
            self.over(i).wait_send()
            self.relay(i).wait_send()
        if self.cores:
            for i in range(4):
                self.across(i).wait()


class Collect:
    @staticmethod
    def scratch(rows, width):
        return [
            pltpu.VMEM((4, rows, width), bf16), pltpu.VMEM((3, rows, width), bf16),
            pltpu.VMEM((2, rows // 2, width), bf16), pltpu.VMEM((2, rows, width), bf16),
            pltpu.VMEM((rows, width), f32), DMA((4,)), DMA((4,)), DMA((6,)), DMA((6,)),
        ]

    def __init__(self, part, rows, scratch, strip=16):
        self.part, self.rows, self.strip = part, rows, strip
        self.cx, self.out, self.rd, self.rx, self.total, self.s1, self.r1, self.s2, self.r2 = scratch
        _, self.p, self.c = here()
        self.around = beside(self.p)

    def first(self, q, c):
        return pl.multiple_of((q * 2 + c) * self.rows, 16)

    def owner(self, i):
        return self.p if i == 3 else self.around[i]

    def across(self, i):
        spot = self.part.at[pl.ds(self.first(self.owner(i), 1 - self.c), self.rows)]
        return rcopy(spot, self.cx.at[i], self.s1.at[i], self.r1.at[i], head=1 - self.c)

    def over(self, i, half):
        at = pl.ds(half * (self.rows // 2), self.rows // 2)
        k = 2 * i + half
        if i == 2:
            return rcopy(self.out.at[2, at], self.rd.at[half], self.s2.at[k], self.r2.at[k], p=self.around[half])
        return rcopy(self.out.at[i, at], self.rx.at[i, at], self.s2.at[k], self.r2.at[k], p=self.around[i])

    def strips(self, body, lo=0, hi=None):
        hi = self.rows if hi is None else hi

        def one(n, carry):
            body(lo + n * self.strip)
            return carry

        lax.fori_loop(0, (hi - lo) // self.strip, one, 0)

    def at(self, first):
        return pl.ds(pl.multiple_of(first, self.strip), self.strip)

    def add(self, i, half=None, relayed=None):
        first = self.first(self.owner(i), self.c)
        size = self.rows // 2

        def one(at):
            v = self.part[self.at(first + at)].astype(f32) + self.cx[i, self.at(at)].astype(f32)
            if relayed is not None:
                v = v + self.rd[relayed, self.at(at - half * size)].astype(f32)
            if i == 3:
                self.total[self.at(at)] = v
            else:
                self.out[i, self.at(at)] = v.astype(bf16)

        if half is None:
            self.strips(one)
        else:
            self.strips(one, half * size, (half + 1) * size)

    def start(self):
        for i in (2, 0, 1, 3):
            self.across(i).start()

    def middle(self):
        self.across(2).wait_recv()
        for half in (0, 1):
            self.add(2, half)
            self.over(2, half).start()
        for i in (0, 1):
            self.across(i).wait_recv()
            self.add(i, i)
            self.over(i, i).start()
        self.across(3).wait_recv()
        self.add(3)
        for i in (0, 1):
            self.over(2, 1 - i).wait_recv()
            self.add(i, 1 - i, 1 - i)
            self.over(i, 1 - i).start()

    def arrive(self):
        for half in (0, 1):
            for i in (0, 1):
                self.over(i, i if half == 0 else 1 - i).wait_recv()

    def sum_of(self, at):
        r = self.at(at)
        return self.total[r] + self.rx[0, r].astype(f32) + self.rx[1, r].astype(f32)

    def finish(self):
        for i in range(4):
            self.across(i).wait_send()
        for i in range(3):
            for half in (0, 1):
                self.over(i, half).wait_send()


def call(body, name_id, outs, out_specs, ins, in_specs, scratch, us=20):
    return pl.pallas_call(
        body,
        out_shape=outs,
        in_specs=in_specs,
        out_specs=out_specs,
        scratch_shapes=scratch,
        cost_estimate=pl.CostEstimate(flops=0, bytes_accessed=us * 3_500_000, transcendentals=0),
        compiler_params=pltpu.CompilerParams(
            collective_id=name_id, has_side_effects=True, vmem_limit_bytes=48 * 2**20
        ),
    )(*ins)


def shape(dims, kind):
    return jax.ShapeDtypeStruct(dims, kind)


def exchange_copies(pieces, sems, keep):
    _, p, _ = here()
    away, own = [], []
    for i, (source, width, target, first, led) in enumerate(pieces):
        rows = source.shape[-2]
        spot = target.at[pl.ds(pl.multiple_of(p * rows, 16), rows), pl.ds(first, width)]
        for d in range(G):
            q = ring(p, d)
            taken = source.at[q] if led else source.at[:, pl.ds(pl.multiple_of(q * width, 128), width)]
            if d:
                away.append(rcopy(taken, spot, sems[0].at[d - 1, i], sems[1].at[d - 1, i], p=q))
            else:
                own.append(pltpu.make_async_copy(taken, spot, keep.at[i]))
    return away, own


def exchange_a_body(x_ref, q_ref, small_ref, out_ref, send, recv, keep):
    _, p, c = here()
    greet(*[{"p": ring(p, d)} for d in range(1, G)])
    xw, qw = (r.shape[1] // G for r in (x_ref, q_ref))
    pieces = [
        (x_ref, xw, out_ref, 0, False), (q_ref, qw, out_ref, xw, False),
        (small_ref, small_ref.shape[2], out_ref, xw + qw, True),
    ]
    away, own = exchange_copies(pieces, (send, recv), keep)
    for copy in away + own:
        copy.start()
    for copy in own + away:
        copy.wait()


def exchange_b_body(z_ref, out_ref, o_ref, wb, send, recv, keep):
    _, p, c = here()
    greet(*[{"p": ring(p, d)} for d in range(1, G)])
    zw, ow, aw = (r.shape[1] // G for r in (z_ref, out_ref, o_ref))
    pieces = [(z_ref, zw, wb, 0, False), (out_ref, ow, wb, zw, False), (o_ref, aw, wb, zw + ow, False)]
    away, own = exchange_copies(pieces, (send, recv), keep)
    for copy in away + own:
        copy.start()
    for copy in own + away:
        copy.wait()


def start_body(planes, gate_w, up_w, down_w, first, low, docs, wc, wd, n1, ol, all_docs, *sems):
    z, p, c = here()
    greet(*plane_partners(p, c), *line_partners(z, planes))
    send, recv, keep, rim_s, rim_r, ps, pr, zs, zr, dk = sems[:10]
    rows = first.shape[0]
    a = Spread(first, n1, lambda q, k: pl.multiple_of(RIM + (q * 2 + k) * rows, 16), rows, sems[10:17])
    b = Spread(low, ol, lambda q, k: pl.multiple_of((q * 2 + k) * rows, 16), rows, sems[17:24])
    gw, uw, dw = (r.shape[1] // G for r in (gate_w, up_w, down_w))
    pieces = [(gate_w, gw, wc, 0, False), (up_w, uw, wc, gw, False), (down_w, dw, wd, 0, False)]
    away, own = exchange_copies(pieces, (send, recv), keep)
    near = [rcopy(docs, all_docs.at[z, p], ps.at[d - 1], pr.at[d - 1], p=ring(p, d)) for d in (1, 2, 3)]
    own_docs = pltpu.make_async_copy(docs, all_docs.at[z, p], dk)
    a.start()
    for copy in near:
        copy.start()
    own_docs.start()
    for copy in own:
        copy.start()
    a.pass_on()
    for copy in away:
        copy.start()
    b.start()
    a.finish()
    last = n1.at[pl.ds(n1.shape[0] - RIM, RIM)]
    rim = rcopy(last, n1.at[pl.ds(0, RIM)], rim_s, rim_r, z=lax.rem(z + 1, planes))
    rim.start()
    own_docs.wait()
    for copy in near:
        copy.wait()
    far = [
        rcopy(all_docs.at[z], all_docs.at[z], zs.at[d - 1], zr.at[d - 1], z=lax.rem(z + d, planes)) for d in range(1, planes)
    ]
    for copy in far:
        copy.start()
    b.pass_on()
    for copy in own + away:
        copy.wait()
    b.finish()
    rim.wait()
    for copy in far:
        copy.wait()


def spread_body(planes, block, kv, out, lines, zs, zr, zk, *sems):
    z, p, c = here()
    greet(*plane_partners(p, c), *line_partners(z, planes))
    rows = block.shape[0]
    far = [rcopy(kv, lines.at[z], zs.at[d - 1], zr.at[d - 1], z=lax.rem(z + d, planes)) for d in range(1, planes)]
    keep = pltpu.make_async_copy(kv, lines.at[z], zk)
    for copy in far:
        copy.start()
    keep.start()
    s = Spread(block, out, lambda q, k: pl.multiple_of((k * G + q) * rows, 16), rows, sems)
    s.start()
    s.pass_on()
    s.finish()
    keep.wait()
    for copy in far:
        copy.wait()


def state_copies(planes, upward, state, factor, states, factors, sems):
    z, _, _ = here()
    s1, r1, s2, r2 = sems
    way = 1 if upward else -1

    def pair(d):
        to = lax.rem(z + way * d + planes, planes)
        return (
            rcopy(state, states.at[d - 1], s1.at[d - 1], r1.at[d - 1], z=to),
            rcopy(factor, factors.at[d - 1], s2.at[d - 1], r2.at[d - 1], z=to),
        )

    def start():
        for d in range(1, planes):
            @pl.when((z + d < planes) if upward else (z - d >= 0))
            def _():
                for copy in pair(d):
                    copy.start()

    def wait():
        for d in range(1, planes):
            @pl.when((z - d >= 0) if upward else (z + d < planes))
            def _():
                for copy in pair(d):
                    copy.wait_recv()

            @pl.when((z + d < planes) if upward else (z - d >= 0))
            def _():
                for copy in pair(d):
                    copy.wait_send()

    return start, wait


def up_body(planes, state, factor, lines, states, factors, kv, *sems):
    z, p, c = here()
    greet(*plane_partners(p, c), *line_partners(z, planes))
    start, wait = state_copies(planes, True, state, factor, states, factors, sems[:4])
    start()
    s = Spread(lines, kv, lambda q, k: q * planes, planes, sems[4:], cores=False)
    s.start()
    s.pass_on()
    s.finish()
    wait()


def down_body(planes, state, factor, dkv, states, factors, kv, *sems):
    z, p, c = here()
    greet(*plane_partners(p, c), *line_partners(z, planes))
    start, wait = state_copies(planes, False, state, factor, states, factors, sems[:4])
    start()
    ks, kr, kk = sems[4:]
    over = [rcopy(dkv.at[ring(p, d)], kv.at[d], ks.at[d - 1], kr.at[d - 1], p=ring(p, d)) for d in (1, 2, 3)]
    keep = pltpu.make_async_copy(dkv.at[p], kv.at[0], kk)
    for copy in over:
        copy.start()
    keep.start()
    keep.wait()
    for copy in over:
        copy.wait()
    wait()


def hidden_body(part, x_ref, gain, hidden, second, *scratch):
    _, p, c = here()
    greet(*plane_partners(p, c))
    rows = x_ref.shape[0]
    s = Collect(part, rows, scratch[:9])
    stage = scratch[9]
    s.start()
    s.middle()
    s.arrive()

    def one(at):
        r = s.at(at)
        h = x_ref[r] + s.sum_of(at)
        hidden[r] = h
        scale = lax.rsqrt(jnp.mean(h * h, axis=-1, keepdims=True) + norm_eps)
        stage[r] = (h * scale * gain[...]).astype(bf16)

    s.strips(one)
    g = Spread(stage, second, s.first, rows, scratch[10:17])
    g.start()
    g.pass_on()
    s.finish()
    g.finish()


def branch_body(part, hidden, cot, gain, d_hidden, gain_grad, branch, *scratch):
    _, p, c = here()
    greet(*plane_partners(p, c))
    rows = hidden.shape[0]
    s = Collect(part, rows, scratch[:9])
    stage = scratch[9]
    gain_grad[...] = jnp.zeros_like(gain_grad)
    s.start()
    s.middle()
    s.arrive()

    def one(at):
        r = s.at(at)
        h = hidden[r]
        scale = lax.rsqrt(jnp.mean(h * h, axis=-1, keepdims=True) + norm_eps)
        grad = s.sum_of(at)
        gain_grad[pl.ds(0, 1)] += jnp.sum(grad * h * scale, axis=0, keepdims=True)
        u = grad * gain[...]
        d = cot[r] + scale * u - h * (scale * scale * scale * jnp.mean(u * h, axis=-1, keepdims=True))
        d_hidden[r] = d
        stage[r] = d.astype(bf16)

    s.strips(one)
    g = Spread(stage, branch, s.first, rows, scratch[10:17])
    g.start()
    g.pass_on()
    s.finish()
    g.finish()


def final_body(planes, part, x_ref, d_hidden, layer, gain, small, grad_in, layer_out, sums, *scratch):
    z, p, c = here()
    greet(*plane_partners(p, c), *line_partners(z, planes))
    rows = x_ref.shape[0]
    s = Collect(part, rows, scratch[:9])
    stage, mine, others, zs, zr, es, er, ek = scratch[9:17]
    half = pl.ds(pl.multiple_of(c * rows, 16), rows)

    def halves(i, source, target):
        return (
            rcopy(source, target.at[half], es.at[i], er.at[i], head=1 - c),
            pltpu.make_async_copy(source, target.at[half], ek.at[i]),
        )

    s.start()
    first = halves(0, layer, layer_out)
    for copy in first:
        copy.start()
    mine[...] = small[...]
    s.middle()
    s.arrive()

    def one(at):
        r = s.at(at)
        v = x_ref[r]
        scale = lax.rsqrt(jnp.mean(v * v, axis=-1, keepdims=True) + norm_eps)
        grad = s.sum_of(at)
        mine[pl.ds(3, 1)] += jnp.sum(grad * v * scale, axis=0, keepdims=True)
        u = grad * gain[...]
        stage[r] = d_hidden[r] + scale * u - v * (scale * scale * scale * jnp.mean(u * v, axis=-1, keepdims=True))

    s.strips(one)
    second = halves(1, stage, grad_in)
    for copy in second:
        copy.start()
    lines = [
        rcopy(mine, others.at[d - 1], zs.at[d - 1], zr.at[d - 1], z=lax.rem(z + d, planes)) for d in range(1, planes)
    ]
    for copy in lines:
        copy.start()
    for copy in lines:
        copy.wait()
    total = mine[...]
    for d in range(1, planes):
        total = total + others[d - 1]
    mine[...] = total
    g = Spread(mine, sums, lambda q, k: pl.multiple_of((q * 2 + k) * RIM, RIM), RIM, scratch[17:24])
    g.start()
    g.pass_on()
    s.finish()
    for copy in first + second:
        copy.wait()
    g.finish()


def back_body(planes, dbc, dkv, d_silu_bc, gx, g_bc, rim_bc, rim_x, kv_out, *scratch):
    z, p, c = here()
    greet(*plane_partners(p, c), *line_partners(z, planes))
    (cx, bx, rbc, skv, zkv, acc, xs, xr, bs, br, zs, zr, ms, mr) = scratch
    rows = rbc.shape[1]
    across = rcopy(
        dbc.at[pl.ds(pl.multiple_of((1 - c) * G * rows, 16), G * rows)], cx, xs, xr, head=1 - c
    )
    across.start()

    def add_kv(i, carry):
        v = dkv[0, i].astype(f32)
        for d in (1, 2, 3):
            v = v + dkv[d, i].astype(f32)
        skv[i] = v.astype(bf16)
        return carry

    lax.fori_loop(0, planes, add_kv, 0)

    def kv_down(d):
        to = lax.rem(z - d + planes, planes)
        return rcopy(skv.at[to], zkv.at[d - 1], zs.at[d - 1], zr.at[d - 1], z=to)

    for d in range(1, planes):
        @pl.when(z - d >= 0)
        def _():
            kv_down(d).start()

    across.wait_recv()
    bc_over = []
    for d in (1, 2, 3, 0):
        q = ring(p, d)
        own = dbc[pl.ds(pl.multiple_of((c * G + q) * rows, 16), rows)].astype(f32)
        own = own + cx[pl.ds(pl.multiple_of(q * rows, 16), rows)].astype(f32)
        if d:
            bx[d - 1] = own.astype(bf16)
            bc_over.append(rcopy(bx.at[d - 1], rbc.at[d - 1], bs.at[d - 1], br.at[d - 1], p=q))
            bc_over[-1].start()
        else:
            acc[...] = own
    for copy in bc_over:
        copy.wait_recv()
    g = acc[...]
    for d in range(3):
        g = g + rbc[d].astype(f32)
    g_bc[...] = g * d_silu_bc[...]
    before = lax.rem(z - 1 + planes, planes)
    rims = [
        rcopy(g_bc.at[:, pl.ds(0, 128)], rim_bc, ms.at[0], mr.at[0], z=before),
        rcopy(gx, rim_x, ms.at[1], mr.at[1], z=before),
    ]
    for copy in rims:
        copy.start()
    kv_out[...] = skv[z].astype(f32)
    for d in range(1, planes):
        @pl.when(z + d < planes)
        def _():
            kv_down(d).wait_recv()
            kv_out[...] += zkv[d - 1].astype(f32)

        @pl.when(z - d >= 0)
        def _():
            kv_down(d).wait_send()

    for copy in rims:
        copy.wait()
    across.wait_send()
    for copy in bc_over:
        copy.wait_send()


def mm(a, b, ca, cb):
    return lax.dot_general(a.astype(bf16), b.astype(bf16), (((ca,), (cb,)), ((), ())), preferred_element_type=f32)


def mm_exact(a, b, ca, cb):
    return lax.dot_general(a, b, (((ca,), (cb,)), ((), ())), precision=highest, preferred_element_type=f32)


def iota(dims, axis):
    return lax.broadcasted_iota(jnp.int32, dims, axis)


def soft(v):
    return jnp.maximum(v, 0.0) + jnp.log1p(jnp.exp(-jnp.abs(v)))


def sig(v):
    return 1.0 / (1.0 + jnp.exp(-v))


def rates_of(raw, bias, rates, heads):
    lane = iota((CHUNK, 128), 1)
    step = jnp.where(lane < heads, soft(raw + bias), 0.0)
    log_decay = -jnp.exp(rates) * step
    lower = (iota((CHUNK, CHUNK), 0) >= iota((CHUNK, CHUNK), 1)).astype(f32)
    return step, log_decay, mm_exact(lower, log_decay, 1, 0)


def pair_of(v, pair):
    left = iota((CHUNK, 128), 1) < P_SIZE
    return jnp.where(left, v[:, 2 * pair : 2 * pair + 1], v[:, 2 * pair + 1 : 2 * pair + 2])


def lanes(v, pair):
    return v[:, pair * 128 : (pair + 1) * 128]


def halves_of(a, b):
    return jnp.where(iota(a.shape, 1) < P_SIZE, a, b)


def head_means(v):
    same = (iota((128, 128), 0) // P_SIZE == iota((128, 128), 1) // P_SIZE).astype(f32) / P_SIZE
    return jnp.concatenate([mm_exact(lanes(v, k), same, 1, 0) for k in range(v.shape[1] // 128)], axis=1)


def head_sums(v, heads):
    chan = v.shape[1]
    pick = (iota((chan, 128), 0) // P_SIZE == iota((chan, 128), 1)).astype(f32)
    return mm_exact(v, pick, 1, 0)


def scale_rows(v, factor, heads):
    return jnp.concatenate(
        [v[h * P_SIZE : (h + 1) * P_SIZE] * factor[h : h + 1, :1] for h in range(heads)], axis=0
    )


def conv_of(pa_ref, taps_ref, starts, place, c, chan, first):
    block = pa_ref[pl.ds(pl.multiple_of(c * CHUNK + RIM - 8, 8), CHUNK + 8), first : first + chan]
    total = jnp.zeros((CHUNK, chan), f32)
    for lag in range(K):
        back = K - 1 - lag
        total = total + jnp.where(place - back >= starts, block[8 - back : 8 - back + CHUNK] * taps_ref[lag : lag + 1], 0.0)
    return total


def places_of(base_ref, c):
    return base_ref[0] + c * CHUNK + iota((CHUNK, 1), 0)


def weights_of(h, cs, cs_t, visible):
    span = cs[:, h : h + 1] - cs_t[h : h + 1]
    return jnp.where(visible, jnp.exp(jnp.where(visible, span, 0.0)), 0.0)


def visible_of(base_ref, c, starts, place):
    across = base_ref[0] + c * CHUNK + iota((CHUNK, CHUNK), 1)
    return (starts <= across) & (across <= place)


def decays_of(cs, starts, place):
    first = place[:1]
    decay_in = jnp.where(starts < first, jnp.exp(cs), 0.0)
    closing = jnp.where(starts[CHUNK - 1 :] <= place, jnp.exp(cs[CHUNK - 1 :] - cs), 0.0)
    return decay_in, closing


def scan_body(heads, base_ref, pa_ref, bc_ref, starts_ref, taps_ref, bias_ref, rates_ref,
              y_ref, cv_ref, enter_ref, reach_ref, state_out, through_out, state, through):
    c = pl.program_id(0)
    chan = heads * P_SIZE

    @pl.when(c == 0)
    def _():
        state[...] = jnp.zeros_like(state)
        through[...] = jnp.ones_like(through)

    starts, place = starts_ref[...], places_of(base_ref, c)
    raw = pa_ref[pl.ds(pl.multiple_of(c * CHUNK + RIM, 16), CHUNK), chan + 2 * HD :]
    step, _, cs = rates_of(raw, bias_ref[...], rates_ref[...], heads)
    cs_t = cs.T
    cv = conv_of(pa_ref, taps_ref, starts, place, c, chan, 0)
    cv_ref[...] = cv
    x = cv * sig(cv)
    b_rows, c_rows = bc_ref[:, :N], bc_ref[:, N:]
    inter = mm(c_rows, b_rows, 1, 1)
    visible = visible_of(base_ref, c, starts, place)
    decay_in, closing = decays_of(cs, starts, place)
    ends = decay_in.T
    for k in range(heads // 2):
        driven = lanes(x, k) * pair_of(step, k)
        mixed = [mm(weights_of(2 * k + i, cs, cs_t, visible) * inter, driven, 1, 0) for i in (0, 1)]
        y_ref[:, k * 128 : (k + 1) * 128] = halves_of(*mixed)
        local = mm(driven * pair_of(closing, k), b_rows, 0, 0)
        at = pl.ds(k * 128, 128)
        old = state[at]
        enter_ref[0, at] = old
        both = jnp.concatenate(
            [old[i * P_SIZE : (i + 1) * P_SIZE] * ends[2 * k + i : 2 * k + i + 1, CHUNK - 1 :] for i in (0, 1)], axis=0
        )
        state[at] = both + local
    factor = jnp.broadcast_to(ends[:8, CHUNK - 1 :], (8, 128))
    reach_ref[0, :8] = through[...]
    reach_ref[0, 8:] = factor
    through[...] = through[...] * factor
    state_out[...] = state[...].astype(bf16)
    through_out[...] = through[...]


def gate_parts(y_scan, cv, z, skip, gain):
    x = cv * sig(cv)
    ssm = y_scan + skip * x
    s = sig(z)
    gated = ssm * (z * s)
    r = lax.rsqrt(head_means(gated * gated) + norm_eps)
    return x, ssm, s, gated, r


def gate_body(heads, base_ref, pa_ref, bc_ref, starts_ref, bias_ref, rates_ref, y_ref, cv_ref, enter_ref, reach_ref,
              before_ref, z_ref, skip_ref, gain_ref, low_ref, scan_ref):
    c = pl.program_id(0)
    chan = heads * P_SIZE
    starts, place = starts_ref[...], places_of(base_ref, c)
    raw = pa_ref[pl.ds(pl.multiple_of(c * CHUNK + RIM, 16), CHUNK), chan + 2 * HD :]
    _, _, cs = rates_of(raw, bias_ref[...], rates_ref[...], heads)
    decay_in, _ = decays_of(cs, starts, place)
    state_in = enter_ref[0] + scale_rows(before_ref[...], reach_ref[0], heads)
    c_rows = bc_ref[:, N:]
    off = [mm(c_rows, state_in[k * 128 : (k + 1) * 128], 1, 1) * pair_of(decay_in, k) for k in range(heads // 2)]
    y_scan = y_ref[...] + jnp.concatenate(off, axis=1)
    scan_ref[...] = y_scan
    _, _, _, gated, r = gate_parts(y_scan, cv_ref[...], z_ref[...], skip_ref[...], gain_ref[...])
    low_ref[...] = (gated * r * gain_ref[...]).astype(bf16)


def gate_back_body(heads, chunks, base_ref, pa_ref, bc_ref, starts_ref, bias_ref, rates_ref, d_ref, scan_ref, cv_ref,
                   reach_ref, z_ref, skip_ref, gain_ref, dz_ref, dy_ref, leave_ref, tail_ref, state_out, gain_out, state, tail):
    c = chunks - 1 - pl.program_id(0)
    chan = heads * P_SIZE

    @pl.when(c == chunks - 1)
    def _():
        state[...] = jnp.zeros_like(state)
        tail[...] = jnp.ones_like(tail)
        gain_out[...] = jnp.zeros_like(gain_out)

    starts, place = starts_ref[...], places_of(base_ref, c)
    raw = pa_ref[pl.ds(pl.multiple_of(c * CHUNK + RIM, 16), CHUNK), chan + 2 * HD :]
    _, _, cs = rates_of(raw, bias_ref[...], rates_ref[...], heads)
    decay_in, _ = decays_of(cs, starts, place)
    z = z_ref[...]
    x, ssm, s, gated, r = gate_parts(scan_ref[...], cv_ref[...], z, skip_ref[...], gain_ref[...])
    d = d_ref[...]
    gain_out[:1] += jnp.sum(d * gated * r, axis=0, keepdims=True)
    u = d * gain_ref[...]
    d_gated = r * u - gated * (r * r * r * head_means(u * gated))
    dz_ref[...] = (d_gated * ssm * (s * (1.0 + z * (1.0 - s)))).astype(bf16)
    dy = d_gated * (z * s)
    dy_ref[...] = dy
    c_rows = bc_ref[:, N:]
    leave_ref[0] = state[...]
    tail_ref[0] = tail[...]
    factor = reach_ref[0, 8:]
    local = [mm(lanes(dy, k) * pair_of(decay_in, k), c_rows, 0, 0) for k in range(heads // 2)]
    state[...] = scale_rows(state[...], factor, heads) + jnp.concatenate(local, axis=0)
    tail[...] = tail[...] * factor
    state_out[...] = state[...].astype(bf16)


def scan_back_body(heads, base_ref, pa_ref, bc_ref, starts_ref, bias_ref, rates_ref, dy_ref, cv_ref,
                   enter_ref, reach_ref, before_ref, leave_ref, tail_ref, after_ref, skip_ref,
                   gx_ref, dbc_ref, raw_out, rows_out, skip_out):
    c = pl.program_id(0)
    chan = heads * P_SIZE

    @pl.when(c == 0)
    def _():
        rows_out[...] = jnp.zeros_like(rows_out)
        skip_out[...] = jnp.zeros_like(skip_out)

    starts, place = starts_ref[...], places_of(base_ref, c)
    raw = pa_ref[pl.ds(pl.multiple_of(c * CHUNK + RIM, 16), CHUNK), chan + 2 * HD :]
    step, log_decay, cs = rates_of(raw, bias_ref[...], rates_ref[...], heads)
    cs_t = cs.T
    visible = visible_of(base_ref, c, starts, place)
    decay_in, closing = decays_of(cs, starts, place)
    b_rows, c_rows = bc_ref[:, :N], bc_ref[:, N:]
    inter = mm(c_rows, b_rows, 1, 1)
    cv = cv_ref[...]
    s = sig(cv)
    x = cv * s
    dy = dy_ref[...]
    state_in = enter_ref[0] + scale_rows(before_ref[...], reach_ref[0], heads)
    d_state = leave_ref[0] + scale_rows(after_ref[...], tail_ref[0], heads)
    left = iota((CHUNK, 128), 1) < P_SIZE
    d_inter = jnp.zeros((CHUNK, CHUNK), f32)
    d_b = jnp.zeros((CHUNK, N), f32)
    d_c = jnp.zeros((CHUNK, N), f32)
    inside, outside, closes, drives = [], [], [], []
    for k in range(heads // 2):
        at = slice(k * 128, (k + 1) * 128)
        driven = (lanes(x, k) * pair_of(step, k)).astype(bf16)
        dyk = lanes(dy, k)
        dyb = dyk.astype(bf16)
        d_mixed, y_mixed = [], []
        for i in (0, 1):
            w = weights_of(2 * k + i, cs, cs_t, visible)
            mix = (w * inter).astype(bf16)
            half = jnp.where(left if i == 0 else ~left, dyb, jnp.zeros_like(dyb))
            d_inter = d_inter + w * mm(half, driven, 1, 1)
            d_mixed.append(mm(mix, dyb, 0, 0))
            y_mixed.append(mm(mix, driven, 1, 0))
        d_mix = halves_of(*d_mixed)
        close = pair_of(closing, k)
        d_close = mm(b_rows, d_state[at], 1, 1)
        closed = driven.astype(f32) * close
        enter = pair_of(decay_in, k)
        y_off = mm(c_rows, state_in[at], 1, 1) * enter
        d_c = d_c + mm(dyk * enter, state_in[at], 1, 0)
        d_b = d_b + mm(closed, d_state[at], 1, 0)
        inside.append(dyb.astype(f32) * halves_of(*y_mixed) - driven.astype(f32) * d_mix)
        outside.append(dyk * y_off)
        closes.append(closed * d_close)
        drives.append(d_mix + close * d_close)
    d_c = d_c + mm(d_inter, b_rows, 1, 0)
    d_b = d_b + mm(d_inter, c_rows, 0, 0)
    dbc_ref[:, :N] = d_b.astype(bf16)
    dbc_ref[:, N:] = d_c.astype(bf16)
    d_driven = jnp.concatenate(drives, axis=1)
    closes = head_sums(jnp.concatenate(closes, axis=1), heads)
    d_cs = head_sums(jnp.concatenate(inside, axis=1) + jnp.concatenate(outside, axis=1), heads) - closes
    kept = head_sums_t(d_state * state_in, heads)
    whole = decay_in[CHUNK - 1 :] * kept + jnp.sum(closes, axis=0, keepdims=True)
    upper = (iota((CHUNK, CHUNK), 0) <= iota((CHUNK, CHUNK), 1)).astype(f32)
    d_la = mm_exact(upper, d_cs, 1, 0) + whole
    d_step = head_sums(d_driven * x, heads)
    d_raw = (d_step - jnp.exp(rates_ref[...]) * d_la) * sig(raw + bias_ref[...])
    d_raw = jnp.where(iota((CHUNK, 128), 1) < heads, d_raw, 0.0)
    raw_out[...] = d_raw.astype(bf16)
    rows_out[:1] += jnp.sum(d_raw, axis=0, keepdims=True)
    rows_out[1:2] += jnp.sum(d_la * log_decay, axis=0, keepdims=True)
    skip_out[:1] += jnp.sum(dy * x, axis=0, keepdims=True)
    wide = jnp.concatenate([pair_of(step, k) for k in range(heads // 2)], axis=1)
    gx_ref[...] = (d_driven * wide + skip_ref[...] * dy) * (s * (1.0 + cv * (1.0 - s)))


def head_sums_t(v, heads):
    column = jnp.sum(v, axis=1, keepdims=True)
    pick = (iota((v.shape[0], 128), 0) // P_SIZE == iota((v.shape[0], 128), 1)).astype(f32)
    return jnp.sum(column * pick, axis=0, keepdims=True)


def chunked(body, chunks, outs, out_specs, ins, in_specs, scratch=()):
    return pl.pallas_call(
        body,
        grid=(chunks,),
        out_shape=outs,
        in_specs=in_specs,
        out_specs=out_specs,
        scratch_shapes=list(scratch),
        cost_estimate=pl.CostEstimate(flops=2_000_000_000, bytes_accessed=40_000_000, transcendentals=0),
        compiler_params=pltpu.CompilerParams(vmem_limit_bytes=48 * 2**20),
    )(*ins)


def dot(a, b, ca, cb):
    return lax.dot_general(a, b, (((ca,), (cb,)), ((), ())), preferred_element_type=f32)


def exact(text, *operands):
    return jnp.einsum(text, *operands, precision=highest, preferred_element_type=f32)


def d_silu(v):
    s = jax.nn.sigmoid(v)
    return s * (1.0 + v * (1.0 - s))


def shifted(block, axis, distance):
    count = lax.axis_size(axis)
    route = [(i - distance, i) for i in range(count) if 0 <= i - distance < count]
    return lax.ppermute(block, axis, route)


def rope_tables(offsets, first, count):
    half = HD // 2
    index = (first + jnp.arange(count)).astype(f32)
    freqs = rope_base ** (-2.0 * index / HD)
    angles = offsets.astype(f32)[:, None] * freqs[None, :]
    return jnp.cos(angles), jnp.sin(angles)


def turn(v, cosine, sine):
    half = v.shape[-1] // 2
    a, b = v[:, :half], v[:, half:]
    return jnp.concatenate([a * cosine - b * sine, b * cosine + a * sine], axis=-1)


def conv_rows(padded, taps, starts, places):
    length = starts.shape[0]
    total = jnp.zeros((length, padded.shape[1]), f32)
    for lag in range(K):
        back = K - 1 - lag
        valid = (places - back >= starts)[:, None]
        total = total + jnp.where(valid, padded[RIM - back : RIM - back + length] * taps[lag][None, :], 0.0)
    return total


def conv_back(grad, grad_next, padded, taps, starts, places, starts_next):
    length = starts.shape[0]
    edge = K - 1
    longer = jnp.concatenate([grad, grad_next], axis=0)
    starts_long = jnp.concatenate([starts, starts_next])
    total = jnp.zeros_like(grad)
    tap_grads = []
    for lag in range(K):
        ahead = edge - lag
        seen = (places >= starts_long[ahead : ahead + length])[:, None]
        total = total + jnp.where(seen, longer[ahead : ahead + length], 0.0) * taps[lag][None, :]
        valid = (places - ahead >= starts)[:, None]
        tap_grads.append(jnp.sum(jnp.where(valid, grad * padded[RIM - ahead : RIM - ahead + length], 0.0), axis=0))
    return total, jnp.stack(tap_grads)


def mixer_row(v):
    return v.reshape(1, -1)


def on_device(
    layer_input, doc_start, mixer_gain, ffn_gain,
    z_weight, x_weight, bc_weight, dt_weight, q_weight, k_weight, v_weight,
    o_weight, out_weight, gate_weight, up_weight, down_weight,
    conv_inner, conv_state, decay_log, dt_bias, skip_coef, ssm_gain, cotangent,
):
    tokens, width = layer_input.shape
    rows = z_weight.shape[0]
    planes = lax.axis_size("z")
    cores = lax.axis_size("head")
    zi, pi, hi = (lax.axis_index(a) for a in ("z", "p", "head"))
    T = tokens * G
    total_tokens = T * planes
    offset = zi * T
    places = offset + jnp.arange(T, dtype=jnp.int32)
    own = tokens // cores
    heads = decay_log.shape[0] // G
    chan = heads * P_SIZE
    bcs = 2 * N // cores // G
    quarter_half = HD // 2 // G

    def my_slice(v, size, index, axis):
        return lax.dynamic_slice_in_dim(v, index * size, size, axis)

    taps_inner = my_slice(conv_inner, chan, pi, 1)
    taps_state = my_slice(conv_state, bcs, hi * G + pi, 1)
    rates = my_slice(decay_log, heads, pi, 0)
    bias = my_slice(dt_bias, heads, pi, 0)
    skip = my_slice(skip_coef, heads, pi, 0)
    gain_s = my_slice(ssm_gain, chan, pi, 0)

    def cut(w):
        return w.reshape(rows, G, -1)

    bc_mine = lax.dynamic_slice_in_dim(bc_weight, hi * (2 * N // cores), 2 * N // cores, 1)
    k_cut = jnp.moveaxis(k_weight.reshape(rows, 2, G, quarter_half), 2, 1).reshape(rows, G, -1)
    a_sizes = [chan, HD, bcs, 2 * quarter_half, 2 * quarter_half, heads]
    a_at = [sum(a_sizes[:i]) for i in range(len(a_sizes))]
    pad = -sum(a_sizes) % 128
    small_w = jnp.concatenate(
        [cut(bc_mine), k_cut, cut(v_weight), cut(dt_weight), jnp.zeros((rows, G, pad), bf16)], axis=2
    )
    small_w = jnp.moveaxis(small_w, 1, 0)
    a_cols = sum(a_sizes) + pad

    def gather(w):
        return lax.all_gather(w, "z", axis=0, tiled=True)

    exchange_sems = lambda n: [DMA((3, n)), DMA((3, n)), DMA((n,))]
    wa = gather(call(
        exchange_a_body, 0, shape((G * rows, a_cols), bf16), HBM,
        (x_weight, q_weight, small_w), [HBM] * 3, exchange_sems(3),
    ))

    def half(v):
        return lax.dynamic_slice_in_dim(v, hi * own, own, 0)

    x_own, cot_own = half(layer_input), half(cotangent)
    r1 = lax.rsqrt(jnp.mean(x_own * x_own, axis=-1, keepdims=True) + norm_eps)
    first_own = (x_own * r1 * mixer_gain).astype(bf16)
    wb = gather(call(
        exchange_b_body, 9, shape((G * rows, 2 * chan + HD), bf16), HBM,
        (z_weight, out_weight, o_weight), [HBM] * 3, exchange_sems(3),
    ))
    wc, wd, first_rim, out_low, docs = call(
        functools.partial(start_body, planes), 1,
        (shape((G * rows, gate_weight.shape[1] * 2 // G), bf16),
         shape((G * rows, down_weight.shape[1] // G), bf16), shape((RIM + T, width), bf16), shape((T, width), bf16),
         shape((planes, G, 8, tokens), jnp.int32)),
        (HBM,) * 5,
        (gate_weight, up_weight, down_weight, first_own, cot_own.astype(bf16), jnp.broadcast_to(doc_start[None], (8, tokens))),
        [HBM] * 3 + [VMEM] * 3,
        exchange_sems(3) + [DMA(()), DMA(()), DMA((3,)), DMA((3,)), DMA((planes - 1,)), DMA((planes - 1,)), DMA(())]
        + Spread.sems * 2, us=55,
    )
    wc, wd = gather(wc), gather(wd)
    wz, wb = wb[:, :chan], wb[:, chan:]
    first = first_rim[RIM:]
    all_starts = docs[:, :, 0].reshape(-1)
    starts = lax.dynamic_slice_in_dim(all_starts, offset, T, 0)

    def line_sum(grad):
        return lax.psum_scatter(grad, "z", scatter_dimension=0, tiled=True)

    def scatter(g):
        g = lax.all_to_all(g.reshape(G, rows, -1), "p", 0, 0, tiled=True)
        return jnp.moveaxis(g, 0, 1).astype(f32)

    edge = K - 1
    pa = dot(first_rim, wa, 1, 0)
    z_part = dot(first, wz, 1, 0)
    q_proj, bc_pre, k_proj, v_proj = (pa[RIM:, a : a + s] for a, s in zip(a_at[1:5], a_sizes[1:5]))
    bc_ext = pa[:, a_at[2] : a_at[2] + bcs]
    cv_bc = conv_rows(bc_ext, taps_state, starts, places)
    bc_low = jax.nn.silu(cv_bc).astype(bf16)
    offsets = places - starts
    cos_q, sin_q = rope_tables(offsets, 0, HD // 2)
    cos_k, sin_k = rope_tables(offsets, pi * quarter_half, quarter_half)
    scale = HD ** (-0.5)
    kvr = 4 * quarter_half
    query = (turn(q_proj, cos_q, sin_q) * scale).astype(bf16)
    kv_own = jnp.concatenate([turn(k_proj, cos_k, sin_k).astype(bf16), v_proj.astype(bf16)], axis=1)
    line_sems = [DMA((planes - 1,)), DMA((planes - 1,))]
    bc_t, kv_line = call(
        functools.partial(spread_body, planes), 2, (shape((2 * N, T), bf16), shape((planes, kvr, T), bf16)), (HBM, HBM),
        (bc_low.T, kv_own.T), [HBM, HBM], line_sems + [DMA(())] + Spread.sems,
    )
    bc_all = bc_t.T

    L = CHUNK
    nc = T // L
    base = jnp.full((1,), offset, jnp.int32)
    starts_col = starts[:, None]

    def row128(v):
        return jnp.pad(v, (0, 128 - v.shape[0]))[None]

    bias_row, rates_row = row128(bias), row128(rates)
    skip_row, gain_row = jnp.repeat(skip, P_SIZE)[None], gain_s[None]
    smem = pl.BlockSpec(memory_space=pltpu.SMEM)

    def specs(turned=False):
        at = (lambda c: nc - 1 - c) if turned else (lambda c: c)
        return (
            lambda cols: pl.BlockSpec((L, cols), lambda c: (at(c), 0)),
            lambda *dims: pl.BlockSpec(dims, lambda c: (0,) * len(dims)),
            lambda rows, cols: pl.BlockSpec((1, rows, cols), lambda c: (at(c), 0, 0)),
        )

    tile, fixed, stack = specs()
    pa_spec = fixed(*pa.shape)
    y_diag, cv_x, enter, reach, state, through = chunked(
        functools.partial(scan_body, heads), nc,
        (shape((T, chan), f32), shape((T, chan), f32), shape((nc, chan, N), f32), shape((nc, 16, 128), f32),
         shape((chan, N), bf16), shape((8, 128), f32)),
        (tile(chan), tile(chan), stack(chan, N), stack(16, 128), fixed(chan, N), fixed(8, 128)),
        (base, pa, bc_all, starts_col, taps_inner, bias_row, rates_row),
        [smem, pa_spec, tile(2 * N), tile(1), fixed(K, chan), fixed(1, 128), fixed(1, 128)],
        [pltpu.VMEM((chan, N), f32), pltpu.VMEM((8, 128), f32)],
    )

    def entering(upward, states, factors):
        total = jnp.zeros((chan, N), f32)
        for d in reversed(range(1, planes)):
            there = (zi - d >= 0) if upward else (zi + d < planes)
            factor = jnp.repeat(factors[d - 1, :heads, :1], P_SIZE, axis=0)
            total = jnp.where(there, total * factor + states[d - 1].astype(f32), total)
        return total

    state_shapes = (shape((planes - 1, chan, N), bf16), shape((planes - 1, 8, 128), f32))
    states, factors, kv_all = call(
        functools.partial(up_body, planes), 3, state_shapes + (shape((G * planes, kvr, T), bf16),), (HBM,) * 3,
        (state, through, kv_line), [HBM] * 3, line_sems * 2 + Spread.sems, us=28,
    )
    before = entering(True, states, factors)
    ssm_low, y_scan = chunked(
        functools.partial(gate_body, heads), nc,
        (shape((T, chan), bf16), shape((T, chan), f32)), (tile(chan), tile(chan)),
        (base, pa, bc_all, starts_col, bias_row, rates_row, y_diag, cv_x, enter, reach, before, z_part, skip_row, gain_row),
        [smem, pa_spec, tile(2 * N), tile(1), fixed(1, 128), fixed(1, 128), tile(chan), tile(chan), stack(chan, N),
         stack(16, 128), fixed(chan, N), tile(chan), fixed(1, chan), fixed(1, chan)],
    )

    kv_all = kv_all.reshape(G, planes, 4, quarter_half, T)
    keys = kv_all[:, :, :2].transpose(1, 4, 2, 0, 3).reshape(total_tokens, HD)
    values = kv_all[:, :, 2:].transpose(1, 4, 0, 2, 3).reshape(total_tokens, HD)
    key_len = min(512, total_tokens)
    first_block = starts[0] // key_len
    last_block = (offset + T - 1) // key_len

    def key_block(index):
        begin = index * key_len
        kb = lax.dynamic_slice_in_dim(keys, begin, key_len, 0)
        vb = lax.dynamic_slice_in_dim(values, begin, key_len, 0)
        at = begin + jnp.arange(key_len, dtype=jnp.int32)
        seen = (at[None, :] >= starts[:, None]) & (at[None, :] <= places[:, None])
        return kb, vb, seen, dot(query, kb, 1, 1)

    def running(index, carry):
        peak, mass = carry
        _, _, seen, scores = key_block(index)
        new = jnp.maximum(peak, jnp.max(jnp.where(seen, scores, -1e30), axis=-1))
        mass = mass * jnp.exp(peak - new) + jnp.sum(jnp.where(seen, jnp.exp(scores - new[:, None]), 0.0), axis=-1)
        return new, mass

    peak, mass = lax.fori_loop(
        first_block, last_block + 1, running, (jnp.full((T,), -1e30, f32), jnp.zeros((T,), f32))
    )
    log_mass = peak + jnp.log(mass)

    def weighted(index, total):
        _, vb, seen, scores = key_block(index)
        probs = jnp.where(seen, jnp.exp(scores - log_mass[:, None]), 0.0).astype(bf16)
        return total + dot(probs, vb, 1, 0)

    attended = lax.fori_loop(first_block, last_block + 1, weighted, jnp.zeros((T, HD), f32))
    att_low = attended.astype(bf16)

    both_low = jnp.concatenate([ssm_low, att_low], axis=1)
    collect = Collect.scratch(own, width) + [pltpu.VMEM((own, width), bf16)] + Spread.sems
    hidden, second = call(
        hidden_body, 4, (shape((own, width), f32), shape((T, width), bf16)), (VMEM, HBM),
        (dot(both_low, wb, 1, 1).astype(bf16), x_own, mixer_row(ffn_gain)), [VMEM] * 3, collect, us=50,
    )
    pc = dot(second, wc, 1, 0)
    ff = pc.shape[1] // 2
    gate_pre, up_pre = pc[:, :ff], pc[:, ff:]
    s_gate = jax.nn.silu(gate_pre)
    act_low = (s_gate * up_pre).astype(bf16)
    layer_own = hidden + lax.psum_scatter(
        dot(act_low, wd, 1, 1).astype(bf16), ("p", "head"), scatter_dimension=0, tiled=True
    ).astype(f32)

    grad_d = dot(out_low, act_low, 0, 0)
    d_act = dot(out_low, wd, 1, 0)
    gu_low = jnp.concatenate([d_act * up_pre * d_silu(gate_pre), d_act * s_gate], axis=1).astype(bf16)
    grad_c = dot(second, gu_low, 0, 0)
    part_c = dot(gu_low, wc, 1, 1).astype(bf16)
    grad_c, grad_d, part_c = lax.optimization_barrier((grad_c.astype(bf16), grad_d.astype(bf16), part_c))
    sum_d = line_sum(grad_d)
    sum_c = line_sum(grad_c)
    d_hidden, grad_ffn, branch = call(
        branch_body, 5, (shape((own, width), f32), shape((8, width), f32), shape((T, width), bf16)), (VMEM, VMEM, HBM),
        (part_c, hidden, cot_own, mixer_row(ffn_gain)), [VMEM] * 4, collect, us=50,
    )
    grad_b = dot(branch, both_low, 0, 0)
    d_both = dot(branch, wb, 1, 0)
    d_norm_s, d_att = d_both[:, :chan], d_both[:, chan:].astype(bf16)

    back, _, back_stack = specs(True)
    dz_low, dy, leave, tail, g_state, grad_gain_s = chunked(
        functools.partial(gate_back_body, heads, nc), nc,
        (shape((T, chan), bf16), shape((T, chan), f32), shape((nc, chan, N), f32), shape((nc, 8, 128), f32),
         shape((chan, N), bf16), shape((8, chan), f32)),
        (back(chan), back(chan), back_stack(chan, N), back_stack(8, 128), fixed(chan, N), fixed(8, chan)),
        (base, pa, bc_all, starts_col, bias_row, rates_row, d_norm_s, y_scan, cv_x, reach, z_part, skip_row, gain_row),
        [smem, pa_spec, back(2 * N), back(1), fixed(1, 128), fixed(1, 128), back(chan), back(chan), back(chan),
         back_stack(16, 128), back(chan), fixed(1, chan), fixed(1, chan)],
        [pltpu.VMEM((chan, N), f32), pltpu.VMEM((8, 128), f32)],
    )
    grad_zb = jnp.concatenate([dot(first, dz_low, 0, 0).astype(bf16), grad_b.astype(bf16)], axis=1)
    g_state, sum_d, grad_zb = lax.optimization_barrier((g_state, sum_d, grad_zb))
    sum_zb = line_sum(grad_zb)
    balance = jnp.sum(d_att.astype(f32) * attended, axis=-1, keepdims=True)

    def grads(index, carry):
        d_query, d_keys, d_values = carry
        kb, vb, seen, scores = key_block(index)
        probs = jnp.where(seen, jnp.exp(scores - log_mass[:, None]), 0.0)
        d_scores = (probs * (dot(d_att, vb, 1, 1) - balance)).astype(bf16)
        d_query = d_query + dot(d_scores, kb, 1, 0)
        d_keys = lax.dynamic_update_slice_in_dim(d_keys, dot(d_scores, query, 0, 0), index * key_len, 0)
        d_values = lax.dynamic_update_slice_in_dim(d_values, dot(probs.astype(bf16), d_att, 0, 0), index * key_len, 0)
        return d_query, d_keys, d_values

    zero_keys = jnp.zeros((total_tokens, HD), f32)
    d_query, d_keys, d_values = lax.fori_loop(
        first_block, last_block + 1, grads, (jnp.zeros((T, HD), f32), zero_keys, zero_keys)
    )
    dk_cut = d_keys.astype(bf16).reshape(planes, T, 2, G, quarter_half).transpose(3, 0, 2, 4, 1)
    dv_cut = d_values.astype(bf16).reshape(planes, T, G, 2, quarter_half).transpose(2, 0, 3, 4, 1)
    dkv = jnp.concatenate([dk_cut, dv_cut], axis=2).reshape(G, planes, 4 * quarter_half, T)
    states, factors, dkv = call(
        functools.partial(down_body, planes), 6, state_shapes + (shape((G, planes, kvr, T), bf16),), (HBM,) * 3,
        (g_state, through, dkv), [HBM] * 3, line_sems * 2 + [DMA((3,)), DMA((3,)), DMA(())], us=35,
    )
    after = entering(False, states, factors)
    gx, d_bc_all, d_raw, grad_rows, grad_skip = chunked(
        functools.partial(scan_back_body, heads), nc,
        (shape((T, chan), f32), shape((T, 2 * N), bf16), shape((T, 128), bf16), shape((8, 128), f32), shape((8, chan), f32)),
        (tile(chan), tile(2 * N), tile(128), fixed(8, 128), fixed(8, chan)),
        (base, pa, bc_all, starts_col, bias_row, rates_row, dy, cv_x, enter, reach, before, leave, tail, after, skip_row),
        [smem, pa_spec, tile(2 * N), tile(1), fixed(1, 128), fixed(1, 128), tile(chan), tile(chan),
         stack(chan, N), stack(16, 128), fixed(chan, N), stack(chan, N), stack(8, 128), fixed(chan, N), fixed(1, chan)],
    )
    grad_gain_s = grad_gain_s[0]
    grad_bias, grad_rates = grad_rows[0, :heads], grad_rows[1, :heads]
    grad_skip = jnp.sum(grad_skip[0].reshape(heads, P_SIZE), axis=1)

    gx_first = gx[:RIM]
    d_bc_t, sum_c = lax.optimization_barrier((d_bc_all.T, sum_c))
    g_bc, rim_bc, rim_x, dkv = call(
        functools.partial(back_body, planes), 7,
        (shape((bcs, T), f32), shape((bcs, 128), f32), shape((RIM, chan), f32), shape((kvr, T), f32)), (VMEM,) * 4,
        (d_bc_t, dkv, d_silu(cv_bc).T, gx_first), [VMEM] * 4,
        [pltpu.VMEM((G * bcs, T), bf16), pltpu.VMEM((3, bcs, T), bf16), pltpu.VMEM((3, bcs, T), bf16),
         pltpu.VMEM((planes, kvr, T), bf16), pltpu.VMEM((planes - 1, kvr, T), bf16),
         pltpu.VMEM((bcs, T), f32), DMA(()), DMA(()), DMA((3,)), DMA((3,)),
         DMA((planes - 1,)), DMA((planes - 1,)), DMA((2,)), DMA((2,))],
    )
    dkv = dkv.T
    later = zi < planes - 1
    gx_next = jnp.where(later, rim_x[:edge], 0.0)
    gb_next = jnp.where(later, rim_bc[:, :edge].T, 0.0)
    ends = jnp.minimum(offset + T + jnp.arange(edge), total_tokens - 1)
    starts_next = jnp.where(later, all_starts[ends], total_tokens)
    d_inner_pre, grad_conv_inner = conv_back(gx, gx_next, pa[:, :chan], taps_inner, starts, places, starts_next)
    d_bc_pre, grad_conv_state = conv_back(g_bc.T, gb_next, bc_ext, taps_state, starts, places, starts_next)
    d_q = turn(d_query, cos_q, -sin_q) * scale
    d_k = turn(dkv[:, : 2 * quarter_half], cos_k, -sin_k)
    d_v = dkv[:, 2 * quarter_half :]

    da_low = jnp.concatenate(
        [v.astype(bf16) for v in (d_inner_pre, d_q, d_bc_pre, d_k, d_v)] + [d_raw], axis=1
    )
    grad_a = dot(first, da_low, 0, 0).astype(bf16)
    small = [grad_conv_inner, grad_conv_state, grad_rates, grad_bias, grad_skip, grad_gain_s]
    at = [0]
    for s in small:
        at.append(at[-1] + s.size)
    flat = jnp.concatenate([s.reshape(-1) for s in small] + [jnp.zeros((2 * width - at[-1],), f32)]).reshape(2, width)
    flat = jnp.concatenate([flat, grad_ffn[:1], jnp.zeros((RIM - 3, width), f32)], axis=0)
    gc, gd = scatter(sum_c), scatter(sum_d)
    part_a = (dot(da_low, wa, 1, 1) + dot(dz_low, wz, 1, 1)).astype(bf16)
    part_a, gc, gd = lax.optimization_barrier((part_a, gc, gd))
    sum_a = line_sum(grad_a)
    grad_input, layer_out, sums = call(
        functools.partial(final_body, planes), 8,
        (shape((tokens, width), f32), shape((tokens, width), f32), shape((2 * G * RIM, width), f32)), (HBM, HBM, HBM),
        (part_a, x_own, d_hidden, layer_own, mixer_row(mixer_gain), flat), [VMEM] * 6,
        Collect.scratch(own, width)
        + [pltpu.VMEM((own, width), f32), pltpu.VMEM((RIM, width), f32), pltpu.VMEM((planes - 1, RIM, width), f32),
           DMA((planes - 1,)), DMA((planes - 1,)), DMA((2,)), DMA((2,)), DMA((2,))]
        + Spread.sems, us=45,
    )

    ga, gb = scatter(sum_a), scatter(sum_zb)
    g_z, gb = gb[:, :, :chan], gb[:, :, chan:]
    g_x, g_q, g_bc, g_k, g_v, g_dt = (ga[:, :, a : a + s] for a, s in zip(a_at, a_sizes))
    g_k = jnp.moveaxis(g_k.reshape(rows, G, 2, quarter_half), 1, 2)
    g_bc = lax.all_gather(g_bc.reshape(rows, -1).astype(bf16), "head", axis=1, tiled=True).astype(f32)

    sums = sums.reshape(G, cores, RIM, width)
    every = sums[:, :, :2].reshape(G, cores, 2 * width)
    mine = lax.dynamic_index_in_dim(every, hi, 1, False)
    pieces = [mine[:, a:b] for a, b in zip(at, at[1:])]
    o_conv_inner = jnp.moveaxis(pieces[0].reshape(G, K, chan), 0, 1).reshape(K, G * chan)
    o_conv_state = every[:, :, at[1] : at[2]].reshape(G, cores, K, bcs).transpose(2, 1, 0, 3).reshape(K, 2 * N)
    per = width // (planes * G)
    gains = lax.dynamic_slice_in_dim(jnp.sum(sums[:, :, 2:4], axis=(0, 1)), (zi * G + pi) * per, per, 1)
    gains = (gains[1], gains[0])

    def whole(g):
        return g.reshape(rows, -1)

    return (
        layer_out, grad_input, gains[0], gains[1],
        whole(g_z), whole(g_x), g_bc, whole(g_dt), whole(g_q), whole(g_k), whole(g_v),
        whole(gb[:, :, chan:]), whole(gb[:, :, :chan]),
        whole(gc[:, :, :ff]), whole(gc[:, :, ff:]), whole(gd),
        o_conv_inner, o_conv_state,
        pieces[2].reshape(-1), pieces[3].reshape(-1), pieces[4].reshape(-1), pieces[5].reshape(-1),
    )


def solution(mesh):
    seq, cores = mesh.shape["seq"], mesh.shape["head"]
    planes = Mesh(mesh.devices.reshape(seq // G, G, cores), ("z", "p", "head"))
    s = ("z", "p")
    both, row, head, whole = P(s, "head"), P(s, None), P("head"), P()
    placed = (
        row, P(s), whole, whole, both, both, row, both, both, both, both, both, both, both, both, both,
        P(None, "head"), whole, head, head, head, head, row,
    )
    return jax.shard_map(
        on_device,
        mesh=planes,
        in_specs=placed,
        out_specs=(
            row, row, P(s), P(s), both, both, row, both, both, both, both, both, both, both, both, both,
            P(None, "head"), whole, head, head, head, head,
        ),
        check_vma=False,
    )
```

time: 953 us -> 791 us (0.83)
  other arithmetic: 95.2 us -> 49.1 us
  local copies, waits for them, and re-layouts: 159 us -> 118 us
  blocking collectives: 41.1 us -> 1.89 us
  matrix products: 152 us -> 119 us
  Pallas kernels: 404 us -> 429 us
  waiting for transfers between devices: 46.6 us -> 25.5 us
    pallas_call x0 -> x4, Pallas kernels: none -> 51.5 us  [chunked(): pl.pallas_call(body, grid=(chunks,), out_shape=outs, in_specs=in_specs, o...]
    dot_general x14 -> x0, matrix products: 41.8 us -> none  [exact(): jnp.einsum(text, *operands, precision=highest, preferred_element_type=f32)]
    all_gather x1 -> x0, blocking collectives: 39.2 us -> none  [on_device(): all_starts = lax.all_gather(doc_start, ('z', 'p'), axis=0, tiled=True)]
    pallas_call x9 -> x10, Pallas kernels: 404 us -> 378 us  [call(): pl.pallas_call(body, out_shape=outs, in_specs=in_specs, out_specs=out_spe...]
    mul x7 -> x0, other arithmetic: 22.1 us -> none  [the longest x1 6.87 us: on_device(): conv_x = jax.nn.silu(cv_x)]
    reshape x11 -> x0, local copies, waits for them, and re-layouts: 20.2 us -> none  [the longest x2 6.17 us: by_token(): return v.transpose(0, 2, 1, 3).reshape(T, chan)]
    mul x25 -> x1, local copies, waits for them, and re-layouts: 14.3 us -> 0.01 us  [conv_rows(): padded[RIM - back:RIM - back + length] * taps[lag][None, :]]
    all_to_all x4, waiting for transfers between devices: 30.5 us -> 18.7 us  [scatter(): g = lax.all_to_all(g.reshape(G, rows, -1), 'p', 0, 0, tiled=True)]
  transfers between devices with their start and end apart: 14 -> 13, of which waited for: 5 -> 5; matrix products, arithmetic and copies ran while one was open for 36% -> 28% of each run, Pallas kernels for 35% -> 53%
where the time goes in v3:
time: 791 us; the launch traced here: 777 us
  Pallas kernels  429 us (54%)
  matrix products  119 us (15%)
  local copies, waits for them, and re-layouts  118 us (15%)
  other arithmetic  49.1 us (6%)
  waiting for transfers between devices  25.5 us (3%)
  between operations  18.6 us (2%)
  starting transfers between devices  15.9 us (2%)
    pallas_call x10, Pallas kernels, call(): pl.pallas_call(body, out_shape=outs, in_specs=in_specs, out_specs=out_spe...  378 us
    dot_general x29, matrix products, dot(): lax.dot_general(a, b, (((ca,), (cb,)), ((), ())), preferred_element_type=...  119 us
    unnamed x237, local copies, waits for them, and re-layouts  55.8 us
    pallas_call x4, Pallas kernels, chunked(): pl.pallas_call(body, grid=(chunks,), out_shape=outs, in_specs=in_specs, o...  51.5 us
    all_to_all x4, waiting for transfers between devices, scatter(): g = lax.all_to_all(g.reshape(G, rows, -1), 'p', 0, 0, tiled=True)  18.7 us
  transfers between devices with their start and end apart: 13, of which 5 were waited for; matrix products, arithmetic and copies ran while one was open for 28% of the time, Pallas kernels for 53%

profile of v3, /device:TPU:0, one launch (start us, length us, event | category | flops | bytes accessed | tf_op | source)
XLA Modules:
  0.0 777.3 jit_solution(2548175586361656588)
XLA Ops:
  11.7 13.6 %shard_map.391 = bf16[512,768]{1,0:T(8,128)(2,1)} custom-call(bf16[128,1536]{1,0:T(8,128)(2,1)S(1)} %copy-done.30, bf16[128,512]{1,0:T(8,128)(2,1)S(1)} %copy-done.34, bf16[4,128,256]{2,1,0:T(8,128)(2,1)S(1)} %bitcast.234), custom_call_target="tpu_custom_call" | custom-call | bytes 70000000 | tf_op jit(solution)/shard_map/pallas_call | solution.py:223
  25.5 13.7 %shard_map.395 = bf16[512,896]{1,0:T(8,128)(2,1)} custom-call(bf16[128,1536]{1,0:T(8,128)(2,1)S(1)} %copy-done.28, bf16[128,1536]{1,0:T(8,128)(2,1)S(1)} %copy-done.29, bf16[128,512]{1,0:T(8,128)(2,1)S(1)} %copy-done.33), custom_call_target="tpu_custom_call" | custom-call | bytes 70000000 | tf_op jit(solution)/shard_map/pallas_call | solution.py:223
  43.4 60.8 %shard_map.390 = (bf16[512,1024]{1,0:T(8,128)(2,1)}, bf16[512,512]{1,0:T(8,128)(2,1)}, bf16[1040,2048]{1,0:T(8,128)(2,1)}, bf16[1024,2048]{1,0:T(8,128)(2,1)}, s32[4,4,8,256]{3,2,1,0:T(8,128)S(1)}) custom-call(bf16[128,2048]{1,0:T(8,128)(2,1)S(1)} %copy-done.25, bf16[128,2048]{1,0:T(8,128)(2,1)S(1)} %copy-done.26, bf16[128,2048]{1,0:T(8,128)(2,1)S(1)} %copy-done.27, ...), custom_call_target="tpu_custom_call" | custom-call | bytes 192500000 | tf_op jit(solution)/shard_map/pallas_call | solution.py:223
  112.3 6.3 fusion.141.pa_ref
  122.1 5.6 fusion.80
  133.2 20.2 %shard_map.392 = (bf16[512,1024]{1,0:T(8,128)(2,1)S(1)}, bf16[4,64,1024]{2,1,0:T(8,128)(2,1)S(1)}) custom-call(bf16[64,1024]{1,0:T(8,128)(2,1)S(1)} %fusion.104.block, bf16[64,1024]{1,0:T(8,128)(2,1)S(1)} %maximum_bitcast_fusion.kv), custom_call_target="tpu_custom_call" | custom-call | bytes 70000000 | tf_op jit(solution)/shard_map/pallas_call | solution.py:223
  155.9 11.1 %shard_map.393 = (f32[1024,384]{1,0:T(8,128)S(1)}, f32[1024,384]{1,0:T(8,128)S(1)}, f32[8,384,256]{2,1,0:T(8,128)}, f32[8,16,128]{2,1,0:T(8,128)S(1)}, bf16[384,...) custom-call(s32[1]{0:T(128)} %bitcast.2.base_ref, f32[1040,768]{1,0:T(8,128)} %copy-done.47, bf16[1024,512]{1,0:T(8,128)(2,1)S(1)} %bitcast.226, ...), custom_call_target="tpu_custom_call" | custom-call | flops 2000000000 | bytes 40000000 | tf_op jit(solution)/shard_map/pallas_call | solution.py:862
  169.2 32.0 %shard_map.394 = (bf16[3,384,256]{2,1,0:T(8,128)(2,1)S(1)}, f32[3,8,128]{2,1,0:T(8,128)S(1)}, bf16[16,64,1024]{2,1,0:T(8,128)(2,1)S(1)}) custom-call(bf16[384,256]{1,0:T(8,128)(2,1)S(1)} %get-tuple-element.246.state, f32[8,128]{1,0:T(8,128)S(1)} %get-tuple-element.247.factor, bf16[4,64,1024]{2,1,0:T(8,128)(2,1)S(1)} %get-tuple-element.248.lines), custom_call_target="tpu_custom_call" | custom-call | bytes 98000000 | tf_op jit(solution)/shard_map/pallas_call | solution.py:223
  208.4 4.4 while.39
  219.3 5.8 while.40
  219.3 2.9 fusion.196
  222.2 2.9 fusion.196
  228.8 6.3 fusion.38.z_ref
  235.2 9.5 %shard_map.396 = (bf16[1024,384]{1,0:T(8,128)(2,1)S(1)}, f32[1024,384]{1,0:T(8,128)S(1)}) custom-call(s32[1]{0:T(128)} %bitcast.2.base_ref, f32[1040,768]{1,0:T(8,128)} %copy-done.47, bf16[1024,512]{1,0:T(8,128)(2,1)S(1)} %bitcast.227, s32[1024,1]{1,0:T(8,128)S(1)} %copy.275.starts_ref, f32[1,128]{1,0:T(1,128)S(1)} %get-tuple-element.729.bias_ref, ...), custom_call_target="tpu_custom_call" | custom-call | flops 2000000000 | bytes 40000000 | tf_op jit(solution)/shard_map/pallas_call | solution.py:862
  244.7 4.5 convolution_convert_fusion.1.part
  249.2 48.4 %shard_map.397 = (f32[128,2048]{1,0:T(8,128)S(1)}, bf16[1024,2048]{1,0:T(8,128)(2,1)}) custom-call(bf16[1024,2048]{1,0:T(8,128)(2,1)} %convolution_convert_fusion.1.part, f32[128,2048]{1,0:T(8,128)S(1)} %get-tuple-element.680.x_ref, f32[1,2048]{1,0:T(1,128)S(1)} %bitcast.238), custom_call_target="tpu_custom_call" | custom-call | bytes 175000000 | tf_op jit(solution)/shard_map/pallas_call | solution.py:223
  298.5 10.1 %fusion.142 = f32[1024,1024]{0,1:T(8,128)} fusion(bf16[1024,2048]{1,0:T(8,128)(2,1)} %get-tuple-element.256, bf16[2048,1024]{1,0:T(8,128)(2,1)} %all-gather.11.cloned.1.call-done), kind=kOutput, calls=%fused_computation.269 | convolution fusion | flops 4294967296 | bytes 12582912 | tf_op jit(solution)/shard_map/dot_general | solution.py:875
  308.7 5.6 all-gather.9.cloned.1.call-done
  314.3 8.6 %multiply_convert_fusion.2 = (bf16[1024,512]{0,1:T(8,128)(2,1)}, bf16[1024,512]{0,1:T(8,128)(2,1)}, bf16[1024,512]{0,1:T(8,128)(2,1)S(1)}) fusion(f32[1024,1024]{0,1:T(8,128)} %fusion.142, bf16[1024,2048]{1,0:T(8,128)(2,1)} %get-tuple-element.257, bf16[2048,512]{1,0:T(8,128)(2,1)} %all-gather.9.cloned.1.call-done), kind=kOutput, calls=%fused_computation.69 | convolution fusion | flops 2155347968 | bytes 13631488 | tf_op jit(solution)/shard_map/dot_general | solution.py:875
  323.8 3.8 convolution_convert_fusion.6
  327.6 9.9 %convolution_convert_fusion.3 = bf16[2048,1024]{1,0:T(8,128)(2,1)} fusion(bf16[1024,2048]{1,0:T(8,128)(2,1)} %get-tuple-element.256, bf16[1024,512]{0,1:T(8,128)(2,1)} %get-tuple-element.684, bf16[1024,512]{0,1:T(8,128)(2,1)} %get-tuple-element.683), kind=kOutput, calls=%fused_computation.51 | convolution fusion | flops 4301258752 | bytes 10485760 | tf_op jit(solution)/shard_map/dot_general | solution.py:875
  337.5 9.4 %convolution_convert_fusion.2.part = bf16[1024,2048]{1,0:T(8,128)(2,1)} fusion(bf16[2048,1024]{1,0:T(8,128)(2,1)} %all-gather.11.cloned.1.call-done, bf16[1024,512]{0,1:T(8,128)(2,1)} %get-tuple-element.684, bf16[1024,512]{0,1:T(8,128)(2,1)} %get-tuple-element.683), kind=kOutput, calls=%fused_computation.50 | convolution fusion | flops 4301258752 | bytes 10485760 | tf_op jit(solution)/shard_map/dot_general | solution.py:875
  347.6 6.3 convolution_convert_fusion
  359.9 49.5 %shard_map.398 = (f32[128,2048]{1,0:T(8,128)S(1)}, f32[8,2048]{1,0:T(8,128)S(1)}, bf16[1024,2048]{1,0:T(8,128)(2,1)}) custom-call(bf16[1024,2048]{1,0:T(8,128)(2,1)} %convolution_convert_fusion.2.part, f32[128,2048]{1,0:T(8,128)S(1)} %copy-done.9, f32[128,2048]{1,0:T(8,128)S(1)} %copy-done.7, f32[1,2048]{1,0:T(1,128)S(1)} %bitcast.239), custom_call_target="tpu_custom_call" | custom-call | bytes 175000000 | tf_op jit(solution)/shard_map/pallas_call | solution.py:223
  409.5 5.0 fusion.44
  419.0 3.0 copy.308.d_ref
  424.1 11.3 %shard_map.399 = (bf16[1024,384]{1,0:T(8,128)(2,1)S(1)}, f32[1024,384]{1,0:T(8,128)S(1)}, f32[8,384,256]{2,1,0:T(8,128)}, f32[8,8,128]{2,1,0:T(8,128)S(1)}, bf16...) custom-call(s32[1]{0:T(128)} %bitcast.2.base_ref, f32[1040,768]{1,0:T(8,128)} %copy-done.47, ...), custom_call_target="tpu_custom_call" | custom-call | flops 2000000000 | bytes 40000000 | tf_op jit(solution)/shard_map/pallas_call | solution.py:862
  435.5 4.9 fusion.40
  448.0 15.2 %while.41 = (s32[]{:T(128)}, f32[1024,128]{1,0:T(8,128)}, bf16[4096,128]{1,0:T(8,128)(2,1)}, bf16[4096,128]{1,0:T(8,128)(2,1)}, s32[]{:T(128)}, /*index=5*/s32[1...) while((s32[]{:T(128)}, f32[1024,128]{1,0:T(8,128)}, ...), condition=%wide.region_10.11_spmd.clone, body=%wide.region_9.10_spmd.clone.sunk | while | flops 675939840 | bytes 18784628 | solution.py:1193
  465.7 2.6 reshape.308
  475.8 2.9 pad_maximum_fusion.2
  482.9 62.1 %shard_map.400 = (bf16[3,384,256]{2,1,0:T(8,128)(2,1)S(1)}, f32[3,8,128]{2,1,0:T(8,128)S(1)}, bf16[4,4,64,1024]{3,2,1,0:T(8,128)(2,1)S(1)}) custom-call(bf16[384,256]{1,0:T(8,128)(2,1)S(1)} %get-tuple-element.270.state, f32[8,128]{1,0:T(8,128)S(1)} %get-tuple-element.247.factor, bf16[4,4,64,1024]{3,2,1,0:T(8,128)(2,1)S(1)} %bitcast.230), custom_call_target="tpu_custom_call" | custom-call | bytes 122500000 | tf_op jit(solution)/shard_map/pallas_call | solution.py:223
  549.9 19.6 %shard_map.401 = (f32[1024,384]{1,0:T(8,128)S(1)}, bf16[1024,512]{1,0:T(8,128)(2,1)S(1)}, bf16[1024,128]{1,0:T(8,128)(2,1)S(1)}, f32[8,128]{1,0:T(8,128)S(1)}, f32[8,384]{1,0:T(8,128)S(1)}) custom-call(s32[1]{0:T(128)} %bitcast.2.base_ref, f32[1040,768]{1,0:T(8,128)} %copy-done.47, bf16[1024,512]{1,0:T(8,128)(2,1)S(1)} %bitcast.229, ...), custom_call_target="tpu_custom_call" | custom-call | flops 2000000000 | bytes 40000000 | tf_op jit(solution)/shard_map/pallas_call | solution.py:862
  577.6 29.3 %shard_map.402 = (f32[64,1024]{1,0:T(8,128)S(1)}, f32[64,128]{1,0:T(8,128)S(1)}, f32[16,384]{1,0:T(8,128)S(1)}, f32[64,1024]{1,0:T(8,128)S(1)}) custom-call(bf16[512,1024]{1,0:T(8,128)(2,1)S(1)} %bitcast.231, bf16[4,4,64,1024]{3,2,1,0:T(8,128)(2,1)S(1)} %copy-done.12, f32[64,1024]{1,0:T(8,128)S(1)} %get-tuple-element.671.d_silu_bc, f32[16,384]{1,0:T(8,128)S(1)} %slice.335.gx), custom_call_target="tpu_custom_call" | custom-call | bytes 70000000 | tf_op jit(solution)/shard_map/pallas_call | solution.py:223
  616.9 3.3 fusion.53
  620.2 3.9 concatenate.61
  624.1 8.0 %convolution_convert_fusion.4 = bf16[2048,768]{1,0:T(8,128)(2,1)} fusion(bf16[1024,768]{1,0:T(8,128)(2,1)} %concatenate.61, bf16[1040,2048]{1,0:T(8,128)(2,1)} %get-tuple-element.240), kind=kOutput, calls=%fused_computation.53 | convolution fusion | flops 3222798336 | bytes 8912896 | tf_op jit(solution)/shard_map/dot_general | solution.py:875
  633.7 4.8 fusion.64
  638.6 3.6 all-to-all-start.1
  642.4 8.0 %all-to-all-done.1 = bf16[4,128,512]{2,1,0:T(8,128)(2,1)S(1)} async-done(((bf16[4,128,512]{2,1,0:T(8,128)(2,1)}), bf16[4,128,512]{2,1,0:T(8,128)(2,1)S(1)}, u32[]{:S(2)}, u32[]{:S(2)}) %all-to-all-start.1) | async-done | bytes 524320 | tf_op jit(solution)/shard_map/all_to_all | solution.py:1022
  654.4 4.2 all-to-all-start
  658.6 5.9 fusion.143
  664.6 5.8 add_convert_fusion.part
  671.8 2.8 convert_bitcast_fusion
  674.6 48.2 %shard_map.403 = (f32[256,2048]{1,0:T(8,128)}, f32[256,2048]{1,0:T(8,128)}, f32[128,2048]{1,0:T(8,128)S(1)}) custom-call(bf16[1024,2048]{1,0:T(8,128)(2,1)} %add_convert_fusion.part, f32[128,2048]{1,0:T(8,128)S(1)} %get-tuple-element.680.x_ref, f32[128,2048]{1,0:T(8,128)S(1)} %copy-done.20, f32[128,2048]{1,0:T(8,128)S(1)} %convert_add_fusion.layer, ...), custom_call_target="tpu_custom_call" | custom-call | bytes 157500000 | tf_op jit(solution)/shard_map/pallas_call | solution.py:223
  725.5 3.5 all-to-all-start.2
  733.2 9.2 %all-to-all-done.2 = bf16[4,128,896]{1,2,0:T(8,128)(2,1)S(1)} async-done(((bf16[4,128,896]{1,2,0:T(8,128)(2,1)}), bf16[4,128,896]{1,2,0:T(8,128)(2,1)S(1)}, u32[]{:S(2)}, u32[]{:S(2)}) %all-to-all-start.2) | async-done | bytes 917536 | tf_op jit(solution)/shard_map/all_to_all | solution.py:1022
  742.4 4.2 all-to-all-start.3
  (465 shorter events, 161.5 us)
Async XLA Ops:
  7.2 105.1 %all-gather.5.cloned.1.call-start = ((), (), s32[]{:S(2)}) async-start(), calls=%async_computation.9 | async-start | bytes 3932160 | tf_op jit(solution)/shard_map/all_gather | solution.py:983
  8.4 17.1 %copy-start.28 = (bf16[128,1536]{1,0:T(8,128)(2,1)S(1)}, bf16[128,1536]{1,0:T(8,128)(2,1)}, u32[]{:S(2)}) copy-start(bf16[128,1536]{1,0:T(8,128)(2,1)} %z_ref.1) | copy-start | bytes 1179652
  8.4 17.1 %copy-start.29 = (bf16[128,1536]{1,0:T(8,128)(2,1)S(1)}, bf16[128,1536]{1,0:T(8,128)(2,1)}, u32[]{:S(2)}) copy-start(bf16[128,1536]{1,0:T(8,128)(2,1)} %out_ref.1) | copy-start | bytes 1179652
  8.4 17.1 %copy-start.33 = (bf16[128,512]{1,0:T(8,128)(2,1)S(1)}, bf16[128,512]{1,0:T(8,128)(2,1)}, u32[]{:S(2)}) copy-start(bf16[128,512]{1,0:T(8,128)(2,1)} %o_ref.1) | copy-start | bytes 393220
  25.4 203.5 %all-gather.7.cloned.1.call-start = ((), (), s32[]{:S(2)}) async-start(), calls=%async_computation.10 | async-start | bytes 4587520 | tf_op jit(solution)/shard_map/all_gather | solution.py:983
  39.1 259.4 %all-gather.11.cloned.1.call-start = ((), (), s32[]{:S(2)}) async-start(), calls=%async_computation.12 | async-start | bytes 5242880 | tf_op jit(solution)/shard_map/all_gather | solution.py:983
  43.4 67.1 %copy-start.104 = (f32[24]{0:T(128)S(1)}, f32[24]{0:T(128)}, u32[]{:S(2)}) copy-start(f32[24]{0:T(128)} %param.48) | copy-start | bytes 292
  43.4 67.2 %copy-start.105 = (f32[24]{0:T(128)S(1)}, f32[24]{0:T(128)}, u32[]{:S(2)}) copy-start(f32[24]{0:T(128)} %param.47) | copy-start | bytes 292
  43.4 67.2 %copy-start.106 = (f32[24]{0:T(128)S(1)}, f32[24]{0:T(128)}, u32[]{:S(2)}) copy-start(f32[24]{0:T(128)} %param.49) | copy-start | bytes 292
  104.2 210.1 %all-gather.9.cloned.1.call-start = ((), (), s32[]{:S(2)}) async-start(), calls=%async_computation.11 | async-start | bytes 2621440 | tf_op jit(solution)/shard_map/all_gather | solution.py:983
  104.8 340.2 %reduce-scatter.6.cloned.1.call-start = ((), (), s32[]{:S(2)}) async-start(), calls=%async_computation.13 | async-start | bytes 2621440 | tf_op jit(solution)/shard_map/reduce_scatter | solution.py:1019
  104.8 17.3 %copy-start.99 = (f32[64]{0:T(128)}, f32[64]{0:T(128)S(1)}, u32[]{:S(2)}) copy-start(f32[64]{0:T(128)S(1)} %multiply_power_fusion) | copy-start | bytes 772
  104.9 26.2 %copy-start.75 = (f32[1024]{0:T(1024)}, f32[1024]{0:T(1024)S(1)}, u32[]{:S(2)}) copy-start(f32[1024]{0:T(1024)S(1)} %get-tuple-element.675) | copy-start | bytes 12292
  108.1 23.1 %copy-start.98 = (f32[16]{0:T(128)}, f32[16]{0:T(128)S(1)}, u32[]{:S(2)}) copy-start(f32[16]{0:T(128)S(1)} %multiply_power_fusion.1) | copy-start | bytes 196
  109.4 21.3 %copy-start.78 = (pred[1024]{0:T(1024)(128)(4,1)}, pred[1024]{0:T(1024)(128)(4,1)S(1)}, u32[]{:S(2)}) copy-start(pred[1024]{0:T(1024)(128)(4,1)S(1)} %get-tuple-element.718) | copy-start | bytes 3076
  109.4 21.3 %copy-start.80 = (pred[1024]{0:T(1024)(128)(4,1)}, pred[1024]{0:T(1024)(128)(4,1)S(1)}, u32[]{:S(2)}) copy-start(pred[1024]{0:T(1024)(128)(4,1)S(1)} %get-tuple-element.719) | copy-start | bytes 3076
  109.4 21.3 %copy-start.82 = (pred[1024]{0:T(1024)(128)(4,1)}, pred[1024]{0:T(1024)(128)(4,1)S(1)}, u32[]{:S(2)}) copy-start(pred[1024]{0:T(1024)(128)(4,1)S(1)} %get-tuple-element.720) | copy-start | bytes 3076
  109.4 21.3 %copy-start.84 = (pred[1024]{0:T(1024)(128)(4,1)}, pred[1024]{0:T(1024)(128)(4,1)S(1)}, u32[]{:S(2)}) copy-start(pred[1024]{0:T(1024)(128)(4,1)S(1)} %get-tuple-element.721) | copy-start | bytes 3076
  110.2 20.5 %copy-start.93 = (f32[64]{0:T(128)}, f32[64]{0:T(128)S(1)}, u32[]{:S(2)}) copy-start(f32[64]{0:T(128)S(1)} %get-tuple-element.722) | copy-start | bytes 772
  110.2 20.6 %copy-start.94 = (f32[64]{0:T(128)}, f32[64]{0:T(128)S(1)}, u32[]{:S(2)}) copy-start(f32[64]{0:T(128)S(1)} %get-tuple-element.723) | copy-start | bytes 772
  110.2 20.6 %copy-start.95 = (f32[64]{0:T(128)}, f32[64]{0:T(128)S(1)}, u32[]{:S(2)}) copy-start(f32[64]{0:T(128)S(1)} %get-tuple-element.724) | copy-start | bytes 772
  110.2 20.6 %copy-start.96 = (f32[64]{0:T(128)}, f32[64]{0:T(128)S(1)}, u32[]{:S(2)}) copy-start(f32[64]{0:T(128)S(1)} %get-tuple-element.725) | copy-start | bytes 772
  112.3 122.8 %copy-start.40 = (f32[1,128]{1,0:T(1,128)}, f32[1,128]{1,0:T(1,128)S(1)}, u32[]{:S(2)}) copy-start(f32[1,128]{1,0:T(1,128)S(1)} %get-tuple-element.729.bias_ref) | copy-start | bytes 1540
  129.1 24.2 %copy-start.61 = (f32[1024,64]{0,1:T(8,128)}, f32[1024,64]{0,1:T(8,128)S(1)}, u32[]{:S(2)}) copy-start(f32[1024,64]{0,1:T(8,128)S(1)} %copy.300) | copy-start | bytes 786436
  130.5 22.9 %copy-start.62 = (f32[1024,64]{0,1:T(8,128)}, f32[1024,64]{0,1:T(8,128)S(1)}, u32[]{:S(2)}) copy-start(f32[1024,64]{0,1:T(8,128)S(1)} %copy.301) | copy-start | bytes 786436
  130.7 22.7 %copy-start.63 = (f32[1024,64]{0,1:T(8,128)}, f32[1024,64]{0,1:T(8,128)S(1)}, u32[]{:S(2)}) copy-start(f32[1024,64]{0,1:T(8,128)S(1)} %copy.302) | copy-start | bytes 786436
  225.1 10.0 %copy-start.70 = (s32[1024]{0:T(1024)}, s32[1024]{0:T(1024)S(1)}, u32[]{:S(2)}) copy-start(s32[1024]{0:T(1024)S(1)} %get-tuple-element.1129) | copy-start | bytes 12292
  225.1 10.0 %copy-start.97 = (f32[1024]{0:T(1024)}, f32[1024]{0:T(1024)S(1)}, u32[]{:S(2)}) copy-start(f32[1024]{0:T(1024)S(1)} %get-tuple-element.1130) | copy-start | bytes 12292
  346.9 227.8 %reduce-scatter.8.cloned.1.call-start = ((), (), s32[]{:S(2)}) async-start(), calls=%async_computation.14 | async-start | bytes 5242880 | tf_op jit(solution)/shard_map/reduce_scatter | solution.py:1019
  347.5 304.0 %reduce-scatter.10.cloned.1.call-start = ((), (), s32[]{:S(2)}) async-start(), calls=%async_computation.15 | async-start | bytes 4718592 | tf_op jit(solution)/shard_map/reduce_scatter | solution.py:1146
  353.8 369.3 %reduce-scatter.12.cloned.1.call-start = ((), (), s32[]{:S(2)}) async-start(), calls=%async_computation.16 | async-start | bytes 4587520 | tf_op jit(solution)/shard_map/reduce_scatter | solution.py:1019
  359.9 49.5 %copy-start.69 = (bf16[2048,896]{1,0:T(8,128)(2,1)S(1)}, bf16[2048,896]{1,0:T(8,128)(2,1)}, u32[]{:S(2)}) copy-start(bf16[2048,896]{1,0:T(8,128)(2,1)} %all-gather.7.cloned.1.call-done) | copy-start | bytes 11010052
  445.0 285.8 %reduce-scatter.14.cloned.1.call-start = ((), (), s32[]{:S(2)}) async-start(), calls=%async_computation.17 | async-start | bytes 3932160 | tf_op jit(solution)/shard_map/reduce_scatter | solution.py:1019
  482.0 67.1 %copy-start.42 = (f32[1,128]{1,0:T(1,128)S(1)}, f32[1,128]{1,0:T(1,128)}, u32[]{:S(2)}) copy-start(f32[1,128]{1,0:T(1,128)} %copy-done.40) | copy-start | bytes 1540
  574.7 32.9 %copy-start.77 = (f32[1024]{0:T(1024)S(1)}, f32[1024]{0:T(1024)}, u32[]{:S(2)}) copy-start(f32[1024]{0:T(1024)} %copy-done.75) | copy-start | bytes 12292
  577.6 34.1 %copy-start.79 = (pred[1024]{0:T(1024)(128)(4,1)S(1)}, pred[1024]{0:T(1024)(128)(4,1)}, u32[]{:S(2)}) copy-start(pred[1024]{0:T(1024)(128)(4,1)} %copy-done.78) | copy-start | bytes 3076
  577.6 34.1 %copy-start.86 = (pred[1024]{0:T(1024)(128)(4,1)S(1)}, pred[1024]{0:T(1024)(128)(4,1)}, u32[]{:S(2)}) copy-start(pred[1024]{0:T(1024)(128)(4,1)} %get-tuple-element.713) | copy-start | bytes 3076
  577.6 34.1 %copy-start.87 = (pred[1024]{0:T(1024)(128)(4,1)S(1)}, pred[1024]{0:T(1024)(128)(4,1)}, u32[]{:S(2)}) copy-start(pred[1024]{0:T(1024)(128)(4,1)} %get-tuple-element.714) | copy-start | bytes 3076
  607.0 9.9 %copy-start.88 = (pred[1024]{0:T(1024)(128)(4,1)S(1)}, pred[1024]{0:T(1024)(128)(4,1)}, u32[]{:S(2)}) copy-start(pred[1024]{0:T(1024)(128)(4,1)} %get-tuple-element.715) | copy-start | bytes 3076
  609.2 11.0 %copy-start.32 = (bf16[1024,128]{1,0:T(8,128)(2,1)S(1)}, bf16[1024,128]{1,0:T(8,128)(2,1)}, u32[]{:S(2)}) copy-start(bf16[1024,128]{1,0:T(8,128)(2,1)} %copy-done.31) | copy-start | bytes 786436
  609.2 11.0 %copy-start.67 = (bf16[1024,128]{1,0:T(8,128)(2,1)S(1)}, bf16[1024,128]{1,0:T(8,128)(2,1)}, u32[]{:S(2)}) copy-start(bf16[1024,128]{1,0:T(8,128)(2,1)} %fusion.83) | copy-start | bytes 786436
  638.5 13.0 %copy-start.10 = (f32[128,2048]{1,0:T(8,128)S(1)}, f32[128,2048]{1,0:T(8,128)}, u32[]{:S(2)}) copy-start(f32[128,2048]{1,0:T(8,128)} %copy-done.8) | copy-start | bytes 3145732
  638.6 11.8 %all-to-all-start.1 = ((bf16[4,128,512]{2,1,0:T(8,128)(2,1)}), bf16[4,128,512]{2,1,0:T(8,128)(2,1)S(1)}, u32[]{:S(2)}, u32[]{:S(2)}) async-start(bf16[4,128,512]{2,1,0:T(8,128)(2,1)} %bitcast.260), calls=%async_computation.3 | async-start | bytes 1048576 | tf_op jit(solution)/shard_map/all_to_all | solution.py:1022
  654.4 17.4 %all-to-all-start = ((bf16[4,128,1024]{2,1,0:T(8,128)(2,1)}), bf16[4,128,1024]{2,1,0:T(8,128)(2,1)}, u32[]{:S(2)}, u32[]{:S(2)}) async-start(bf16[4,128,1024]{2,1,0:T(8,128)(2,1)} %bitcast.253), calls=%async_computation.2 | async-start | bytes 2097152 | tf_op jit(solution)/shard_map/all_to_all | solution.py:1022
  725.5 16.9 %all-to-all-start.2 = ((bf16[4,128,896]{1,2,0:T(8,128)(2,1)}), bf16[4,128,896]{1,2,0:T(8,128)(2,1)S(1)}, u32[]{:S(2)}, u32[]{:S(2)}) async-start(bf16[4,128,896]{1,2,0:T(8,128)(2,1)} %copy_bitcast_fusion.1), calls=%async_computation.6 | async-start | bytes 1835008 | tf_op jit(solution)/shard_map/all_to_all | solution.py:1022
  730.8 20.2 %copy-start.57 = (f32[4,16,8,512]{3,2,1,0:T(8,128)S(1)}, f32[4,16,8,512]{3,2,1,0:T(8,128)}, u32[]{:S(2)}) copy-start(f32[4,16,8,512]{3,2,1,0:T(8,128)} %get-tuple-element.695) | copy-start | bytes 3145732
  733.2 18.9 %copy-start.56 = (f32[4,16,8,512]{3,2,1,0:T(8,128)S(1)}, f32[4,16,8,512]{3,2,1,0:T(8,128)}, u32[]{:S(2)}) copy-start(f32[4,16,8,512]{3,2,1,0:T(8,128)} %get-tuple-element.694) | copy-start | bytes 3145732
  742.4 15.3 %all-to-all-start.3 = ((bf16[4,128,768]{1,2,0:T(8,128)(2,1)}), bf16[4,128,768]{1,2,0:T(8,128)(2,1)}, u32[]{:S(2)}, u32[]{:S(2)}) async-start(bf16[4,128,768]{1,2,0:T(8,128)(2,1)} %copy.282), calls=%async_computation.8 | async-start | bytes 1572864 | tf_op jit(solution)/shard_map/all_to_all | solution.py:1022
  (78 other events, 262.0 us)
Sparse Core Ops, SparseCore 0:
  25.5 68.6 all-gather.4
  95.8 81.7 all-gather.6
  179.2 82.0 all-gather.10
  262.7 51.4 all-gather.8
  347.0 57.4 reduce-scatter.5
  406.8 76.0 reduce-scatter.7
  486.2 68.9 reduce-scatter.9
  557.6 78.0 reduce-scatter.11
  638.2 61.9 reduce-scatter.13

commit v4 on v3

--- a/solution.py
+++ b/solution.py
@@ -1,4 +1,5 @@
 import functools
+import math
 
 import jax
 import jax.numpy as jnp
@@ -240,12 +241,13 @@
 def exchange_copies(pieces, sems, keep):
     _, p, _ = here()
     away, own = [], []
-    for i, (source, width, target, first, led) in enumerate(pieces):
+    for i, (source, width, target, first, led, *part) in enumerate(pieces):
+        whole, skip = part or (width, 0)
         rows = source.shape[-2]
         spot = target.at[pl.ds(pl.multiple_of(p * rows, 16), rows), pl.ds(first, width)]
         for d in range(G):
             q = ring(p, d)
-            taken = source.at[q] if led else source.at[:, pl.ds(pl.multiple_of(q * width, 128), width)]
+            taken = source.at[q] if led else source.at[:, pl.ds(pl.multiple_of(q * whole + skip, 128), width)]
             if d:
                 away.append(rcopy(taken, spot, sems[0].at[d - 1, i], sems[1].at[d - 1, i], p=q))
             else:
@@ -253,14 +255,11 @@
     return away, own
 
 
-def exchange_a_body(x_ref, q_ref, small_ref, out_ref, send, recv, keep):
+def exchange_a_body(x_ref, small_ref, out_ref, send, recv, keep):
     _, p, c = here()
     greet(*[{"p": ring(p, d)} for d in range(1, G)])
-    xw, qw = (r.shape[1] // G for r in (x_ref, q_ref))
-    pieces = [
-        (x_ref, xw, out_ref, 0, False), (q_ref, qw, out_ref, xw, False),
-        (small_ref, small_ref.shape[2], out_ref, xw + qw, True),
-    ]
+    xw = x_ref.shape[1] // G
+    pieces = [(x_ref, xw, out_ref, 0, False), (small_ref, small_ref.shape[2], out_ref, xw, True)]
     away, own = exchange_copies(pieces, (send, recv), keep)
     for copy in away + own:
         copy.start()
@@ -268,11 +267,13 @@
         copy.wait()
 
 
-def exchange_b_body(z_ref, out_ref, o_ref, wb, send, recv, keep):
+def exchange_b_body(z_ref, q_ref, out_ref, o_ref, wb, send, recv, keep):
     _, p, c = here()
     greet(*[{"p": ring(p, d)} for d in range(1, G)])
-    zw, ow, aw = (r.shape[1] // G for r in (z_ref, out_ref, o_ref))
-    pieces = [(z_ref, zw, wb, 0, False), (out_ref, ow, wb, zw, False), (o_ref, aw, wb, zw + ow, False)]
+    pieces, at = [], 0
+    for ref in (z_ref, q_ref, out_ref, o_ref):
+        pieces.append((ref, ref.shape[1] // G, wb, at, False))
+        at += ref.shape[1] // G
     away, own = exchange_copies(pieces, (send, recv), keep)
     for copy in away + own:
         copy.start()
@@ -280,15 +281,18 @@
         copy.wait()
 
 
-def start_body(planes, gate_w, up_w, down_w, first, low, docs, wc, wd, n1, ol, all_docs, *sems):
+def start_body(planes, gate_w, up_w, down_w, first, docs, w1, w2, n1, all_docs, *sems):
     z, p, c = here()
     greet(*plane_partners(p, c), *line_partners(z, planes))
     send, recv, keep, rim_s, rim_r, ps, pr, zs, zr, dk = sems[:10]
     rows = first.shape[0]
     a = Spread(first, n1, lambda q, k: pl.multiple_of(RIM + (q * 2 + k) * rows, 16), rows, sems[10:17])
-    b = Spread(low, ol, lambda q, k: pl.multiple_of((q * 2 + k) * rows, 16), rows, sems[17:24])
-    gw, uw, dw = (r.shape[1] // G for r in (gate_w, up_w, down_w))
-    pieces = [(gate_w, gw, wc, 0, False), (up_w, uw, wc, gw, False), (down_w, dw, wd, 0, False)]
+    units = gate_w.shape[1] // G
+    part = units // 2
+    pieces = [
+        (ref, part, to, i * part, False, units, k * part)
+        for k, to in enumerate((w1, w2)) for i, ref in enumerate((gate_w, up_w, down_w))
+    ]
     away, own = exchange_copies(pieces, (send, recv), keep)
     near = [rcopy(docs, all_docs.at[z, p], ps.at[d - 1], pr.at[d - 1], p=ring(p, d)) for d in (1, 2, 3)]
     own_docs = pltpu.make_async_copy(docs, all_docs.at[z, p], dk)
@@ -301,7 +305,6 @@
     a.pass_on()
     for copy in away:
         copy.start()
-    b.start()
     a.finish()
     last = n1.at[pl.ds(n1.shape[0] - RIM, RIM)]
     rim = rcopy(last, n1.at[pl.ds(0, RIM)], rim_s, rim_r, z=lax.rem(z + 1, planes))
@@ -314,10 +317,8 @@
     ]
     for copy in far:
         copy.start()
-    b.pass_on()
     for copy in own + away:
         copy.wait()
-    b.finish()
     rim.wait()
     for copy in far:
         copy.wait()
@@ -375,32 +376,47 @@
     return start, wait
 
 
-def up_body(planes, state, factor, lines, states, factors, kv, *sems):
+def up_body(planes, state, factor, lines, low, states, factors, kv, ol, *sems):
     z, p, c = here()
     greet(*plane_partners(p, c), *line_partners(z, planes))
     start, wait = state_copies(planes, True, state, factor, states, factors, sems[:4])
     start()
-    s = Spread(lines, kv, lambda q, k: q * planes, planes, sems[4:], cores=False)
+    rows = low.shape[0]
+    s = Spread(lines, kv, lambda q, k: q * planes, planes, sems[4:11], cores=False)
+    b = Spread(low, ol, lambda q, k: pl.multiple_of((q * 2 + k) * rows, 16), rows, sems[11:18])
     s.start()
+    b.start()
     s.pass_on()
+    b.pass_on()
     s.finish()
+    b.finish()
     wait()
 
 
-def down_body(planes, state, factor, dkv, states, factors, kv, *sems):
+def down_body(planes, state, factor, dkv, part, hidden, states, factors, kv, layer, *sems):
     z, p, c = here()
     greet(*plane_partners(p, c), *line_partners(z, planes))
     start, wait = state_copies(planes, False, state, factor, states, factors, sems[:4])
     start()
-    ks, kr, kk = sems[4:]
+    ks, kr, kk = sems[4:7]
+    s = Collect(part, hidden.shape[0], sems[7:])
+    s.start()
     over = [rcopy(dkv.at[ring(p, d)], kv.at[d], ks.at[d - 1], kr.at[d - 1], p=ring(p, d)) for d in (1, 2, 3)]
     keep = pltpu.make_async_copy(dkv.at[p], kv.at[0], kk)
     for copy in over:
         copy.start()
     keep.start()
+    s.middle()
+    s.arrive()
+
+    def one(at):
+        layer[s.at(at)] = hidden[s.at(at)] + s.sum_of(at)
+
+    s.strips(one)
     keep.wait()
     for copy in over:
         copy.wait()
+    s.finish()
     wait()
 
 
@@ -459,13 +475,14 @@
     g.finish()
 
 
-def final_body(planes, part, x_ref, d_hidden, layer, gain, small, grad_in, layer_out, sums, *scratch):
+def final_body(part, x_ref, d_hidden, layer, gain, small, sum_zb, grad_in, layer_out, mine, got_zb, *scratch):
     z, p, c = here()
-    greet(*plane_partners(p, c), *line_partners(z, planes))
+    greet(*plane_partners(p, c))
     rows = x_ref.shape[0]
     s = Collect(part, rows, scratch[:9])
-    stage, mine, others, zs, zr, es, er, ek = scratch[9:17]
+    stage, gain_row, es, er, ek, zs, zr, zk = scratch[9:]
     half = pl.ds(pl.multiple_of(c * rows, 16), rows)
+    wide = got_zb.shape[1]
 
     def halves(i, source, target):
         return (
@@ -473,12 +490,20 @@
             pltpu.make_async_copy(source, target.at[half], ek.at[i]),
         )
 
+    def zb_of(q):
+        return sum_zb.at[pl.ds(pl.multiple_of(q * wide, 16), wide)]
+
     s.start()
     first = halves(0, layer, layer_out)
     for copy in first:
         copy.start()
     mine[...] = small[...]
+    gain_row[...] = jnp.zeros_like(gain_row)
     s.middle()
+    zb = [rcopy(zb_of(ring(p, d)), got_zb.at[p], zs.at[d - 1], zr.at[d - 1], p=ring(p, d)) for d in (1, 2, 3)]
+    zb.append(pltpu.make_async_copy(zb_of(p), got_zb.at[p], zk))
+    for copy in zb:
+        copy.start()
     s.arrive()
 
     def one(at):
@@ -486,7 +511,7 @@
         v = x_ref[r]
         scale = lax.rsqrt(jnp.mean(v * v, axis=-1, keepdims=True) + norm_eps)
         grad = s.sum_of(at)
-        mine[pl.ds(3, 1)] += jnp.sum(grad * v * scale, axis=0, keepdims=True)
+        gain_row[pl.ds(0, 1)] += jnp.sum(grad * v * scale, axis=0, keepdims=True)
         u = grad * gain[...]
         stage[r] = d_hidden[r] + scale * u - v * (scale * scale * scale * jnp.mean(u * v, axis=-1, keepdims=True))
 
@@ -494,30 +519,20 @@
     second = halves(1, stage, grad_in)
     for copy in second:
         copy.start()
-    lines = [
-        rcopy(mine, others.at[d - 1], zs.at[d - 1], zr.at[d - 1], z=lax.rem(z + d, planes)) for d in range(1, planes)
-    ]
-    for copy in lines:
-        copy.start()
-    for copy in lines:
-        copy.wait()
-    total = mine[...]
-    for d in range(1, planes):
-        total = total + others[d - 1]
-    mine[...] = total
-    g = Spread(mine, sums, lambda q, k: pl.multiple_of((q * 2 + k) * RIM, RIM), RIM, scratch[17:24])
-    g.start()
-    g.pass_on()
+    lane = mine.shape[1]
+    for j in range(4):
+        mine[12 + j : 13 + j] = gain_row[:1, j * lane : (j + 1) * lane]
     s.finish()
     for copy in first + second:
         copy.wait()
-    g.finish()
-
-
-def back_body(planes, dbc, dkv, d_silu_bc, gx, g_bc, rim_bc, rim_x, kv_out, *scratch):
+    for copy in zb:
+        copy.wait()
+
+
+def back_body(planes, dbc, dkv, d_silu_bc, gx, sum_1, sum_2, g_bc, rim_bc, rim_x, kv_out, got_1, got_2, *scratch):
     z, p, c = here()
     greet(*plane_partners(p, c), *line_partners(z, planes))
-    (cx, bx, rbc, skv, zkv, acc, xs, xr, bs, br, zs, zr, ms, mr) = scratch
+    (cx, bx, rbc, skv, zkv, acc, xs, xr, bs, br, zs, zr, ms, mr, ws, wr, wk) = scratch
     rows = rbc.shape[1]
     across = rcopy(
         dbc.at[pl.ds(pl.multiple_of((1 - c) * G * rows, 16), G * rows)], cx, xs, xr, head=1 - c
@@ -544,6 +559,17 @@
 
     across.wait_recv()
     bc_over = []
+    grads = list(enumerate(((sum_1, got_1), (sum_2, got_2))))
+    wide = got_1.shape[1]
+
+    def rows_of(q):
+        return pl.ds(pl.multiple_of(q * wide, 16), wide)
+
+    w_over = [
+        rcopy(have.at[rows_of(ring(p, d))], got.at[p], ws.at[i, d - 1], wr.at[i, d - 1], p=ring(p, d))
+        for i, (have, got) in grads for d in (1, 2, 3)
+    ]
+    w_own = [pltpu.make_async_copy(have.at[rows_of(p)], got.at[p], wk.at[i]) for i, (have, got) in grads]
     for d in (1, 2, 3, 0):
         q = ring(p, d)
         own = dbc[pl.ds(pl.multiple_of((c * G + q) * rows, 16), rows)].astype(f32)
@@ -554,6 +580,8 @@
             bc_over[-1].start()
         else:
             acc[...] = own
+    for copy in w_over + w_own:
+        copy.start()
     for copy in bc_over:
         copy.wait_recv()
     g = acc[...]
@@ -583,6 +611,90 @@
     across.wait_send()
     for copy in bc_over:
         copy.wait_send()
+    for copy in w_own + w_over:
+        copy.wait()
+
+
+def last_body(planes, sum_a, small, got_x, got_s, sums, mine, others, xs, xr, ss, sr, keep, ls, lr, *spread):
+    z, p, c = here()
+    pairs = [(d, k) for k in (0, 1) for d in range(G) if d or k]
+    greet(*[{"p": ring(p, d), "head": lax.rem(c + k, 2)} for d, k in pairs], *line_partners(z, planes))
+    rows, chan = got_x.shape[1], got_x.shape[2]
+
+    def part(q, first, cols):
+        return sum_a.at[pl.ds(pl.multiple_of(q * rows, 16), rows), pl.ds(first, cols)]
+
+    def narrow(d, k):
+        cols = 128 if k else got_s.shape[2]
+        to = got_s.at[c * G + p, :, pl.ds(0, cols)]
+        i = k * G + d - 1
+        return rcopy(part(ring(p, d), chan, cols), to, ss.at[i], sr.at[i], p=ring(p, d), head=lax.rem(c + k, 2))
+
+    lines = [
+        rcopy(small, others.at[d - 1], ls.at[d - 1], lr.at[d - 1], z=lax.rem(z + d, planes)) for d in range(1, planes)
+    ]
+    copies = [
+        rcopy(part(ring(p, d), 0, chan), got_x.at[p], xs.at[d - 1], xr.at[d - 1], p=ring(p, d)) for d in (1, 2, 3)
+    ] + [narrow(d, k) for d, k in pairs] + [
+        pltpu.make_async_copy(part(p, 0, chan), got_x.at[p], keep.at[0]),
+        pltpu.make_async_copy(part(p, chan, got_s.shape[2]), got_s.at[c * G + p], keep.at[1]),
+    ]
+    for copy in lines + copies:
+        copy.start()
+    for copy in lines:
+        copy.wait()
+    total = small[...]
+    for d in range(1, planes):
+        total = total + others[d - 1]
+    mine[...] = total
+    g = Spread(mine, sums, lambda q, k: pl.multiple_of((q * 2 + k) * RIM, RIM), RIM, spread)
+    g.start()
+    g.pass_on()
+    for copy in copies:
+        copy.wait()
+    g.finish()
+
+
+def give_body(sizes, core_ref, zb, f1, f2, x_, s_, z_o, x_o, bc_o, dt_o, q_o, k_o, v_o, o_o, out_o, gate_o, up_o, down_o):
+    bcs, heads, quarter = sizes
+    chan, part = x_.shape[2], f1.shape[2] // 3
+    for p in range(G):
+        for ref, got, first, cols in (
+            (z_o, zb, 0, chan), (q_o, zb, chan, HD), (out_o, zb, chan + HD, chan), (o_o, zb, 2 * chan + HD, HD),
+            (x_o, x_, 0, chan),
+        ):
+            ref[:, p * cols : (p + 1) * cols] = got[p, :, first : first + cols].astype(f32)
+
+        for i, ref in enumerate((gate_o, up_o, down_o)):
+            for k, got in enumerate((f1, f2)):
+                at = (2 * p + k) * part
+                ref[:, at : at + part] = got[p, :, i * part : (i + 1) * part].astype(f32)
+
+    def place(first, cols, target):
+        i = iota((256, 256), 0) - first
+        return ((i >= 0) & (i < cols) & (iota((256, 256), 1) == target(i))).astype(bf16)
+
+    def bc_place(p):
+        return (iota((128, 256), 0) + p * bcs == iota((128, 256), 1)).astype(bf16) * (iota((128, 256), 0) < bcs).astype(bf16)
+
+    mine = core_ref[0]
+    k_sum = v_sum = dt_sum = jnp.zeros((x_.shape[1], 256), f32)
+    halves = []
+    for k in (0, 1):
+        total = jnp.zeros((x_.shape[1], 256), f32)
+        for p in range(G):
+            total = total + mm(s_[k * G + p, :, :128], bc_place(p), 1, 0)
+        halves.append(total)
+    bc_o[:, :256] = halves[0]
+    bc_o[:, 256:] = halves[1]
+    for p in range(G):
+        own = s_[mine * G + p]
+        k_sum = k_sum + mm(own, place(bcs, 2 * quarter, lambda i: (i // quarter) * (quarter * G) + p * quarter + i % quarter), 1, 0)
+        v_sum = v_sum + mm(own, place(bcs + 2 * quarter, 2 * quarter, lambda i: i + p * 2 * quarter), 1, 0)
+        dt_sum = dt_sum + mm(own, place(bcs + 4 * quarter, heads, lambda i: i + p * heads), 1, 0)
+    k_o[...] = k_sum[:, :HD]
+    v_o[...] = v_sum[:, :HD]
+    dt_o[...] = dt_sum[:, : dt_o.shape[1]]
 
 
 def mm(a, b, ca, cb):
@@ -684,7 +796,7 @@
         through[...] = jnp.ones_like(through)
 
     starts, place = starts_ref[...], places_of(base_ref, c)
-    raw = pa_ref[pl.ds(pl.multiple_of(c * CHUNK + RIM, 16), CHUNK), chan + 2 * HD :]
+    raw = pa_ref[pl.ds(pl.multiple_of(c * CHUNK + RIM, 16), CHUNK), chan + HD :]
     step, _, cs = rates_of(raw, bias_ref[...], rates_ref[...], heads)
     cs_t = cs.T
     cv = conv_of(pa_ref, taps_ref, starts, place, c, chan, 0)
@@ -729,7 +841,7 @@
     c = pl.program_id(0)
     chan = heads * P_SIZE
     starts, place = starts_ref[...], places_of(base_ref, c)
-    raw = pa_ref[pl.ds(pl.multiple_of(c * CHUNK + RIM, 16), CHUNK), chan + 2 * HD :]
+    raw = pa_ref[pl.ds(pl.multiple_of(c * CHUNK + RIM, 16), CHUNK), chan + HD :]
     _, _, cs = rates_of(raw, bias_ref[...], rates_ref[...], heads)
     decay_in, _ = decays_of(cs, starts, place)
     state_in = enter_ref[0] + scale_rows(before_ref[...], reach_ref[0], heads)
@@ -753,7 +865,7 @@
         gain_out[...] = jnp.zeros_like(gain_out)
 
     starts, place = starts_ref[...], places_of(base_ref, c)
-    raw = pa_ref[pl.ds(pl.multiple_of(c * CHUNK + RIM, 16), CHUNK), chan + 2 * HD :]
+    raw = pa_ref[pl.ds(pl.multiple_of(c * CHUNK + RIM, 16), CHUNK), chan + HD :]
     _, _, cs = rates_of(raw, bias_ref[...], rates_ref[...], heads)
     decay_in, _ = decays_of(cs, starts, place)
     z = z_ref[...]
@@ -787,7 +899,7 @@
         skip_out[...] = jnp.zeros_like(skip_out)
 
     starts, place = starts_ref[...], places_of(base_ref, c)
-    raw = pa_ref[pl.ds(pl.multiple_of(c * CHUNK + RIM, 16), CHUNK), chan + 2 * HD :]
+    raw = pa_ref[pl.ds(pl.multiple_of(c * CHUNK + RIM, 16), CHUNK), chan + HD :]
     step, log_decay, cs = rates_of(raw, bias_ref[...], rates_ref[...], heads)
     cs_t = cs.T
     visible = visible_of(base_ref, c, starts, place)
@@ -832,8 +944,8 @@
         drives.append(d_mix + close * d_close)
     d_c = d_c + mm(d_inter, b_rows, 1, 0)
     d_b = d_b + mm(d_inter, c_rows, 0, 0)
-    dbc_ref[:, :N] = d_b.astype(bf16)
-    dbc_ref[:, N:] = d_c.astype(bf16)
+    dbc_ref[:N] = d_b.astype(bf16).T
+    dbc_ref[N:] = d_c.astype(bf16).T
     d_driven = jnp.concatenate(drives, axis=1)
     closes = head_sums(jnp.concatenate(closes, axis=1), heads)
     d_cs = head_sums(jnp.concatenate(inside, axis=1) + jnp.concatenate(outside, axis=1), heads) - closes
@@ -852,6 +964,182 @@
     gx_ref[...] = (d_driven * wide + skip_ref[...] * dy) * (s * (1.0 + cv * (1.0 - s)))
 
 
+def unshuffled(v, back=False):
+    quarter = HD // 2 // G
+    i, j = (iota((HD, HD), 1), iota((HD, HD), 0)) if back else (iota((HD, HD), 0), iota((HD, HD), 1))
+    half, rest = i // (HD // 2), i % (HD // 2)
+    to = (rest // quarter) * 2 * quarter + half * quarter + rest % quarter
+    return mm_exact(v, (to == j).astype(f32), 1, 0)
+
+
+def keys_of(kv_ref, begin, size, tokens):
+    plane, at = begin // tokens, pl.ds(pl.multiple_of(begin % tokens, 128), size)
+    half = kv_ref.shape[2] // 2
+    keys = jnp.concatenate([kv_ref[p, plane, :half, at] for p in range(G)], axis=0)
+    values = jnp.concatenate([kv_ref[p, plane, half:, at] for p in range(G)], axis=0)
+    return plane, at, keys, values
+
+
+def seen_of(begin, size, starts, place):
+    at = begin + iota((starts.shape[0], size), 1)
+    return (at >= starts) & (at <= place)
+
+
+def attend_body(size, tokens, base_ref, first_ref, q_ref, starts_ref, cos_ref, sin_ref, kv_ref,
+                query_ref, low_ref, out_ref, mass_ref):
+    i = pl.program_id(0)
+    rows = q_ref.shape[0]
+    v = q_ref[...]
+    turned = (v * cos_ref[...] - pltpu.roll(v, HD // 2, 1) * sin_ref[...]) * HD ** (-0.5)
+    query = unshuffled(turned.astype(bf16).astype(f32)).astype(bf16)
+    query_ref[...] = query
+    starts = starts_ref[...]
+    place = base_ref[0] + i * rows + iota((rows, 1), 0)
+
+    def step(n, carry):
+        peak, mass, total = carry
+        begin = n * size
+        _, _, keys, values = keys_of(kv_ref, begin, size, tokens)
+        scores = jnp.where(seen_of(begin, size, starts, place), mm(query, keys, 1, 0), -1e30)
+        new = jnp.maximum(peak, jnp.max(scores, axis=1, keepdims=True))
+        probs = jnp.where(scores > -1e29, jnp.exp(scores - new), 0.0)
+        keep = jnp.exp(peak - new)
+        return new, mass * keep + jnp.sum(probs, axis=1, keepdims=True), total * keep + mm(probs, values, 1, 1)
+
+    begin = first_ref[i] // size
+    end = (base_ref[0] + (i + 1) * rows - 1) // size + 1
+    start = (jnp.full((rows, 1), -1e30, f32), jnp.zeros((rows, 1), f32), jnp.zeros((rows, HD), f32))
+    peak, mass, total = lax.fori_loop(begin, end, step, start)
+    attended = total / mass
+    out_ref[...] = attended
+    low_ref[...] = attended.astype(bf16)
+    mass_ref[...] = peak + jnp.log(mass)
+
+
+def attend_back_body(size, tokens, base_ref, first_ref, query_ref, starts_ref, cos_ref, sin_ref, kv_ref, d_ref, out_ref, mass_ref,
+                     dq_ref, dkv_ref, d_keys, d_values):
+    i = pl.program_id(0)
+    rows = query_ref.shape[0]
+
+    @pl.when(i == 0)
+    def _():
+        d_keys[...] = jnp.zeros_like(d_keys)
+        d_values[...] = jnp.zeros_like(d_values)
+
+    query = query_ref[...]
+    d_low = d_ref[...].astype(bf16)
+    balance = jnp.sum(d_low.astype(f32) * out_ref[...], axis=1, keepdims=True)
+    query_t, d_t = query.T, d_low.T
+    starts, mass = starts_ref[...], mass_ref[...]
+    place = base_ref[0] + i * rows + iota((rows, 1), 0)
+
+    def step(n, total):
+        begin = n * size
+        plane, at, keys, values = keys_of(kv_ref, begin, size, tokens)
+        seen = seen_of(begin, size, starts, place)
+        probs = jnp.where(seen, jnp.exp(jnp.where(seen, mm(query, keys, 1, 0) - mass, 0.0)), 0.0)
+        d_scores = (probs * (mm(d_low, values, 1, 0) - balance)).astype(bf16)
+        d_keys[plane, :, at] += mm(query_t, d_scores, 1, 0)
+        d_values[plane, :, at] += mm(d_t, probs, 1, 0)
+        return total + mm(d_scores, keys, 1, 1)
+
+    begin = first_ref[i] // size
+    end = (base_ref[0] + (i + 1) * rows - 1) // size + 1
+    d_query = unshuffled(lax.fori_loop(begin, end, step, jnp.zeros((rows, HD), f32)), True)
+    d_query = (d_query * cos_ref[...] + pltpu.roll(d_query, HD // 2, 1) * sin_ref[...]) * HD ** (-0.5)
+    dq_ref[...] = d_query.astype(bf16)
+
+    @pl.when(i == pl.num_programs(0) - 1)
+    def _():
+        half = dkv_ref.shape[2] // 2
+
+        def give(plane, carry):
+            for p in range(G):
+                dkv_ref[p, plane, :half] = d_keys[plane, p * half : (p + 1) * half].astype(bf16)
+                dkv_ref[p, plane, half:] = d_values[plane, p * half : (p + 1) * half].astype(bf16)
+            return carry
+
+        lax.fori_loop(0, dkv_ref.shape[1], give, 0)
+
+
+def ffn_units(part, second, low, w_ref):
+    gate = mm(second, w_ref[:, :part], 1, 0)
+    up = mm(second, w_ref[:, part : 2 * part], 1, 0)
+    d_act = mm(low, w_ref[:, 2 * part :], 1, 0)
+    s = sig(gate)
+    silu = gate * s
+    return jnp.concatenate(
+        [(d_act * up * (s * (1.0 + gate * (1.0 - s)))).astype(bf16), (d_act * silu).astype(bf16), (silu * up).astype(bf16)],
+        axis=1,
+    )
+
+
+def ffn_first_body(part, second_ref, low_ref, w_ref, h_ref):
+    h_ref[...] = ffn_units(part, second_ref[...], low_ref[...], w_ref)
+
+
+def ffn_second_body(part, second_ref, low_ref, w1_ref, w2_ref, h1_ref, h_ref, layer_ref, back_ref):
+    h1 = h1_ref[...]
+    h2 = ffn_units(part, second_ref[...], low_ref[...], w2_ref)
+    h_ref[...] = h2
+    two = 2 * part
+    layer = mm(h1[:, two:], w1_ref[:, two:], 1, 1) + mm(h2[:, two:], w2_ref[:, two:], 1, 1)
+    layer_ref[...] = layer.astype(bf16)
+    back = mm(h1[:, :two], w1_ref[:, :two], 1, 1) + mm(h2[:, :two], w2_ref[:, :two], 1, 1)
+    back_ref[...] = back.astype(bf16)
+
+
+def ffn_grad_body(part, second_ref, low_ref, h_ref, out_ref):
+    two = 2 * part
+    out_ref[:, :two] = mm(second_ref[...], h_ref[:, :two], 0, 0).astype(bf16)
+    out_ref[:, two:] = mm(low_ref[...], h_ref[:, two:], 0, 0).astype(bf16)
+
+
+def finish_body(chunks, chan, base_ref, pa_ref, gx_ref, rim_x, g_bc, rim_bc, dkv, raw_ref, starts_ref, taps_ref, cos_ref, sin_ref,
+                out_ref, taps_out):
+    c = pl.program_id(0)
+    wide = chan + 128
+
+    @pl.when(c == 0)
+    def _():
+        taps_out[...] = jnp.zeros_like(taps_out)
+
+    rows = g_bc.shape[0]
+    here_ = pl.ds(pl.multiple_of(c * CHUNK, CHUNK), CHUNK)
+    last = c == chunks - 1
+    ahead_at = jnp.minimum((c + 1) * CHUNK, (chunks - 1) * CHUNK)
+    next_ = pl.ds(pl.multiple_of(ahead_at, CHUNK), CHUNK)
+
+    def put(first):
+        return (iota((rows, 128), 1) == iota((rows, 128), 0) + first).astype(f32)
+
+    bc_here = mm_exact(g_bc[:, here_], put(0), 0, 0)
+    bc_next = mm_exact(jnp.where(last, rim_bc[...], g_bc[:, next_]), put(0), 0, 0)[:8]
+    gx_next = jnp.where(last, rim_x[:8], gx_ref[pl.ds(pl.multiple_of(ahead_at, 8), 8)])
+    longer = jnp.concatenate([
+        jnp.concatenate([gx_ref[here_], bc_here], axis=1), jnp.concatenate([gx_next, bc_next], axis=1)
+    ], axis=0)
+    starts = starts_ref[pl.ds(pl.multiple_of(c * CHUNK, 8), CHUNK + 8)]
+    place = places_of(base_ref, c)
+    block = pa_ref[pl.ds(pl.multiple_of(c * CHUNK + RIM - 8, 8), CHUNK + 8), :wide]
+    total = jnp.zeros((CHUNK, wide), f32)
+    for lag in range(K):
+        ahead = K - 1 - lag
+        seen = place >= starts[ahead : ahead + CHUNK]
+        total = total + jnp.where(seen, longer[ahead : ahead + CHUNK], 0.0) * taps_ref[lag : lag + 1]
+        valid = place - ahead >= starts[:CHUNK]
+        part = jnp.where(valid, longer[:CHUNK] * block[8 - ahead : 8 - ahead + CHUNK], 0.0)
+        taps_out[lag : lag + 1] += jnp.sum(part, axis=0, keepdims=True)
+    quarter = cos_ref.shape[0]
+    kv = dkv[:, here_]
+    a, b = kv[:quarter], kv[quarter : 2 * quarter]
+    cosine, sine = cos_ref[:, here_], sin_ref[:, here_]
+    kv = jnp.concatenate([a * cosine + b * sine, b * cosine - a * sine, kv[2 * quarter :]], axis=0)
+    out_ref[:, :chan] = total[:, :chan].astype(bf16)
+    out_ref[:, chan:wide] = (total[:, chan:] + mm(kv, put(rows), 0, 0)).astype(bf16)
+    out_ref[:, wide:] = raw_ref[...]
+
+
 def head_sums_t(v, heads):
     column = jnp.sum(v, axis=1, keepdims=True)
     pick = (iota((v.shape[0], 128), 0) // P_SIZE == iota((v.shape[0], 128), 1)).astype(f32)
@@ -912,22 +1200,6 @@
         valid = (places - back >= starts)[:, None]
         total = total + jnp.where(valid, padded[RIM - back : RIM - back + length] * taps[lag][None, :], 0.0)
     return total
-
-
-def conv_back(grad, grad_next, padded, taps, starts, places, starts_next):
-    length = starts.shape[0]
-    edge = K - 1
-    longer = jnp.concatenate([grad, grad_next], axis=0)
-    starts_long = jnp.concatenate([starts, starts_next])
-    total = jnp.zeros_like(grad)
-    tap_grads = []
-    for lag in range(K):
-        ahead = edge - lag
-        seen = (places >= starts_long[ahead : ahead + length])[:, None]
-        total = total + jnp.where(seen, longer[ahead : ahead + length], 0.0) * taps[lag][None, :]
-        valid = (places - ahead >= starts)[:, None]
-        tap_grads.append(jnp.sum(jnp.where(valid, grad * padded[RIM - ahead : RIM - ahead + length], 0.0), axis=0))
-    return total, jnp.stack(tap_grads)
 
 
 def mixer_row(v):
@@ -970,7 +1242,7 @@
 
     bc_mine = lax.dynamic_slice_in_dim(bc_weight, hi * (2 * N // cores), 2 * N // cores, 1)
     k_cut = jnp.moveaxis(k_weight.reshape(rows, 2, G, quarter_half), 2, 1).reshape(rows, G, -1)
-    a_sizes = [chan, HD, bcs, 2 * quarter_half, 2 * quarter_half, heads]
+    a_sizes = [chan, bcs, 2 * quarter_half, 2 * quarter_half, heads]
     a_at = [sum(a_sizes[:i]) for i in range(len(a_sizes))]
     pad = -sum(a_sizes) % 128
     small_w = jnp.concatenate(
@@ -985,7 +1257,7 @@
     exchange_sems = lambda n: [DMA((3, n)), DMA((3, n)), DMA((n,))]
     wa = gather(call(
         exchange_a_body, 0, shape((G * rows, a_cols), bf16), HBM,
-        (x_weight, q_weight, small_w), [HBM] * 3, exchange_sems(3),
+        (x_weight, small_w), [HBM] * 2, exchange_sems(2),
     ))
 
     def half(v):
@@ -995,22 +1267,22 @@
     r1 = lax.rsqrt(jnp.mean(x_own * x_own, axis=-1, keepdims=True) + norm_eps)
     first_own = (x_own * r1 * mixer_gain).astype(bf16)
     wb = gather(call(
-        exchange_b_body, 9, shape((G * rows, 2 * chan + HD), bf16), HBM,
-        (z_weight, out_weight, o_weight), [HBM] * 3, exchange_sems(3),
+        exchange_b_body, 9, shape((G * rows, 2 * (chan + HD)), bf16), HBM,
+        (z_weight, q_weight, out_weight, o_weight), [HBM] * 4, exchange_sems(4),
     ))
-    wc, wd, first_rim, out_low, docs = call(
+    part = gate_weight.shape[1] // G // 2
+    w1, w2, first_rim, docs = call(
         functools.partial(start_body, planes), 1,
-        (shape((G * rows, gate_weight.shape[1] * 2 // G), bf16),
-         shape((G * rows, down_weight.shape[1] // G), bf16), shape((RIM + T, width), bf16), shape((T, width), bf16),
+        (shape((G * rows, 3 * part), bf16), shape((G * rows, 3 * part), bf16), shape((RIM + T, width), bf16),
          shape((planes, G, 8, tokens), jnp.int32)),
-        (HBM,) * 5,
-        (gate_weight, up_weight, down_weight, first_own, cot_own.astype(bf16), jnp.broadcast_to(doc_start[None], (8, tokens))),
-        [HBM] * 3 + [VMEM] * 3,
-        exchange_sems(3) + [DMA(()), DMA(()), DMA((3,)), DMA((3,)), DMA((planes - 1,)), DMA((planes - 1,)), DMA(())]
-        + Spread.sems * 2, us=55,
-    )
-    wc, wd = gather(wc), gather(wd)
-    wz, wb = wb[:, :chan], wb[:, chan:]
+        (HBM,) * 4,
+        (gate_weight, up_weight, down_weight, first_own, jnp.broadcast_to(doc_start[None], (8, tokens))),
+        [HBM] * 3 + [VMEM] * 2,
+        exchange_sems(6) + [DMA(()), DMA(()), DMA((3,)), DMA((3,)), DMA((planes - 1,)), DMA((planes - 1,)), DMA(())]
+        + Spread.sems, us=40,
+    )
+    w1, w2 = gather(w1), gather(w2)
+    wz, wb = wb[:, : chan + HD], wb[:, chan + HD :]
     first = first_rim[RIM:]
     all_starts = docs[:, :, 0].reshape(-1)
     starts = lax.dynamic_slice_in_dim(all_starts, offset, T, 0)
@@ -1018,23 +1290,19 @@
     def line_sum(grad):
         return lax.psum_scatter(grad, "z", scatter_dimension=0, tiled=True)
 
-    def scatter(g):
-        g = lax.all_to_all(g.reshape(G, rows, -1), "p", 0, 0, tiled=True)
-        return jnp.moveaxis(g, 0, 1).astype(f32)
-
     edge = K - 1
     pa = dot(first_rim, wa, 1, 0)
-    z_part = dot(first, wz, 1, 0)
-    q_proj, bc_pre, k_proj, v_proj = (pa[RIM:, a : a + s] for a, s in zip(a_at[1:5], a_sizes[1:5]))
-    bc_ext = pa[:, a_at[2] : a_at[2] + bcs]
+    zq = dot(first, wz, 1, 0)
+    bc_pre, k_proj, v_proj = (pa[RIM:, a : a + s] for a, s in zip(a_at[1:4], a_sizes[1:4]))
+    bc_ext = pa[:, a_at[1] : a_at[1] + bcs]
     cv_bc = conv_rows(bc_ext, taps_state, starts, places)
     bc_low = jax.nn.silu(cv_bc).astype(bf16)
     offsets = places - starts
     cos_q, sin_q = rope_tables(offsets, 0, HD // 2)
     cos_k, sin_k = rope_tables(offsets, pi * quarter_half, quarter_half)
-    scale = HD ** (-0.5)
+    cos_row = jnp.concatenate([cos_q, cos_q], axis=1)
+    sin_row = jnp.concatenate([sin_q, -sin_q], axis=1)
     kvr = 4 * quarter_half
-    query = (turn(q_proj, cos_q, sin_q) * scale).astype(bf16)
     kv_own = jnp.concatenate([turn(k_proj, cos_k, sin_k).astype(bf16), v_proj.astype(bf16)], axis=1)
     line_sems = [DMA((planes - 1,)), DMA((planes - 1,))]
     bc_t, kv_line = call(
@@ -1084,53 +1352,36 @@
         return total
 
     state_shapes = (shape((planes - 1, chan, N), bf16), shape((planes - 1, 8, 128), f32))
-    states, factors, kv_all = call(
-        functools.partial(up_body, planes), 3, state_shapes + (shape((G * planes, kvr, T), bf16),), (HBM,) * 3,
-        (state, through, kv_line), [HBM] * 3, line_sems * 2 + Spread.sems, us=28,
+    states, factors, kv_all, out_low = call(
+        functools.partial(up_body, planes), 3, state_shapes + (shape((G * planes, kvr, T), bf16), shape((T, width), bf16)), (HBM,) * 4,
+        (state, through, kv_line, cot_own.astype(bf16)), [HBM] * 4, line_sems * 2 + Spread.sems * 2, us=38,
     )
     before = entering(True, states, factors)
     ssm_low, y_scan = chunked(
         functools.partial(gate_body, heads), nc,
         (shape((T, chan), bf16), shape((T, chan), f32)), (tile(chan), tile(chan)),
-        (base, pa, bc_all, starts_col, bias_row, rates_row, y_diag, cv_x, enter, reach, before, z_part, skip_row, gain_row),
+        (base, pa, bc_all, starts_col, bias_row, rates_row, y_diag, cv_x, enter, reach, before, zq, skip_row, gain_row),
         [smem, pa_spec, tile(2 * N), tile(1), fixed(1, 128), fixed(1, 128), tile(chan), tile(chan), stack(chan, N),
          stack(16, 128), fixed(chan, N), tile(chan), fixed(1, chan), fixed(1, chan)],
     )
 
-    kv_all = kv_all.reshape(G, planes, 4, quarter_half, T)
-    keys = kv_all[:, :, :2].transpose(1, 4, 2, 0, 3).reshape(total_tokens, HD)
-    values = kv_all[:, :, 2:].transpose(1, 4, 0, 2, 3).reshape(total_tokens, HD)
-    key_len = min(512, total_tokens)
-    first_block = starts[0] // key_len
-    last_block = (offset + T - 1) // key_len
-
-    def key_block(index):
-        begin = index * key_len
-        kb = lax.dynamic_slice_in_dim(keys, begin, key_len, 0)
-        vb = lax.dynamic_slice_in_dim(values, begin, key_len, 0)
-        at = begin + jnp.arange(key_len, dtype=jnp.int32)
-        seen = (at[None, :] >= starts[:, None]) & (at[None, :] <= places[:, None])
-        return kb, vb, seen, dot(query, kb, 1, 1)
-
-    def running(index, carry):
-        peak, mass = carry
-        _, _, seen, scores = key_block(index)
-        new = jnp.maximum(peak, jnp.max(jnp.where(seen, scores, -1e30), axis=-1))
-        mass = mass * jnp.exp(peak - new) + jnp.sum(jnp.where(seen, jnp.exp(scores - new[:, None]), 0.0), axis=-1)
-        return new, mass
-
-    peak, mass = lax.fori_loop(
-        first_block, last_block + 1, running, (jnp.full((T,), -1e30, f32), jnp.zeros((T,), f32))
-    )
-    log_mass = peak + jnp.log(mass)
-
-    def weighted(index, total):
-        _, vb, seen, scores = key_block(index)
-        probs = jnp.where(seen, jnp.exp(scores - log_mass[:, None]), 0.0).astype(bf16)
-        return total + dot(probs, vb, 1, 0)
-
-    attended = lax.fori_loop(first_block, last_block + 1, weighted, jnp.zeros((T, HD), f32))
-    att_low = attended.astype(bf16)
+    size = math.gcd(512, T)
+    qrows = math.gcd(256, T)
+    kv_all = kv_all.reshape(G, planes, kvr, T)
+    firsts = starts.reshape(-1, qrows)[:, 0]
+
+    def column(at, cols):
+        return pl.BlockSpec((qrows, cols), lambda i: (i, at))
+
+    kv_spec = pl.BlockSpec((G, planes, kvr, T), lambda i: (0, 0, 0, 0))
+    at_q = chan // HD
+    query, att_low, attended, log_mass = chunked(
+        functools.partial(attend_body, size, T), T // qrows,
+        (shape((T, HD), bf16), shape((T, HD), bf16), shape((T, HD), f32), shape((T, 1), f32)),
+        (column(0, HD), column(0, HD), column(0, HD), column(0, 1)),
+        (base, firsts, zq, starts_col, cos_row, sin_row, kv_all),
+        [smem, smem, column(at_q, HD), column(0, 1), column(0, HD), column(0, HD), kv_spec],
+    )
 
     both_low = jnp.concatenate([ssm_low, att_low], axis=1)
     collect = Collect.scratch(own, width) + [pltpu.VMEM((own, width), bf16)] + Spread.sems
@@ -1138,30 +1389,45 @@
         hidden_body, 4, (shape((own, width), f32), shape((T, width), bf16)), (VMEM, HBM),
         (dot(both_low, wb, 1, 1).astype(bf16), x_own, mixer_row(ffn_gain)), [VMEM] * 3, collect, us=50,
     )
-    pc = dot(second, wc, 1, 0)
-    ff = pc.shape[1] // 2
-    gate_pre, up_pre = pc[:, :ff], pc[:, ff:]
-    s_gate = jax.nn.silu(gate_pre)
-    act_low = (s_gate * up_pre).astype(bf16)
-    layer_own = hidden + lax.psum_scatter(
-        dot(act_low, wd, 1, 1).astype(bf16), ("p", "head"), scatter_dimension=0, tiled=True
-    ).astype(f32)
-
-    grad_d = dot(out_low, act_low, 0, 0)
-    d_act = dot(out_low, wd, 1, 0)
-    gu_low = jnp.concatenate([d_act * up_pre * d_silu(gate_pre), d_act * s_gate], axis=1).astype(bf16)
-    grad_c = dot(second, gu_low, 0, 0)
-    part_c = dot(gu_low, wc, 1, 1).astype(bf16)
-    grad_c, grad_d, part_c = lax.optimization_barrier((grad_c.astype(bf16), grad_d.astype(bf16), part_c))
-    sum_d = line_sum(grad_d)
-    sum_c = line_sum(grad_c)
+    ftile = math.gcd(256, T)
+    wide = 3 * part
+
+    def rows_spec(cols):
+        return pl.BlockSpec((ftile, cols), lambda i: (i, 0))
+
+    def all_spec(v):
+        return pl.BlockSpec(v.shape, lambda i: (0,) * len(v.shape))
+
+    h1 = chunked(
+        functools.partial(ffn_first_body, part), T // ftile, shape((T, wide), bf16), rows_spec(wide),
+        (second, out_low, w1), [rows_spec(width), rows_spec(width), all_spec(w1)],
+    )
+
+    def ffn_grads(h):
+        tile_d = math.gcd(256, width)
+        columns = pl.BlockSpec((T, tile_d), lambda i: (0, i))
+        return chunked(
+            functools.partial(ffn_grad_body, part), width // tile_d, shape((width, wide), bf16),
+            pl.BlockSpec((tile_d, wide), lambda i: (i, 0)), (second, out_low, h), [columns, columns, all_spec(h)],
+        )
+
+    grad_1 = ffn_grads(h1)
+    w2, grad_1 = lax.optimization_barrier((w2, grad_1))
+    sum_1 = line_sum(grad_1)
+    h2, part_l, part_c = chunked(
+        functools.partial(ffn_second_body, part), T // ftile,
+        (shape((T, wide), bf16), shape((T, width), bf16), shape((T, width), bf16)),
+        (rows_spec(wide), rows_spec(width), rows_spec(width)),
+        (second, out_low, w1, w2, h1), [rows_spec(width), rows_spec(width), all_spec(w1), all_spec(w2), rows_spec(wide)],
+    )
     d_hidden, grad_ffn, branch = call(
         branch_body, 5, (shape((own, width), f32), shape((8, width), f32), shape((T, width), bf16)), (VMEM, VMEM, HBM),
         (part_c, hidden, cot_own, mixer_row(ffn_gain)), [VMEM] * 4, collect, us=50,
     )
+    h2, branch = lax.optimization_barrier((h2, branch))
+    sum_2 = line_sum(ffn_grads(h2))
     grad_b = dot(branch, both_low, 0, 0)
     d_both = dot(branch, wb, 1, 0)
-    d_norm_s, d_att = d_both[:, :chan], d_both[:, chan:].astype(bf16)
 
     back, _, back_stack = specs(True)
     dz_low, dy, leave, tail, g_state, grad_gain_s = chunked(
@@ -1169,42 +1435,34 @@
         (shape((T, chan), bf16), shape((T, chan), f32), shape((nc, chan, N), f32), shape((nc, 8, 128), f32),
          shape((chan, N), bf16), shape((8, chan), f32)),
         (back(chan), back(chan), back_stack(chan, N), back_stack(8, 128), fixed(chan, N), fixed(8, chan)),
-        (base, pa, bc_all, starts_col, bias_row, rates_row, d_norm_s, y_scan, cv_x, reach, z_part, skip_row, gain_row),
+        (base, pa, bc_all, starts_col, bias_row, rates_row, d_both, y_scan, cv_x, reach, zq, skip_row, gain_row),
         [smem, pa_spec, back(2 * N), back(1), fixed(1, 128), fixed(1, 128), back(chan), back(chan), back(chan),
          back_stack(16, 128), back(chan), fixed(1, chan), fixed(1, chan)],
         [pltpu.VMEM((chan, N), f32), pltpu.VMEM((8, 128), f32)],
     )
-    grad_zb = jnp.concatenate([dot(first, dz_low, 0, 0).astype(bf16), grad_b.astype(bf16)], axis=1)
-    g_state, sum_d, grad_zb = lax.optimization_barrier((g_state, sum_d, grad_zb))
+    dq_low, dkv = chunked(
+        functools.partial(attend_back_body, size, T), T // qrows,
+        (shape((T, HD), bf16), shape((G, planes, kvr, T), bf16)), (column(0, HD), kv_spec),
+        (base, firsts, query, starts_col, cos_row, sin_row, kv_all, d_both, attended, log_mass),
+        [smem, smem, column(0, HD), column(0, 1), column(0, HD), column(0, HD), kv_spec, column(at_q, HD), column(0, HD),
+         column(0, 1)],
+        [pltpu.VMEM((planes, HD, T), f32), pltpu.VMEM((planes, HD, T), f32)],
+    )
+    dzq_low = jnp.concatenate([dz_low, dq_low], axis=1)
+    grad_zb = jnp.concatenate([dot(first, dzq_low, 0, 0).astype(bf16), grad_b.astype(bf16)], axis=1)
+    g_state, sum_1, grad_zb = lax.optimization_barrier((g_state, sum_1, grad_zb))
+    states, factors, dkv, layer_own = call(
+        functools.partial(down_body, planes), 6, state_shapes + (shape((G, planes, kvr, T), bf16), shape((own, width), f32)),
+        (HBM,) * 3 + (VMEM,), (g_state, through, dkv, part_l, hidden), [HBM] * 3 + [VMEM] * 2,
+        line_sems * 2 + [DMA((3,)), DMA((3,)), DMA(())] + Collect.scratch(own, width), us=45,
+    )
+    states, grad_zb = lax.optimization_barrier((states, grad_zb))
     sum_zb = line_sum(grad_zb)
-    balance = jnp.sum(d_att.astype(f32) * attended, axis=-1, keepdims=True)
-
-    def grads(index, carry):
-        d_query, d_keys, d_values = carry
-        kb, vb, seen, scores = key_block(index)
-        probs = jnp.where(seen, jnp.exp(scores - log_mass[:, None]), 0.0)
-        d_scores = (probs * (dot(d_att, vb, 1, 1) - balance)).astype(bf16)
-        d_query = d_query + dot(d_scores, kb, 1, 0)
-        d_keys = lax.dynamic_update_slice_in_dim(d_keys, dot(d_scores, query, 0, 0), index * key_len, 0)
-        d_values = lax.dynamic_update_slice_in_dim(d_values, dot(probs.astype(bf16), d_att, 0, 0), index * key_len, 0)
-        return d_query, d_keys, d_values
-
-    zero_keys = jnp.zeros((total_tokens, HD), f32)
-    d_query, d_keys, d_values = lax.fori_loop(
-        first_block, last_block + 1, grads, (jnp.zeros((T, HD), f32), zero_keys, zero_keys)
-    )
-    dk_cut = d_keys.astype(bf16).reshape(planes, T, 2, G, quarter_half).transpose(3, 0, 2, 4, 1)
-    dv_cut = d_values.astype(bf16).reshape(planes, T, G, 2, quarter_half).transpose(2, 0, 3, 4, 1)
-    dkv = jnp.concatenate([dk_cut, dv_cut], axis=2).reshape(G, planes, 4 * quarter_half, T)
-    states, factors, dkv = call(
-        functools.partial(down_body, planes), 6, state_shapes + (shape((G, planes, kvr, T), bf16),), (HBM,) * 3,
-        (g_state, through, dkv), [HBM] * 3, line_sems * 2 + [DMA((3,)), DMA((3,)), DMA(())], us=35,
-    )
     after = entering(False, states, factors)
     gx, d_bc_all, d_raw, grad_rows, grad_skip = chunked(
         functools.partial(scan_back_body, heads), nc,
-        (shape((T, chan), f32), shape((T, 2 * N), bf16), shape((T, 128), bf16), shape((8, 128), f32), shape((8, chan), f32)),
-        (tile(chan), tile(2 * N), tile(128), fixed(8, 128), fixed(8, chan)),
+        (shape((T, chan), f32), shape((2 * N, T), bf16), shape((T, 128), bf16), shape((8, 128), f32), shape((8, chan), f32)),
+        (tile(chan), pl.BlockSpec((2 * N, L), lambda c: (0, c)), tile(128), fixed(8, 128), fixed(8, chan)),
         (base, pa, bc_all, starts_col, bias_row, rates_row, dy, cv_x, enter, reach, before, leave, tail, after, skip_row),
         [smem, pa_spec, tile(2 * N), tile(1), fixed(1, 128), fixed(1, 128), tile(chan), tile(chan),
          stack(chan, N), stack(16, 128), fixed(chan, N), stack(chan, N), stack(8, 128), fixed(chan, N), fixed(1, chan)],
@@ -1214,78 +1472,91 @@
     grad_skip = jnp.sum(grad_skip[0].reshape(heads, P_SIZE), axis=1)
 
     gx_first = gx[:RIM]
-    d_bc_t, sum_c = lax.optimization_barrier((d_bc_all.T, sum_c))
-    g_bc, rim_bc, rim_x, dkv = call(
+    d_bc_t, sum_2 = lax.optimization_barrier((d_bc_all, sum_2))
+    g_bc, rim_bc, rim_x, dkv, got_1, got_2 = call(
         functools.partial(back_body, planes), 7,
-        (shape((bcs, T), f32), shape((bcs, 128), f32), shape((RIM, chan), f32), shape((kvr, T), f32)), (VMEM,) * 4,
-        (d_bc_t, dkv, d_silu(cv_bc).T, gx_first), [VMEM] * 4,
+        (shape((bcs, T), f32), shape((bcs, 128), f32), shape((RIM, chan), f32), shape((kvr, T), f32))
+        + tuple(shape((G, rows, v.shape[1]), bf16) for v in (sum_1, sum_2)), (VMEM,) * 4 + (HBM,) * 2,
+        (d_bc_t, dkv, d_silu(cv_bc).T, gx_first, sum_1, sum_2), [VMEM] * 4 + [HBM] * 2,
         [pltpu.VMEM((G * bcs, T), bf16), pltpu.VMEM((3, bcs, T), bf16), pltpu.VMEM((3, bcs, T), bf16),
          pltpu.VMEM((planes, kvr, T), bf16), pltpu.VMEM((planes - 1, kvr, T), bf16),
          pltpu.VMEM((bcs, T), f32), DMA(()), DMA(()), DMA((3,)), DMA((3,)),
-         DMA((planes - 1,)), DMA((planes - 1,)), DMA((2,)), DMA((2,))],
-    )
-    dkv = dkv.T
-    later = zi < planes - 1
-    gx_next = jnp.where(later, rim_x[:edge], 0.0)
-    gb_next = jnp.where(later, rim_bc[:, :edge].T, 0.0)
-    ends = jnp.minimum(offset + T + jnp.arange(edge), total_tokens - 1)
-    starts_next = jnp.where(later, all_starts[ends], total_tokens)
-    d_inner_pre, grad_conv_inner = conv_back(gx, gx_next, pa[:, :chan], taps_inner, starts, places, starts_next)
-    d_bc_pre, grad_conv_state = conv_back(g_bc.T, gb_next, bc_ext, taps_state, starts, places, starts_next)
-    d_q = turn(d_query, cos_q, -sin_q) * scale
-    d_k = turn(dkv[:, : 2 * quarter_half], cos_k, -sin_k)
-    d_v = dkv[:, 2 * quarter_half :]
-
-    da_low = jnp.concatenate(
-        [v.astype(bf16) for v in (d_inner_pre, d_q, d_bc_pre, d_k, d_v)] + [d_raw], axis=1
+         DMA((planes - 1,)), DMA((planes - 1,)), DMA((2,)), DMA((2,)), DMA((2, 3)), DMA((2, 3)), DMA((2,))], us=30,
+    )
+    starts_long = jnp.concatenate([all_starts, jnp.full((8,), total_tokens, jnp.int32)])
+    starts_long = lax.dynamic_slice_in_dim(starts_long, offset, T + 8, 0)[:, None]
+    taps_both = jnp.concatenate([taps_inner, taps_state, jnp.zeros((K, 128 - bcs), f32)], axis=1)
+    da_low, grad_taps = chunked(
+        functools.partial(finish_body, nc, chan), nc,
+        (shape((T, a_cols), bf16), shape((8, chan + 128), f32)), (tile(a_cols), fixed(8, chan + 128)),
+        (base, pa, gx, rim_x, g_bc, rim_bc, dkv, d_raw, starts_long, taps_both, cos_k.T, sin_k.T),
+        [smem, pa_spec, fixed(T, chan), fixed(RIM, chan), fixed(bcs, T), fixed(bcs, 128), fixed(kvr, T), tile(128),
+         fixed(T + 8, 1), fixed(K, chan + 128), fixed(quarter_half, T), fixed(quarter_half, T)],
     )
     grad_a = dot(first, da_low, 0, 0).astype(bf16)
-    small = [grad_conv_inner, grad_conv_state, grad_rates, grad_bias, grad_skip, grad_gain_s]
-    at = [0]
-    for s in small:
-        at.append(at[-1] + s.size)
-    flat = jnp.concatenate([s.reshape(-1) for s in small] + [jnp.zeros((2 * width - at[-1],), f32)]).reshape(2, width)
-    flat = jnp.concatenate([flat, grad_ffn[:1], jnp.zeros((RIM - 3, width), f32)], axis=0)
-    gc, gd = scatter(sum_c), scatter(sum_d)
-    part_a = (dot(da_low, wa, 1, 1) + dot(dz_low, wz, 1, 1)).astype(bf16)
-    part_a, gc, gd = lax.optimization_barrier((part_a, gc, gd))
+    grad_a, sum_zb = lax.optimization_barrier((grad_a, sum_zb))
     sum_a = line_sum(grad_a)
-    grad_input, layer_out, sums = call(
-        functools.partial(final_body, planes), 8,
-        (shape((tokens, width), f32), shape((tokens, width), f32), shape((2 * G * RIM, width), f32)), (HBM, HBM, HBM),
-        (part_a, x_own, d_hidden, layer_own, mixer_row(mixer_gain), flat), [VMEM] * 6,
+    lane = width // 4
+
+    def lines_of(*parts):
+        both = jnp.concatenate(parts, axis=1)
+        return jnp.pad(both, ((0, 0), (0, lane - both.shape[1])))
+
+    flat = jnp.concatenate(
+        [grad_taps[:K], lines_of(grad_gain_s[None]),
+         lines_of(row128(grad_rates), row128(grad_bias), row128(grad_skip)), jnp.zeros((2, lane), f32),
+         grad_ffn[:1].reshape(4, lane), jnp.zeros((4, lane), f32)], axis=0,
+    )
+    part_a = (dot(da_low, wa, 1, 1) + dot(dzq_low, wz, 1, 1)).astype(bf16)
+    grad_input, layer_out, mine, got_zb = call(
+        final_body, 8,
+        (shape((tokens, width), f32), shape((tokens, width), f32), shape((RIM, lane), f32),
+         shape((G, rows, sum_zb.shape[1]), bf16)), (HBM, HBM, VMEM, HBM),
+        (part_a, x_own, d_hidden, layer_own, mixer_row(mixer_gain), flat, sum_zb), [VMEM] * 6 + [HBM],
         Collect.scratch(own, width)
-        + [pltpu.VMEM((own, width), f32), pltpu.VMEM((RIM, width), f32), pltpu.VMEM((planes - 1, RIM, width), f32),
-           DMA((planes - 1,)), DMA((planes - 1,)), DMA((2,)), DMA((2,)), DMA((2,))]
-        + Spread.sems, us=45,
-    )
-
-    ga, gb = scatter(sum_a), scatter(sum_zb)
-    g_z, gb = gb[:, :, :chan], gb[:, :, chan:]
-    g_x, g_q, g_bc, g_k, g_v, g_dt = (ga[:, :, a : a + s] for a, s in zip(a_at, a_sizes))
-    g_k = jnp.moveaxis(g_k.reshape(rows, G, 2, quarter_half), 1, 2)
-    g_bc = lax.all_gather(g_bc.reshape(rows, -1).astype(bf16), "head", axis=1, tiled=True).astype(f32)
-
-    sums = sums.reshape(G, cores, RIM, width)
-    every = sums[:, :, :2].reshape(G, cores, 2 * width)
-    mine = lax.dynamic_index_in_dim(every, hi, 1, False)
-    pieces = [mine[:, a:b] for a, b in zip(at, at[1:])]
-    o_conv_inner = jnp.moveaxis(pieces[0].reshape(G, K, chan), 0, 1).reshape(K, G * chan)
-    o_conv_state = every[:, :, at[1] : at[2]].reshape(G, cores, K, bcs).transpose(2, 1, 0, 3).reshape(K, 2 * N)
+        + [pltpu.VMEM((own, width), f32), pltpu.VMEM((8, width), f32), DMA((2,)), DMA((2,)), DMA((2,)),
+           DMA((3,)), DMA((3,)), DMA(())], us=40,
+    )
+
+    got_x, got_s, sums = call(
+        functools.partial(last_body, planes), 10,
+        (shape((G, rows, chan), bf16), shape((2 * G, rows, a_cols - chan), bf16), shape((2 * G * RIM, lane), f32)),
+        (HBM,) * 3, (sum_a, mine), [HBM, VMEM],
+        [pltpu.VMEM((RIM, lane), f32), pltpu.VMEM((planes - 1, RIM, lane), f32), DMA((3,)), DMA((3,)), DMA((2 * G,)), DMA((2 * G,)),
+         DMA((2,)), DMA((planes - 1,)), DMA((planes - 1,))] + Spread.sems,
+    )
+    strip = min(32, rows)
+
+    def got(v):
+        return pl.BlockSpec((v.shape[0], strip, v.shape[2]), lambda c: (0, c, 0))
+
+    def given(cols):
+        return pl.BlockSpec((strip, cols), lambda c: (c, 0))
+
+    widths = [w.shape[1] for w in (
+        z_weight, x_weight, bc_weight, dt_weight, q_weight, k_weight, v_weight, o_weight, out_weight,
+        gate_weight, up_weight, down_weight,
+    )]
+    gathered = (got_zb, got_1, got_2, got_x, got_s)
+    weights = chunked(
+        functools.partial(give_body, (bcs, heads, quarter_half)), rows // strip,
+        tuple(shape((rows, w), f32) for w in widths), tuple(given(w) for w in widths),
+        (jnp.full((1,), hi, jnp.int32),) + gathered, [smem] + [got(v) for v in gathered],
+    )
+
+    sums = sums.reshape(G, cores, RIM, lane)
+    mine = lax.dynamic_index_in_dim(sums, hi, 1, False)
+    o_conv_inner = mine[:, :K, :chan].transpose(1, 0, 2).reshape(K, G * chan)
+    o_conv_state = sums[:, :, :K, chan : chan + bcs].transpose(2, 1, 0, 3).reshape(K, 2 * N)
     per = width // (planes * G)
-    gains = lax.dynamic_slice_in_dim(jnp.sum(sums[:, :, 2:4], axis=(0, 1)), (zi * G + pi) * per, per, 1)
-    gains = (gains[1], gains[0])
-
-    def whole(g):
-        return g.reshape(rows, -1)
+    gains = jnp.sum(sums[:, :, 8:], axis=(0, 1)).reshape(2, width)
+    gains = lax.dynamic_slice_in_dim(gains, (zi * G + pi) * per, per, 1)
 
     return (
-        layer_out, grad_input, gains[0], gains[1],
-        whole(g_z), whole(g_x), g_bc, whole(g_dt), whole(g_q), whole(g_k), whole(g_v),
-        whole(gb[:, :, chan:]), whole(gb[:, :, :chan]),
-        whole(gc[:, :, :ff]), whole(gc[:, :, ff:]), whole(gd),
+        layer_out, grad_input, gains[1], gains[0], *weights,
         o_conv_inner, o_conv_state,
-        pieces[2].reshape(-1), pieces[3].reshape(-1), pieces[4].reshape(-1), pieces[5].reshape(-1),
+        mine[:, 5, :heads].reshape(-1), mine[:, 5, 128 : 128 + heads].reshape(-1),
+        mine[:, 5, 256 : 256 + heads].reshape(-1), mine[:, 4, :chan].reshape(-1),
     )
 
 

time: 791 us -> 685 us (0.87)
  matrix products: 119 us -> 49.7 us
  Pallas kernels: 429 us -> 488 us
  local copies, waits for them, and re-layouts: 118 us -> 74.6 us
  other arithmetic: 49.1 us -> 17.6 us
  starting transfers between devices: 15.9 us -> 0.32 us
    dot_general x29 -> x9, matrix products: 119 us -> 49.7 us  [dot(): lax.dot_general(a, b, (((ca,), (cb,)), ((), ())), preferred_element_type=...]
    pallas_call x4 -> x12, Pallas kernels: 51.5 us -> 115 us  [chunked(): pl.pallas_call(body, grid=(chunks,), out_shape=outs, in_specs=in_specs, o...]
    reshape x19 -> x4, local copies, waits for them, and re-layouts: 19.8 us -> 0.72 us  [the longest x1 0.68 us: on_device(): sums[:, :, :K, chan:chan + bcs].transpose(2, 1, 0, 3).reshape(K, 2 * N)]
    all_to_all x4 -> x0, waiting for transfers between devices: 18.7 us -> none  [scatter(): g = lax.all_to_all(g.reshape(G, rows, -1), 'p', 0, 0, tiled=True)]
    all_to_all x4 -> x0, starting transfers between devices: 15.6 us -> none  [scatter(): g = lax.all_to_all(g.reshape(G, rows, -1), 'p', 0, 0, tiled=True)]
    convert_element_type x9 -> x0, other arithmetic: 14.3 us -> none  [the longest x3 5.88 us: on_device(): v.astype(bf16)]
    all_gather x4, waiting for transfers between devices: 5.66 us -> 18.9 us  [gather(): return lax.all_gather(w, 'z', axis=0, tiled=True)]
    reduce_scatter x4, waiting for transfers between devices: 0.04 us -> 12.9 us  [line_sum(): return lax.psum_scatter(grad, 'z', scatter_dimension=0, tiled=True)]
  transfers between devices with their start and end apart: 13 -> 8, of which waited for: 5 -> 3; matrix products, arithmetic and copies ran while one was open for 28% -> 13% of each run, Pallas kernels for 53% -> 67%
where the time goes in v4:
time: 685 us; the launch traced here: 678 us
  Pallas kernels  488 us (71%)
  local copies, waits for them, and re-layouts  74.6 us (11%)
  matrix products  49.7 us (7%)
  waiting for transfers between devices  32.5 us (5%)
  other arithmetic  17.6 us (3%)
  between operations  15.9 us (2%)
    pallas_call x11, Pallas kernels, call(): pl.pallas_call(body, out_shape=outs, in_specs=in_specs, out_specs=out_spe...  372 us
    pallas_call x12, Pallas kernels, chunked(): pl.pallas_call(body, grid=(chunks,), out_shape=outs, in_specs=in_specs, o...  115 us
    unnamed x233, local copies, waits for them, and re-layouts  55 us
    dot_general x9, matrix products, dot(): lax.dot_general(a, b, (((ca,), (cb,)), ((), ())), preferred_element_type=...  49.7 us
    all_gather x4, waiting for transfers between devices, gather(): return lax.all_gather(w, 'z', axis=0, tiled=True)  18.9 us
  transfers between devices with their start and end apart: 8, of which 3 were waited for; matrix products, arithmetic and copies ran while one was open for 13% of the time, Pallas kernels for 67%

profile of v4, /device:TPU:0, one launch (start us, length us, event | category | flops | bytes accessed | tf_op | source)
XLA Modules:
  0.0 678.4 jit_solution(2668626756270714189)
XLA Ops:
  11.8 12.1 %shard_map.391 = bf16[512,640]{1,0:T(8,128)(2,1)} custom-call(bf16[128,1536]{1,0:T(8,128)(2,1)S(1)} %copy-done.45, bf16[4,128,256]{2,1,0:T(8,128)(2,1)S(1)} %bitcast.100), custom_call_target="tpu_custom_call" | custom-call | bytes 70000000 | tf_op jit(solution)/shard_map/pallas_call | solution.py:224
  25.1 15.1 %shard_map.395 = bf16[512,1024]{1,0:T(8,128)(2,1)} custom-call(bf16[128,1536]{1,0:T(8,128)(2,1)S(1)} %copy-done.43, bf16[128,512]{1,0:T(8,128)(2,1)S(1)} %copy-done.46, bf16[128,1536]{1,0:T(8,128)(2,1)S(1)} %copy-done.44, bf16[128,512]{1,0:T(8,128)(2,1)S(1)} %copy-done.47), custom_call_target="tpu_custom_call" | custom-call | bytes 70000000 | tf_op jit(solution)/shard_map/pallas_call | solution.py:224
  42.0 39.3 %shard_map.390 = (bf16[512,768]{1,0:T(8,128)(2,1)}, bf16[512,768]{1,0:T(8,128)(2,1)}, bf16[1040,2048]{1,0:T(8,128)(2,1)}, s32[4,4,8,256]{3,2,1,0:T(8,128)S(1)}) custom-call(bf16[128,2048]{1,0:T(8,128)(2,1)S(1)} %copy-done.40, bf16[128,2048]{1,0:T(8,128)(2,1)S(1)} %copy-done.41, bf16[128,2048]{1,0:T(8,128)(2,1)S(1)} %copy-done.42, ...), custom_call_target="tpu_custom_call" | custom-call | bytes 140000000 | tf_op jit(solution)/shard_map/pallas_call | solution.py:224
  85.3 2.3 fusion.36
  88.0 1.9 multiply_sine_fusion
  91.3 6.6 fusion.40.pa_ref
  97.9 1.5 copy-done.85
  100.3 1.5 fusion.37
  102.8 2.9 fusion.38
  107.0 1.9 copy.149
  113.4 20.5 %shard_map.392 = (bf16[512,1024]{1,0:T(8,128)(2,1)S(1)}, bf16[4,64,1024]{2,1,0:T(8,128)(2,1)S(1)}) custom-call(bf16[64,1024]{1,0:T(8,128)(2,1)S(1)} %fusion.26.block, bf16[64,1024]{1,0:T(8,128)(2,1)S(1)} %maximum_bitcast_fusion.kv), custom_call_target="tpu_custom_call" | custom-call | bytes 70000000 | tf_op jit(solution)/shard_map/pallas_call | solution.py:224
  135.7 1.5 copy.130
  137.2 11.0 %shard_map.393 = (f32[1024,384]{1,0:T(8,128)S(1)}, f32[1024,384]{1,0:T(8,128)S(1)}, f32[8,384,256]{2,1,0:T(8,128)}, f32[8,16,128]{2,1,0:T(8,128)S(1)}, bf16[384,...) custom-call(s32[1]{0:T(128)} %bitcast.base_ref, f32[1040,640]{1,0:T(8,128)} %copy-done.85, bf16[1024,512]{1,0:T(8,128)(2,1)S(1)} %bitcast.96, ...), custom_call_target="tpu_custom_call" | custom-call | flops 2000000000 | bytes 40000000 | tf_op jit(solution)/shard_map/pallas_call | solution.py:1150
  150.6 49.2 %shard_map.394 = (bf16[3,384,256]{2,1,0:T(8,128)(2,1)S(1)}, f32[3,8,128]{2,1,0:T(8,128)S(1)}, bf16[16,64,1024]{2,1,0:T(8,128)(2,1)S(1)}, bf16[1024,2048]{1,0:T(8,128)(2,1)}) custom-call(bf16[384,256]{1,0:T(8,128)(2,1)S(1)} %get-tuple-element.116.state, f32[8,128]{1,0:T(8,128)S(1)} %get-tuple-element.117.factor, bf16[4,64,1024]{2,1,0:T(8,128)(2,1)S(1)} %copy-done.39, ...), custom_call_target="tpu_custom_call" | custom-call | bytes 133000000 | tf_op jit(solution)/shard_map/pallas_call | solution.py:224
  203.9 6.6 fusion.4.z_ref.q_ref
  210.5 9.3 %shard_map.396 = (bf16[1024,384]{1,0:T(8,128)(2,1)S(1)}, f32[1024,384]{1,0:T(8,128)S(1)}) custom-call(s32[1]{0:T(128)} %bitcast.base_ref, f32[1040,640]{1,0:T(8,128)} %copy-done.85, bf16[1024,512]{1,0:T(8,128)(2,1)S(1)} %bitcast.97, s32[1024,1]{1,0:T(8,128)S(1)} %copy.138.starts_ref, f32[1,128]{1,0:T(1,128)S(1)} %get-tuple-element.327.bias_ref, ...), custom_call_target="tpu_custom_call" | custom-call | flops 2000000000 | bytes 40000000 | tf_op jit(solution)/shard_map/pallas_call | solution.py:1150
  221.2 6.9 %shard_map.397 = (bf16[1024,128]{1,0:T(8,128)(2,1)S(1)}, bf16[1024,128]{1,0:T(8,128)(2,1)S(1)}, f32[1024,128]{1,0:T(8,128)S(1)}, f32[1024,1]{1,0:T(8,128)S(1)}) custom-call(s32[1]{0:T(128)} %bitcast.base_ref, s32[4]{0:T(128)S(1)} %slice_reduce_fusion.6.first_ref, f32[1024,512]{1,0:T(8,128)S(1)} %copy-done.8, s32[1024,1]{1,0:T(8,128)S(1)} %copy.138.starts_ref, ...), custom_call_target="tpu_custom_call" | custom-call | flops 2000000000 | bytes 40000000 | tf_op jit(solution)/shard_map/pallas_call | solution.py:1150
  228.2 4.4 convolution_convert_fusion.part
  232.6 48.1 %shard_map.398 = (f32[128,2048]{1,0:T(8,128)S(1)}, bf16[1024,2048]{1,0:T(8,128)(2,1)}) custom-call(bf16[1024,2048]{1,0:T(8,128)(2,1)} %convolution_convert_fusion.part, f32[128,2048]{1,0:T(8,128)S(1)} %get-tuple-element.297.x_ref, f32[1,2048]{1,0:T(1,128)S(1)} %bitcast.104), custom_call_target="tpu_custom_call" | custom-call | bytes 175000000 | tf_op jit(solution)/shard_map/pallas_call | solution.py:224
  281.7 1.9 copy-done.7
  283.6 6.3 shard_map.399.h_ref.h1_ref
  289.9 8.6 %shard_map.400 = bf16[2048,768]{1,0:T(8,128)(2,1)S(1)} custom-call(bf16[1024,2048]{1,0:T(8,128)(2,1)} %get-tuple-element.124.second_ref, bf16[1024,2048]{1,0:T(8,128)(2,1)} %get-tuple-element.125.low_ref, bf16[1024,768]{1,0:T(8,128)(2,1)S(1)} %shard_map.399.h_ref.h1_ref), custom_call_target="tpu_custom_call" | custom-call | flops 2000000000 | bytes 40000000 | tf_op jit(solution)/shard_map/pallas_call | solution.py:1150
  299.7 1.6 copy-done.6
  301.3 18.9 %all-gather.11.cloned.1.call-done.w2_ref = bf16[2048,768]{1,0:T(8,128)(2,1)} async-done(((bf16[512,768]{1,0:T(8,128)(2,1)}), bf16[2048,768]{1,0:T(8,128)(2,1)}) %all-gather.11.cloned.1.call-update) | async-done | bytes 3145744 | tf_op jit(solution)/shard_map/all_gather | solution.py:1255
  321.7 15.5 %shard_map.401 = (bf16[1024,768]{1,0:T(8,128)(2,1)S(1)}, bf16[1024,2048]{1,0:T(8,128)(2,1)}, bf16[1024,2048]{1,0:T(8,128)(2,1)}) custom-call(bf16[1024,2048]{1,0:T(8,128)(2,1)} %get-tuple-element.124.second_ref, bf16[1024,2048]{1,0:T(8,128)(2,1)} %get-tuple-element.125.low_ref, bf16[2048,768]{1,0:T(8,128)(2,1)} %all-gather.9.cloned.1.call-done.w_ref.w1_ref, ...), custom_call_target="tpu_custom_call" | custom-call | flops 2000000000 | bytes 40000000 | tf_op jit(solution)/shard_map/pallas_call | solution.py:1150
  337.2 49.2 %shard_map.402 = (f32[128,2048]{1,0:T(8,128)S(1)}, f32[8,2048]{1,0:T(8,128)S(1)}, bf16[1024,2048]{1,0:T(8,128)(2,1)}) custom-call(bf16[1024,2048]{1,0:T(8,128)(2,1)} %get-tuple-element.130.part, f32[128,2048]{1,0:T(8,128)S(1)} %copy-done.10, f32[128,2048]{1,0:T(8,128)S(1)} %copy-done.12, f32[1,2048]{1,0:T(1,128)S(1)} %bitcast.105), custom_call_target="tpu_custom_call" | custom-call | bytes 175000000 | tf_op jit(solution)/shard_map/pallas_call | solution.py:224
  387.4 8.2 %shard_map.407 = bf16[2048,768]{1,0:T(8,128)(2,1)S(1)} custom-call(bf16[1024,2048]{1,0:T(8,128)(2,1)} %get-tuple-element.124.second_ref, bf16[1024,2048]{1,0:T(8,128)(2,1)} %get-tuple-element.125.low_ref, bf16[1024,768]{1,0:T(8,128)(2,1)S(1)} %get-tuple-element.154.h_ref), custom_call_target="tpu_custom_call" | custom-call | flops 2000000000 | bytes 40000000 | tf_op jit(solution)/shard_map/pallas_call | solution.py:1150
  395.7 1.7 copy-done.5
  397.5 6.6 fusion.12.d_ref
  404.2 11.3 %shard_map.403 = (bf16[1024,384]{1,0:T(8,128)(2,1)S(1)}, f32[1024,384]{1,0:T(8,128)S(1)}, f32[8,384,256]{2,1,0:T(8,128)}, f32[8,8,128]{2,1,0:T(8,128)S(1)}, bf16...) custom-call(s32[1]{0:T(128)} %bitcast.base_ref, f32[1040,640]{1,0:T(8,128)} %copy-done.85, bf16[1024,512]{1,0:T(8,128)(2,1)S(1)} %bitcast.98, ...), custom_call_target="tpu_custom_call" | custom-call | flops 2000000000 | bytes 40000000 | tf_op jit(solution)/shard_map/pallas_call | solution.py:1150
  417.9 8.4 %shard_map.404 = (bf16[1024,128]{1,0:T(8,128)(2,1)S(1)}, bf16[4,4,64,1024]{3,2,1,0:T(8,128)(2,1)S(1)}) custom-call(s32[1]{0:T(128)} %bitcast.base_ref, s32[4]{0:T(128)S(1)} %copy-done.67, bf16[1024,128]{1,0:T(8,128)(2,1)S(1)} %copy-done.83, s32[1024,1]{1,0:T(8,128)S(1)} %copy.138.starts_ref, f32[1024,128]{1,0:T(8,128)S(1)} %copy-done.35, ...), custom_call_target="tpu_custom_call" | custom-call | flops 2000000000 | bytes 40000000 | tf_op jit(solution)/shard_map/pallas_call | solution.py:1150
  426.4 5.6 convolution_convert_fusion.1
  432.1 2.4 fusion.9
  434.6 2.7 pad_maximum_fusion
  438.5 53.8 %shard_map.405 = (bf16[3,384,256]{2,1,0:T(8,128)(2,1)S(1)}, f32[3,8,128]{2,1,0:T(8,128)S(1)}, bf16[4,4,64,1024]{3,2,1,0:T(8,128)(2,1)S(1)}, f32[128,2048]{1,0:T(8,128)S(1)}) custom-call(bf16[384,256]{1,0:T(8,128)(2,1)S(1)} %get-tuple-element.145.state, f32[8,128]{1,0:T(8,128)S(1)} %get-tuple-element.117.factor, bf16[4,4,64,1024]{3,2,1,0:T(8,128)(2,1)} %copy-done.14, ...), custom_call_target="tpu_custom_call" | custom-call | bytes 157500000 | tf_op jit(solution)/shard_map/pallas_call | solution.py:224
  499.5 1.6 fusion.17.after_ref
  501.1 19.7 %shard_map.406 = (f32[1024,384]{1,0:T(8,128)S(1)}, bf16[512,1024]{1,0:T(8,128)(2,1)S(1)}, bf16[1024,128]{1,0:T(8,128)(2,1)S(1)}, f32[8,128]{1,0:T(8,128)S(1)}, f32[8,384]{1,0:T(8,128)S(1)}) custom-call(s32[1]{0:T(128)} %bitcast.base_ref, f32[1040,640]{1,0:T(8,128)} %copy-done.85, bf16[1024,512]{1,0:T(8,128)(2,1)S(1)} %bitcast.99, ...), custom_call_target="tpu_custom_call" | custom-call | flops 2000000000 | bytes 40000000 | tf_op jit(solution)/shard_map/pallas_call | solution.py:1150
  527.9 30.6 %shard_map.408 = (f32[64,1024]{1,0:T(8,128)S(1)}, f32[64,128]{1,0:T(8,128)S(1)}, f32[16,384]{1,0:T(8,128)S(1)}, f32[64,1024]{1,0:T(8,128)S(1)}, bf16[4,128,768]{...) custom-call(bf16[512,1024]{1,0:T(8,128)(2,1)S(1)} %copy-done.26, bf16[4,4,64,1024]{3,2,1,0:T(8,128)(2,1)} %copy-done.13, ...), custom_call_target="tpu_custom_call" | custom-call | bytes 105000000 | tf_op jit(solution)/shard_map/pallas_call | solution.py:224
  560.5 6.7 shard_map.409
  568.3 7.3 %fusion.6 = bf16[2048,640]{1,0:T(8,128)(2,1)} fusion(bf16[1024,640]{1,0:T(8,128)(2,1)S(1)} %get-tuple-element.164, bf16[1040,2048]{1,0:T(8,128)(2,1)} %get-tuple-element.109), kind=kOutput, calls=%fused_computation.9 | convolution fusion | flops 2685665280 | bytes 8126464 | tf_op jit(solution)/shard_map/dot_general | solution.py:1163
  575.5 5.4 reduce-scatter.9.cloned.1.call-done.sum_zb
  582.9 5.7 fusion.41
  588.7 4.4 add_convert_fusion.part
  593.1 36.7 %shard_map.410 = (f32[256,2048]{1,0:T(8,128)}, f32[256,2048]{1,0:T(8,128)}, f32[16,512]{1,0:T(8,128)S(1)}, bf16[4,128,1024]{2,1,0:T(8,128)(2,1)S(1)}) custom-call(bf16[1024,2048]{1,0:T(8,128)(2,1)} %add_convert_fusion.part, f32[128,2048]{1,0:T(8,128)S(1)} %get-tuple-element.297.x_ref, f32[128,2048]{1,0:T(8,128)S(1)} %copy-done.21, ...), custom_call_target="tpu_custom_call" | custom-call | bytes 140000000 | tf_op jit(solution)/shard_map/pallas_call | solution.py:224
  629.9 7.5 %reduce-scatter.11.cloned.1.call-done.sum_a = bf16[512,640]{1,0:T(8,128)(2,1)} async-done(((bf16[2048,640]{1,0:T(8,128)(2,1)}), bf16[512,640]{1,0:T(8,128)(2,1)}) %reduce-scatter.11.cloned.1.call-update) | async-done | bytes 655376 | tf_op jit(solution)/shard_map/reduce_scatter | solution.py:1291
  638.4 17.7 %shard_map.411 = (bf16[4,128,384]{2,1,0:T(8,128)(2,1)S(1)}, bf16[8,128,256]{2,1,0:T(8,128)(2,1)S(1)}, f32[128,512]{1,0:T(8,128)S(1)}) custom-call(bf16[512,640]{1,0:T(8,128)(2,1)S(1)} %copy-done.30, f32[16,512]{1,0:T(8,128)S(1)} %get-tuple-element.177.small), custom_call_target="tpu_custom_call" | custom-call | bytes 70000000 | tf_op jit(solution)/shard_map/pallas_call | solution.py:224
  662.7 3.5 shard_map.412
  666.9 3.2 copy.160
  (342 shorter events, 66.8 us)
Async XLA Ops:
  7.2 16.9 %copy-start.44 = (bf16[128,1536]{1,0:T(8,128)(2,1)S(1)}, bf16[128,1536]{1,0:T(8,128)(2,1)}, u32[]{:S(2)}) copy-start(bf16[128,1536]{1,0:T(8,128)(2,1)} %out_ref.1) | copy-start | bytes 1179652
  7.2 16.9 %copy-start.46 = (bf16[128,512]{1,0:T(8,128)(2,1)S(1)}, bf16[128,512]{1,0:T(8,128)(2,1)}, u32[]{:S(2)}) copy-start(bf16[128,512]{1,0:T(8,128)(2,1)} %q_ref.1) | copy-start | bytes 393220
  7.2 16.9 %copy-start.43 = (bf16[128,1536]{1,0:T(8,128)(2,1)S(1)}, bf16[128,1536]{1,0:T(8,128)(2,1)}, u32[]{:S(2)}) copy-start(bf16[128,1536]{1,0:T(8,128)(2,1)} %z_ref.1) | copy-start | bytes 1179652
  7.2 84.0 %all-gather.5.cloned.1.call-start = ((), (), s32[]{:S(2)}) async-start(), calls=%async_computation.4 | async-start | bytes 3276800 | tf_op jit(solution)/shard_map/all_gather | solution.py:1255
  24.0 17.8 %copy-start.51 = (f32[2048]{0:T(1024)S(1)}, f32[2048]{0:T(1024)}, u32[]{:S(2)}) copy-start(f32[2048]{0:T(1024)} %param.25) | copy-start | bytes 24580
  24.0 18.0 %copy-start.40 = (bf16[128,2048]{1,0:T(8,128)(2,1)S(1)}, bf16[128,2048]{1,0:T(8,128)(2,1)}, u32[]{:S(2)}) copy-start(bf16[128,2048]{1,0:T(8,128)(2,1)} %gate_w.1) | copy-start | bytes 1572868
  24.0 18.0 %copy-start.41 = (bf16[128,2048]{1,0:T(8,128)(2,1)S(1)}, bf16[128,2048]{1,0:T(8,128)(2,1)}, u32[]{:S(2)}) copy-start(bf16[128,2048]{1,0:T(8,128)(2,1)} %up_w.1) | copy-start | bytes 1572868
  24.0 18.0 %copy-start.42 = (bf16[128,2048]{1,0:T(8,128)(2,1)S(1)}, bf16[128,2048]{1,0:T(8,128)(2,1)}, u32[]{:S(2)}) copy-start(bf16[128,2048]{1,0:T(8,128)(2,1)} %down_w.1) | copy-start | bytes 1572868
  24.0 179.8 %all-gather.7.cloned.1.call-start = ((), (), s32[]{:S(2)}) async-start(), calls=%async_computation.5 | async-start | bytes 5242880 | tf_op jit(solution)/shard_map/all_gather | solution.py:1255
  25.1 16.9 %copy-start.100 = (s32[256]{0:T(256)S(1)}, s32[256]{0:T(256)}, u32[]{:S(2)}) copy-start(s32[256]{0:T(256)} %param.24) | copy-start | bytes 3076
  40.3 241.4 %all-gather.9.cloned.1.call-start = ((), (), s32[]{:S(2)}) async-start(), calls=%async_computation.6 | async-start | bytes 3932160 | tf_op jit(solution)/shard_map/all_gather | solution.py:1255
  41.7 40.4 %copy-start.103 = (f32[24]{0:T(128)S(1)}, f32[24]{0:T(128)}, u32[]{:S(2)}) copy-start(f32[24]{0:T(128)} %param.41) | copy-start | bytes 292
  41.8 40.5 %copy-start.104 = (f32[24]{0:T(128)S(1)}, f32[24]{0:T(128)}, u32[]{:S(2)}) copy-start(f32[24]{0:T(128)} %param.42) | copy-start | bytes 292
  41.8 40.6 %copy-start.105 = (f32[24]{0:T(128)S(1)}, f32[24]{0:T(128)}, u32[]{:S(2)}) copy-start(f32[24]{0:T(128)} %param.43) | copy-start | bytes 292
  81.4 238.9 %all-gather.11.cloned.1.call-start = ((), (), s32[]{:S(2)}) async-start(), calls=%async_computation.7 | async-start | bytes 3932160 | tf_op jit(solution)/shard_map/all_gather | solution.py:1255
  82.0 355.4 %reduce-scatter.5.cloned.1.call-start = ((), (), s32[]{:S(2)}) async-start(), calls=%async_computation.8 | async-start | bytes 3932160 | tf_op jit(solution)/shard_map/reduce_scatter | solution.py:1291
  82.1 9.2 %copy-start.91 = (s32[4,4,1,256]{3,2,1,0:T(1,128)}, s32[4,4,1,256]{3,2,1,0:T(1,128)S(1)}, u32[]{:S(2)}) copy-start(s32[4,4,1,256]{3,2,1,0:T(1,128)S(1)} %slice.141) | copy-start | bytes 49156
  82.1 27.9 %copy-start.93 = (f32[1024]{0:T(1024)}, f32[1024]{0:T(1024)S(1)}, u32[]{:S(2)}) copy-start(f32[1024]{0:T(1024)S(1)} %get-tuple-element.294) | copy-start | bytes 12292
  82.2 27.8 %copy-start.97 = (f32[16]{0:T(128)}, f32[16]{0:T(128)S(1)}, u32[]{:S(2)}) copy-start(f32[16]{0:T(128)S(1)} %multiply_power_fusion.1) | copy-start | bytes 196
  83.2 127.3 %copy-start.54 = (f32[1,384]{1,0:T(1,128)}, f32[1,384]{1,0:T(1,128)S(1)}, u32[]{:S(2)}) copy-start(f32[1,384]{1,0:T(1,128)S(1)} %broadcast_in_dim.136.gain_ref) | copy-start | bytes 4612
  83.9 7.3 %copy-start.95 = (f32[4,64]{1,0:T(4,128)}, f32[4,64]{1,0:T(4,128)S(1)}, u32[]{:S(2)}) copy-start(f32[4,64]{1,0:T(4,128)S(1)} %constant_dynamic-slice_fusion.4) | copy-start | bytes 3076
  85.3 51.9 %copy-start.52 = (f32[4,384]{1,0:T(4,128)}, f32[4,384]{1,0:T(4,128)S(1)}, u32[]{:S(2)}) copy-start(f32[4,384]{1,0:T(4,128)S(1)} %constant_dynamic-slice_fusion.3.taps_ref) | copy-start | bytes 18436
  87.8 133.4 %copy-start.66 = (s32[4]{0:T(128)}, s32[4]{0:T(128)S(1)}, u32[]{:S(2)}) copy-start(s32[4]{0:T(128)S(1)} %slice_reduce_fusion.6.first_ref) | copy-start | bytes 52
  88.0 122.5 %copy-start.58 = (f32[1,128]{1,0:T(1,128)}, f32[1,128]{1,0:T(1,128)S(1)}, u32[]{:S(2)}) copy-start(f32[1,128]{1,0:T(1,128)S(1)} %get-tuple-element.326.rates_ref) | copy-start | bytes 1540
  88.0 122.5 %copy-start.61 = (f32[1,128]{1,0:T(1,128)}, f32[1,128]{1,0:T(1,128)S(1)}, u32[]{:S(2)}) copy-start(f32[1,128]{1,0:T(1,128)S(1)} %get-tuple-element.327.bias_ref) | copy-start | bytes 1540
  102.8 9.2 %copy-start.99 = (f32[64]{0:T(128)S(1)}, f32[64]{0:T(128)}, u32[]{:S(2)}) copy-start(f32[64]{0:T(128)} %get-tuple-element.323) | copy-start | bytes 772
  137.2 13.3 %copy-start.39 = (bf16[4,64,1024]{2,1,0:T(8,128)(2,1)S(1)}, bf16[4,64,1024]{2,1,0:T(8,128)(2,1)}, u32[]{:S(2)}) copy-start(bf16[4,64,1024]{2,1,0:T(8,128)(2,1)} %copy-done.38) | copy-start | bytes 1572868
  210.5 10.6 %copy-start.8 = (f32[1024,512]{1,0:T(8,128)S(1)}, f32[1024,512]{1,0:T(8,128)}, u32[]{:S(2)}) copy-start(f32[1024,512]{1,0:T(8,128)} %fusion.4.z_ref.q_ref) | copy-start | bytes 6291460
  210.5 10.6 %copy-start.34 = (f32[1024,128]{1,0:T(8,128)S(1)}, f32[1024,128]{1,0:T(8,128)}, u32[]{:S(2)}) copy-start(f32[1024,128]{1,0:T(8,128)} %get-tuple-element.328.cos_ref) | copy-start | bytes 1572868
  210.5 10.6 %copy-start.36 = (f32[1024,128]{1,0:T(8,128)S(1)}, f32[1024,128]{1,0:T(8,128)}, u32[]{:S(2)}) copy-start(f32[1024,128]{1,0:T(8,128)} %get-tuple-element.329.sin_ref) | copy-start | bytes 1572868
  221.2 7.0 %copy-start.101 = (bf16[2048,1024]{1,0:T(8,128)(2,1)S(1)}, bf16[2048,1024]{1,0:T(8,128)(2,1)}, u32[]{:S(2)}) copy-start(bf16[2048,1024]{1,0:T(8,128)(2,1)} %all-gather.7.cloned.1.call-done) | copy-start | bytes 12582916
  320.3 203.4 %reduce-scatter.7.cloned.1.call-start = ((), (), s32[]{:S(2)}) async-start(), calls=%async_computation.9 | async-start | bytes 3932160 | tf_op jit(solution)/shard_map/reduce_scatter | solution.py:1291
  321.7 15.5 %copy-start.10 = (f32[128,2048]{1,0:T(8,128)S(1)}, f32[128,2048]{1,0:T(8,128)}, u32[]{:S(2)}) copy-start(f32[128,2048]{1,0:T(8,128)} %copy-done.9) | copy-start | bytes 3145732
  321.7 15.5 %copy-start.12 = (f32[128,2048]{1,0:T(8,128)S(1)}, f32[128,2048]{1,0:T(8,128)}, u32[]{:S(2)}) copy-start(f32[128,2048]{1,0:T(8,128)} %get-tuple-element.293.cot) | copy-start | bytes 3145732
  387.4 8.3 %copy-start.65 = (f32[8,2048]{1,0:T(8,128)}, f32[8,2048]{1,0:T(8,128)S(1)}, u32[]{:S(2)}) copy-start(f32[8,2048]{1,0:T(8,128)S(1)} %get-tuple-element.171) | copy-start | bytes 196612
  397.4 183.5 %reduce-scatter.9.cloned.1.call-start = ((), (), s32[]{:S(2)}) async-start(), calls=%async_computation.10 | async-start | bytes 5242880 | tf_op jit(solution)/shard_map/reduce_scatter | solution.py:1291
  404.1 13.7 %copy-start.35 = (f32[1024,128]{1,0:T(8,128)S(1)}, f32[1024,128]{1,0:T(8,128)}, u32[]{:S(2)}) copy-start(f32[1024,128]{1,0:T(8,128)} %get-tuple-element.328.cos_ref) | copy-start | bytes 1572868
  404.1 13.7 %copy-start.37 = (f32[1024,128]{1,0:T(8,128)S(1)}, f32[1024,128]{1,0:T(8,128)}, u32[]{:S(2)}) copy-start(f32[1024,128]{1,0:T(8,128)} %get-tuple-element.329.sin_ref) | copy-start | bytes 1572868
  404.1 13.7 %copy-start.67 = (s32[4]{0:T(128)S(1)}, s32[4]{0:T(128)}, u32[]{:S(2)}) copy-start(s32[4]{0:T(128)} %copy-done.66) | copy-start | bytes 52
  404.2 13.7 %copy-start.79 = (f32[1024,128]{1,0:T(8,128)S(1)}, f32[1024,128]{1,0:T(8,128)}, u32[]{:S(2)}) copy-start(f32[1024,128]{1,0:T(8,128)} %copy-done.78) | copy-start | bytes 1572868
  404.2 13.7 %copy-start.81 = (f32[1024,1]{1,0:T(8,128)S(1)}, f32[1024,1]{1,0:T(8,128)}, u32[]{:S(2)}) copy-start(f32[1024,1]{1,0:T(8,128)} %copy-done.80) | copy-start | bytes 12292
  404.2 13.7 %copy-start.83 = (bf16[1024,128]{1,0:T(8,128)(2,1)S(1)}, bf16[1024,128]{1,0:T(8,128)(2,1)}, u32[]{:S(2)}) copy-start(bf16[1024,128]{1,0:T(8,128)(2,1)} %copy-done.82) | copy-start | bytes 786436
  417.9 8.5 %copy-start.90 = (bf16[1024,512]{1,0:T(8,128)(2,1)S(1)}, bf16[1024,512]{1,0:T(8,128)(2,1)}, u32[]{:S(2)}) copy-start(bf16[1024,512]{1,0:T(8,128)(2,1)} %copy-done.89) | copy-start | bytes 3145732
  417.9 14.2 %slice-start = ((s8[4259840]{0:T(1024)(128)(4,1)}), s8[4194304]{0:T(1024)(128)(4,1)S(1)}, s32[]{:S(2)}) async-start(s8[4259840]{0:T(1024)(128)(4,1)} %bitcast.120), calls=%async_computation.12 | async-start | bytes 8388608
  496.2 141.2 %reduce-scatter.11.cloned.1.call-start = ((), (), s32[]{:S(2)}) async-start(), calls=%async_computation.11 | async-start | bytes 3276800 | tf_op jit(solution)/shard_map/reduce_scatter | solution.py:1291
  523.7 35.8 %copy-start.64 = (f32[4,512]{1,0:T(4,128)S(1)}, f32[4,512]{1,0:T(4,128)}, u32[]{:S(2)}) copy-start(f32[4,512]{1,0:T(4,128)} %maximum_maximum_fusion.taps_ref) | copy-start | bytes 24580
  527.9 31.5 %copy-start.69 = (f32[1024,384]{1,0:T(8,128)S(1)}, f32[1024,384]{1,0:T(8,128)}, u32[]{:S(2)}) copy-start(f32[1024,384]{1,0:T(8,128)} %copy-done.68) | copy-start | bytes 4718596
  527.9 31.5 %copy-start.77 = (bf16[1024,128]{1,0:T(8,128)(2,1)S(1)}, bf16[1024,128]{1,0:T(8,128)(2,1)}, u32[]{:S(2)}) copy-start(bf16[1024,128]{1,0:T(8,128)(2,1)} %copy-done.76) | copy-start | bytes 786436
  (68 other events, 180.6 us)
Sparse Core Ops, SparseCore 0:
  24.1 60.1 all-gather.4
  85.9 91.8 all-gather.6
  179.3 77.2 all-gather.8
  258.0 62.2 all-gather.10
  322.4 58.8 reduce-scatter.4
  397.5 59.7 reduce-scatter.6
  496.3 84.5 reduce-scatter.8
  583.3 53.9 reduce-scatter.10

commit v5 on v4

--- a/solution.py
+++ b/solution.py
@@ -123,21 +123,21 @@
 
 class Collect:
     @staticmethod
-    def scratch(rows, width):
+    def scratch(rows, width, cores=True):
         return [
-            pltpu.VMEM((4, rows, width), bf16), pltpu.VMEM((3, rows, width), bf16),
+            pltpu.VMEM((4, rows, width) if cores else (1, 16, 128), bf16), pltpu.VMEM((3, rows, width), bf16),
             pltpu.VMEM((2, rows // 2, width), bf16), pltpu.VMEM((2, rows, width), bf16),
             pltpu.VMEM((rows, width), f32), DMA((4,)), DMA((4,)), DMA((6,)), DMA((6,)),
         ]
 
-    def __init__(self, part, rows, scratch, strip=16):
-        self.part, self.rows, self.strip = part, rows, strip
+    def __init__(self, part, rows, scratch, strip=16, cores=True):
+        self.part, self.rows, self.strip, self.cores = part, rows, strip, cores
         self.cx, self.out, self.rd, self.rx, self.total, self.s1, self.r1, self.s2, self.r2 = scratch
         _, self.p, self.c = here()
         self.around = beside(self.p)
 
     def first(self, q, c):
-        return pl.multiple_of((q * 2 + c) * self.rows, 16)
+        return pl.multiple_of(((q * 2 + c) if self.cores else q) * self.rows, 16)
 
     def owner(self, i):
         return self.p if i == 3 else self.around[i]
@@ -170,7 +170,9 @@
         size = self.rows // 2
 
         def one(at):
-            v = self.part[self.at(first + at)].astype(f32) + self.cx[i, self.at(at)].astype(f32)
+            v = self.part[self.at(first + at)].astype(f32)
+            if self.cores:
+                v = v + self.cx[i, self.at(at)].astype(f32)
             if relayed is not None:
                 v = v + self.rd[relayed, self.at(at - half * size)].astype(f32)
             if i == 3:
@@ -184,25 +186,36 @@
             self.strips(one, half * size, (half + 1) * size)
 
     def start(self):
-        for i in (2, 0, 1, 3):
-            self.across(i).start()
-
-    def middle(self):
-        self.across(2).wait_recv()
+        if self.cores:
+            for i in (2, 0, 1, 3):
+                self.across(i).start()
+
+    def crossed(self, i):
+        if self.cores:
+            self.across(i).wait_recv()
+
+    def begin(self):
+        self.crossed(2)
         for half in (0, 1):
             self.add(2, half)
             self.over(2, half).start()
         for i in (0, 1):
-            self.across(i).wait_recv()
+            self.crossed(i)
             self.add(i, i)
             self.over(i, i).start()
-        self.across(3).wait_recv()
+        self.crossed(3)
         self.add(3)
+
+    def relay(self):
         for i in (0, 1):
             self.over(2, 1 - i).wait_recv()
             self.add(i, 1 - i, 1 - i)
             self.over(i, 1 - i).start()
 
+    def middle(self):
+        self.begin()
+        self.relay()
+
     def arrive(self):
         for half in (0, 1):
             for i in (0, 1):
@@ -213,14 +226,15 @@
         return self.total[r] + self.rx[0, r].astype(f32) + self.rx[1, r].astype(f32)
 
     def finish(self):
-        for i in range(4):
-            self.across(i).wait_send()
+        if self.cores:
+            for i in range(4):
+                self.across(i).wait_send()
         for i in range(3):
             for half in (0, 1):
                 self.over(i, half).wait_send()
 
 
-def call(body, name_id, outs, out_specs, ins, in_specs, scratch, us=20):
+def call(body, name_id, outs, out_specs, ins, in_specs, scratch, us=20, mib=12):
     return pl.pallas_call(
         body,
         out_shape=outs,
@@ -229,7 +243,7 @@
         scratch_shapes=scratch,
         cost_estimate=pl.CostEstimate(flops=0, bytes_accessed=us * 3_500_000, transcendentals=0),
         compiler_params=pltpu.CompilerParams(
-            collective_id=name_id, has_side_effects=True, vmem_limit_bytes=48 * 2**20
+            collective_id=name_id, has_side_effects=True, vmem_limit_bytes=mib * 2**20
         ),
     )(*ins)
 
@@ -281,50 +295,41 @@
         copy.wait()
 
 
-def start_body(planes, gate_w, up_w, down_w, first, docs, w1, w2, n1, all_docs, *sems):
+def start_body(planes, first, docs, steps, n1, all_docs, all_steps, *sems):
     z, p, c = here()
     greet(*plane_partners(p, c), *line_partners(z, planes))
-    send, recv, keep, rim_s, rim_r, ps, pr, zs, zr, dk = sems[:10]
+    rim_s, rim_r, ps, pr, zs, zr, dk = sems[:7]
     rows = first.shape[0]
-    a = Spread(first, n1, lambda q, k: pl.multiple_of(RIM + (q * 2 + k) * rows, 16), rows, sems[10:17])
-    units = gate_w.shape[1] // G
-    part = units // 2
-    pieces = [
-        (ref, part, to, i * part, False, units, k * part)
-        for k, to in enumerate((w1, w2)) for i, ref in enumerate((gate_w, up_w, down_w))
+    a = Spread(first, n1, lambda q, k: pl.multiple_of(RIM + (q * 2 + k) * rows, 16), rows, sems[7:])
+    near = [
+        rcopy(have(ring(p, d)), every.at[z, p], ps.at[i, d - 1], pr.at[i, d - 1], p=ring(p, d))
+        for i, (have, every) in enumerate(((lambda q: docs, all_docs), (lambda q: steps.at[q], all_steps))) for d in (1, 2, 3)
     ]
-    away, own = exchange_copies(pieces, (send, recv), keep)
-    near = [rcopy(docs, all_docs.at[z, p], ps.at[d - 1], pr.at[d - 1], p=ring(p, d)) for d in (1, 2, 3)]
-    own_docs = pltpu.make_async_copy(docs, all_docs.at[z, p], dk)
+    own = [
+        pltpu.make_async_copy(docs, all_docs.at[z, p], dk.at[0]), pltpu.make_async_copy(steps.at[p], all_steps.at[z, p], dk.at[1])
+    ]
     a.start()
-    for copy in near:
+    for copy in near + own:
         copy.start()
-    own_docs.start()
-    for copy in own:
+    for copy in own + near:
+        copy.wait()
+    far = [
+        rcopy(every.at[z], every.at[z], zs.at[i, d - 1], zr.at[i, d - 1], z=lax.rem(z + d, planes))
+        for i, every in enumerate((all_docs, all_steps)) for d in range(1, planes)
+    ]
+    for copy in far:
         copy.start()
     a.pass_on()
-    for copy in away:
-        copy.start()
     a.finish()
     last = n1.at[pl.ds(n1.shape[0] - RIM, RIM)]
     rim = rcopy(last, n1.at[pl.ds(0, RIM)], rim_s, rim_r, z=lax.rem(z + 1, planes))
     rim.start()
-    own_docs.wait()
-    for copy in near:
-        copy.wait()
-    far = [
-        rcopy(all_docs.at[z], all_docs.at[z], zs.at[d - 1], zr.at[d - 1], z=lax.rem(z + d, planes)) for d in range(1, planes)
-    ]
     for copy in far:
-        copy.start()
-    for copy in own + away:
         copy.wait()
     rim.wait()
-    for copy in far:
-        copy.wait()
-
-
-def spread_body(planes, block, kv, out, lines, zs, zr, zk, *sems):
+
+
+def spread_body(planes, block, kv, gate_w, up_w, down_w, out, lines, w1, w2, zs, zr, zk, send, recv, hold, *sems):
     z, p, c = here()
     greet(*plane_partners(p, c), *line_partners(z, planes))
     rows = block.shape[0]
@@ -334,9 +339,20 @@
         copy.start()
     keep.start()
     s = Spread(block, out, lambda q, k: pl.multiple_of((k * G + q) * rows, 16), rows, sems)
+    units = gate_w.shape[1] // G
+    pieces = [
+        (ref, part, to, i * part, False, units, skip)
+        for to, part, skip in ((w1, w1.shape[1] // 3, 0), (w2, w2.shape[1] // 3, w1.shape[1] // 3))
+        for i, ref in enumerate((gate_w, up_w, down_w))
+    ]
+    away, own = exchange_copies(pieces, (send, recv), hold)
     s.start()
+    for copy in away + own:
+        copy.start()
     s.pass_on()
     s.finish()
+    for copy in own + away:
+        copy.wait()
     keep.wait()
     for copy in far:
         copy.wait()
@@ -398,24 +414,26 @@
     greet(*plane_partners(p, c), *line_partners(z, planes))
     start, wait = state_copies(planes, False, state, factor, states, factors, sems[:4])
     start()
-    ks, kr, kk = sems[4:7]
-    s = Collect(part, hidden.shape[0], sems[7:])
+    k = Collect(dkv, kv.shape[0], sems[4:13], cores=False)
+    s = Collect(part, hidden.shape[0], sems[13:])
     s.start()
-    over = [rcopy(dkv.at[ring(p, d)], kv.at[d], ks.at[d - 1], kr.at[d - 1], p=ring(p, d)) for d in (1, 2, 3)]
-    keep = pltpu.make_async_copy(dkv.at[p], kv.at[0], kk)
-    for copy in over:
-        copy.start()
-    keep.start()
-    s.middle()
+    k.begin()
+    s.begin()
+    k.relay()
+    s.relay()
+    k.arrive()
+
+    def sum_kv(at):
+        kv[k.at(at)] = k.sum_of(at).astype(bf16)
+
+    k.strips(sum_kv)
     s.arrive()
 
     def one(at):
         layer[s.at(at)] = hidden[s.at(at)] + s.sum_of(at)
 
     s.strips(one)
-    keep.wait()
-    for copy in over:
-        copy.wait()
+    k.finish()
     s.finish()
     wait()
 
@@ -475,14 +493,14 @@
     g.finish()
 
 
-def final_body(part, x_ref, d_hidden, layer, gain, small, sum_zb, grad_in, layer_out, mine, got_zb, *scratch):
+def final_body(part, x_ref, d_hidden, layer, gain, taps, norm, rows_ref, ffn, sum_z, sum_b, grad_in, layer_out, mine, got_z, got_b, *scratch):
     z, p, c = here()
     greet(*plane_partners(p, c))
     rows = x_ref.shape[0]
     s = Collect(part, rows, scratch[:9])
     stage, gain_row, es, er, ek, zs, zr, zk = scratch[9:]
     half = pl.ds(pl.multiple_of(c * rows, 16), rows)
-    wide = got_zb.shape[1]
+    wide = got_z.shape[1]
 
     def halves(i, source, target):
         return (
@@ -490,18 +508,29 @@
             pltpu.make_async_copy(source, target.at[half], ek.at[i]),
         )
 
-    def zb_of(q):
-        return sum_zb.at[pl.ds(pl.multiple_of(q * wide, 16), wide)]
+    def rows_of(v, q):
+        cols = got_z.shape[2]
+        return v.at[pl.ds(pl.multiple_of(q * wide, 16), wide), pl.ds(v.shape[1] - cols, cols)]
 
     s.start()
     first = halves(0, layer, layer_out)
     for copy in first:
         copy.start()
-    mine[...] = small[...]
+    lane = mine.shape[1]
+    mine[...] = jnp.zeros_like(mine)
+    mine[:K, : taps.shape[1]] = taps[:K]
+    mine[4:5, : norm.shape[1]] = norm[:1]
+    for j in range(3):
+        mine[5:6, j * 128 : (j + 1) * 128] = rows_ref[j : j + 1]
+    for j in range(4):
+        mine[8 + j : 9 + j] = ffn[:1, j * lane : (j + 1) * lane]
     gain_row[...] = jnp.zeros_like(gain_row)
     s.middle()
-    zb = [rcopy(zb_of(ring(p, d)), got_zb.at[p], zs.at[d - 1], zr.at[d - 1], p=ring(p, d)) for d in (1, 2, 3)]
-    zb.append(pltpu.make_async_copy(zb_of(p), got_zb.at[p], zk))
+    zb = []
+    for i, (have, got) in enumerate(((sum_z, got_z), (sum_b, got_b))):
+        for d in (1, 2, 3):
+            zb.append(rcopy(rows_of(have, ring(p, d)), got.at[p], zs.at[i, d - 1], zr.at[i, d - 1], p=ring(p, d)))
+        zb.append(pltpu.make_async_copy(rows_of(have, p), got.at[p], zk.at[i]))
     for copy in zb:
         copy.start()
     s.arrive()
@@ -519,7 +548,6 @@
     second = halves(1, stage, grad_in)
     for copy in second:
         copy.start()
-    lane = mine.shape[1]
     for j in range(4):
         mine[12 + j : 13 + j] = gain_row[:1, j * lane : (j + 1) * lane]
     s.finish()
@@ -532,25 +560,16 @@
 def back_body(planes, dbc, dkv, d_silu_bc, gx, sum_1, sum_2, g_bc, rim_bc, rim_x, kv_out, got_1, got_2, *scratch):
     z, p, c = here()
     greet(*plane_partners(p, c), *line_partners(z, planes))
-    (cx, bx, rbc, skv, zkv, acc, xs, xr, bs, br, zs, zr, ms, mr, ws, wr, wk) = scratch
+    (cx, bx, rbc, zkv, acc, xs, xr, bs, br, zs, zr, ms, mr, ws, wr, wk) = scratch
     rows = rbc.shape[1]
     across = rcopy(
         dbc.at[pl.ds(pl.multiple_of((1 - c) * G * rows, 16), G * rows)], cx, xs, xr, head=1 - c
     )
     across.start()
 
-    def add_kv(i, carry):
-        v = dkv[0, i].astype(f32)
-        for d in (1, 2, 3):
-            v = v + dkv[d, i].astype(f32)
-        skv[i] = v.astype(bf16)
-        return carry
-
-    lax.fori_loop(0, planes, add_kv, 0)
-
     def kv_down(d):
         to = lax.rem(z - d + planes, planes)
-        return rcopy(skv.at[to], zkv.at[d - 1], zs.at[d - 1], zr.at[d - 1], z=to)
+        return rcopy(dkv.at[to], zkv.at[d - 1], zs.at[d - 1], zr.at[d - 1], z=to)
 
     for d in range(1, planes):
         @pl.when(z - d >= 0)
@@ -566,10 +585,10 @@
         return pl.ds(pl.multiple_of(q * wide, 16), wide)
 
     w_over = [
-        rcopy(have.at[rows_of(ring(p, d))], got.at[p], ws.at[i, d - 1], wr.at[i, d - 1], p=ring(p, d))
+        rcopy(have.at[rows_of(ring(p, d)), pl.ds(0, got.shape[2])], got.at[p], ws.at[i, d - 1], wr.at[i, d - 1], p=ring(p, d))
         for i, (have, got) in grads for d in (1, 2, 3)
     ]
-    w_own = [pltpu.make_async_copy(have.at[rows_of(p)], got.at[p], wk.at[i]) for i, (have, got) in grads]
+    w_own = [pltpu.make_async_copy(have.at[rows_of(p), pl.ds(0, got.shape[2])], got.at[p], wk.at[i]) for i, (have, got) in grads]
     for d in (1, 2, 3, 0):
         q = ring(p, d)
         own = dbc[pl.ds(pl.multiple_of((c * G + q) * rows, 16), rows)].astype(f32)
@@ -591,11 +610,11 @@
     before = lax.rem(z - 1 + planes, planes)
     rims = [
         rcopy(g_bc.at[:, pl.ds(0, 128)], rim_bc, ms.at[0], mr.at[0], z=before),
-        rcopy(gx, rim_x, ms.at[1], mr.at[1], z=before),
+        rcopy(gx.at[pl.ds(0, RIM)], rim_x, ms.at[1], mr.at[1], z=before),
     ]
     for copy in rims:
         copy.start()
-    kv_out[...] = skv[z].astype(f32)
+    kv_out[...] = dkv[z].astype(f32)
     for d in range(1, planes):
         @pl.when(z + d < planes)
         def _():
@@ -615,7 +634,8 @@
         copy.wait()
 
 
-def last_body(planes, sum_a, small, got_x, got_s, sums, mine, others, xs, xr, ss, sr, keep, ls, lr, *spread):
+def last_body(planes, sum_a, small, steps, got_x, got_s, sums, got_t, mine, others, t_own, t_far, xs, xr, ss, sr, keep, ls, lr,
+              ts, tr, qs, qr, tk, *spread):
     z, p, c = here()
     pairs = [(d, k) for k in (0, 1) for d in range(G) if d or k]
     greet(*[{"p": ring(p, d), "head": lax.rem(c + k, 2)} for d, k in pairs], *line_partners(z, planes))
@@ -625,13 +645,15 @@
         return sum_a.at[pl.ds(pl.multiple_of(q * rows, 16), rows), pl.ds(first, cols)]
 
     def narrow(d, k):
-        cols = 128 if k else got_s.shape[2]
-        to = got_s.at[c * G + p, :, pl.ds(0, cols)]
+        cols, to = got_s.shape[2], got_s.at[c * G + p]
         i = k * G + d - 1
         return rcopy(part(ring(p, d), chan, cols), to, ss.at[i], sr.at[i], p=ring(p, d), head=lax.rem(c + k, 2))
 
     lines = [
         rcopy(small, others.at[d - 1], ls.at[d - 1], lr.at[d - 1], z=lax.rem(z + d, planes)) for d in range(1, planes)
+    ] + [
+        rcopy(steps.at[lax.rem(z + d, planes)], t_far.at[d - 1], ts.at[d - 1], tr.at[d - 1], z=lax.rem(z + d, planes))
+        for d in range(1, planes)
     ]
     copies = [
         rcopy(part(ring(p, d), 0, chan), got_x.at[p], xs.at[d - 1], xr.at[d - 1], p=ring(p, d)) for d in (1, 2, 3)
@@ -649,41 +671,53 @@
     mine[...] = total
     g = Spread(mine, sums, lambda q, k: pl.multiple_of((q * 2 + k) * RIM, RIM), RIM, spread)
     g.start()
+    total = steps[z]
+    for d in range(1, planes):
+        total = total + t_far[d - 1]
+    t_own[...] = total
+    back = [rcopy(t_own.at[ring(p, d)], got_t.at[p], qs.at[d - 1], qr.at[d - 1], p=ring(p, d)) for d in (1, 2, 3)]
+    back.append(pltpu.make_async_copy(t_own.at[p], got_t.at[p], tk))
+    for copy in back:
+        copy.start()
     g.pass_on()
-    for copy in copies:
+    for copy in copies + back:
         copy.wait()
     g.finish()
 
 
-def give_body(sizes, core_ref, zb, f1, f2, x_, s_, z_o, x_o, bc_o, dt_o, q_o, k_o, v_o, o_o, out_o, gate_o, up_o, down_o):
-    bcs, heads, quarter = sizes
-    chan, part = x_.shape[2], f1.shape[2] // 3
+def give_body(sizes, core_ref, zq, ob, f1, f2, x_, s_, layer, grad, z_o, x_o, bc_o, q_o, k_o, v_o, o_o, out_o, gate_o, up_o, down_o,
+              layer_o, grad_o):
+    bcs, quarter = sizes
+    layer_o[...] = layer[...]
+    grad_o[...] = grad[...]
+    chan, units = x_.shape[2], (f1.shape[2] + f2.shape[2]) // 3
     for p in range(G):
         for ref, got, first, cols in (
-            (z_o, zb, 0, chan), (q_o, zb, chan, HD), (out_o, zb, chan + HD, chan), (o_o, zb, 2 * chan + HD, HD),
+            (z_o, zq, 0, chan), (q_o, zq, chan, HD), (out_o, ob, 0, chan), (o_o, ob, chan, HD),
             (x_o, x_, 0, chan),
         ):
             ref[:, p * cols : (p + 1) * cols] = got[p, :, first : first + cols].astype(f32)
 
         for i, ref in enumerate((gate_o, up_o, down_o)):
-            for k, got in enumerate((f1, f2)):
-                at = (2 * p + k) * part
+            for got, skip in ((f1, 0), (f2, f1.shape[2] // 3)):
+                part = got.shape[2] // 3
+                at = p * units + skip
                 ref[:, at : at + part] = got[p, :, i * part : (i + 1) * part].astype(f32)
 
     def place(first, cols, target):
-        i = iota((256, 256), 0) - first
-        return ((i >= 0) & (i < cols) & (iota((256, 256), 1) == target(i))).astype(bf16)
+        i = iota((128, 128), 0) - first
+        return ((i >= 0) & (i < cols) & (iota((128, 128), 1) == target(i))).astype(bf16)
 
     def bc_place(p):
         return (iota((128, 256), 0) + p * bcs == iota((128, 256), 1)).astype(bf16) * (iota((128, 256), 0) < bcs).astype(bf16)
 
     mine = core_ref[0]
-    k_sum = v_sum = dt_sum = jnp.zeros((x_.shape[1], 256), f32)
+    k_sum = v_sum = jnp.zeros((x_.shape[1], 128), f32)
     halves = []
     for k in (0, 1):
         total = jnp.zeros((x_.shape[1], 256), f32)
         for p in range(G):
-            total = total + mm(s_[k * G + p, :, :128], bc_place(p), 1, 0)
+            total = total + mm(s_[k * G + p], bc_place(p), 1, 0)
         halves.append(total)
     bc_o[:, :256] = halves[0]
     bc_o[:, 256:] = halves[1]
@@ -691,10 +725,8 @@
         own = s_[mine * G + p]
         k_sum = k_sum + mm(own, place(bcs, 2 * quarter, lambda i: (i // quarter) * (quarter * G) + p * quarter + i % quarter), 1, 0)
         v_sum = v_sum + mm(own, place(bcs + 2 * quarter, 2 * quarter, lambda i: i + p * 2 * quarter), 1, 0)
-        dt_sum = dt_sum + mm(own, place(bcs + 4 * quarter, heads, lambda i: i + p * heads), 1, 0)
-    k_o[...] = k_sum[:, :HD]
-    v_o[...] = v_sum[:, :HD]
-    dt_o[...] = dt_sum[:, : dt_o.shape[1]]
+    k_o[...] = k_sum
+    v_o[...] = v_sum
 
 
 def mm(a, b, ca, cb):
@@ -785,7 +817,7 @@
     return decay_in, closing
 
 
-def scan_body(heads, base_ref, pa_ref, bc_ref, starts_ref, taps_ref, bias_ref, rates_ref,
+def scan_body(heads, base_ref, raw_ref, pa_ref, bc_ref, starts_ref, taps_ref, bias_ref, rates_ref,
               y_ref, cv_ref, enter_ref, reach_ref, state_out, through_out, state, through):
     c = pl.program_id(0)
     chan = heads * P_SIZE
@@ -796,7 +828,7 @@
         through[...] = jnp.ones_like(through)
 
     starts, place = starts_ref[...], places_of(base_ref, c)
-    raw = pa_ref[pl.ds(pl.multiple_of(c * CHUNK + RIM, 16), CHUNK), chan + HD :]
+    raw = raw_ref[...]
     step, _, cs = rates_of(raw, bias_ref[...], rates_ref[...], heads)
     cs_t = cs.T
     cv = conv_of(pa_ref, taps_ref, starts, place, c, chan, 0)
@@ -836,12 +868,12 @@
     return x, ssm, s, gated, r
 
 
-def gate_body(heads, base_ref, pa_ref, bc_ref, starts_ref, bias_ref, rates_ref, y_ref, cv_ref, enter_ref, reach_ref,
+def gate_body(heads, base_ref, raw_ref, bc_ref, starts_ref, bias_ref, rates_ref, y_ref, cv_ref, enter_ref, reach_ref,
               before_ref, z_ref, skip_ref, gain_ref, low_ref, scan_ref):
     c = pl.program_id(0)
     chan = heads * P_SIZE
     starts, place = starts_ref[...], places_of(base_ref, c)
-    raw = pa_ref[pl.ds(pl.multiple_of(c * CHUNK + RIM, 16), CHUNK), chan + HD :]
+    raw = raw_ref[...]
     _, _, cs = rates_of(raw, bias_ref[...], rates_ref[...], heads)
     decay_in, _ = decays_of(cs, starts, place)
     state_in = enter_ref[0] + scale_rows(before_ref[...], reach_ref[0], heads)
@@ -853,7 +885,7 @@
     low_ref[...] = (gated * r * gain_ref[...]).astype(bf16)
 
 
-def gate_back_body(heads, chunks, base_ref, pa_ref, bc_ref, starts_ref, bias_ref, rates_ref, d_ref, scan_ref, cv_ref,
+def gate_back_body(heads, chunks, base_ref, raw_ref, bc_ref, starts_ref, bias_ref, rates_ref, d_ref, scan_ref, cv_ref,
                    reach_ref, z_ref, skip_ref, gain_ref, dz_ref, dy_ref, leave_ref, tail_ref, state_out, gain_out, state, tail):
     c = chunks - 1 - pl.program_id(0)
     chan = heads * P_SIZE
@@ -865,7 +897,7 @@
         gain_out[...] = jnp.zeros_like(gain_out)
 
     starts, place = starts_ref[...], places_of(base_ref, c)
-    raw = pa_ref[pl.ds(pl.multiple_of(c * CHUNK + RIM, 16), CHUNK), chan + HD :]
+    raw = raw_ref[...]
     _, _, cs = rates_of(raw, bias_ref[...], rates_ref[...], heads)
     decay_in, _ = decays_of(cs, starts, place)
     z = z_ref[...]
@@ -887,19 +919,18 @@
     state_out[...] = state[...].astype(bf16)
 
 
-def scan_back_body(heads, base_ref, pa_ref, bc_ref, starts_ref, bias_ref, rates_ref, dy_ref, cv_ref,
+def scan_back_body(heads, base_ref, raw_ref, bc_ref, starts_ref, bias_ref, rates_ref, dy_ref, cv_ref,
                    enter_ref, reach_ref, before_ref, leave_ref, tail_ref, after_ref, skip_ref,
-                   gx_ref, dbc_ref, raw_out, rows_out, skip_out):
+                   gx_ref, dbc_ref, raw_out, rows_out):
     c = pl.program_id(0)
     chan = heads * P_SIZE
 
     @pl.when(c == 0)
     def _():
         rows_out[...] = jnp.zeros_like(rows_out)
-        skip_out[...] = jnp.zeros_like(skip_out)
 
     starts, place = starts_ref[...], places_of(base_ref, c)
-    raw = pa_ref[pl.ds(pl.multiple_of(c * CHUNK + RIM, 16), CHUNK), chan + HD :]
+    raw = raw_ref[...]
     step, log_decay, cs = rates_of(raw, bias_ref[...], rates_ref[...], heads)
     cs_t = cs.T
     visible = visible_of(base_ref, c, starts, place)
@@ -957,9 +988,9 @@
     d_raw = (d_step - jnp.exp(rates_ref[...]) * d_la) * sig(raw + bias_ref[...])
     d_raw = jnp.where(iota((CHUNK, 128), 1) < heads, d_raw, 0.0)
     raw_out[...] = d_raw.astype(bf16)
-    rows_out[:1] += jnp.sum(d_raw, axis=0, keepdims=True)
-    rows_out[1:2] += jnp.sum(d_la * log_decay, axis=0, keepdims=True)
-    skip_out[:1] += jnp.sum(dy * x, axis=0, keepdims=True)
+    rows_out[:1] += jnp.sum(d_la * log_decay, axis=0, keepdims=True)
+    rows_out[1:2] += jnp.sum(d_raw, axis=0, keepdims=True)
+    rows_out[2:3] += jnp.sum(head_sums(dy * x, heads), axis=0, keepdims=True)
     wide = jnp.concatenate([pair_of(step, k) for k in range(heads // 2)], axis=1)
     gx_ref[...] = (d_driven * wide + skip_ref[...] * dy) * (s * (1.0 + cv * (1.0 - s)))
 
@@ -1074,18 +1105,17 @@
     )
 
 
-def ffn_first_body(part, second_ref, low_ref, w_ref, h_ref):
-    h_ref[...] = ffn_units(part, second_ref[...], low_ref[...], w_ref)
-
-
-def ffn_second_body(part, second_ref, low_ref, w1_ref, w2_ref, h1_ref, h_ref, layer_ref, back_ref):
-    h1 = h1_ref[...]
-    h2 = ffn_units(part, second_ref[...], low_ref[...], w2_ref)
-    h_ref[...] = h2
+def ffn_body(part, second_ref, low_ref, w_ref, *refs):
+    *done, h_ref, layer_ref, back_ref = refs
+    h = ffn_units(part, second_ref[...], low_ref[...], w_ref)
+    h_ref[...] = h
     two = 2 * part
-    layer = mm(h1[:, two:], w1_ref[:, two:], 1, 1) + mm(h2[:, two:], w2_ref[:, two:], 1, 1)
+    layer = mm(h[:, two:], w_ref[:, two:], 1, 1)
+    back = mm(h[:, :two], w_ref[:, :two], 1, 1)
+    if done:
+        layer = layer + done[0][...].astype(f32)
+        back = back + done[1][...].astype(f32)
     layer_ref[...] = layer.astype(bf16)
-    back = mm(h1[:, :two], w1_ref[:, :two], 1, 1) + mm(h2[:, :two], w2_ref[:, :two], 1, 1)
     back_ref[...] = back.astype(bf16)
 
 
@@ -1095,7 +1125,7 @@
     out_ref[:, two:] = mm(low_ref[...], h_ref[:, two:], 0, 0).astype(bf16)
 
 
-def finish_body(chunks, chan, base_ref, pa_ref, gx_ref, rim_x, g_bc, rim_bc, dkv, raw_ref, starts_ref, taps_ref, cos_ref, sin_ref,
+def finish_body(chunks, chan, base_ref, pa_ref, gx_ref, rim_x, g_bc, rim_bc, dkv, starts_ref, taps_ref, cos_ref, sin_ref,
                 out_ref, taps_out):
     c = pl.program_id(0)
     wide = chan + 128
@@ -1137,7 +1167,27 @@
     kv = jnp.concatenate([a * cosine + b * sine, b * cosine - a * sine, kv[2 * quarter :]], axis=0)
     out_ref[:, :chan] = total[:, :chan].astype(bf16)
     out_ref[:, chan:wide] = (total[:, chan:] + mm(kv, put(rows), 0, 0)).astype(bf16)
-    out_ref[:, wide:] = raw_ref[...]
+
+
+def prepare_body(chan, base_ref, pa_ref, starts_ref, taps_ref, cos_ref, sin_ref, bc_ref, slope_ref, kv_ref):
+    c = pl.program_id(0)
+    cv = conv_of(pa_ref, taps_ref, starts_ref[...], places_of(base_ref, c), c, 128, chan).T
+    rows, quarter = bc_ref.shape[0], cos_ref.shape[0]
+    cv = cv[:rows]
+    s = sig(cv)
+    bc_ref[...] = (cv * s).astype(bf16)
+    slope_ref[...] = s * (1.0 + cv * (1.0 - s))
+    kv = pa_ref[pl.ds(pl.multiple_of(c * CHUNK + RIM, 16), CHUNK), chan : chan + 128].T[rows:]
+    a, b = kv[:quarter], kv[quarter : 2 * quarter]
+    cosine, sine = cos_ref[...], sin_ref[...]
+    kv_ref[:quarter] = (a * cosine - b * sine).astype(bf16)
+    kv_ref[quarter : 2 * quarter] = (b * cosine + a * sine).astype(bf16)
+    kv_ref[2 * quarter :] = kv[2 * quarter :].astype(bf16)
+
+
+def back_part_body(da_ref, dz_ref, raw_ref, wa_ref, wz_ref, ws_ref, out_ref):
+    total = mm(da_ref[...], wa_ref[...], 1, 1) + mm(dz_ref[...], wz_ref[...], 1, 1) + mm(raw_ref[...], ws_ref[...], 1, 0)
+    out_ref[...] = total.astype(bf16)
 
 
 def head_sums_t(v, heads):
@@ -1146,7 +1196,17 @@
     return jnp.sum(column * pick, axis=0, keepdims=True)
 
 
-def chunked(body, chunks, outs, out_specs, ins, in_specs, scratch=()):
+def chunked(body, chunks, outs, out_specs, ins, in_specs, scratch=(), mib=16, near=(), keep=()):
+    ins = [
+        pltpu.with_memory_space_constraint(v, pltpu.HBM) if s.memory_space is None and v.size > 20000 and i not in near else v
+        for i, (v, s) in enumerate(zip(ins, in_specs))
+    ]
+    if isinstance(outs, tuple):
+        outs = tuple(
+            (pltpu.VMEM if i in keep else pltpu.HBM)(v.shape, v.dtype) if v.size > 20000 else v for i, v in enumerate(outs)
+        )
+    else:
+        outs = (pltpu.VMEM if keep else pltpu.HBM)(outs.shape, outs.dtype)
     return pl.pallas_call(
         body,
         grid=(chunks,),
@@ -1155,7 +1215,7 @@
         out_specs=out_specs,
         scratch_shapes=list(scratch),
         cost_estimate=pl.CostEstimate(flops=2_000_000_000, bytes_accessed=40_000_000, transcendentals=0),
-        compiler_params=pltpu.CompilerParams(vmem_limit_bytes=48 * 2**20),
+        compiler_params=pltpu.CompilerParams(vmem_limit_bytes=mib * 2**20),
     )(*ins)
 
 
@@ -1242,14 +1302,10 @@
 
     bc_mine = lax.dynamic_slice_in_dim(bc_weight, hi * (2 * N // cores), 2 * N // cores, 1)
     k_cut = jnp.moveaxis(k_weight.reshape(rows, 2, G, quarter_half), 2, 1).reshape(rows, G, -1)
-    a_sizes = [chan, bcs, 2 * quarter_half, 2 * quarter_half, heads]
-    a_at = [sum(a_sizes[:i]) for i in range(len(a_sizes))]
-    pad = -sum(a_sizes) % 128
-    small_w = jnp.concatenate(
-        [cut(bc_mine), k_cut, cut(v_weight), cut(dt_weight), jnp.zeros((rows, G, pad), bf16)], axis=2
-    )
+    small_w = jnp.concatenate([cut(bc_mine), k_cut, cut(v_weight)], axis=2)
     small_w = jnp.moveaxis(small_w, 1, 0)
-    a_cols = sum(a_sizes) + pad
+    a_cols = chan + 128
+    own_steps = jnp.pad(dt_weight.T.reshape(G, heads, rows), ((0, 0), (0, 16 - heads), (0, 0)))
 
     def gather(w):
         return lax.all_gather(w, "z", axis=0, tiled=True)
@@ -1270,18 +1326,14 @@
         exchange_b_body, 9, shape((G * rows, 2 * (chan + HD)), bf16), HBM,
         (z_weight, q_weight, out_weight, o_weight), [HBM] * 4, exchange_sems(4),
     ))
-    part = gate_weight.shape[1] // G // 2
-    w1, w2, first_rim, docs = call(
+    first_rim, docs, steps = call(
         functools.partial(start_body, planes), 1,
-        (shape((G * rows, 3 * part), bf16), shape((G * rows, 3 * part), bf16), shape((RIM + T, width), bf16),
-         shape((planes, G, 8, tokens), jnp.int32)),
-        (HBM,) * 4,
-        (gate_weight, up_weight, down_weight, first_own, jnp.broadcast_to(doc_start[None], (8, tokens))),
-        [HBM] * 3 + [VMEM] * 2,
-        exchange_sems(6) + [DMA(()), DMA(()), DMA((3,)), DMA((3,)), DMA((planes - 1,)), DMA((planes - 1,)), DMA(())]
-        + Spread.sems, us=40,
-    )
-    w1, w2 = gather(w1), gather(w2)
+        (shape((RIM + T, width), bf16), shape((planes, G, 8, tokens), jnp.int32), shape((planes, G, 16, rows), bf16)), (HBM,) * 3,
+        (first_own, jnp.broadcast_to(doc_start[None], (8, tokens)), own_steps), [VMEM] * 3,
+        [DMA(()), DMA(()), DMA((2, 3)), DMA((2, 3)), DMA((2, planes - 1)), DMA((2, planes - 1)), DMA((2,))] + Spread.sems, us=25,
+    )
+    w_step = jnp.pad(steps.transpose(2, 0, 1, 3).reshape(16, width), ((0, 112), (0, 0)))
+    w_zqob = wb
     wz, wb = wb[:, : chan + HD], wb[:, chan + HD :]
     first = first_rim[RIM:]
     all_starts = docs[:, :, 0].reshape(-1)
@@ -1290,38 +1342,47 @@
     def line_sum(grad):
         return lax.psum_scatter(grad, "z", scatter_dimension=0, tiled=True)
 
-    edge = K - 1
+    raw = dot(first, w_step, 1, 1)
     pa = dot(first_rim, wa, 1, 0)
     zq = dot(first, wz, 1, 0)
-    bc_pre, k_proj, v_proj = (pa[RIM:, a : a + s] for a, s in zip(a_at[1:4], a_sizes[1:4]))
-    bc_ext = pa[:, a_at[1] : a_at[1] + bcs]
-    cv_bc = conv_rows(bc_ext, taps_state, starts, places)
-    bc_low = jax.nn.silu(cv_bc).astype(bf16)
     offsets = places - starts
     cos_q, sin_q = rope_tables(offsets, 0, HD // 2)
-    cos_k, sin_k = rope_tables(offsets, pi * quarter_half, quarter_half)
     cos_row = jnp.concatenate([cos_q, cos_q], axis=1)
     sin_row = jnp.concatenate([sin_q, -sin_q], axis=1)
+    cos_k, sin_k = (v.T for v in rope_tables(offsets, pi * quarter_half, quarter_half))
     kvr = 4 * quarter_half
-    kv_own = jnp.concatenate([turn(k_proj, cos_k, sin_k).astype(bf16), v_proj.astype(bf16)], axis=1)
-    line_sems = [DMA((planes - 1,)), DMA((planes - 1,))]
-    bc_t, kv_line = call(
-        functools.partial(spread_body, planes), 2, (shape((2 * N, T), bf16), shape((planes, kvr, T), bf16)), (HBM, HBM),
-        (bc_low.T, kv_own.T), [HBM, HBM], line_sems + [DMA(())] + Spread.sems,
-    )
-    bc_all = bc_t.T
-
     L = CHUNK
     nc = T // L
     base = jnp.full((1,), offset, jnp.int32)
     starts_col = starts[:, None]
+    smem = pl.BlockSpec(memory_space=pltpu.SMEM)
+    taps_pair = jnp.concatenate([taps_state, jnp.zeros((K, 128 - bcs), f32)], axis=1)
+    along = lambda rows_: pl.BlockSpec((rows_, L), lambda c: (0, c))
+    bc_low, slope_bc, kv_own = chunked(
+        functools.partial(prepare_body, chan), nc,
+        (shape((bcs, T), bf16), shape((bcs, T), f32), shape((kvr, T), bf16)), (along(bcs), along(bcs), along(kvr)),
+        (base, pa, starts_col, taps_pair, cos_k, sin_k),
+        [smem, pl.BlockSpec(pa.shape, lambda c: (0, 0)), pl.BlockSpec((L, 1), lambda c: (c, 0)), pl.BlockSpec((K, 128), lambda c: (0, 0)),
+         along(quarter_half), along(quarter_half)],
+    )
+    line_sems = [DMA((planes - 1,)), DMA((planes - 1,))]
+    units = gate_weight.shape[1] // G
+    parts = (units - 128, 128)
+    bc_t, kv_line, w1, w2 = call(
+        functools.partial(spread_body, planes), 2,
+        (shape((2 * N, T), bf16), shape((planes, kvr, T), bf16)) + tuple(shape((G * rows, 3 * n), bf16) for n in parts), (HBM,) * 4,
+        (bc_low, kv_own, gate_weight, up_weight, down_weight), [HBM] * 5,
+        line_sems + [DMA(())] + exchange_sems(6) + Spread.sems, us=28,
+    )
+    w1, w2 = gather(w1), gather(w2)
+    bc_all = bc_t.T
+
 
     def row128(v):
         return jnp.pad(v, (0, 128 - v.shape[0]))[None]
 
     bias_row, rates_row = row128(bias), row128(rates)
     skip_row, gain_row = jnp.repeat(skip, P_SIZE)[None], gain_s[None]
-    smem = pl.BlockSpec(memory_space=pltpu.SMEM)
 
     def specs(turned=False):
         at = (lambda c: nc - 1 - c) if turned else (lambda c: c)
@@ -1338,8 +1399,8 @@
         (shape((T, chan), f32), shape((T, chan), f32), shape((nc, chan, N), f32), shape((nc, 16, 128), f32),
          shape((chan, N), bf16), shape((8, 128), f32)),
         (tile(chan), tile(chan), stack(chan, N), stack(16, 128), fixed(chan, N), fixed(8, 128)),
-        (base, pa, bc_all, starts_col, taps_inner, bias_row, rates_row),
-        [smem, pa_spec, tile(2 * N), tile(1), fixed(K, chan), fixed(1, 128), fixed(1, 128)],
+        (base, raw, pa, bc_all, starts_col, taps_inner, bias_row, rates_row),
+        [smem, tile(128), pa_spec, tile(2 * N), tile(1), fixed(K, chan), fixed(1, 128), fixed(1, 128)],
         [pltpu.VMEM((chan, N), f32), pltpu.VMEM((8, 128), f32)],
     )
 
@@ -1360,8 +1421,8 @@
     ssm_low, y_scan = chunked(
         functools.partial(gate_body, heads), nc,
         (shape((T, chan), bf16), shape((T, chan), f32)), (tile(chan), tile(chan)),
-        (base, pa, bc_all, starts_col, bias_row, rates_row, y_diag, cv_x, enter, reach, before, zq, skip_row, gain_row),
-        [smem, pa_spec, tile(2 * N), tile(1), fixed(1, 128), fixed(1, 128), tile(chan), tile(chan), stack(chan, N),
+        (base, raw, bc_all, starts_col, bias_row, rates_row, y_diag, cv_x, enter, reach, before, zq, skip_row, gain_row),
+        [smem, tile(128), tile(2 * N), tile(1), fixed(1, 128), fixed(1, 128), tile(chan), tile(chan), stack(chan, N),
          stack(16, 128), fixed(chan, N), tile(chan), fixed(1, chan), fixed(1, chan)],
     )
 
@@ -1380,7 +1441,7 @@
         (shape((T, HD), bf16), shape((T, HD), bf16), shape((T, HD), f32), shape((T, 1), f32)),
         (column(0, HD), column(0, HD), column(0, HD), column(0, 1)),
         (base, firsts, zq, starts_col, cos_row, sin_row, kv_all),
-        [smem, smem, column(at_q, HD), column(0, 1), column(0, HD), column(0, HD), kv_spec],
+        [smem, smem, column(at_q, HD), column(0, 1), column(0, HD), column(0, HD), kv_spec], mib=12 + 2 * planes,
     )
 
     both_low = jnp.concatenate([ssm_low, att_low], axis=1)
@@ -1390,7 +1451,6 @@
         (dot(both_low, wb, 1, 1).astype(bf16), x_own, mixer_row(ffn_gain)), [VMEM] * 3, collect, us=50,
     )
     ftile = math.gcd(256, T)
-    wide = 3 * part
 
     def rows_spec(cols):
         return pl.BlockSpec((ftile, cols), lambda i: (i, 0))
@@ -1398,35 +1458,36 @@
     def all_spec(v):
         return pl.BlockSpec(v.shape, lambda i: (0,) * len(v.shape))
 
-    h1 = chunked(
-        functools.partial(ffn_first_body, part), T // ftile, shape((T, wide), bf16), rows_spec(wide),
-        (second, out_low, w1), [rows_spec(width), rows_spec(width), all_spec(w1)],
-    )
+    def ffn(w, *done):
+        wide = w.shape[1]
+        return chunked(
+            functools.partial(ffn_body, wide // 3), T // ftile,
+            (shape((T, wide), bf16), shape((T, width), bf16), shape((T, width), bf16)),
+            (rows_spec(wide), rows_spec(width), rows_spec(width)),
+            (second, out_low, w) + done, [rows_spec(width), rows_spec(width), all_spec(w)] + [rows_spec(width)] * len(done), mib=36, keep=(2,) if done else (),
+        )
 
     def ffn_grads(h):
+        wide = h.shape[1]
         tile_d = math.gcd(256, width)
         columns = pl.BlockSpec((T, tile_d), lambda i: (0, i))
         return chunked(
-            functools.partial(ffn_grad_body, part), width // tile_d, shape((width, wide), bf16),
-            pl.BlockSpec((tile_d, wide), lambda i: (i, 0)), (second, out_low, h), [columns, columns, all_spec(h)],
+            functools.partial(ffn_grad_body, wide // 3), width // tile_d, shape((width, wide), bf16),
+            pl.BlockSpec((tile_d, wide), lambda i: (i, 0)), (second, out_low, h), [columns, columns, all_spec(h)], mib=24,
         )
 
+    h1, part_l, part_c = ffn(w1)
     grad_1 = ffn_grads(h1)
     w2, grad_1 = lax.optimization_barrier((w2, grad_1))
     sum_1 = line_sum(grad_1)
-    h2, part_l, part_c = chunked(
-        functools.partial(ffn_second_body, part), T // ftile,
-        (shape((T, wide), bf16), shape((T, width), bf16), shape((T, width), bf16)),
-        (rows_spec(wide), rows_spec(width), rows_spec(width)),
-        (second, out_low, w1, w2, h1), [rows_spec(width), rows_spec(width), all_spec(w1), all_spec(w2), rows_spec(wide)],
-    )
+    h2, part_l, part_c = ffn(w2, part_l, part_c)
     d_hidden, grad_ffn, branch = call(
         branch_body, 5, (shape((own, width), f32), shape((8, width), f32), shape((T, width), bf16)), (VMEM, VMEM, HBM),
         (part_c, hidden, cot_own, mixer_row(ffn_gain)), [VMEM] * 4, collect, us=50,
     )
     h2, branch = lax.optimization_barrier((h2, branch))
-    sum_2 = line_sum(ffn_grads(h2))
-    grad_b = dot(branch, both_low, 0, 0)
+    grad_2 = ffn_grads(h2)
+    grad_2b = jnp.concatenate([grad_2, dot(branch, both_low, 0, 0).astype(bf16)], axis=1)
     d_both = dot(branch, wb, 1, 0)
 
     back, _, back_stack = specs(True)
@@ -1435,95 +1496,90 @@
         (shape((T, chan), bf16), shape((T, chan), f32), shape((nc, chan, N), f32), shape((nc, 8, 128), f32),
          shape((chan, N), bf16), shape((8, chan), f32)),
         (back(chan), back(chan), back_stack(chan, N), back_stack(8, 128), fixed(chan, N), fixed(8, chan)),
-        (base, pa, bc_all, starts_col, bias_row, rates_row, d_both, y_scan, cv_x, reach, zq, skip_row, gain_row),
-        [smem, pa_spec, back(2 * N), back(1), fixed(1, 128), fixed(1, 128), back(chan), back(chan), back(chan),
+        (base, raw, bc_all, starts_col, bias_row, rates_row, d_both, y_scan, cv_x, reach, zq, skip_row, gain_row),
+        [smem, back(128), back(2 * N), back(1), fixed(1, 128), fixed(1, 128), back(chan), back(chan), back(chan),
          back_stack(16, 128), back(chan), fixed(1, chan), fixed(1, chan)],
         [pltpu.VMEM((chan, N), f32), pltpu.VMEM((8, 128), f32)],
     )
+    grad_2b, sum_1, dz_low = lax.optimization_barrier((grad_2b, sum_1, dz_low))
+    sum_2 = line_sum(grad_2b)
+
     dq_low, dkv = chunked(
         functools.partial(attend_back_body, size, T), T // qrows,
         (shape((T, HD), bf16), shape((G, planes, kvr, T), bf16)), (column(0, HD), kv_spec),
         (base, firsts, query, starts_col, cos_row, sin_row, kv_all, d_both, attended, log_mass),
         [smem, smem, column(0, HD), column(0, 1), column(0, HD), column(0, HD), kv_spec, column(at_q, HD), column(0, HD),
          column(0, 1)],
-        [pltpu.VMEM((planes, HD, T), f32), pltpu.VMEM((planes, HD, T), f32)],
+        [pltpu.VMEM((planes, HD, T), f32), pltpu.VMEM((planes, HD, T), f32)], mib=14 + 3 * planes,
     )
     dzq_low = jnp.concatenate([dz_low, dq_low], axis=1)
-    grad_zb = jnp.concatenate([dot(first, dzq_low, 0, 0).astype(bf16), grad_b.astype(bf16)], axis=1)
-    g_state, sum_1, grad_zb = lax.optimization_barrier((g_state, sum_1, grad_zb))
+    grad_z = dot(first, dzq_low, 0, 0).astype(bf16)
+    g_state, sum_1, grad_z = lax.optimization_barrier((g_state, sum_1, grad_z))
     states, factors, dkv, layer_own = call(
-        functools.partial(down_body, planes), 6, state_shapes + (shape((G, planes, kvr, T), bf16), shape((own, width), f32)),
-        (HBM,) * 3 + (VMEM,), (g_state, through, dkv, part_l, hidden), [HBM] * 3 + [VMEM] * 2,
-        line_sems * 2 + [DMA((3,)), DMA((3,)), DMA(())] + Collect.scratch(own, width), us=45,
-    )
-    states, grad_zb = lax.optimization_barrier((states, grad_zb))
-    sum_zb = line_sum(grad_zb)
+        functools.partial(down_body, planes), 6, state_shapes + (shape((planes * kvr, T), bf16), shape((own, width), f32)),
+        (HBM,) * 2 + (VMEM,) * 2, (g_state, through, dkv.reshape(-1, T), part_l, hidden), [HBM] * 2 + [VMEM] * 3,
+        line_sems * 2 + Collect.scratch(planes * kvr, T, False) + Collect.scratch(own, width), us=45, mib=14 + 2 * planes,
+    )
+    states, grad_z = lax.optimization_barrier((states, grad_z))
+    sum_z = line_sum(grad_z)
     after = entering(False, states, factors)
-    gx, d_bc_all, d_raw, grad_rows, grad_skip = chunked(
+    gx, d_bc_all, d_raw, grad_rows = chunked(
         functools.partial(scan_back_body, heads), nc,
-        (shape((T, chan), f32), shape((2 * N, T), bf16), shape((T, 128), bf16), shape((8, 128), f32), shape((8, chan), f32)),
-        (tile(chan), pl.BlockSpec((2 * N, L), lambda c: (0, c)), tile(128), fixed(8, 128), fixed(8, chan)),
-        (base, pa, bc_all, starts_col, bias_row, rates_row, dy, cv_x, enter, reach, before, leave, tail, after, skip_row),
-        [smem, pa_spec, tile(2 * N), tile(1), fixed(1, 128), fixed(1, 128), tile(chan), tile(chan),
+        (shape((T, chan), f32), shape((2 * N, T), bf16), shape((T, 128), bf16), shape((8, 128), f32)),
+        (tile(chan), pl.BlockSpec((2 * N, L), lambda c: (0, c)), tile(128), fixed(8, 128)),
+        (base, raw, bc_all, starts_col, bias_row, rates_row, dy, cv_x, enter, reach, before, leave, tail, after, skip_row),
+        [smem, tile(128), tile(2 * N), tile(1), fixed(1, 128), fixed(1, 128), tile(chan), tile(chan),
          stack(chan, N), stack(16, 128), fixed(chan, N), stack(chan, N), stack(8, 128), fixed(chan, N), fixed(1, chan)],
     )
-    grad_gain_s = grad_gain_s[0]
-    grad_bias, grad_rates = grad_rows[0, :heads], grad_rows[1, :heads]
-    grad_skip = jnp.sum(grad_skip[0].reshape(heads, P_SIZE), axis=1)
-
-    gx_first = gx[:RIM]
+
     d_bc_t, sum_2 = lax.optimization_barrier((d_bc_all, sum_2))
     g_bc, rim_bc, rim_x, dkv, got_1, got_2 = call(
         functools.partial(back_body, planes), 7,
         (shape((bcs, T), f32), shape((bcs, 128), f32), shape((RIM, chan), f32), shape((kvr, T), f32))
-        + tuple(shape((G, rows, v.shape[1]), bf16) for v in (sum_1, sum_2)), (VMEM,) * 4 + (HBM,) * 2,
-        (d_bc_t, dkv, d_silu(cv_bc).T, gx_first, sum_1, sum_2), [VMEM] * 4 + [HBM] * 2,
+        + tuple(shape((G, rows, v.shape[1]), bf16) for v in (h1, h2)), (VMEM,) * 4 + (HBM,) * 2,
+        (d_bc_t, dkv.reshape(planes, kvr, T), slope_bc, gx, sum_1, sum_2), [VMEM] * 3 + [HBM] * 3,
         [pltpu.VMEM((G * bcs, T), bf16), pltpu.VMEM((3, bcs, T), bf16), pltpu.VMEM((3, bcs, T), bf16),
-         pltpu.VMEM((planes, kvr, T), bf16), pltpu.VMEM((planes - 1, kvr, T), bf16),
-         pltpu.VMEM((bcs, T), f32), DMA(()), DMA(()), DMA((3,)), DMA((3,)),
+         pltpu.VMEM((planes - 1, kvr, T), bf16), pltpu.VMEM((bcs, T), f32), DMA(()), DMA(()), DMA((3,)), DMA((3,)),
          DMA((planes - 1,)), DMA((planes - 1,)), DMA((2,)), DMA((2,)), DMA((2, 3)), DMA((2, 3)), DMA((2,))], us=30,
     )
     starts_long = jnp.concatenate([all_starts, jnp.full((8,), total_tokens, jnp.int32)])
     starts_long = lax.dynamic_slice_in_dim(starts_long, offset, T + 8, 0)[:, None]
-    taps_both = jnp.concatenate([taps_inner, taps_state, jnp.zeros((K, 128 - bcs), f32)], axis=1)
+    taps_both = jnp.concatenate([taps_inner, taps_pair], axis=1)
     da_low, grad_taps = chunked(
         functools.partial(finish_body, nc, chan), nc,
         (shape((T, a_cols), bf16), shape((8, chan + 128), f32)), (tile(a_cols), fixed(8, chan + 128)),
-        (base, pa, gx, rim_x, g_bc, rim_bc, dkv, d_raw, starts_long, taps_both, cos_k.T, sin_k.T),
-        [smem, pa_spec, fixed(T, chan), fixed(RIM, chan), fixed(bcs, T), fixed(bcs, 128), fixed(kvr, T), tile(128),
-         fixed(T + 8, 1), fixed(K, chan + 128), fixed(quarter_half, T), fixed(quarter_half, T)],
+        (base, pa, gx, rim_x, g_bc, rim_bc, dkv, starts_long, taps_both, cos_k, sin_k),
+        [smem, pa_spec, fixed(T, chan), fixed(RIM, chan), fixed(bcs, T), fixed(bcs, 128), fixed(kvr, T),
+         fixed(T + 8, 1), fixed(K, chan + 128), fixed(quarter_half, T), fixed(quarter_half, T)], near=(3, 4, 5, 6),
     )
     grad_a = dot(first, da_low, 0, 0).astype(bf16)
-    grad_a, sum_zb = lax.optimization_barrier((grad_a, sum_zb))
+    grad_a, sum_z = lax.optimization_barrier((grad_a, sum_z))
     sum_a = line_sum(grad_a)
     lane = width // 4
-
-    def lines_of(*parts):
-        both = jnp.concatenate(parts, axis=1)
-        return jnp.pad(both, ((0, 0), (0, lane - both.shape[1])))
-
-    flat = jnp.concatenate(
-        [grad_taps[:K], lines_of(grad_gain_s[None]),
-         lines_of(row128(grad_rates), row128(grad_bias), row128(grad_skip)), jnp.zeros((2, lane), f32),
-         grad_ffn[:1].reshape(4, lane), jnp.zeros((4, lane), f32)], axis=0,
-    )
-    part_a = (dot(da_low, wa, 1, 1) + dot(dzq_low, wz, 1, 1)).astype(bf16)
-    grad_input, layer_out, mine, got_zb = call(
+    part_a = chunked(
+        back_part_body, T // ftile, shape((T, width), bf16), rows_spec(width), (da_low, dzq_low, d_raw, wa, w_zqob, w_step),
+        [rows_spec(v.shape[1]) for v in (da_low, dzq_low, d_raw)] + [all_spec(v) for v in (wa, wz, w_step)], mib=28, keep=(0,),
+    )
+    grad_step = dot(d_raw, first, 0, 0)[:16].reshape(16, planes, G, rows).transpose(1, 2, 0, 3)
+    groups = (shape((G, rows, chan + HD), bf16),) * 2
+    grad_input, layer_out, mine, got_z, got_b = call(
         final_body, 8,
-        (shape((tokens, width), f32), shape((tokens, width), f32), shape((RIM, lane), f32),
-         shape((G, rows, sum_zb.shape[1]), bf16)), (HBM, HBM, VMEM, HBM),
-        (part_a, x_own, d_hidden, layer_own, mixer_row(mixer_gain), flat, sum_zb), [VMEM] * 6 + [HBM],
+        (shape((tokens, width), f32), shape((tokens, width), f32), shape((RIM, lane), f32)) + groups, (HBM, HBM, VMEM, HBM, HBM),
+        (part_a, x_own, d_hidden, layer_own, mixer_row(mixer_gain), grad_taps, grad_gain_s, grad_rows, grad_ffn, sum_z, sum_2),
+        [VMEM] * 9 + [HBM] * 2,
         Collect.scratch(own, width)
         + [pltpu.VMEM((own, width), f32), pltpu.VMEM((8, width), f32), DMA((2,)), DMA((2,)), DMA((2,)),
-           DMA((3,)), DMA((3,)), DMA(())], us=40,
-    )
-
-    got_x, got_s, sums = call(
+           DMA((2, 3)), DMA((2, 3)), DMA((2,))], us=40,
+    )
+
+    got_x, got_s, sums, got_t = call(
         functools.partial(last_body, planes), 10,
-        (shape((G, rows, chan), bf16), shape((2 * G, rows, a_cols - chan), bf16), shape((2 * G * RIM, lane), f32)),
-        (HBM,) * 3, (sum_a, mine), [HBM, VMEM],
-        [pltpu.VMEM((RIM, lane), f32), pltpu.VMEM((planes - 1, RIM, lane), f32), DMA((3,)), DMA((3,)), DMA((2 * G,)), DMA((2 * G,)),
-         DMA((2,)), DMA((planes - 1,)), DMA((planes - 1,))] + Spread.sems,
+        (shape((G, rows, chan), bf16), shape((2 * G, rows, a_cols - chan), bf16), shape((2 * G * RIM, lane), f32),
+         shape((G, 16, rows), f32)), (HBM,) * 4, (sum_a, mine, grad_step), [HBM, VMEM, VMEM],
+        [pltpu.VMEM((RIM, lane), f32), pltpu.VMEM((planes - 1, RIM, lane), f32), pltpu.VMEM((G, 16, rows), f32),
+         pltpu.VMEM((planes - 1, G, 16, rows), f32), DMA((3,)), DMA((3,)), DMA((2 * G,)), DMA((2 * G,)),
+         DMA((2,)), DMA((planes - 1,)), DMA((planes - 1,)), DMA((planes - 1,)), DMA((planes - 1,)), DMA((3,)), DMA((3,)), DMA(())]
+        + Spread.sems,
     )
     strip = min(32, rows)
 
@@ -1534,15 +1590,19 @@
         return pl.BlockSpec((strip, cols), lambda c: (c, 0))
 
     widths = [w.shape[1] for w in (
-        z_weight, x_weight, bc_weight, dt_weight, q_weight, k_weight, v_weight, o_weight, out_weight,
+        z_weight, x_weight, bc_weight, q_weight, k_weight, v_weight, o_weight, out_weight,
         gate_weight, up_weight, down_weight,
     )]
-    gathered = (got_zb, got_1, got_2, got_x, got_s)
-    weights = chunked(
-        functools.partial(give_body, (bcs, heads, quarter_half)), rows // strip,
-        tuple(shape((rows, w), f32) for w in widths), tuple(given(w) for w in widths),
-        (jnp.full((1,), hi, jnp.int32),) + gathered, [smem] + [got(v) for v in gathered],
-    )
+    gathered = (got_z, got_b, got_1, got_2, got_x, got_s)
+    steps_ = rows // strip
+    moved = pl.BlockSpec((tokens // steps_, width), lambda c: (c, 0))
+    *weights, layer_out, grad_input = chunked(
+        functools.partial(give_body, (bcs, quarter_half)), steps_,
+        tuple(shape((rows, w), f32) for w in widths) + (shape((tokens, width), f32),) * 2,
+        tuple(given(w) for w in widths) + (moved, moved),
+        (jnp.full((1,), hi, jnp.int32),) + gathered + (layer_out, grad_input), [smem] + [got(v) for v in gathered] + [moved, moved], mib=40,
+    )
+    weights.insert(3, got_t[:, :heads].reshape(G * heads, rows).T)
 
     sums = sums.reshape(G, cores, RIM, lane)
     mine = lax.dynamic_index_in_dim(sums, hi, 1, False)

time: 685 us -> 649 us (0.947)
  waiting for transfers between devices: 32.5 us -> 8.73 us
  local copies, waits for them, and re-layouts: 74.6 us -> 61.3 us
  Pallas kernels: 488 us -> 501 us
  matrix products: 49.7 us -> 39.5 us
    pallas_call x12 -> x14, Pallas kernels: 115 us -> 150 us  [chunked(): pl.pallas_call(body, grid=(chunks,), out_shape=outs, in_specs=in_specs, o...]
    pallas_call x11, Pallas kernels: 372 us -> 350 us  [call(): pl.pallas_call(body, out_shape=outs, in_specs=in_specs, out_specs=out_spe...]
    reduce_scatter x4, waiting for transfers between devices: 12.9 us -> 0.02 us  [line_sum(): return lax.psum_scatter(grad, 'z', scatter_dimension=0, tiled=True)]
    all_gather x4, waiting for transfers between devices: 18.9 us -> 8.57 us  [gather(): return lax.all_gather(w, 'z', axis=0, tiled=True)]
    dot_general x9, matrix products: 49.7 us -> 39.5 us  [dot(): lax.dot_general(a, b, (((ca,), (cb,)), ((), ())), preferred_element_type=...]
    unnamed x233 -> x151, local copies, waits for them, and re-layouts: 55 us -> 46.1 us
    slice x8 -> x1, local copies, waits for them, and re-layouts: 6.93 us -> 0.01 us  [on_device(): weights.insert(3, got_t[:, :heads].reshape(G * heads, rows).T)]
  transfers between devices with their start and end apart: 8 -> 8, of which waited for: 3 -> 2; matrix products, arithmetic and copies ran while one was open for 13% -> 10% of each run, Pallas kernels for 67% -> 72%
where the time goes in v5:
time: 649 us; the launch traced here: 640 us
  Pallas kernels  501 us (77%)
  local copies, waits for them, and re-layouts  61.3 us (9%)
  matrix products  39.5 us (6%)
  between operations  15.4 us (2%)
  other arithmetic  13.2 us (2%)
  waiting for transfers between devices  8.73 us (1%)
    pallas_call x11, Pallas kernels, call(): pl.pallas_call(body, out_shape=outs, in_specs=in_specs, out_specs=out_spe...  350 us
    pallas_call x14, Pallas kernels, chunked(): pl.pallas_call(body, grid=(chunks,), out_shape=outs, in_specs=in_specs, o...  150 us
    unnamed x151, local copies, waits for them, and re-layouts  46.1 us
    dot_general x9, matrix products, dot(): lax.dot_general(a, b, (((ca,), (cb,)), ((), ())), preferred_element_type=...  39.5 us
  transfers between devices with their start and end apart: 8, of which 2 were waited for; matrix products, arithmetic and copies ran while one was open for 10% of the time, Pallas kernels for 72%

profile of v5, /device:TPU:0, one launch (start us, length us, event | category | flops | bytes accessed | tf_op | source)
XLA Modules:
  0.0 640.0 jit_solution(5189208438346444791)
XLA Ops:
  11.6 10.7 %shard_map.391 = bf16[512,512]{1,0:T(8,128)(2,1)} custom-call(bf16[128,1536]{1,0:T(8,128)(2,1)S(1)} %copy-done.41, bf16[4,128,128]{2,1,0:T(8,128)(2,1)S(1)} %maximum_bitcast_fusion.small_ref), custom_call_target="tpu_custom_call" | custom-call | bytes 70000000 | tf_op jit(solution)/shard_map/pallas_call | solution.py:238
  26.2 15.1 %shard_map.396 = bf16[512,1024]{1,0:T(8,128)(2,1)} custom-call(bf16[128,1536]{1,0:T(8,128)(2,1)S(1)} %copy-done.38, bf16[128,512]{1,0:T(8,128)(2,1)S(1)} %copy-done.50, bf16[128,1536]{1,0:T(8,128)(2,1)S(1)} %copy-done.39, bf16[128,512]{1,0:T(8,128)(2,1)S(1)} %copy-done.51), custom_call_target="tpu_custom_call" | custom-call | bytes 70000000 | tf_op jit(solution)/shard_map/pallas_call | solution.py:238
  41.4 1.9 multiply_reduce_fusion
  43.6 31.0 %shard_map.390 = (bf16[1040,2048]{1,0:T(8,128)(2,1)S(1)}, s32[4,4,8,256]{3,2,1,0:T(8,128)S(1)}, bf16[4,4,16,128]{3,2,1,0:T(8,128)(2,1)S(1)}) custom-call(bf16[128,2048]{1,0:T(8,128)(2,1)S(1)} %multiply_convert_fusion.first, s32[8,256]{1,0:T(8,128)S(1)} %broadcast_in_dim.69.docs, bf16[4,16,128]{2,1,0:T(8,128)(2,1)S(1)} %pad.17.steps), custom_call_target="tpu_custom_call" | custom-call | bytes 87500000 | tf_op jit(solution)/shard_map/pallas_call | solution.py:238
  74.5 2.0 copy-done.8
  78.0 6.6 %fusion.26.pa_ref = f32[1040,512]{1,0:T(8,128)} fusion(bf16[1040,2048]{1,0:T(8,128)(2,1)} %copy-done.8, bf16[2048,512]{1,0:T(8,128)(2,1)} %all-gather.5.cloned.1.call-done.wa_ref), kind=kOutput, calls=%fused_computation.79 | convolution fusion | flops 2181038080 | bytes 8486912 | tf_op jit(solution)/shard_map/dot_general | solution.py:1223
  84.6 5.5 shard_map.392
  92.0 25.4 %shard_map.393 = (bf16[512,1024]{1,0:T(8,128)(2,1)S(1)}, bf16[4,64,1024]{2,1,0:T(8,128)(2,1)S(1)}, bf16[512,1152]{1,0:T(8,128)(2,1)S(1)}, bf16[512,384]{1,0:T(8,128)(2,1)S(1)}) custom-call(bf16[64,1024]{1,0:T(8,128)(2,1)S(1)} %copy-done.48, bf16[64,1024]{1,0:T(8,128)(2,1)S(1)} %copy-done.49, bf16[128,2048]{1,0:T(8,128)(2,1)S(1)} %copy-done.27, ...), custom_call_target="tpu_custom_call" | custom-call | bytes 98000000 | tf_op jit(solution)/shard_map/pallas_call | solution.py:238
  123.1 1.9 multiply_sine_fusion
  127.0 4.2 fusion.6.raw_ref
  131.2 2.3 copy.81
  133.5 11.2 %shard_map.394 = (f32[1024,384]{1,0:T(8,128)}, f32[1024,384]{1,0:T(8,128)}, f32[8,384,256]{2,1,0:T(8,128)}, f32[8,16,128]{2,1,0:T(8,128)S(1)}, bf16[384,256]{1,0:T(8,128)(2,1)}, /*index=5*/f32[8,128]{1,0:T(8,128)S(1)}) custom-call(s32[1]{0:T(128)} %bitcast.1.base_ref, f32[1024,128]{1,0:T(8,128)} %fusion.6.raw_ref, f32[1040,512]{1,0:T(8,128)} %fusion.26.pa_ref, ...), custom_call_target="tpu_custom_call" | custom-call | flops 2000000000 | bytes 40000000 | tf_op jit(solution)/shard_map/pallas_call | solution.py:1210
  145.7 42.9 %shard_map.395 = (bf16[3,384,256]{2,1,0:T(8,128)(2,1)S(1)}, f32[3,8,128]{2,1,0:T(8,128)S(1)}, bf16[16,64,1024]{2,1,0:T(8,128)(2,1)S(1)}, bf16[1024,2048]{1,0:T(8,128)(2,1)S(1)}) custom-call(bf16[384,256]{1,0:T(8,128)(2,1)S(1)} %copy-done.46, f32[8,128]{1,0:T(8,128)S(1)} %get-tuple-element.132.factor, bf16[4,64,1024]{2,1,0:T(8,128)(2,1)S(1)} %copy-done.34, ...), custom_call_target="tpu_custom_call" | custom-call | bytes 133000000 | tf_op jit(solution)/shard_map/pallas_call | solution.py:238
  188.6 2.0 copy-done.2
  193.9 2.2 fusion.16.before_ref
  196.1 6.5 %fusion.4.z_ref.q_ref = f32[1024,512]{1,0:T(8,128)} fusion(bf16[1040,2048]{1,0:T(8,128)(2,1)} %copy-done.8, bf16[2048,1024]{1,0:T(8,128)(2,1)} %all-gather.7.cloned.1.call-done.wz_ref), kind=kOutput, calls=%fused_computation.9 | convolution fusion | flops 2147483648 | bytes 8388608 | tf_op jit(solution)/shard_map/dot_general | solution.py:1223
  202.6 9.9 %shard_map.397 = (bf16[1024,384]{1,0:T(8,128)(2,1)}, f32[1024,384]{1,0:T(8,128)}) custom-call(s32[1]{0:T(128)} %bitcast.1.base_ref, f32[1024,128]{1,0:T(8,128)} %fusion.6.raw_ref, bf16[1024,512]{1,0:T(8,128)(2,1)} %bitcast.91, s32[1024,1]{1,0:T(8,128)S(1)} %copy.80.starts_ref, f32[1,128]{1,0:T(1,128)S(1)} %get-tuple-element.245.bias_ref, ...), custom_call_target="tpu_custom_call" | custom-call | flops 2000000000 | bytes 40000000 | tf_op jit(solution)/shard_map/pallas_call | solution.py:1210
  213.7 7.8 %shard_map.398 = (bf16[1024,128]{1,0:T(8,128)(2,1)}, bf16[1024,128]{1,0:T(8,128)(2,1)}, f32[1024,128]{1,0:T(8,128)}, f32[1024,1]{1,0:T(8,128)S(1)}) custom-call(s32[1]{0:T(128)} %bitcast.1.base_ref, s32[4]{0:T(128)S(1)} %slice_reduce_fusion.5.first_ref, f32[1024,512]{1,0:T(8,128)} %fusion.4.z_ref.q_ref, s32[1024,1]{1,0:T(8,128)S(1)} %copy.80.starts_ref, ...), custom_call_target="tpu_custom_call" | custom-call | flops 2000000000 | bytes 40000000 | tf_op jit(solution)/shard_map/pallas_call | solution.py:1210
  223.4 2.4 convolution_convert_fusion.part
  225.7 45.0 %shard_map.399 = (f32[128,2048]{1,0:T(8,128)S(1)}, bf16[1024,2048]{1,0:T(8,128)(2,1)S(1)}) custom-call(bf16[1024,2048]{1,0:T(8,128)(2,1)S(1)} %convolution_convert_fusion.part, f32[128,2048]{1,0:T(8,128)S(1)} %get-tuple-element.231.x_ref, f32[1,2048]{1,0:T(1,128)S(1)} %bitcast.85), custom_call_target="tpu_custom_call" | custom-call | bytes 175000000 | tf_op jit(solution)/shard_map/pallas_call | solution.py:238
  270.7 2.0 copy-done.3
  274.0 16.9 %shard_map.400 = (bf16[1024,1152]{1,0:T(8,128)(2,1)}, bf16[1024,2048]{1,0:T(8,128)(2,1)}, bf16[1024,2048]{1,0:T(8,128)(2,1)}) custom-call(bf16[1024,2048]{1,0:T(8,128)(2,1)} %copy-done.3, bf16[1024,2048]{1,0:T(8,128)(2,1)} %copy-done.2, bf16[2048,1152]{1,0:T(8,128)(2,1)} %all-gather.11.cloned.1.call-done.w_ref), custom_call_target="tpu_custom_call" | custom-call | flops 2000000000 | bytes 40000000 | tf_op jit(solution)/shard_map/pallas_call | solution.py:1210
  290.8 11.8 %shard_map.401 = bf16[2048,1152]{1,0:T(8,128)(2,1)} custom-call(bf16[1024,2048]{1,0:T(8,128)(2,1)} %copy-done.3, bf16[1024,2048]{1,0:T(8,128)(2,1)} %copy-done.2, bf16[1024,1152]{1,0:T(8,128)(2,1)} %get-tuple-element.143.h_ref), custom_call_target="tpu_custom_call" | custom-call | flops 2000000000 | bytes 40000000 | tf_op jit(solution)/shard_map/pallas_call | solution.py:1210
  302.7 8.3 %all-gather.9.cloned.1.call-done.w_ref = bf16[2048,384]{1,0:T(8,128)(2,1)} async-done(((bf16[512,384]{1,0:T(8,128)(2,1)}), bf16[2048,384]{1,0:T(8,128)(2,1)}) %all-gather.9.cloned.1.call-update) | async-done | bytes 1572880 | tf_op jit(solution)/shard_map/all_gather | solution.py:1311
  311.2 11.8 %shard_map.402 = (bf16[1024,384]{1,0:T(8,128)(2,1)}, bf16[1024,2048]{1,0:T(8,128)(2,1)}, bf16[1024,2048]{1,0:T(8,128)(2,1)S(1)}) custom-call(bf16[1024,2048]{1,0:T(8,128)(2,1)} %copy-done.3, bf16[1024,2048]{1,0:T(8,128)(2,1)} %copy-done.2, bf16[2048,384]{1,0:T(8,128)(2,1)} %all-gather.9.cloned.1.call-done.w_ref, ...), custom_call_target="tpu_custom_call" | custom-call | flops 2000000000 | bytes 40000000 | tf_op jit(solution)/shard_map/pallas_call | solution.py:1210
  323.1 46.5 %shard_map.403 = (f32[128,2048]{1,0:T(8,128)S(1)}, f32[8,2048]{1,0:T(8,128)S(1)}, bf16[1024,2048]{1,0:T(8,128)(2,1)S(1)}) custom-call(bf16[1024,2048]{1,0:T(8,128)(2,1)S(1)} %get-tuple-element.148.part, f32[128,2048]{1,0:T(8,128)S(1)} %copy-done.6, f32[128,2048]{1,0:T(8,128)S(1)} %get-tuple-element.243.cot, f32[1,2048]{1,0:T(1,128)S(1)} %bitcast.86), custom_call_target="tpu_custom_call" | custom-call | bytes 175000000 | tf_op jit(solution)/shard_map/pallas_call | solution.py:238
  369.6 9.3 %shard_map.405 = bf16[2048,384]{1,0:T(8,128)(2,1)} custom-call(bf16[1024,2048]{1,0:T(8,128)(2,1)} %copy-done.3, bf16[1024,2048]{1,0:T(8,128)(2,1)} %copy-done.2, bf16[1024,384]{1,0:T(8,128)(2,1)} %get-tuple-element.157.h_ref), custom_call_target="tpu_custom_call" | custom-call | flops 2000000000 | bytes 40000000 | tf_op jit(solution)/shard_map/pallas_call | solution.py:1210
  378.9 3.6 fusion.9.d_ref
  382.6 10.8 %shard_map.404 = (bf16[1024,384]{1,0:T(8,128)(2,1)}, f32[1024,384]{1,0:T(8,128)}, f32[8,384,256]{2,1,0:T(8,128)}, f32[8,8,128]{2,1,0:T(8,128)S(1)}, bf16[384,256]{1,0:T(8,128)(2,1)}, /*index=5*/f32[8,384]{1,0:T(8,128)S(1)}) custom-call(s32[1]{0:T(128)} %bitcast.1.base_ref, f32[1024,128]{1,0:T(8,128)} %fusion.6.raw_ref, bf16[1024,512]{1,0:T(8,128)(2,1)} %bitcast.92, ...), custom_call_target="tpu_custom_call" | custom-call | flops 2000000000 | bytes 40000000 | tf_op jit(solution)/shard_map/pallas_call | solution.py:1210
  393.4 2.4 convolution_convert_fusion.3
  395.9 2.1 pad_maximum_fusion
  398.3 9.9 %shard_map.406 = (bf16[1024,128]{1,0:T(8,128)(2,1)}, bf16[4,4,64,1024]{3,2,1,0:T(8,128)(2,1)}) custom-call(s32[1]{0:T(128)} %bitcast.1.base_ref, s32[4]{0:T(128)S(1)} %slice_reduce_fusion.5.first_ref, bf16[1024,128]{1,0:T(8,128)(2,1)} %get-tuple-element.162.query_ref, s32[1024,1]{1,0:T(8,128)S(1)} %copy.80.starts_ref, ...), custom_call_target="tpu_custom_call" | custom-call | flops 2000000000 | bytes 40000000 | tf_op jit(solution)/shard_map/pallas_call | solution.py:1210
  410.4 6.0 convolution_convert_fusion.2
  416.3 2.2 copy-done.4
  418.5 1.7 copy-done.11
  420.2 52.3 %shard_map.407 = (bf16[3,384,256]{2,1,0:T(8,128)(2,1)S(1)}, f32[3,8,128]{2,1,0:T(8,128)S(1)}, bf16[256,1024]{1,0:T(8,128)(2,1)S(1)}, f32[128,2048]{1,0:T(8,128)S(1)}) custom-call(bf16[384,256]{1,0:T(8,128)(2,1)S(1)} %copy-done.47, f32[8,128]{1,0:T(8,128)S(1)} %get-tuple-element.132.factor, bf16[1024,1024]{1,0:T(8,128)(2,1)S(1)} %bitcast.78, ...), custom_call_target="tpu_custom_call" | custom-call | bytes 157500000 | tf_op jit(solution)/shard_map/pallas_call | solution.py:238
  476.9 2.1 fusion.12.after_ref
  479.0 21.2 %shard_map.408 = (f32[1024,384]{1,0:T(8,128)}, bf16[512,1024]{1,0:T(8,128)(2,1)}, bf16[1024,128]{1,0:T(8,128)(2,1)}, f32[8,128]{1,0:T(8,128)S(1)}) custom-call(s32[1]{0:T(128)} %bitcast.1.base_ref, f32[1024,128]{1,0:T(8,128)} %fusion.6.raw_ref, bf16[1024,512]{1,0:T(8,128)(2,1)} %bitcast.93, s32[1024,1]{1,0:T(8,128)S(1)} %copy.80.starts_ref, ...), custom_call_target="tpu_custom_call" | custom-call | flops 2000000000 | bytes 40000000 | tf_op jit(solution)/shard_map/pallas_call | solution.py:1210
  501.5 1.4 copy-done.14
  505.2 29.7 %shard_map.409 = (f32[64,1024]{1,0:T(8,128)S(1)}, f32[64,128]{1,0:T(8,128)S(1)}, f32[16,384]{1,0:T(8,128)S(1)}, f32[64,1024]{1,0:T(8,128)S(1)}, bf16[4,128,1152]...) custom-call(bf16[512,1024]{1,0:T(8,128)(2,1)S(1)} %copy-done.23, bf16[4,64,1024]{2,1,0:T(8,128)(2,1)S(1)} %bitcast.80, ...), custom_call_target="tpu_custom_call" | custom-call | bytes 105000000 | tf_op jit(solution)/shard_map/pallas_call | solution.py:238
  537.7 7.5 %shard_map.410 = (bf16[1024,512]{1,0:T(8,128)(2,1)}, f32[8,512]{1,0:T(8,128)S(1)}) custom-call(s32[1]{0:T(128)} %bitcast.1.base_ref, f32[1040,512]{1,0:T(8,128)} %fusion.26.pa_ref, f32[1024,384]{1,0:T(8,128)} %get-tuple-element.173.gx.gx_ref, f32[16,384]{1,0:T(8,128)S(1)} %get-tuple-element.181.rim_x, f32[64,1024]{1,0:T(8,128)S(1)} %get-tuple-element.182.g_bc, ...), custom_call_target="tpu_custom_call" | custom-call | flops 2000000000 | bytes 40000000 | tf_op jit(solution)/shard_map/pallas_call | solution.py:1210
  545.3 5.0 convolution_convert_fusion.1
  551.1 2.9 fusion
  554.2 9.1 %shard_map.411.part = bf16[1024,2048]{1,0:T(8,128)(2,1)S(1)} custom-call(bf16[1024,512]{1,0:T(8,128)(2,1)} %get-tuple-element.185.da_ref, bf16[1024,512]{1,0:T(8,128)(2,1)} %copy-done.60, bf16[1024,128]{1,0:T(8,128)(2,1)} %get-tuple-element.186.raw_ref, bf16[2048,512]{1,0:T(8,128)(2,1)} %all-gather.5.cloned.1.call-done.wa_ref, ...), custom_call_target="tpu_custom_call" | custom-call | flops 2000000000 | bytes 40000000 | tf_op jit(solution)/shard_map/pallas_call | solution.py:1210
  563.4 32.8 %shard_map.412 = (f32[256,2048]{1,0:T(8,128)S(1)}, f32[256,2048]{1,0:T(8,128)S(1)}, f32[16,512]{1,0:T(8,128)S(1)}, bf16[4,128,512]{2,1,0:T(8,128)(2,1)S(1)}, bf16[4,128,512]{2,1,0:T(8,128)(2,1)S(1)}) custom-call(bf16[1024,2048]{1,0:T(8,128)(2,1)S(1)} %shard_map.411.part, f32[128,2048]{1,0:T(8,128)S(1)} %get-tuple-element.231.x_ref, ...), custom_call_target="tpu_custom_call" | custom-call | bytes 140000000 | tf_op jit(solution)/shard_map/pallas_call | solution.py:238
  596.2 1.4 copy-done.12
  601.6 18.8 %shard_map.413 = (bf16[4,128,384]{2,1,0:T(8,128)(2,1)S(1)}, bf16[8,128,128]{2,1,0:T(8,128)(2,1)S(1)}, f32[128,512]{1,0:T(8,128)S(1)}, f32[4,16,128]{2,1,0:T(8,128)S(1)}) custom-call(bf16[512,512]{1,0:T(8,128)(2,1)S(1)} %copy-done.35, f32[16,512]{1,0:T(8,128)S(1)} %get-tuple-element.200.small, f32[4,4,16,128]{3,2,1,0:T(8,128)S(1)} %bitcast.79), custom_call_target="tpu_custom_call" | custom-call | bytes 70000000 | tf_op jit(solution)/shard_map/pallas_call | solution.py:238
  625.5 7.4 %shard_map.414 = (f32[128,1536]{1,0:T(8,128)}, f32[128,1536]{1,0:T(8,128)}, f32[128,512]{1,0:T(8,128)}, f32[128,512]{1,0:T(8,128)}, f32[128,128]{1,0:T(8,128)}, ...) custom-call(s32[1]{0:T(128)} %bitcast.core_ref, ...), custom_call_target="tpu_custom_call" | custom-call | flops 2000000000 | bytes 40000000 | tf_op jit(solution)/shard_map/pallas_call | solution.py:1210
  (243 shorter events, 51.0 us)
Async XLA Ops:
  7.2 34.2 %copy-start.65 = (bf16[128,24]{0,1:T(8,128)(2,1)S(1)}, bf16[128,24]{0,1:T(8,128)(2,1)}, u32[]{:S(2)}) copy-start(bf16[128,24]{0,1:T(8,128)(2,1)} %param.30) | copy-start | bytes 18436
  7.2 70.7 %all-gather.5.cloned.1.call-start = ((), (), s32[]{:S(2)}) async-start(), calls=%async_computation.4 | async-start | bytes 2621440 | tf_op jit(solution)/shard_map/all_gather | solution.py:1311
  22.3 21.1 %copy-start.53 = (f32[2048]{0:T(1024)S(1)}, f32[2048]{0:T(1024)}, u32[]{:S(2)}) copy-start(f32[2048]{0:T(1024)} %param.25) | copy-start | bytes 24580
  22.3 173.8 %all-gather.7.cloned.1.call-start = ((), (), s32[]{:S(2)}) async-start(), calls=%async_computation.5 | async-start | bytes 5242880 | tf_op jit(solution)/shard_map/all_gather | solution.py:1311
  41.3 2.2 copy-start.66
  41.3 232.6 %all-gather.11.cloned.1.call-start = ((), (), s32[]{:S(2)}) async-start(), calls=%async_computation.7 | async-start | bytes 5898240 | tf_op jit(solution)/shard_map/all_gather | solution.py:1311
  74.5 2.1 copy-start.8
  84.5 5.6 copy-start.27
  84.6 5.6 copy-start.28
  84.6 5.6 copy-start.29
  84.6 36.5 %copy-start.67 = (f32[24]{0:T(128)S(1)}, f32[24]{0:T(128)}, u32[]{:S(2)}) copy-start(f32[24]{0:T(128)} %param.42) | copy-start | bytes 292
  84.6 36.6 %copy-start.68 = (f32[24]{0:T(128)S(1)}, f32[24]{0:T(128)}, u32[]{:S(2)}) copy-start(f32[24]{0:T(128)} %param.41) | copy-start | bytes 292
  84.6 36.7 %copy-start.69 = (f32[24]{0:T(128)S(1)}, f32[24]{0:T(128)}, u32[]{:S(2)}) copy-start(f32[24]{0:T(128)} %param.43) | copy-start | bytes 292
  120.9 190.0 %all-gather.9.cloned.1.call-start = ((), (), s32[]{:S(2)}) async-start(), calls=%async_computation.6 | async-start | bytes 1966080 | tf_op jit(solution)/shard_map/all_gather | solution.py:1311
  133.5 11.2 %copy-start.34 = (bf16[4,64,1024]{2,1,0:T(8,128)(2,1)S(1)}, bf16[4,64,1024]{2,1,0:T(8,128)(2,1)}, u32[]{:S(2)}) copy-start(bf16[4,64,1024]{2,1,0:T(8,128)(2,1)} %copy-done.33) | copy-start | bytes 1572868
  188.6 2.0 copy-start.2
  193.3 204.7 %reduce-scatter.5.cloned.1.call-start = ((), (), s32[]{:S(2)}) async-start(), calls=%async_computation.8 | async-start | bytes 5898240 | tf_op jit(solution)/shard_map/reduce_scatter | solution.py:1343
  213.7 9.6 %copy-start.58 = (bf16[2048,1024]{1,0:T(8,128)(2,1)S(1)}, bf16[2048,1024]{1,0:T(8,128)(2,1)}, u32[]{:S(2)}) copy-start(bf16[2048,1024]{1,0:T(8,128)(2,1)} %all-gather.7.cloned.1.call-done.wz_ref) | copy-start | bytes 12582916
  223.3 2.4 copy-start.63
  223.3 2.4 copy-start.52
  270.7 2.0 copy-start.3
  311.0 189.3 %reduce-scatter.7.cloned.1.call-start = ((), (), s32[]{:S(2)}) async-start(), calls=%async_computation.9 | async-start | bytes 4587520 | tf_op jit(solution)/shard_map/reduce_scatter | solution.py:1343
  311.2 11.8 %copy-start.6 = (f32[128,2048]{1,0:T(8,128)S(1)}, f32[128,2048]{1,0:T(8,128)}, u32[]{:S(2)}) copy-start(f32[128,2048]{1,0:T(8,128)} %copy-done.5) | copy-start | bytes 3145732
  369.6 9.4 %copy-start.18 = (f32[128,2048]{1,0:T(8,128)}, f32[128,2048]{1,0:T(8,128)S(1)}, u32[]{:S(2)}) copy-start(f32[128,2048]{1,0:T(8,128)S(1)} %get-tuple-element.187.d_hidden) | copy-start | bytes 3145732
  369.6 9.3 %copy-start.59 = (bf16[2048,1024]{1,0:T(8,128)(2,1)S(1)}, bf16[2048,1024]{1,0:T(8,128)(2,1)}, u32[]{:S(2)}) copy-start(bf16[2048,1024]{1,0:T(8,128)(2,1)} %all-gather.7.cloned.1.call-done.wz_ref) | copy-start | bytes 12582916
  382.6 10.8 %copy-start.64 = (bf16[1024,512]{1,0:T(8,128)(2,1)S(1)}, bf16[1024,512]{1,0:T(8,128)(2,1)}, u32[]{:S(2)}) copy-start(bf16[1024,512]{1,0:T(8,128)(2,1)} %copy-done.63) | copy-start | bytes 3145732
  393.4 2.4 copy-start.57
  395.9 2.4 copy-start.56
  398.0 10.2 %copy-start.62 = (bf16[1024,384]{1,0:T(8,128)(2,1)S(1)}, bf16[1024,384]{1,0:T(8,128)(2,1)}, u32[]{:S(2)}) copy-start(bf16[1024,384]{1,0:T(8,128)(2,1)} %get-tuple-element.161) | copy-start | bytes 2359300
  398.1 152.2 %reduce-scatter.9.cloned.1.call-start = ((), (), s32[]{:S(2)}) async-start(), calls=%async_computation.10 | async-start | bytes 2621440 | tf_op jit(solution)/shard_map/reduce_scatter | solution.py:1343
  410.3 6.0 copy-start.7
  410.3 6.0 copy-start.47
  416.3 2.2 copy-start.4
  418.5 1.7 copy-start.11
  475.1 125.5 %reduce-scatter.11.cloned.1.call-start = ((), (), s32[]{:S(2)}) async-start(), calls=%async_computation.11 | async-start | bytes 2621440 | tf_op jit(solution)/shard_map/reduce_scatter | solution.py:1343
  479.0 21.3 %copy-start.16 = (bf16[512,1152]{1,0:T(8,128)(2,1)S(1)}, bf16[512,1152]{1,0:T(8,128)(2,1)}, u32[]{:S(2)}) copy-start(bf16[512,1152]{1,0:T(8,128)(2,1)} %reduce-scatter.5.cloned.1.call-done.sum_1) | copy-start | bytes 3538948
  479.0 21.3 %copy-start.44 = (f32[64,1024]{1,0:T(8,128)S(1)}, f32[64,1024]{1,0:T(8,128)}, u32[]{:S(2)}) copy-start(f32[64,1024]{1,0:T(8,128)} %get-tuple-element.178.d_silu_bc) | copy-start | bytes 786436
  479.0 66.2 %slice-start = ((s8[4259840]{0:T(1024)(128)(4,1)}), s8[65536]{0:T(1024)(128)(4,1)S(1)}, s32[]{:S(2)}) async-start(s8[4259840]{0:T(1024)(128)(4,1)} %bitcast.76), calls=%async_computation.12 | async-start | bytes 131072
  501.5 1.4 copy-start.14
  505.2 40.1 %slice-start.1 = ((s8[4259840]{0:T(1024)(128)(4,1)}), s8[4194304]{0:T(1024)(128)(4,1)S(1)}, s32[]{:S(2)}) async-start(s8[4259840]{0:T(1024)(128)(4,1)} %bitcast.76), calls=%async_computation.13 | async-start | bytes 8388608
  545.3 5.9 copy-start.61
  554.1 9.2 %copy-start.10 = (bf16[512,896]{1,0:T(8,128)(2,1)S(1)}, bf16[512,896]{1,0:T(8,128)(2,1)}, u32[]{:S(2)}) copy-start(bf16[512,896]{1,0:T(8,128)(2,1)} %reduce-scatter.7.cloned.1.call-done.sum_2.sum_b) | copy-start | bytes 2752516
  554.1 9.2 %copy-start.19 = (f32[128,2048]{1,0:T(8,128)S(1)}, f32[128,2048]{1,0:T(8,128)}, u32[]{:S(2)}) copy-start(f32[128,2048]{1,0:T(8,128)} %copy-done.18) | copy-start | bytes 3145732
  554.1 9.2 %copy-start.21 = (f32[128,2048]{1,0:T(8,128)S(1)}, f32[128,2048]{1,0:T(8,128)}, u32[]{:S(2)}) copy-start(f32[128,2048]{1,0:T(8,128)} %copy-done.20) | copy-start | bytes 3145732
  554.2 9.2 %copy-start.30 = (bf16[512,512]{1,0:T(8,128)(2,1)S(1)}, bf16[512,512]{1,0:T(8,128)(2,1)}, u32[]{:S(2)}) copy-start(bf16[512,512]{1,0:T(8,128)(2,1)} %reduce-scatter.9.cloned.1.call-done.sum_z) | copy-start | bytes 1572868
  620.4 5.1 copy-start.43
  620.4 5.1 copy-start.45
  620.4 12.5 %copy-start.1 = (bf16[128,512]{1,0:T(8,128)(2,1)S(1)}, bf16[128,512]{1,0:T(8,128)(2,1)}, u32[]{:S(2)}) copy-start(bf16[128,512]{1,0:T(8,128)(2,1)} %param.29) | copy-start | bytes 393220
  (32 other events, 31.1 us)
Sparse Core Ops, SparseCore 0:
  22.4 52.6 all-gather.4
  76.7 93.8 all-gather.6
  172.2 101.7 all-gather.10
  275.4 35.5 all-gather.8
  313.1 84.1 reduce-scatter.4
  399.4 81.8 reduce-scatter.6
  484.2 56.6 reduce-scatter.8
  550.4 44.5 reduce-scatter.10

commit v6 on v5

--- a/solution.py
+++ b/solution.py
@@ -235,6 +235,11 @@
 
 
 def call(body, name_id, outs, out_specs, ins, in_specs, scratch, us=20, mib=12):
+    ins = [pltpu.with_memory_space_constraint(v, pltpu.HBM) if s is HBM and v.size > 20000 else v for v, s in zip(ins, in_specs)]
+    if isinstance(outs, tuple):
+        outs = tuple(pltpu.HBM(v.shape, v.dtype) if s is HBM else v for v, s in zip(outs, out_specs))
+    elif out_specs is HBM:
+        outs = pltpu.HBM(outs.shape, outs.dtype)
     return pl.pallas_call(
         body,
         out_shape=outs,
@@ -635,7 +640,7 @@
 
 
 def last_body(planes, sum_a, small, steps, got_x, got_s, sums, got_t, mine, others, t_own, t_far, xs, xr, ss, sr, keep, ls, lr,
-              ts, tr, qs, qr, tk, *spread):
+              ts, tr, qs, qr, tk, gs, gr, gk):
     z, p, c = here()
     pairs = [(d, k) for k in (0, 1) for d in range(G) if d or k]
     greet(*[{"p": ring(p, d), "head": lax.rem(c + k, 2)} for d, k in pairs], *line_partners(z, planes))
@@ -669,8 +674,13 @@
     for d in range(1, planes):
         total = total + others[d - 1]
     mine[...] = total
-    g = Spread(mine, sums, lambda q, k: pl.multiple_of((q * 2 + k) * RIM, RIM), RIM, spread)
-    g.start()
+    place = sums.at[pl.ds(pl.multiple_of((p * 2 + c) * RIM, RIM), RIM)]
+    shares = [
+        rcopy(mine, place, gs.at[k * G + d - 1], gr.at[k * G + d - 1], p=ring(p, d), head=lax.rem(c + k, 2)) for d, k in pairs
+    ]
+    shares.append(pltpu.make_async_copy(mine, place, gk))
+    for copy in shares:
+        copy.start()
     total = steps[z]
     for d in range(1, planes):
         total = total + t_far[d - 1]
@@ -679,10 +689,8 @@
     back.append(pltpu.make_async_copy(t_own.at[p], got_t.at[p], tk))
     for copy in back:
         copy.start()
-    g.pass_on()
-    for copy in copies + back:
+    for copy in copies + back + shares:
         copy.wait()
-    g.finish()
 
 
 def give_body(sizes, core_ref, zq, ob, f1, f2, x_, s_, layer, grad, z_o, x_o, bc_o, q_o, k_o, v_o, o_o, out_o, gate_o, up_o, down_o,
@@ -1119,10 +1127,15 @@
     back_ref[...] = back.astype(bf16)
 
 
-def ffn_grad_body(part, second_ref, low_ref, h_ref, out_ref):
+def ffn_grad_body(part, second_ref, low_ref, h_ref, out_ref, turned):
     two = 2 * part
-    out_ref[:, :two] = mm(second_ref[...], h_ref[:, :two], 0, 0).astype(bf16)
-    out_ref[:, two:] = mm(low_ref[...], h_ref[:, two:], 0, 0).astype(bf16)
+
+    @pl.when(pl.program_id(0) == 0)
+    def _():
+        turned[...] = h_ref[...].T
+
+    out_ref[:, :two] = mm(turned[:two], second_ref[...], 1, 0).astype(bf16).T
+    out_ref[:, two:] = mm(turned[two:], low_ref[...], 1, 0).astype(bf16).T
 
 
 def finish_body(chunks, chan, base_ref, pa_ref, gx_ref, rim_x, g_bc, rim_bc, dkv, starts_ref, taps_ref, cos_ref, sin_ref,
@@ -1464,7 +1477,7 @@
             functools.partial(ffn_body, wide // 3), T // ftile,
             (shape((T, wide), bf16), shape((T, width), bf16), shape((T, width), bf16)),
             (rows_spec(wide), rows_spec(width), rows_spec(width)),
-            (second, out_low, w) + done, [rows_spec(width), rows_spec(width), all_spec(w)] + [rows_spec(width)] * len(done), mib=36, keep=(2,) if done else (),
+            (second, out_low, w) + done, [rows_spec(width), rows_spec(width), all_spec(w)] + [rows_spec(width)] * len(done), mib=36, keep=(1, 2) if done else (),
         )
 
     def ffn_grads(h):
@@ -1473,7 +1486,8 @@
         columns = pl.BlockSpec((T, tile_d), lambda i: (0, i))
         return chunked(
             functools.partial(ffn_grad_body, wide // 3), width // tile_d, shape((width, wide), bf16),
-            pl.BlockSpec((tile_d, wide), lambda i: (i, 0)), (second, out_low, h), [columns, columns, all_spec(h)], mib=24,
+            pl.BlockSpec((tile_d, wide), lambda i: (i, 0)), (second, out_low, h), [columns, columns, all_spec(h)],
+            [pltpu.VMEM((wide, T), bf16)], mib=24,
         )
 
     h1, part_l, part_c = ffn(w1)
@@ -1578,8 +1592,8 @@
          shape((G, 16, rows), f32)), (HBM,) * 4, (sum_a, mine, grad_step), [HBM, VMEM, VMEM],
         [pltpu.VMEM((RIM, lane), f32), pltpu.VMEM((planes - 1, RIM, lane), f32), pltpu.VMEM((G, 16, rows), f32),
          pltpu.VMEM((planes - 1, G, 16, rows), f32), DMA((3,)), DMA((3,)), DMA((2 * G,)), DMA((2 * G,)),
-         DMA((2,)), DMA((planes - 1,)), DMA((planes - 1,)), DMA((planes - 1,)), DMA((planes - 1,)), DMA((3,)), DMA((3,)), DMA(())]
-        + Spread.sems,
+         DMA((2,)), DMA((planes - 1,)), DMA((planes - 1,)), DMA((planes - 1,)), DMA((planes - 1,)), DMA((3,)), DMA((3,)), DMA(()),
+         DMA((2 * G,)), DMA((2 * G,)), DMA(())],
     )
     strip = min(32, rows)
 

time: 649 us -> 640 us (0.986)
  local copies, waits for them, and re-layouts: 61.3 us -> 32.7 us
  waiting for transfers between devices: 8.73 us -> 20.8 us
    unnamed x151 -> x75, local copies, waits for them, and re-layouts: 46.1 us -> 14.2 us
    all_gather x4, waiting for transfers between devices: 8.57 us -> 20.6 us  [gather(): return lax.all_gather(w, 'z', axis=0, tiled=True)]
  transfers between devices with their start and end apart: 8 -> 8, of which waited for: 2 -> 2; matrix products, arithmetic and copies ran while one was open for 10% -> 11% of each run, Pallas kernels for 72% -> 74%
where the time goes in v6:
time: 640 us; the launch traced here: 631 us
  Pallas kernels  503 us (79%)
  matrix products  40.9 us (6%)
  local copies, waits for them, and re-layouts  32.7 us (5%)
  waiting for transfers between devices  20.8 us (3%)
  other arithmetic  16.8 us (3%)
  between operations  15.2 us (2%)
    pallas_call x11, Pallas kernels, call(): pl.pallas_call(body, out_shape=outs, in_specs=in_specs, out_specs=out_spe...  352 us
    pallas_call x14, Pallas kernels, chunked(): pl.pallas_call(body, grid=(chunks,), out_shape=outs, in_specs=in_specs, o...  151 us
    dot_general x9, matrix products, dot(): lax.dot_general(a, b, (((ca,), (cb,)), ((), ())), preferred_element_type=...  40.9 us
    all_gather x4, waiting for transfers between devices, gather(): return lax.all_gather(w, 'z', axis=0, tiled=True)  20.6 us
    unnamed x75, local copies, waits for them, and re-layouts  14.2 us
  transfers between devices with their start and end apart: 8, of which 2 were waited for; matrix products, arithmetic and copies ran while one was open for 11% of the time, Pallas kernels for 74%

profile of v6, /device:TPU:0, one launch (start us, length us, event | category | flops | bytes accessed | tf_op | source)
XLA Modules:
  0.0 630.7 jit_solution(6639961048337106666)
XLA Ops:
  11.2 10.9 %shard_map.391 = bf16[512,512]{1,0:T(8,128)(2,1)} custom-call(bf16[128,1536]{1,0:T(8,128)(2,1)} %x_ref.1, bf16[4,128,128]{2,1,0:T(8,128)(2,1)} %maximum_bitcast_fusion.small_ref), custom_call_target="tpu_custom_call" | custom-call | bytes 70000000 | tf_op jit(solution)/shard_map/pallas_call | solution.py:243
  22.2 15.4 %shard_map.396 = bf16[512,1024]{1,0:T(8,128)(2,1)} custom-call(bf16[128,1536]{1,0:T(8,128)(2,1)} %z_ref.1, bf16[128,512]{1,0:T(8,128)(2,1)} %q_ref.1, bf16[128,1536]{1,0:T(8,128)(2,1)} %out_ref.1, bf16[128,512]{1,0:T(8,128)(2,1)} %o_ref.1), custom_call_target="tpu_custom_call" | custom-call | bytes 70000000 | tf_op jit(solution)/shard_map/pallas_call | solution.py:243
  37.7 2.6 multiply_reduce_fusion
  40.5 32.1 %shard_map.390 = (bf16[1040,2048]{1,0:T(8,128)(2,1)}, s32[4,4,8,256]{3,2,1,0:T(8,128)}, bf16[4,4,16,128]{3,2,1,0:T(8,128)(2,1)}) custom-call(bf16[128,2048]{1,0:T(8,128)(2,1)S(1)} %multiply_convert_fusion.first, s32[8,256]{1,0:T(8,128)S(1)} %broadcast_in_dim.69.docs, bf16[4,16,128]{2,1,0:T(8,128)(2,1)S(1)} %pad.17.steps), custom_call_target="tpu_custom_call" | custom-call | bytes 87500000 | tf_op jit(solution)/shard_map/pallas_call | solution.py:243
  75.5 6.6 %fusion.26.pa_ref = f32[1040,512]{1,0:T(8,128)} fusion(bf16[1040,2048]{1,0:T(8,128)(2,1)} %get-tuple-element.121, bf16[2048,512]{1,0:T(8,128)(2,1)} %all-gather.5.cloned.1.call-done.wa_ref), kind=kOutput, calls=%fused_computation.79 | convolution fusion | flops 2181038080 | bytes 8486912 | tf_op jit(solution)/shard_map/dot_general | solution.py:1236
  82.1 5.5 shard_map.392
  87.7 26.2 %shard_map.393 = (bf16[512,1024]{1,0:T(8,128)(2,1)}, bf16[4,64,1024]{2,1,0:T(8,128)(2,1)}, bf16[512,1152]{1,0:T(8,128)(2,1)}, bf16[512,384]{1,0:T(8,128)(2,1)}) custom-call(bf16[64,1024]{1,0:T(8,128)(2,1)} %get-tuple-element.124.block, bf16[64,1024]{1,0:T(8,128)(2,1)} %get-tuple-element.125.kv, bf16[128,2048]{1,0:T(8,128)(2,1)} %gate_w.1, ...), custom_call_target="tpu_custom_call" | custom-call | bytes 98000000 | tf_op jit(solution)/shard_map/pallas_call | solution.py:243
  116.0 1.9 multiply_sine_fusion
  118.9 1.1 pad_maximum_fusion.2.sin_ref
  120.0 4.3 fusion.6.raw_ref
  124.3 2.3 copy.81
  126.5 11.2 %shard_map.394 = (f32[1024,384]{1,0:T(8,128)}, f32[1024,384]{1,0:T(8,128)}, f32[8,384,256]{2,1,0:T(8,128)}, f32[8,16,128]{2,1,0:T(8,128)S(1)}, bf16[384,256]{1,0:T(8,128)(2,1)}, /*index=5*/f32[8,128]{1,0:T(8,128)S(1)}) custom-call(s32[1]{0:T(128)} %bitcast.1.base_ref, f32[1024,128]{1,0:T(8,128)} %fusion.6.raw_ref, f32[1040,512]{1,0:T(8,128)} %fusion.26.pa_ref, ...), custom_call_target="tpu_custom_call" | custom-call | flops 2000000000 | bytes 40000000 | tf_op jit(solution)/shard_map/pallas_call | solution.py:1223
  137.7 43.2 %shard_map.395 = (bf16[3,384,256]{2,1,0:T(8,128)(2,1)}, f32[3,8,128]{2,1,0:T(8,128)}, bf16[16,64,1024]{2,1,0:T(8,128)(2,1)}, bf16[1024,2048]{1,0:T(8,128)(2,1)}) custom-call(bf16[384,256]{1,0:T(8,128)(2,1)} %get-tuple-element.131.state, f32[8,128]{1,0:T(8,128)S(1)} %get-tuple-element.132.factor, bf16[4,64,1024]{2,1,0:T(8,128)(2,1)} %get-tuple-element.133.lines, ...), custom_call_target="tpu_custom_call" | custom-call | bytes 133000000 | tf_op jit(solution)/shard_map/pallas_call | solution.py:243
  182.8 2.1 fusion.16.before_ref
  184.9 6.5 %fusion.4.z_ref.q_ref = f32[1024,512]{1,0:T(8,128)} fusion(bf16[1040,2048]{1,0:T(8,128)(2,1)} %get-tuple-element.121, bf16[2048,1024]{1,0:T(8,128)(2,1)} %all-gather.7.cloned.1.call-done.wz_ref), kind=kOutput, calls=%fused_computation.9 | convolution fusion | flops 2147483648 | bytes 8388608 | tf_op jit(solution)/shard_map/dot_general | solution.py:1236
  191.4 10.3 %shard_map.397 = (bf16[1024,384]{1,0:T(8,128)(2,1)}, f32[1024,384]{1,0:T(8,128)}) custom-call(s32[1]{0:T(128)} %bitcast.1.base_ref, f32[1024,128]{1,0:T(8,128)} %fusion.6.raw_ref, bf16[1024,512]{1,0:T(8,128)(2,1)} %bitcast.83, s32[1024,1]{1,0:T(8,128)S(1)} %copy.80.starts_ref, f32[1,128]{1,0:T(1,128)S(1)} %get-tuple-element.245.bias_ref, ...), custom_call_target="tpu_custom_call" | custom-call | flops 2000000000 | bytes 40000000 | tf_op jit(solution)/shard_map/pallas_call | solution.py:1223
  201.7 1.2 constant_dynamic-update-slice_fusion.1
  203.0 7.8 %shard_map.398 = (bf16[1024,128]{1,0:T(8,128)(2,1)}, bf16[1024,128]{1,0:T(8,128)(2,1)}, f32[1024,128]{1,0:T(8,128)}, f32[1024,1]{1,0:T(8,128)S(1)}) custom-call(s32[1]{0:T(128)} %bitcast.1.base_ref, s32[4]{0:T(128)S(1)} %slice_reduce_fusion.5.first_ref, f32[1024,512]{1,0:T(8,128)} %fusion.4.z_ref.q_ref, s32[1024,1]{1,0:T(8,128)S(1)} %copy.80.starts_ref, ...), custom_call_target="tpu_custom_call" | custom-call | flops 2000000000 | bytes 40000000 | tf_op jit(solution)/shard_map/pallas_call | solution.py:1223
  210.8 1.2 constant_dynamic-update-slice_fusion
  212.0 2.4 convolution_convert_fusion.part
  214.4 45.5 %shard_map.399 = (f32[128,2048]{1,0:T(8,128)S(1)}, bf16[1024,2048]{1,0:T(8,128)(2,1)}) custom-call(bf16[1024,2048]{1,0:T(8,128)(2,1)S(1)} %convolution_convert_fusion.part, f32[128,2048]{1,0:T(8,128)S(1)} %get-tuple-element.231.x_ref, f32[1,2048]{1,0:T(1,128)S(1)} %bitcast.79), custom_call_target="tpu_custom_call" | custom-call | bytes 175000000 | tf_op jit(solution)/shard_map/pallas_call | solution.py:243
  260.8 12.9 %all-gather.11.cloned.1.call-done.w_ref = bf16[2048,1152]{1,0:T(8,128)(2,1)} async-done(((bf16[512,1152]{1,0:T(8,128)(2,1)}), bf16[2048,1152]{1,0:T(8,128)(2,1)}) %all-gather.11.cloned.1.call-update) | async-done | bytes 4718608 | tf_op jit(solution)/shard_map/all_gather | solution.py:1324
  273.7 16.9 %shard_map.400 = (bf16[1024,1152]{1,0:T(8,128)(2,1)}, bf16[1024,2048]{1,0:T(8,128)(2,1)}, bf16[1024,2048]{1,0:T(8,128)(2,1)}) custom-call(bf16[1024,2048]{1,0:T(8,128)(2,1)} %get-tuple-element.139.second_ref, bf16[1024,2048]{1,0:T(8,128)(2,1)} %get-tuple-element.140.low_ref, bf16[2048,1152]{1,0:T(8,128)(2,1)} %all-gather.11.cloned.1.call-done.w_ref), custom_call_target="tpu_custom_call" | custom-call | flops 2000000000 | bytes 40000000 | tf_op jit(solution)/shard_map/pallas_call | solution.py:1223
  290.6 12.4 %shard_map.401 = bf16[2048,1152]{1,0:T(8,128)(2,1)} custom-call(bf16[1024,2048]{1,0:T(8,128)(2,1)} %get-tuple-element.139.second_ref, bf16[1024,2048]{1,0:T(8,128)(2,1)} %get-tuple-element.140.low_ref, bf16[1024,1152]{1,0:T(8,128)(2,1)} %get-tuple-element.143.h_ref), custom_call_target="tpu_custom_call" | custom-call | flops 2000000000 | bytes 40000000 | tf_op jit(solution)/shard_map/pallas_call | solution.py:1223
  303.0 7.7 %all-gather.9.cloned.1.call-done.w_ref = bf16[2048,384]{1,0:T(8,128)(2,1)} async-done(((bf16[512,384]{1,0:T(8,128)(2,1)}), bf16[2048,384]{1,0:T(8,128)(2,1)}) %all-gather.9.cloned.1.call-update) | async-done | bytes 1572880 | tf_op jit(solution)/shard_map/all_gather | solution.py:1324
  311.0 11.0 %shard_map.402 = (bf16[1024,384]{1,0:T(8,128)(2,1)}, bf16[1024,2048]{1,0:T(8,128)(2,1)S(1)}, bf16[1024,2048]{1,0:T(8,128)(2,1)S(1)}) custom-call(bf16[1024,2048]{1,0:T(8,128)(2,1)} %get-tuple-element.139.second_ref, bf16[1024,2048]{1,0:T(8,128)(2,1)} %get-tuple-element.140.low_ref, bf16[2048,384]{1,0:T(8,128)(2,1)} %all-gather.9.cloned.1.call-done.w_ref, ...), custom_call_target="tpu_custom_call" | custom-call | flops 2000000000 | bytes 40000000 | tf_op jit(solution)/shard_map/pallas_call | solution.py:1223
  322.0 47.2 %shard_map.403 = (f32[128,2048]{1,0:T(8,128)S(1)}, f32[8,2048]{1,0:T(8,128)S(1)}, bf16[1024,2048]{1,0:T(8,128)(2,1)}) custom-call(bf16[1024,2048]{1,0:T(8,128)(2,1)S(1)} %get-tuple-element.148.part, f32[128,2048]{1,0:T(8,128)S(1)} %copy-done.5, f32[128,2048]{1,0:T(8,128)S(1)} %get-tuple-element.243.cot, f32[1,2048]{1,0:T(1,128)S(1)} %bitcast.80), custom_call_target="tpu_custom_call" | custom-call | bytes 175000000 | tf_op jit(solution)/shard_map/pallas_call | solution.py:243
  370.2 9.8 %shard_map.405 = bf16[2048,384]{1,0:T(8,128)(2,1)} custom-call(bf16[1024,2048]{1,0:T(8,128)(2,1)} %get-tuple-element.139.second_ref, bf16[1024,2048]{1,0:T(8,128)(2,1)} %get-tuple-element.140.low_ref, bf16[1024,384]{1,0:T(8,128)(2,1)} %get-tuple-element.157.h_ref), custom_call_target="tpu_custom_call" | custom-call | flops 2000000000 | bytes 40000000 | tf_op jit(solution)/shard_map/pallas_call | solution.py:1223
  380.1 3.6 fusion.9.d_ref
  383.7 10.9 %shard_map.404 = (bf16[1024,384]{1,0:T(8,128)(2,1)}, f32[1024,384]{1,0:T(8,128)}, f32[8,384,256]{2,1,0:T(8,128)}, f32[8,8,128]{2,1,0:T(8,128)S(1)}, bf16[384,256]{1,0:T(8,128)(2,1)}, /*index=5*/f32[8,384]{1,0:T(8,128)S(1)}) custom-call(s32[1]{0:T(128)} %bitcast.1.base_ref, f32[1024,128]{1,0:T(8,128)} %fusion.6.raw_ref, bf16[1024,512]{1,0:T(8,128)(2,1)} %bitcast.84, ...), custom_call_target="tpu_custom_call" | custom-call | flops 2000000000 | bytes 40000000 | tf_op jit(solution)/shard_map/pallas_call | solution.py:1223
  394.7 2.4 convolution_convert_fusion.3
  397.1 2.1 pad_maximum_fusion
  399.5 10.0 %shard_map.406 = (bf16[1024,128]{1,0:T(8,128)(2,1)}, bf16[4,4,64,1024]{3,2,1,0:T(8,128)(2,1)}) custom-call(s32[1]{0:T(128)} %bitcast.1.base_ref, s32[4]{0:T(128)S(1)} %slice_reduce_fusion.5.first_ref, bf16[1024,128]{1,0:T(8,128)(2,1)} %get-tuple-element.162.query_ref, s32[1024,1]{1,0:T(8,128)S(1)} %copy.80.starts_ref, ...), custom_call_target="tpu_custom_call" | custom-call | flops 2000000000 | bytes 40000000 | tf_op jit(solution)/shard_map/pallas_call | solution.py:1223
  411.6 6.0 convolution_convert_fusion.2
  417.5 2.2 copy-done.3
  419.8 1.6 copy-done.7
  421.4 49.7 %shard_map.407 = (bf16[3,384,256]{2,1,0:T(8,128)(2,1)}, f32[3,8,128]{2,1,0:T(8,128)}, bf16[256,1024]{1,0:T(8,128)(2,1)S(1)}, f32[128,2048]{1,0:T(8,128)S(1)}) custom-call(bf16[384,256]{1,0:T(8,128)(2,1)} %get-tuple-element.166.state, f32[8,128]{1,0:T(8,128)S(1)} %get-tuple-element.132.factor, bf16[1024,1024]{1,0:T(8,128)(2,1)S(1)} %bitcast.76, ...), custom_call_target="tpu_custom_call" | custom-call | bytes 157500000 | tf_op jit(solution)/shard_map/pallas_call | solution.py:243
  474.6 2.1 fusion.12.after_ref
  476.6 21.2 %shard_map.408 = (f32[1024,384]{1,0:T(8,128)}, bf16[512,1024]{1,0:T(8,128)(2,1)}, bf16[1024,128]{1,0:T(8,128)(2,1)}, f32[8,128]{1,0:T(8,128)S(1)}) custom-call(s32[1]{0:T(128)} %bitcast.1.base_ref, f32[1024,128]{1,0:T(8,128)} %fusion.6.raw_ref, bf16[1024,512]{1,0:T(8,128)(2,1)} %bitcast.85, s32[1024,1]{1,0:T(8,128)S(1)} %copy.80.starts_ref, ...), custom_call_target="tpu_custom_call" | custom-call | flops 2000000000 | bytes 40000000 | tf_op jit(solution)/shard_map/pallas_call | solution.py:1223
  497.9 1.2 copy-done.12
  499.1 29.5 %shard_map.409 = (f32[64,1024]{1,0:T(8,128)S(1)}, f32[64,128]{1,0:T(8,128)S(1)}, f32[16,384]{1,0:T(8,128)S(1)}, f32[64,1024]{1,0:T(8,128)S(1)}, bf16[4,128,1152]...) custom-call(bf16[512,1024]{1,0:T(8,128)(2,1)S(1)} %copy-done.12, bf16[4,64,1024]{2,1,0:T(8,128)(2,1)S(1)} %bitcast.78, ...), custom_call_target="tpu_custom_call" | custom-call | bytes 105000000 | tf_op jit(solution)/shard_map/pallas_call | solution.py:243
  528.6 7.6 %shard_map.410 = (bf16[1024,512]{1,0:T(8,128)(2,1)}, f32[8,512]{1,0:T(8,128)S(1)}) custom-call(s32[1]{0:T(128)} %bitcast.1.base_ref, f32[1040,512]{1,0:T(8,128)} %fusion.26.pa_ref, f32[1024,384]{1,0:T(8,128)} %get-tuple-element.173.gx.gx_ref, f32[16,384]{1,0:T(8,128)S(1)} %get-tuple-element.181.rim_x, f32[64,1024]{1,0:T(8,128)S(1)} %get-tuple-element.182.g_bc, ...), custom_call_target="tpu_custom_call" | custom-call | flops 2000000000 | bytes 40000000 | tf_op jit(solution)/shard_map/pallas_call | solution.py:1223
  536.2 6.3 convolution_convert_fusion.1
  543.3 2.9 fusion
  546.4 9.1 %shard_map.411.part = bf16[1024,2048]{1,0:T(8,128)(2,1)S(1)} custom-call(bf16[1024,512]{1,0:T(8,128)(2,1)} %get-tuple-element.185.da_ref, bf16[1024,512]{1,0:T(8,128)(2,1)} %copy-done.21, bf16[1024,128]{1,0:T(8,128)(2,1)} %get-tuple-element.186.raw_ref, bf16[2048,512]{1,0:T(8,128)(2,1)} %all-gather.5.cloned.1.call-done.wa_ref, ...), custom_call_target="tpu_custom_call" | custom-call | flops 2000000000 | bytes 40000000 | tf_op jit(solution)/shard_map/pallas_call | solution.py:1223
  555.5 33.7 %shard_map.412 = (f32[256,2048]{1,0:T(8,128)}, f32[256,2048]{1,0:T(8,128)}, f32[16,512]{1,0:T(8,128)S(1)}, bf16[4,128,512]{2,1,0:T(8,128)(2,1)}, bf16[4,128,512]{2,1,0:T(8,128)(2,1)}) custom-call(bf16[1024,2048]{1,0:T(8,128)(2,1)S(1)} %shard_map.411.part, f32[128,2048]{1,0:T(8,128)S(1)} %get-tuple-element.231.x_ref, f32[128,2048]{1,0:T(8,128)S(1)} %copy-done.9, ...), custom_call_target="tpu_custom_call" | custom-call | bytes 140000000 | tf_op jit(solution)/shard_map/pallas_call | solution.py:243
  589.2 18.6 %shard_map.413 = (bf16[4,128,384]{2,1,0:T(8,128)(2,1)}, bf16[8,128,128]{2,1,0:T(8,128)(2,1)}, f32[128,512]{1,0:T(8,128)}, f32[4,16,128]{2,1,0:T(8,128)}) custom-call(bf16[512,512]{1,0:T(8,128)(2,1)} %reduce-scatter.11.cloned.1.call-done.sum_a, f32[16,512]{1,0:T(8,128)S(1)} %get-tuple-element.200.small, f32[4,4,16,128]{3,2,1,0:T(8,128)S(1)} %bitcast.77), custom_call_target="tpu_custom_call" | custom-call | bytes 70000000 | tf_op jit(solution)/shard_map/pallas_call | solution.py:243
  616.1 7.4 %shard_map.414 = (f32[128,1536]{1,0:T(8,128)}, f32[128,1536]{1,0:T(8,128)}, f32[128,512]{1,0:T(8,128)}, f32[128,512]{1,0:T(8,128)}, f32[128,128]{1,0:T(8,128)}, ...) custom-call(s32[1]{0:T(128)} %bitcast.core_ref, ...), custom_call_target="tpu_custom_call" | custom-call | flops 2000000000 | bytes 40000000 | tf_op jit(solution)/shard_map/pallas_call | solution.py:1223
  (166 shorter events, 29.4 us)
Async XLA Ops:
  7.2 0.9 copy-start
  7.2 30.5 %copy-start.28 = (bf16[128,24]{0,1:T(8,128)(2,1)S(1)}, bf16[128,24]{0,1:T(8,128)(2,1)}, u32[]{:S(2)}) copy-start(bf16[128,24]{0,1:T(8,128)(2,1)} %param.30) | copy-start | bytes 18436
  7.2 68.3 %all-gather.5.cloned.1.call-start = ((), (), s32[]{:S(2)}) async-start(), calls=%async_computation.4 | async-start | bytes 2621440 | tf_op jit(solution)/shard_map/all_gather | solution.py:1324
  22.1 18.2 %copy-start.15 = (f32[2048]{0:T(1024)S(1)}, f32[2048]{0:T(1024)}, u32[]{:S(2)}) copy-start(f32[2048]{0:T(1024)} %param.25) | copy-start | bytes 24580
  22.2 162.7 %all-gather.7.cloned.1.call-start = ((), (), s32[]{:S(2)}) async-start(), calls=%async_computation.5 | async-start | bytes 5242880 | tf_op jit(solution)/shard_map/all_gather | solution.py:1324
  37.6 2.9 copy-start.29
  37.6 236.1 %all-gather.11.cloned.1.call-start = ((), (), s32[]{:S(2)}) async-start(), calls=%async_computation.7 | async-start | bytes 5898240 | tf_op jit(solution)/shard_map/all_gather | solution.py:1324
  73.5 0.6 copy-start.26
  82.1 31.8 %copy-start.27 = (bf16[4,4,16,128]{3,2,1,0:T(8,128)(2,1)S(1)}, bf16[4,4,16,128]{3,2,1,0:T(8,128)(2,1)}, u32[]{:S(2)}) copy-start(bf16[4,4,16,128]{3,2,1,0:T(8,128)(2,1)} %get-tuple-element.122) | copy-start | bytes 196612
  82.1 31.9 %copy-start.31 = (f32[24]{0:T(128)S(1)}, f32[24]{0:T(128)}, u32[]{:S(2)}) copy-start(f32[24]{0:T(128)} %param.42) | copy-start | bytes 292
  82.1 32.0 %copy-start.32 = (f32[24]{0:T(128)S(1)}, f32[24]{0:T(128)}, u32[]{:S(2)}) copy-start(f32[24]{0:T(128)} %param.41) | copy-start | bytes 292
  82.1 32.1 %copy-start.33 = (f32[24]{0:T(128)S(1)}, f32[24]{0:T(128)}, u32[]{:S(2)}) copy-start(f32[24]{0:T(128)} %param.43) | copy-start | bytes 292
  113.9 196.8 %all-gather.9.cloned.1.call-start = ((), (), s32[]{:S(2)}) async-start(), calls=%async_computation.6 | async-start | bytes 1966080 | tf_op jit(solution)/shard_map/all_gather | solution.py:1324
  182.2 217.0 %reduce-scatter.5.cloned.1.call-start = ((), (), s32[]{:S(2)}) async-start(), calls=%async_computation.8 | async-start | bytes 5898240 | tf_op jit(solution)/shard_map/reduce_scatter | solution.py:1356
  202.9 9.0 %copy-start.19 = (bf16[2048,1024]{1,0:T(8,128)(2,1)S(1)}, bf16[2048,1024]{1,0:T(8,128)(2,1)}, u32[]{:S(2)}) copy-start(bf16[2048,1024]{1,0:T(8,128)(2,1)} %all-gather.7.cloned.1.call-done.wz_ref) | copy-start | bytes 12582916
  210.8 3.6 copy-start.16
  212.0 2.4 copy-start.24
  212.0 2.4 copy-start.14
  259.9 1.0 copy-start.4
  310.7 187.1 %reduce-scatter.7.cloned.1.call-start = ((), (), s32[]{:S(2)}) async-start(), calls=%async_computation.9 | async-start | bytes 4587520 | tf_op jit(solution)/shard_map/reduce_scatter | solution.py:1356
  311.0 11.0 %copy-start.5 = (f32[128,2048]{1,0:T(8,128)S(1)}, f32[128,2048]{1,0:T(8,128)}, u32[]{:S(2)}) copy-start(f32[128,2048]{1,0:T(8,128)} %copy-done.4) | copy-start | bytes 3145732
  322.0 58.1 %copy-start.2 = (bf16[1024,2048]{1,0:T(8,128)(2,1)}, bf16[1024,2048]{1,0:T(8,128)(2,1)S(1)}, u32[]{:S(2)}) copy-start(bf16[1024,2048]{1,0:T(8,128)(2,1)S(1)} %get-tuple-element.168.part) | copy-start | bytes 12582916
  369.2 1.0 copy-start.8
  370.2 9.8 %copy-start.20 = (bf16[2048,1024]{1,0:T(8,128)(2,1)S(1)}, bf16[2048,1024]{1,0:T(8,128)(2,1)}, u32[]{:S(2)}) copy-start(bf16[2048,1024]{1,0:T(8,128)(2,1)} %all-gather.7.cloned.1.call-done.wz_ref) | copy-start | bytes 12582916
  370.2 9.8 %copy-start.30 = (bf16[1024,2048]{1,0:T(8,128)(2,1)S(1)}, bf16[1024,2048]{1,0:T(8,128)(2,1)}, u32[]{:S(2)}) copy-start(bf16[1024,2048]{1,0:T(8,128)(2,1)} %get-tuple-element.151) | copy-start | bytes 12582916
  383.7 10.9 %copy-start.25 = (bf16[1024,512]{1,0:T(8,128)(2,1)S(1)}, bf16[1024,512]{1,0:T(8,128)(2,1)}, u32[]{:S(2)}) copy-start(bf16[1024,512]{1,0:T(8,128)(2,1)} %copy-done.24) | copy-start | bytes 3145732
  394.6 2.4 copy-start.18
  397.1 2.4 copy-start.17
  399.2 143.2 %reduce-scatter.9.cloned.1.call-start = ((), (), s32[]{:S(2)}) async-start(), calls=%async_computation.10 | async-start | bytes 2621440 | tf_op jit(solution)/shard_map/reduce_scatter | solution.py:1356
  399.5 10.0 %copy-start.23 = (bf16[1024,384]{1,0:T(8,128)(2,1)S(1)}, bf16[1024,384]{1,0:T(8,128)(2,1)}, u32[]{:S(2)}) copy-start(bf16[1024,384]{1,0:T(8,128)(2,1)} %get-tuple-element.161) | copy-start | bytes 2359300
  410.6 1.0 copy-start.21
  411.6 6.0 copy-start.6
  417.5 2.2 copy-start.3
  419.8 1.6 copy-start.7
  471.1 1.0 copy-start.10
  472.1 117.1 %reduce-scatter.11.cloned.1.call-start = ((), (), s32[]{:S(2)}) async-start(), calls=%async_computation.11 | async-start | bytes 2621440 | tf_op jit(solution)/shard_map/reduce_scatter | solution.py:1356
  476.6 21.2 %copy-start.13 = (f32[64,1024]{1,0:T(8,128)S(1)}, f32[64,1024]{1,0:T(8,128)}, u32[]{:S(2)}) copy-start(f32[64,1024]{1,0:T(8,128)} %get-tuple-element.178.d_silu_bc) | copy-start | bytes 786436
  497.8 1.2 copy-start.12
  536.2 7.1 %copy-start.22 = (bf16[1024,128]{1,0:T(8,128)(2,1)S(1)}, bf16[1024,128]{1,0:T(8,128)(2,1)}, u32[]{:S(2)}) copy-start(bf16[1024,128]{1,0:T(8,128)(2,1)} %get-tuple-element.186.raw_ref) | copy-start | bytes 786436
  546.3 9.1 %copy-start.9 = (f32[128,2048]{1,0:T(8,128)S(1)}, f32[128,2048]{1,0:T(8,128)}, u32[]{:S(2)}) copy-start(f32[128,2048]{1,0:T(8,128)} %copy-done.8) | copy-start | bytes 3145732
  546.3 9.1 %copy-start.11 = (f32[128,2048]{1,0:T(8,128)S(1)}, f32[128,2048]{1,0:T(8,128)}, u32[]{:S(2)}) copy-start(f32[128,2048]{1,0:T(8,128)} %copy-done.10) | copy-start | bytes 3145732
  607.8 15.8 %copy-start.1 = (bf16[128,512]{1,0:T(8,128)(2,1)S(1)}, bf16[128,512]{1,0:T(8,128)(2,1)}, u32[]{:S(2)}) copy-start(bf16[128,512]{1,0:T(8,128)(2,1)} %param.29) | copy-start | bytes 393220
Sparse Core Ops, SparseCore 0:
  22.3 52.6 all-gather.4
  76.6 96.6 all-gather.6
  174.8 98.8 all-gather.10
  275.1 35.5 all-gather.8
  312.9 84.1 reduce-scatter.4
  399.3 81.7 reduce-scatter.6
  484.0 56.5 reduce-scatter.8
  543.5 44.6 reduce-scatter.10

commit v7 on v6

--- a/solution.py
+++ b/solution.py
@@ -571,6 +571,21 @@
         dbc.at[pl.ds(pl.multiple_of((1 - c) * G * rows, 16), G * rows)], cx, xs, xr, head=1 - c
     )
     across.start()
+    grads = list(enumerate(((sum_1, got_1), (sum_2, got_2))))
+    wide = got_1.shape[1]
+
+    def rows_of(q):
+        return pl.ds(pl.multiple_of(q * wide, 16), wide)
+
+    w_over = [
+        rcopy(have.at[rows_of(ring(p, d)), pl.ds(0, got.shape[2])], got.at[p], ws.at[i, d - 1], wr.at[i, d - 1], p=ring(p, d))
+        for i, (have, got) in grads for d in (1, 2, 3)
+    ]
+    w_own = [
+        pltpu.make_async_copy(have.at[rows_of(p), pl.ds(0, got.shape[2])], got.at[p], wk.at[i]) for i, (have, got) in grads
+    ]
+    for copy in w_over[3:] + w_own:
+        copy.start()
 
     def kv_down(d):
         to = lax.rem(z - d + planes, planes)
@@ -583,17 +598,6 @@
 
     across.wait_recv()
     bc_over = []
-    grads = list(enumerate(((sum_1, got_1), (sum_2, got_2))))
-    wide = got_1.shape[1]
-
-    def rows_of(q):
-        return pl.ds(pl.multiple_of(q * wide, 16), wide)
-
-    w_over = [
-        rcopy(have.at[rows_of(ring(p, d)), pl.ds(0, got.shape[2])], got.at[p], ws.at[i, d - 1], wr.at[i, d - 1], p=ring(p, d))
-        for i, (have, got) in grads for d in (1, 2, 3)
-    ]
-    w_own = [pltpu.make_async_copy(have.at[rows_of(p), pl.ds(0, got.shape[2])], got.at[p], wk.at[i]) for i, (have, got) in grads]
     for d in (1, 2, 3, 0):
         q = ring(p, d)
         own = dbc[pl.ds(pl.multiple_of((c * G + q) * rows, 16), rows)].astype(f32)
@@ -604,7 +608,7 @@
             bc_over[-1].start()
         else:
             acc[...] = own
-    for copy in w_over + w_own:
+    for copy in w_over[:3]:
         copy.start()
     for copy in bc_over:
         copy.wait_recv()
@@ -693,24 +697,27 @@
         copy.wait()
 
 
-def give_body(sizes, core_ref, zq, ob, f1, f2, x_, s_, layer, grad, z_o, x_o, bc_o, q_o, k_o, v_o, o_o, out_o, gate_o, up_o, down_o,
-              layer_o, grad_o):
+def give_ffn_body(f1, f2, *outs):
+    units = (f1.shape[2] + f2.shape[2]) // 3
+    for p in range(G):
+        for i, ref in enumerate(outs):
+            for got, skip in ((f1, 0), (f2, f1.shape[2] // 3)):
+                part = got.shape[2] // 3
+                at = p * units + skip
+                ref[:, at : at + part] = got[p, :, i * part : (i + 1) * part].astype(f32)
+
+
+def give_body(sizes, core_ref, zq, ob, x_, s_, layer, grad, z_o, x_o, bc_o, q_o, k_o, v_o, o_o, out_o, layer_o, grad_o):
     bcs, quarter = sizes
     layer_o[...] = layer[...]
     grad_o[...] = grad[...]
-    chan, units = x_.shape[2], (f1.shape[2] + f2.shape[2]) // 3
+    chan = x_.shape[2]
     for p in range(G):
         for ref, got, first, cols in (
             (z_o, zq, 0, chan), (q_o, zq, chan, HD), (out_o, ob, 0, chan), (o_o, ob, chan, HD),
             (x_o, x_, 0, chan),
         ):
             ref[:, p * cols : (p + 1) * cols] = got[p, :, first : first + cols].astype(f32)
-
-        for i, ref in enumerate((gate_o, up_o, down_o)):
-            for got, skip in ((f1, 0), (f2, f1.shape[2] // 3)):
-                part = got.shape[2] // 3
-                at = p * units + skip
-                ref[:, at : at + part] = got[p, :, i * part : (i + 1) * part].astype(f32)
 
     def place(first, cols, target):
         i = iota((128, 128), 0) - first
@@ -741,8 +748,14 @@
     return lax.dot_general(a.astype(bf16), b.astype(bf16), (((ca,), (cb,)), ((), ())), preferred_element_type=f32)
 
 
-def mm_exact(a, b, ca, cb):
-    return lax.dot_general(a, b, (((ca,), (cb,)), ((), ())), precision=highest, preferred_element_type=f32)
+def mm_pieces(a, b, ca, cb, pieces, right=False):
+    rest, total = (b if right else a), None
+    for _ in range(pieces):
+        piece = rest.astype(bf16)
+        rest = rest - piece.astype(f32)
+        part = mm(a, piece, ca, cb) if right else mm(piece, b, ca, cb)
+        total = part if total is None else total + part
+    return total
 
 
 def iota(dims, axis):
@@ -762,7 +775,7 @@
     step = jnp.where(lane < heads, soft(raw + bias), 0.0)
     log_decay = -jnp.exp(rates) * step
     lower = (iota((CHUNK, CHUNK), 0) >= iota((CHUNK, CHUNK), 1)).astype(f32)
-    return step, log_decay, mm_exact(lower, log_decay, 1, 0)
+    return step, log_decay, mm_pieces(lower, log_decay, 1, 0, 3, True)
 
 
 def pair_of(v, pair):
@@ -780,13 +793,13 @@
 
 def head_means(v):
     same = (iota((128, 128), 0) // P_SIZE == iota((128, 128), 1) // P_SIZE).astype(f32) / P_SIZE
-    return jnp.concatenate([mm_exact(lanes(v, k), same, 1, 0) for k in range(v.shape[1] // 128)], axis=1)
+    return jnp.concatenate([mm_pieces(lanes(v, k), same, 1, 0, 2) for k in range(v.shape[1] // 128)], axis=1)
 
 
 def head_sums(v, heads):
     chan = v.shape[1]
     pick = (iota((chan, 128), 0) // P_SIZE == iota((chan, 128), 1)).astype(f32)
-    return mm_exact(v, pick, 1, 0)
+    return mm_pieces(v, pick, 1, 0, 3)
 
 
 def scale_rows(v, factor, heads):
@@ -991,7 +1004,7 @@
     kept = head_sums_t(d_state * state_in, heads)
     whole = decay_in[CHUNK - 1 :] * kept + jnp.sum(closes, axis=0, keepdims=True)
     upper = (iota((CHUNK, CHUNK), 0) <= iota((CHUNK, CHUNK), 1)).astype(f32)
-    d_la = mm_exact(upper, d_cs, 1, 0) + whole
+    d_la = mm_pieces(upper, d_cs, 1, 0, 3, True) + whole
     d_step = head_sums(d_driven * x, heads)
     d_raw = (d_step - jnp.exp(rates_ref[...]) * d_la) * sig(raw + bias_ref[...])
     d_raw = jnp.where(iota((CHUNK, 128), 1) < heads, d_raw, 0.0)
@@ -1008,7 +1021,7 @@
     i, j = (iota((HD, HD), 1), iota((HD, HD), 0)) if back else (iota((HD, HD), 0), iota((HD, HD), 1))
     half, rest = i // (HD // 2), i % (HD // 2)
     to = (rest // quarter) * 2 * quarter + half * quarter + rest % quarter
-    return mm_exact(v, (to == j).astype(f32), 1, 0)
+    return mm_pieces(v, (to == j).astype(f32), 1, 0, 2 if back else 1)
 
 
 def keys_of(kv_ref, begin, size, tokens):
@@ -1127,15 +1140,19 @@
     back_ref[...] = back.astype(bf16)
 
 
-def ffn_grad_body(part, second_ref, low_ref, h_ref, out_ref, turned):
-    two = 2 * part
+def token_grad_body(widths, *refs):
+    count = len(widths)
+    tokens, narrow, out_ref, turned = refs[:count], refs[count : 2 * count], refs[2 * count], refs[2 * count + 1]
+    at = [sum(widths[:i]) for i in range(count)]
 
     @pl.when(pl.program_id(0) == 0)
     def _():
-        turned[...] = h_ref[...].T
-
-    out_ref[:, :two] = mm(turned[:two], second_ref[...], 1, 0).astype(bf16).T
-    out_ref[:, two:] = mm(turned[two:], low_ref[...], 1, 0).astype(bf16).T
+        for first, n, ref in zip(at, widths, narrow):
+            turned[first : first + n] = ref[...].T
+
+    for first, n, ref in zip(at, widths, tokens):
+        rows = ref[ref.shape[0] - turned.shape[1] :]
+        out_ref[:, first : first + n] = mm(turned[first : first + n], rows, 1, 0).astype(bf16).T
 
 
 def finish_body(chunks, chan, base_ref, pa_ref, gx_ref, rim_x, g_bc, rim_bc, dkv, starts_ref, taps_ref, cos_ref, sin_ref,
@@ -1156,8 +1173,8 @@
     def put(first):
         return (iota((rows, 128), 1) == iota((rows, 128), 0) + first).astype(f32)
 
-    bc_here = mm_exact(g_bc[:, here_], put(0), 0, 0)
-    bc_next = mm_exact(jnp.where(last, rim_bc[...], g_bc[:, next_]), put(0), 0, 0)[:8]
+    bc_here = mm_pieces(g_bc[:, here_], put(0), 0, 0, 3)
+    bc_next = mm_pieces(jnp.where(last, rim_bc[...], g_bc[:, next_]), put(0), 0, 0, 3)[:8]
     gx_next = jnp.where(last, rim_x[:8], gx_ref[pl.ds(pl.multiple_of(ahead_at, 8), 8)])
     longer = jnp.concatenate([
         jnp.concatenate([gx_ref[here_], bc_here], axis=1), jnp.concatenate([gx_next, bc_next], axis=1)
@@ -1480,15 +1497,21 @@
             (second, out_low, w) + done, [rows_spec(width), rows_spec(width), all_spec(w)] + [rows_spec(width)] * len(done), mib=36, keep=(1, 2) if done else (),
         )
 
-    def ffn_grads(h):
-        wide = h.shape[1]
-        tile_d = math.gcd(256, width)
-        columns = pl.BlockSpec((T, tile_d), lambda i: (0, i))
+    def token_grads(*groups):
+        tile_d = math.gcd(512, width)
+        widths = tuple(n for *_, n in groups)
         return chunked(
-            functools.partial(ffn_grad_body, wide // 3), width // tile_d, shape((width, wide), bf16),
-            pl.BlockSpec((tile_d, wide), lambda i: (i, 0)), (second, out_low, h), [columns, columns, all_spec(h)],
-            [pltpu.VMEM((wide, T), bf16)], mib=24,
+            functools.partial(token_grad_body, widths), width // tile_d, shape((width, sum(widths)), bf16),
+            pl.BlockSpec((tile_d, sum(widths)), lambda i: (i, 0)),
+            tuple(g[0] for g in groups) + tuple(g[1] for g in groups),
+            [pl.BlockSpec((g[0].shape[0], tile_d), lambda i: (0, i)) for g in groups]
+            + [pl.BlockSpec((T, n), lambda i, at=at: (0, at)) for _, _, at, n in groups],
+            [pltpu.VMEM((sum(widths), T), bf16)], mib=32,
         )
+
+    def ffn_grads(h, *more):
+        n = h.shape[1] // 3
+        return token_grads((second, h, 0, 2 * n), (out_low, h, 2, n), *more)
 
     h1, part_l, part_c = ffn(w1)
     grad_1 = ffn_grads(h1)
@@ -1500,8 +1523,7 @@
         (part_c, hidden, cot_own, mixer_row(ffn_gain)), [VMEM] * 4, collect, us=50,
     )
     h2, branch = lax.optimization_barrier((h2, branch))
-    grad_2 = ffn_grads(h2)
-    grad_2b = jnp.concatenate([grad_2, dot(branch, both_low, 0, 0).astype(bf16)], axis=1)
+    grad_2b = ffn_grads(h2, (branch, both_low, 0, chan + HD))
     d_both = dot(branch, wb, 1, 0)
 
     back, _, back_stack = specs(True)
@@ -1556,6 +1578,19 @@
          pltpu.VMEM((planes - 1, kvr, T), bf16), pltpu.VMEM((bcs, T), f32), DMA(()), DMA(()), DMA((3,)), DMA((3,)),
          DMA((planes - 1,)), DMA((planes - 1,)), DMA((2,)), DMA((2,)), DMA((2, 3)), DMA((2, 3)), DMA((2,))], us=30,
     )
+    strip = min(32, rows)
+
+    def got(v):
+        return pl.BlockSpec((v.shape[0], strip, v.shape[2]), lambda c: (0, c, 0))
+
+    def given(cols):
+        return pl.BlockSpec((strip, cols), lambda c: (c, 0))
+
+    ffn_out = chunked(
+        give_ffn_body, rows // strip, (shape((rows, G * units), f32),) * 3, (given(G * units),) * 3,
+        (got_1, got_2), [got(got_1), got(got_2)], mib=24,
+    )
+    gx, *ffn_out = lax.optimization_barrier((gx, *ffn_out))
     starts_long = jnp.concatenate([all_starts, jnp.full((8,), total_tokens, jnp.int32)])
     starts_long = lax.dynamic_slice_in_dim(starts_long, offset, T + 8, 0)[:, None]
     taps_both = jnp.concatenate([taps_inner, taps_pair], axis=1)
@@ -1595,19 +1630,10 @@
          DMA((2,)), DMA((planes - 1,)), DMA((planes - 1,)), DMA((planes - 1,)), DMA((planes - 1,)), DMA((3,)), DMA((3,)), DMA(()),
          DMA((2 * G,)), DMA((2 * G,)), DMA(())],
     )
-    strip = min(32, rows)
-
-    def got(v):
-        return pl.BlockSpec((v.shape[0], strip, v.shape[2]), lambda c: (0, c, 0))
-
-    def given(cols):
-        return pl.BlockSpec((strip, cols), lambda c: (c, 0))
-
     widths = [w.shape[1] for w in (
         z_weight, x_weight, bc_weight, q_weight, k_weight, v_weight, o_weight, out_weight,
-        gate_weight, up_weight, down_weight,
     )]
-    gathered = (got_z, got_b, got_1, got_2, got_x, got_s)
+    gathered = (got_z, got_b, got_x, got_s)
     steps_ = rows // strip
     moved = pl.BlockSpec((tokens // steps_, width), lambda c: (c, 0))
     *weights, layer_out, grad_input = chunked(
@@ -1627,7 +1653,7 @@
     gains = lax.dynamic_slice_in_dim(gains, (zi * G + pi) * per, per, 1)
 
     return (
-        layer_out, grad_input, gains[1], gains[0], *weights,
+        layer_out, grad_input, gains[1], gains[0], *weights, *ffn_out,
         o_conv_inner, o_conv_state,
         mine[:, 5, :heads].reshape(-1), mine[:, 5, 128 : 128 + heads].reshape(-1),
         mine[:, 5, 256 : 256 + heads].reshape(-1), mine[:, 4, :chan].reshape(-1),

time: 640 us -> 638 us (level)
    pallas_call x14 -> x15, Pallas kernels: 151 us -> 147 us  [chunked(): pl.pallas_call(body, grid=(chunks,), out_shape=outs, in_specs=in_specs, o...]
    dot_general x9 -> x8, matrix products: 40.9 us -> 40.1 us  [dot(): lax.dot_general(a, b, (((ca,), (cb,)), ((), ())), preferred_element_type=...]
    unnamed x75 -> x71, local copies, waits for them, and re-layouts: 14.2 us -> 14.2 us
  transfers between devices with their start and end apart: 8 -> 8, of which waited for: 2 -> 3; matrix products, arithmetic and copies ran while one was open for 11% -> 10% of each run, Pallas kernels for 74% -> 74%
where the time goes in v7:
time: 638 us; the launch traced here: 628 us
  Pallas kernels  501 us (79%)
  matrix products  40.1 us (6%)
  local copies, waits for them, and re-layouts  32.8 us (5%)
  waiting for transfers between devices  23.8 us (4%)
  between operations  15.3 us (2%)
  other arithmetic  14.6 us (2%)
    pallas_call x11, Pallas kernels, call(): pl.pallas_call(body, out_shape=outs, in_specs=in_specs, out_specs=out_spe...  354 us
    pallas_call x15, Pallas kernels, chunked(): pl.pallas_call(body, grid=(chunks,), out_shape=outs, in_specs=in_specs, o...  147 us
    dot_general x8, matrix products, dot(): lax.dot_general(a, b, (((ca,), (cb,)), ((), ())), preferred_element_type=...  40.1 us
    all_gather x4, waiting for transfers between devices, gather(): return lax.all_gather(w, 'z', axis=0, tiled=True)  23.5 us
    unnamed x71, local copies, waits for them, and re-layouts  14.2 us
  transfers between devices with their start and end apart: 8, of which 3 were waited for; matrix products, arithmetic and copies ran while one was open for 10% of the time, Pallas kernels for 74%

profile of v7, /device:TPU:0, one launch (start us, length us, event | category | flops | bytes accessed | tf_op | source)
XLA Modules:
  0.0 628.4 jit_solution(5880570757254770782)
XLA Ops:
  11.2 10.9 %shard_map.391 = bf16[512,512]{1,0:T(8,128)(2,1)} custom-call(bf16[128,1536]{1,0:T(8,128)(2,1)} %x_ref.1, bf16[4,128,128]{2,1,0:T(8,128)(2,1)} %maximum_bitcast_fusion.small_ref), custom_call_target="tpu_custom_call" | custom-call | bytes 70000000 | tf_op jit(solution)/shard_map/pallas_call | solution.py:243
  22.2 15.4 %shard_map.396 = bf16[512,1024]{1,0:T(8,128)(2,1)} custom-call(bf16[128,1536]{1,0:T(8,128)(2,1)} %z_ref.1, bf16[128,512]{1,0:T(8,128)(2,1)} %q_ref.1, bf16[128,1536]{1,0:T(8,128)(2,1)} %out_ref.1, bf16[128,512]{1,0:T(8,128)(2,1)} %o_ref.1), custom_call_target="tpu_custom_call" | custom-call | bytes 70000000 | tf_op jit(solution)/shard_map/pallas_call | solution.py:243
  37.7 2.6 multiply_reduce_fusion
  40.5 32.1 %shard_map.390 = (bf16[1040,2048]{1,0:T(8,128)(2,1)}, s32[4,4,8,256]{3,2,1,0:T(8,128)}, bf16[4,4,16,128]{3,2,1,0:T(8,128)(2,1)}) custom-call(bf16[128,2048]{1,0:T(8,128)(2,1)S(1)} %multiply_convert_fusion.first, s32[8,256]{1,0:T(8,128)S(1)} %broadcast_in_dim.69.docs, bf16[4,16,128]{2,1,0:T(8,128)(2,1)S(1)} %pad.17.steps), custom_call_target="tpu_custom_call" | custom-call | bytes 87500000 | tf_op jit(solution)/shard_map/pallas_call | solution.py:243
  75.5 6.6 %fusion.26.pa_ref = f32[1040,512]{1,0:T(8,128)} fusion(bf16[1040,2048]{1,0:T(8,128)(2,1)} %get-tuple-element.125, bf16[2048,512]{1,0:T(8,128)(2,1)} %all-gather.5.cloned.1.call-done.wa_ref), kind=kOutput, calls=%fused_computation.77 | convolution fusion | flops 2181038080 | bytes 8486912 | tf_op jit(solution)/shard_map/dot_general | solution.py:1253
  82.1 5.5 shard_map.392
  87.6 26.2 %shard_map.393 = (bf16[512,1024]{1,0:T(8,128)(2,1)}, bf16[4,64,1024]{2,1,0:T(8,128)(2,1)}, bf16[512,1152]{1,0:T(8,128)(2,1)}, bf16[512,384]{1,0:T(8,128)(2,1)}) custom-call(bf16[64,1024]{1,0:T(8,128)(2,1)} %get-tuple-element.128.block, bf16[64,1024]{1,0:T(8,128)(2,1)} %get-tuple-element.129.kv, bf16[128,2048]{1,0:T(8,128)(2,1)} %gate_w.1, ...), custom_call_target="tpu_custom_call" | custom-call | bytes 98000000 | tf_op jit(solution)/shard_map/pallas_call | solution.py:243
  116.0 1.9 multiply_sine_fusion
  119.9 4.3 fusion.6.raw_ref
  124.2 2.3 copy.79
  126.4 11.1 %shard_map.394 = (f32[1024,384]{1,0:T(8,128)}, f32[1024,384]{1,0:T(8,128)}, f32[8,384,256]{2,1,0:T(8,128)}, f32[8,16,128]{2,1,0:T(8,128)S(1)}, bf16[384,256]{1,0:T(8,128)(2,1)}, /*index=5*/f32[8,128]{1,0:T(8,128)S(1)}) custom-call(s32[1]{0:T(128)} %bitcast.1.base_ref, f32[1024,128]{1,0:T(8,128)} %fusion.6.raw_ref, f32[1040,512]{1,0:T(8,128)} %fusion.26.pa_ref, ...), custom_call_target="tpu_custom_call" | custom-call | flops 2000000000 | bytes 40000000 | tf_op jit(solution)/shard_map/pallas_call | solution.py:1240
  137.5 43.1 %shard_map.395 = (bf16[3,384,256]{2,1,0:T(8,128)(2,1)}, f32[3,8,128]{2,1,0:T(8,128)}, bf16[16,64,1024]{2,1,0:T(8,128)(2,1)}, bf16[1024,2048]{1,0:T(8,128)(2,1)}) custom-call(bf16[384,256]{1,0:T(8,128)(2,1)} %get-tuple-element.135.state, f32[8,128]{1,0:T(8,128)S(1)} %get-tuple-element.136.factor, bf16[4,64,1024]{2,1,0:T(8,128)(2,1)} %get-tuple-element.137.lines, ...), custom_call_target="tpu_custom_call" | custom-call | bytes 133000000 | tf_op jit(solution)/shard_map/pallas_call | solution.py:243
  182.2 2.1 fusion.16.before_ref
  184.3 6.5 %fusion.4.z_ref.q_ref = f32[1024,512]{1,0:T(8,128)} fusion(bf16[1040,2048]{1,0:T(8,128)(2,1)} %get-tuple-element.125, bf16[2048,1024]{1,0:T(8,128)(2,1)} %all-gather.7.cloned.1.call-done.wz_ref), kind=kOutput, calls=%fused_computation.7 | convolution fusion | flops 2147483648 | bytes 8388608 | tf_op jit(solution)/shard_map/dot_general | solution.py:1253
  190.8 10.0 %shard_map.397 = (bf16[1024,384]{1,0:T(8,128)(2,1)}, f32[1024,384]{1,0:T(8,128)}) custom-call(s32[1]{0:T(128)} %bitcast.1.base_ref, f32[1024,128]{1,0:T(8,128)} %fusion.6.raw_ref, bf16[1024,512]{1,0:T(8,128)(2,1)} %bitcast.81, s32[1024,1]{1,0:T(8,128)S(1)} %copy.78.starts_ref, f32[1,128]{1,0:T(1,128)S(1)} %get-tuple-element.253.bias_ref, ...), custom_call_target="tpu_custom_call" | custom-call | flops 2000000000 | bytes 40000000 | tf_op jit(solution)/shard_map/pallas_call | solution.py:1240
  200.8 1.2 constant_dynamic-update-slice_fusion.1
  202.0 7.5 %shard_map.398 = (bf16[1024,128]{1,0:T(8,128)(2,1)}, bf16[1024,128]{1,0:T(8,128)(2,1)}, f32[1024,128]{1,0:T(8,128)}, f32[1024,1]{1,0:T(8,128)S(1)}) custom-call(s32[1]{0:T(128)} %bitcast.1.base_ref, s32[4]{0:T(128)S(1)} %slice_reduce_fusion.5.first_ref, f32[1024,512]{1,0:T(8,128)} %fusion.4.z_ref.q_ref, s32[1024,1]{1,0:T(8,128)S(1)} %copy.78.starts_ref, ...), custom_call_target="tpu_custom_call" | custom-call | flops 2000000000 | bytes 40000000 | tf_op jit(solution)/shard_map/pallas_call | solution.py:1240
  209.6 1.2 constant_dynamic-update-slice_fusion.refs_5_
  210.8 2.4 convolution_convert_fusion.part
  213.2 45.6 %shard_map.399 = (f32[128,2048]{1,0:T(8,128)S(1)}, bf16[1024,2048]{1,0:T(8,128)(2,1)}) custom-call(bf16[1024,2048]{1,0:T(8,128)(2,1)S(1)} %convolution_convert_fusion.part, f32[128,2048]{1,0:T(8,128)S(1)} %get-tuple-element.239.x_ref, f32[1,2048]{1,0:T(1,128)S(1)} %bitcast.77), custom_call_target="tpu_custom_call" | custom-call | bytes 175000000 | tf_op jit(solution)/shard_map/pallas_call | solution.py:243
  259.8 13.9 %all-gather.11.cloned.1.call-done.w_ref = bf16[2048,1152]{1,0:T(8,128)(2,1)} async-done(((bf16[512,1152]{1,0:T(8,128)(2,1)}), bf16[2048,1152]{1,0:T(8,128)(2,1)}) %all-gather.11.cloned.1.call-update) | async-done | bytes 4718608 | tf_op jit(solution)/shard_map/all_gather | solution.py:1341
  273.7 16.9 %shard_map.400 = (bf16[1024,1152]{1,0:T(8,128)(2,1)}, bf16[1024,2048]{1,0:T(8,128)(2,1)}, bf16[1024,2048]{1,0:T(8,128)(2,1)}) custom-call(bf16[1024,2048]{1,0:T(8,128)(2,1)} %get-tuple-element.143.second_ref.refs_0_, bf16[1024,2048]{1,0:T(8,128)(2,1)} %get-tuple-element.144.low_ref.refs_1_, bf16[2048,1152]{1,0:T(8,128)(2,1)} %all-gather.11.cloned.1.call-done.w_ref), custom_call_target="tpu_custom_call" | custom-call | flops 2000000000 | bytes 40000000 | tf_op jit(solution)/shard_map/pallas_call | solution.py:1240
  290.6 10.5 %shard_map.401 = bf16[2048,1152]{1,0:T(8,128)(2,1)} custom-call(bf16[1024,2048]{1,0:T(8,128)(2,1)} %get-tuple-element.143.second_ref.refs_0_, bf16[1024,2048]{1,0:T(8,128)(2,1)} %get-tuple-element.144.low_ref.refs_1_, bf16[1024,1152]{1,0:T(8,128)(2,1)} %get-tuple-element.147.refs_2_.refs_3_, bf16[1024,1152]{1,0:T(8,128)(2,1)} %get-tuple-element.147.refs_2_.refs_3_), custom_call_target="tpu_custom_call" | custom-call | flops 2000000000 | bytes 40000000 | tf_op jit(solution)/shard_map/pallas_call | solution.py:1240
  301.1 9.6 %all-gather.9.cloned.1.call-done.w_ref = bf16[2048,384]{1,0:T(8,128)(2,1)} async-done(((bf16[512,384]{1,0:T(8,128)(2,1)}), bf16[2048,384]{1,0:T(8,128)(2,1)}) %all-gather.9.cloned.1.call-update) | async-done | bytes 1572880 | tf_op jit(solution)/shard_map/all_gather | solution.py:1341
  311.0 11.0 %shard_map.402 = (bf16[1024,384]{1,0:T(8,128)(2,1)}, bf16[1024,2048]{1,0:T(8,128)(2,1)S(1)}, bf16[1024,2048]{1,0:T(8,128)(2,1)S(1)}) custom-call(bf16[1024,2048]{1,0:T(8,128)(2,1)} %get-tuple-element.143.second_ref.refs_0_, bf16[1024,2048]{1,0:T(8,128)(2,1)} %get-tuple-element.144.low_ref.refs_1_, bf16[2048,384]{1,0:T(8,128)(2,1)} %all-gather.9.cloned.1.call-done.w_ref, ...), custom_call_target="tpu_custom_call" | custom-call | flops 2000000000 | bytes 40000000 | tf_op jit(solution)/shard_map/pallas_call | solution.py:1240
  322.0 47.2 %shard_map.403 = (f32[128,2048]{1,0:T(8,128)S(1)}, f32[8,2048]{1,0:T(8,128)S(1)}, bf16[1024,2048]{1,0:T(8,128)(2,1)}) custom-call(bf16[1024,2048]{1,0:T(8,128)(2,1)S(1)} %get-tuple-element.152.part, f32[128,2048]{1,0:T(8,128)S(1)} %copy-done.5, f32[128,2048]{1,0:T(8,128)S(1)} %get-tuple-element.251.cot, f32[1,2048]{1,0:T(1,128)S(1)} %bitcast.78), custom_call_target="tpu_custom_call" | custom-call | bytes 175000000 | tf_op jit(solution)/shard_map/pallas_call | solution.py:243
  370.3 10.3 %shard_map.405 = bf16[2048,896]{1,0:T(8,128)(2,1)} custom-call(bf16[1024,2048]{1,0:T(8,128)(2,1)} %get-tuple-element.143.second_ref.refs_0_, bf16[1024,2048]{1,0:T(8,128)(2,1)} %get-tuple-element.144.low_ref.refs_1_, bf16[1024,2048]{1,0:T(8,128)(2,1)} %get-tuple-element.155.refs_2_, bf16[1024,384]{1,0:T(8,128)(2,1)} %get-tuple-element.161.refs_3_.refs_4_, ...), custom_call_target="tpu_custom_call" | custom-call | flops 2000000000 | bytes 40000000 | tf_op jit(solution)/shard_map/pallas_call | solution.py:1240
  380.6 6.5 %fusion.9.d_ref = f32[1024,512]{1,0:T(8,128)} fusion(bf16[1024,2048]{1,0:T(8,128)(2,1)} %get-tuple-element.155.refs_2_, bf16[2048,1024]{1,0:T(8,128)(2,1)} %all-gather.7.cloned.1.call-done.wz_ref), kind=kOutput, calls=%fused_computation.12 | convolution fusion | flops 2147483648 | bytes 8388608 | tf_op jit(solution)/shard_map/dot_general | solution.py:1253
  387.1 9.7 %shard_map.404 = (bf16[1024,384]{1,0:T(8,128)(2,1)}, f32[1024,384]{1,0:T(8,128)}, f32[8,384,256]{2,1,0:T(8,128)}, f32[8,8,128]{2,1,0:T(8,128)S(1)}, bf16[384,256]{1,0:T(8,128)(2,1)}, /*index=5*/f32[8,384]{1,0:T(8,128)S(1)}) custom-call(s32[1]{0:T(128)} %bitcast.1.base_ref, f32[1024,128]{1,0:T(8,128)} %fusion.6.raw_ref, bf16[1024,512]{1,0:T(8,128)(2,1)} %bitcast.82, ...), custom_call_target="tpu_custom_call" | custom-call | flops 2000000000 | bytes 40000000 | tf_op jit(solution)/shard_map/pallas_call | solution.py:1240
  397.1 9.7 %shard_map.406 = (bf16[1024,128]{1,0:T(8,128)(2,1)}, bf16[4,4,64,1024]{3,2,1,0:T(8,128)(2,1)}) custom-call(s32[1]{0:T(128)} %bitcast.1.base_ref, s32[4]{0:T(128)S(1)} %slice_reduce_fusion.5.first_ref, bf16[1024,128]{1,0:T(8,128)(2,1)} %get-tuple-element.166.query_ref, s32[1024,1]{1,0:T(8,128)S(1)} %copy.78.starts_ref, f32[1024,128]{1,0:T(8,128)} %pad_maximum_fusion.cos_ref, ...), custom_call_target="tpu_custom_call" | custom-call | flops 2000000000 | bytes 40000000 | tf_op jit(solution)/shard_map/pallas_call | solution.py:1240
  406.9 1.0 constant_dynamic-update-slice_fusion.2.dz_ref
  407.9 1.0 copy-done.20
  408.9 6.0 convolution_convert_fusion.2
  414.9 2.2 copy-done.3
  417.1 1.6 copy-done.7
  418.7 52.5 %shard_map.407 = (bf16[3,384,256]{2,1,0:T(8,128)(2,1)}, f32[3,8,128]{2,1,0:T(8,128)}, bf16[256,1024]{1,0:T(8,128)(2,1)S(1)}, f32[128,2048]{1,0:T(8,128)S(1)}) custom-call(bf16[384,256]{1,0:T(8,128)(2,1)} %get-tuple-element.170.state, f32[8,128]{1,0:T(8,128)S(1)} %get-tuple-element.136.factor, bf16[1024,1024]{1,0:T(8,128)(2,1)S(1)} %bitcast.74, ...), custom_call_target="tpu_custom_call" | custom-call | bytes 157500000 | tf_op jit(solution)/shard_map/pallas_call | solution.py:243
  474.9 2.1 fusion.12.after_ref
  477.0 17.9 %shard_map.408 = (f32[1024,384]{1,0:T(8,128)}, bf16[512,1024]{1,0:T(8,128)(2,1)}, bf16[1024,128]{1,0:T(8,128)(2,1)}, f32[8,128]{1,0:T(8,128)S(1)}) custom-call(s32[1]{0:T(128)} %bitcast.1.base_ref, f32[1024,128]{1,0:T(8,128)} %fusion.6.raw_ref, bf16[1024,512]{1,0:T(8,128)(2,1)} %bitcast.83, s32[1024,1]{1,0:T(8,128)S(1)} %copy.78.starts_ref, ...), custom_call_target="tpu_custom_call" | custom-call | flops 2000000000 | bytes 40000000 | tf_op jit(solution)/shard_map/pallas_call | solution.py:1240
  495.0 1.2 copy-done.12
  496.2 29.4 %shard_map.409 = (f32[64,1024]{1,0:T(8,128)S(1)}, f32[64,128]{1,0:T(8,128)S(1)}, f32[16,384]{1,0:T(8,128)S(1)}, f32[64,1024]{1,0:T(8,128)S(1)}, bf16[4,128,1152]...) custom-call(bf16[512,1024]{1,0:T(8,128)(2,1)S(1)} %copy-done.12, bf16[4,64,1024]{2,1,0:T(8,128)(2,1)S(1)} %bitcast.76, ...), custom_call_target="tpu_custom_call" | custom-call | bytes 105000000 | tf_op jit(solution)/shard_map/pallas_call | solution.py:243
  525.6 3.9 shard_map.410
  529.5 7.2 %shard_map.411 = (bf16[1024,512]{1,0:T(8,128)(2,1)}, f32[8,512]{1,0:T(8,128)S(1)}) custom-call(s32[1]{0:T(128)} %bitcast.1.base_ref, f32[1040,512]{1,0:T(8,128)} %fusion.26.pa_ref, f32[1024,384]{1,0:T(8,128)} %get-tuple-element.190.gx.gx_ref, f32[16,384]{1,0:T(8,128)S(1)} %get-tuple-element.191.rim_x, f32[64,1024]{1,0:T(8,128)S(1)} %get-tuple-element.192.g_bc, ...), custom_call_target="tpu_custom_call" | custom-call | flops 2000000000 | bytes 40000000 | tf_op jit(solution)/shard_map/pallas_call | solution.py:1240
  536.7 5.0 convolution_convert_fusion.1
  542.5 2.9 fusion
  545.6 9.1 %shard_map.412.part = bf16[1024,2048]{1,0:T(8,128)(2,1)S(1)} custom-call(bf16[1024,512]{1,0:T(8,128)(2,1)} %get-tuple-element.195.da_ref, bf16[1024,512]{1,0:T(8,128)(2,1)} %copy-done.20, bf16[1024,128]{1,0:T(8,128)(2,1)} %get-tuple-element.196.raw_ref, bf16[2048,512]{1,0:T(8,128)(2,1)} %all-gather.5.cloned.1.call-done.wa_ref, ...), custom_call_target="tpu_custom_call" | custom-call | flops 2000000000 | bytes 40000000 | tf_op jit(solution)/shard_map/pallas_call | solution.py:1240
  554.7 33.7 %shard_map.413 = (f32[256,2048]{1,0:T(8,128)}, f32[256,2048]{1,0:T(8,128)}, f32[16,512]{1,0:T(8,128)S(1)}, bf16[4,128,512]{2,1,0:T(8,128)(2,1)}, bf16[4,128,512]{2,1,0:T(8,128)(2,1)}) custom-call(bf16[1024,2048]{1,0:T(8,128)(2,1)S(1)} %shard_map.412.part, f32[128,2048]{1,0:T(8,128)S(1)} %get-tuple-element.239.x_ref, f32[128,2048]{1,0:T(8,128)S(1)} %copy-done.9, ...), custom_call_target="tpu_custom_call" | custom-call | bytes 140000000 | tf_op jit(solution)/shard_map/pallas_call | solution.py:243
  588.5 18.0 %shard_map.414 = (bf16[4,128,384]{2,1,0:T(8,128)(2,1)}, bf16[8,128,128]{2,1,0:T(8,128)(2,1)}, f32[128,512]{1,0:T(8,128)}, f32[4,16,128]{2,1,0:T(8,128)}) custom-call(bf16[512,512]{1,0:T(8,128)(2,1)} %reduce-scatter.11.cloned.1.call-done.sum_a, f32[16,512]{1,0:T(8,128)S(1)} %get-tuple-element.208.small, f32[4,4,16,128]{3,2,1,0:T(8,128)S(1)} %bitcast.75), custom_call_target="tpu_custom_call" | custom-call | bytes 70000000 | tf_op jit(solution)/shard_map/pallas_call | solution.py:243
  614.8 6.3 %shard_map.415 = (f32[128,1536]{1,0:T(8,128)}, f32[128,1536]{1,0:T(8,128)}, f32[128,512]{1,0:T(8,128)}, f32[128,512]{1,0:T(8,128)}, f32[128,128]{1,0:T(8,128)}, ...) custom-call(s32[1]{0:T(128)} %bitcast.core_ref, ...), custom_call_target="tpu_custom_call" | custom-call | flops 2000000000 | bytes 40000000 | tf_op jit(solution)/shard_map/pallas_call | solution.py:1240
  (162 shorter events, 28.3 us)
Async XLA Ops:
  7.2 0.9 copy-start
  7.2 30.5 %copy-start.25 = (bf16[128,24]{0,1:T(8,128)(2,1)S(1)}, bf16[128,24]{0,1:T(8,128)(2,1)}, u32[]{:S(2)}) copy-start(bf16[128,24]{0,1:T(8,128)(2,1)} %param.30) | copy-start | bytes 18436
  7.2 68.3 %all-gather.5.cloned.1.call-start = ((), (), s32[]{:S(2)}) async-start(), calls=%async_computation.4 | async-start | bytes 2621440 | tf_op jit(solution)/shard_map/all_gather | solution.py:1341
  22.1 18.2 %copy-start.15 = (f32[2048]{0:T(1024)S(1)}, f32[2048]{0:T(1024)}, u32[]{:S(2)}) copy-start(f32[2048]{0:T(1024)} %param.25) | copy-start | bytes 24580
  22.2 162.1 %all-gather.7.cloned.1.call-start = ((), (), s32[]{:S(2)}) async-start(), calls=%async_computation.5 | async-start | bytes 5242880 | tf_op jit(solution)/shard_map/all_gather | solution.py:1341
  37.6 2.9 copy-start.26
  37.6 236.1 %all-gather.11.cloned.1.call-start = ((), (), s32[]{:S(2)}) async-start(), calls=%async_computation.7 | async-start | bytes 5898240 | tf_op jit(solution)/shard_map/all_gather | solution.py:1341
  73.5 0.6 copy-start.23
  82.1 31.8 %copy-start.24 = (bf16[4,4,16,128]{3,2,1,0:T(8,128)(2,1)S(1)}, bf16[4,4,16,128]{3,2,1,0:T(8,128)(2,1)}, u32[]{:S(2)}) copy-start(bf16[4,4,16,128]{3,2,1,0:T(8,128)(2,1)} %get-tuple-element.126) | copy-start | bytes 196612
  82.1 31.9 %copy-start.27 = (f32[24]{0:T(128)S(1)}, f32[24]{0:T(128)}, u32[]{:S(2)}) copy-start(f32[24]{0:T(128)} %param.42) | copy-start | bytes 292
  82.1 32.0 %copy-start.28 = (f32[24]{0:T(128)S(1)}, f32[24]{0:T(128)}, u32[]{:S(2)}) copy-start(f32[24]{0:T(128)} %param.41) | copy-start | bytes 292
  82.1 32.1 %copy-start.29 = (f32[24]{0:T(128)S(1)}, f32[24]{0:T(128)}, u32[]{:S(2)}) copy-start(f32[24]{0:T(128)} %param.43) | copy-start | bytes 292
  113.8 196.9 %all-gather.9.cloned.1.call-start = ((), (), s32[]{:S(2)}) async-start(), calls=%async_computation.6 | async-start | bytes 1966080 | tf_op jit(solution)/shard_map/all_gather | solution.py:1341
  181.9 215.1 %reduce-scatter.5.cloned.1.call-start = ((), (), s32[]{:S(2)}) async-start(), calls=%async_computation.8 | async-start | bytes 5898240 | tf_op jit(solution)/shard_map/reduce_scatter | solution.py:1373
  202.0 8.7 %copy-start.18 = (bf16[2048,1024]{1,0:T(8,128)(2,1)S(1)}, bf16[2048,1024]{1,0:T(8,128)(2,1)}, u32[]{:S(2)}) copy-start(bf16[2048,1024]{1,0:T(8,128)(2,1)} %all-gather.7.cloned.1.call-done.wz_ref) | copy-start | bytes 12582916
  209.6 3.6 copy-start.16
  210.7 2.4 copy-start.19
  210.8 2.4 copy-start.14
  258.8 1.0 copy-start.4
  310.7 184.2 %reduce-scatter.7.cloned.1.call-start = ((), (), s32[]{:S(2)}) async-start(), calls=%async_computation.9 | async-start | bytes 4587520 | tf_op jit(solution)/shard_map/reduce_scatter | solution.py:1373
  311.0 11.0 %copy-start.5 = (f32[128,2048]{1,0:T(8,128)S(1)}, f32[128,2048]{1,0:T(8,128)}, u32[]{:S(2)}) copy-start(f32[128,2048]{1,0:T(8,128)} %copy-done.4) | copy-start | bytes 3145732
  322.0 47.2 %copy-start.2 = (bf16[1024,2048]{1,0:T(8,128)(2,1)}, bf16[1024,2048]{1,0:T(8,128)(2,1)S(1)}, u32[]{:S(2)}) copy-start(bf16[1024,2048]{1,0:T(8,128)(2,1)S(1)} %get-tuple-element.172.part) | copy-start | bytes 12582916
  369.3 1.0 copy-start.8
  387.1 10.0 %copy-start.17 = (f32[1024,1]{1,0:T(8,128)S(1)}, f32[1024,1]{1,0:T(8,128)}, u32[]{:S(2)}) copy-start(f32[1024,1]{1,0:T(8,128)} %copy-done.16) | copy-start | bytes 12292
  397.0 144.6 %reduce-scatter.9.cloned.1.call-start = ((), (), s32[]{:S(2)}) async-start(), calls=%async_computation.10 | async-start | bytes 2621440 | tf_op jit(solution)/shard_map/reduce_scatter | solution.py:1373
  397.1 9.7 %copy-start.22 = (bf16[1024,384]{1,0:T(8,128)(2,1)S(1)}, bf16[1024,384]{1,0:T(8,128)(2,1)}, u32[]{:S(2)}) copy-start(bf16[1024,384]{1,0:T(8,128)(2,1)} %get-tuple-element.165) | copy-start | bytes 2359300
  407.9 1.0 copy-start.20
  408.9 6.0 copy-start.6
  414.9 2.2 copy-start.3
  417.1 1.6 copy-start.7
  471.2 1.0 copy-start.10
  472.2 116.2 %reduce-scatter.11.cloned.1.call-start = ((), (), s32[]{:S(2)}) async-start(), calls=%async_computation.11 | async-start | bytes 2621440 | tf_op jit(solution)/shard_map/reduce_scatter | solution.py:1373
  477.0 17.9 %copy-start.13 = (f32[64,1024]{1,0:T(8,128)S(1)}, f32[64,1024]{1,0:T(8,128)}, u32[]{:S(2)}) copy-start(f32[64,1024]{1,0:T(8,128)} %get-tuple-element.182.d_silu_bc) | copy-start | bytes 786436
  495.0 1.2 copy-start.12
  496.2 40.5 %slice-start = ((s8[4259840]{0:T(1024)(128)(4,1)}), s8[4194304]{0:T(1024)(128)(4,1)S(1)}, s32[]{:S(2)}) async-start(s8[4259840]{0:T(1024)(128)(4,1)} %bitcast.84), calls=%async_computation.12 | async-start | bytes 8388608
  525.6 11.1 %slice-start.1 = ((s8[4259840]{0:T(1024)(128)(4,1)}), s8[65536]{0:T(1024)(128)(4,1)S(1)}, s32[]{:S(2)}) async-start(s8[4259840]{0:T(1024)(128)(4,1)} %bitcast.84), calls=%async_computation.13 | async-start | bytes 131072
  536.7 5.9 copy-start.21
  545.5 9.1 %copy-start.9 = (f32[128,2048]{1,0:T(8,128)S(1)}, f32[128,2048]{1,0:T(8,128)}, u32[]{:S(2)}) copy-start(f32[128,2048]{1,0:T(8,128)} %copy-done.8) | copy-start | bytes 3145732
  545.6 9.1 %copy-start.11 = (f32[128,2048]{1,0:T(8,128)S(1)}, f32[128,2048]{1,0:T(8,128)}, u32[]{:S(2)}) copy-start(f32[128,2048]{1,0:T(8,128)} %copy-done.10) | copy-start | bytes 3145732
  606.5 14.6 %copy-start.1 = (bf16[128,512]{1,0:T(8,128)(2,1)S(1)}, bf16[128,512]{1,0:T(8,128)(2,1)}, u32[]{:S(2)}) copy-start(bf16[128,512]{1,0:T(8,128)(2,1)} %param.29) | copy-start | bytes 393220
Sparse Core Ops, SparseCore 0:
  22.3 52.6 all-gather.4
  76.6 96.6 all-gather.6
  174.8 98.8 all-gather.10
  275.1 35.5 all-gather.8
  312.9 84.1 reduce-scatter.4
  399.2 81.8 reduce-scatter.6
  484.0 56.5 reduce-scatter.8
  543.5 44.5 reduce-scatter.10

commit v8 on v7

--- a/solution.py
+++ b/solution.py
@@ -1578,7 +1578,7 @@
          pltpu.VMEM((planes - 1, kvr, T), bf16), pltpu.VMEM((bcs, T), f32), DMA(()), DMA(()), DMA((3,)), DMA((3,)),
          DMA((planes - 1,)), DMA((planes - 1,)), DMA((2,)), DMA((2,)), DMA((2, 3)), DMA((2, 3)), DMA((2,))], us=30,
     )
-    strip = min(32, rows)
+    strip = min(64, rows)
 
     def got(v):
         return pl.BlockSpec((v.shape[0], strip, v.shape[2]), lambda c: (0, c, 0))

time: 638 us -> 636 us (level)
  transfers between devices with their start and end apart: 8 -> 8, of which waited for: 3 -> 4; matrix products, arithmetic and copies ran while one was open for 10% -> 10% of each run, Pallas kernels for 74% -> 74%
where the time goes in v8:
time: 636 us; the launch traced here: 627 us
  Pallas kernels  499 us (78%)
  matrix products  40.1 us (6%)
  local copies, waits for them, and re-layouts  32.8 us (5%)
  waiting for transfers between devices  24.2 us (4%)
  between operations  15.3 us (2%)
  other arithmetic  14.6 us (2%)
    pallas_call x11, Pallas kernels, call(): pl.pallas_call(body, out_shape=outs, in_specs=in_specs, out_specs=out_spe...  355 us
    pallas_call x15, Pallas kernels, chunked(): pl.pallas_call(body, grid=(chunks,), out_shape=outs, in_specs=in_specs, o...  144 us
    dot_general x8, matrix products, dot(): lax.dot_general(a, b, (((ca,), (cb,)), ((), ())), preferred_element_type=...  40.1 us
    all_gather x4, waiting for transfers between devices, gather(): return lax.all_gather(w, 'z', axis=0, tiled=True)  23.5 us
    unnamed x71, local copies, waits for them, and re-layouts  14.2 us
  transfers between devices with their start and end apart: 8, of which 4 were waited for; matrix products, arithmetic and copies ran while one was open for 10% of the time, Pallas kernels for 74%

profile of v8, /device:TPU:0, one launch (start us, length us, event | category | flops | bytes accessed | tf_op | source)
XLA Modules:
  0.0 626.9 jit_solution(9110348372204154953)
XLA Ops:
  11.2 10.9 %shard_map.391 = bf16[512,512]{1,0:T(8,128)(2,1)} custom-call(bf16[128,1536]{1,0:T(8,128)(2,1)} %x_ref.1, bf16[4,128,128]{2,1,0:T(8,128)(2,1)} %maximum_bitcast_fusion.small_ref), custom_call_target="tpu_custom_call" | custom-call | bytes 70000000 | tf_op jit(solution)/shard_map/pallas_call | solution.py:243
  22.2 15.4 %shard_map.396 = bf16[512,1024]{1,0:T(8,128)(2,1)} custom-call(bf16[128,1536]{1,0:T(8,128)(2,1)} %z_ref.1, bf16[128,512]{1,0:T(8,128)(2,1)} %q_ref.1, bf16[128,1536]{1,0:T(8,128)(2,1)} %out_ref.1, bf16[128,512]{1,0:T(8,128)(2,1)} %o_ref.1), custom_call_target="tpu_custom_call" | custom-call | bytes 70000000 | tf_op jit(solution)/shard_map/pallas_call | solution.py:243
  37.7 2.6 multiply_reduce_fusion
  40.5 32.1 %shard_map.390 = (bf16[1040,2048]{1,0:T(8,128)(2,1)}, s32[4,4,8,256]{3,2,1,0:T(8,128)}, bf16[4,4,16,128]{3,2,1,0:T(8,128)(2,1)}) custom-call(bf16[128,2048]{1,0:T(8,128)(2,1)S(1)} %multiply_convert_fusion.first, s32[8,256]{1,0:T(8,128)S(1)} %broadcast_in_dim.69.docs, bf16[4,16,128]{2,1,0:T(8,128)(2,1)S(1)} %pad.17.steps), custom_call_target="tpu_custom_call" | custom-call | bytes 87500000 | tf_op jit(solution)/shard_map/pallas_call | solution.py:243
  75.5 6.6 %fusion.26.pa_ref = f32[1040,512]{1,0:T(8,128)} fusion(bf16[1040,2048]{1,0:T(8,128)(2,1)} %get-tuple-element.125, bf16[2048,512]{1,0:T(8,128)(2,1)} %all-gather.5.cloned.1.call-done.wa_ref), kind=kOutput, calls=%fused_computation.77 | convolution fusion | flops 2181038080 | bytes 8486912 | tf_op jit(solution)/shard_map/dot_general | solution.py:1253
  82.1 5.5 shard_map.392
  87.6 26.2 %shard_map.393 = (bf16[512,1024]{1,0:T(8,128)(2,1)}, bf16[4,64,1024]{2,1,0:T(8,128)(2,1)}, bf16[512,1152]{1,0:T(8,128)(2,1)}, bf16[512,384]{1,0:T(8,128)(2,1)}) custom-call(bf16[64,1024]{1,0:T(8,128)(2,1)} %get-tuple-element.128.block, bf16[64,1024]{1,0:T(8,128)(2,1)} %get-tuple-element.129.kv, bf16[128,2048]{1,0:T(8,128)(2,1)} %gate_w.1, ...), custom_call_target="tpu_custom_call" | custom-call | bytes 98000000 | tf_op jit(solution)/shard_map/pallas_call | solution.py:243
  116.0 1.9 multiply_sine_fusion
  119.9 4.3 fusion.6.raw_ref
  124.2 2.3 copy.79
  126.4 11.1 %shard_map.394 = (f32[1024,384]{1,0:T(8,128)}, f32[1024,384]{1,0:T(8,128)}, f32[8,384,256]{2,1,0:T(8,128)}, f32[8,16,128]{2,1,0:T(8,128)S(1)}, bf16[384,256]{1,0:T(8,128)(2,1)}, /*index=5*/f32[8,128]{1,0:T(8,128)S(1)}) custom-call(s32[1]{0:T(128)} %bitcast.1.base_ref, f32[1024,128]{1,0:T(8,128)} %fusion.6.raw_ref, f32[1040,512]{1,0:T(8,128)} %fusion.26.pa_ref, ...), custom_call_target="tpu_custom_call" | custom-call | flops 2000000000 | bytes 40000000 | tf_op jit(solution)/shard_map/pallas_call | solution.py:1240
  137.5 43.1 %shard_map.395 = (bf16[3,384,256]{2,1,0:T(8,128)(2,1)}, f32[3,8,128]{2,1,0:T(8,128)}, bf16[16,64,1024]{2,1,0:T(8,128)(2,1)}, bf16[1024,2048]{1,0:T(8,128)(2,1)}) custom-call(bf16[384,256]{1,0:T(8,128)(2,1)} %get-tuple-element.135.state, f32[8,128]{1,0:T(8,128)S(1)} %get-tuple-element.136.factor, bf16[4,64,1024]{2,1,0:T(8,128)(2,1)} %get-tuple-element.137.lines, ...), custom_call_target="tpu_custom_call" | custom-call | bytes 133000000 | tf_op jit(solution)/shard_map/pallas_call | solution.py:243
  182.2 2.1 fusion.16.before_ref
  184.3 6.5 %fusion.4.z_ref.q_ref = f32[1024,512]{1,0:T(8,128)} fusion(bf16[1040,2048]{1,0:T(8,128)(2,1)} %get-tuple-element.125, bf16[2048,1024]{1,0:T(8,128)(2,1)} %all-gather.7.cloned.1.call-done.wz_ref), kind=kOutput, calls=%fused_computation.7 | convolution fusion | flops 2147483648 | bytes 8388608 | tf_op jit(solution)/shard_map/dot_general | solution.py:1253
  190.8 10.0 %shard_map.397 = (bf16[1024,384]{1,0:T(8,128)(2,1)}, f32[1024,384]{1,0:T(8,128)}) custom-call(s32[1]{0:T(128)} %bitcast.1.base_ref, f32[1024,128]{1,0:T(8,128)} %fusion.6.raw_ref, bf16[1024,512]{1,0:T(8,128)(2,1)} %bitcast.81, s32[1024,1]{1,0:T(8,128)S(1)} %copy.78.starts_ref, f32[1,128]{1,0:T(1,128)S(1)} %get-tuple-element.253.bias_ref, ...), custom_call_target="tpu_custom_call" | custom-call | flops 2000000000 | bytes 40000000 | tf_op jit(solution)/shard_map/pallas_call | solution.py:1240
  200.8 1.2 constant_dynamic-update-slice_fusion.1
  202.0 7.5 %shard_map.398 = (bf16[1024,128]{1,0:T(8,128)(2,1)}, bf16[1024,128]{1,0:T(8,128)(2,1)}, f32[1024,128]{1,0:T(8,128)}, f32[1024,1]{1,0:T(8,128)S(1)}) custom-call(s32[1]{0:T(128)} %bitcast.1.base_ref, s32[4]{0:T(128)S(1)} %slice_reduce_fusion.5.first_ref, f32[1024,512]{1,0:T(8,128)} %fusion.4.z_ref.q_ref, s32[1024,1]{1,0:T(8,128)S(1)} %copy.78.starts_ref, ...), custom_call_target="tpu_custom_call" | custom-call | flops 2000000000 | bytes 40000000 | tf_op jit(solution)/shard_map/pallas_call | solution.py:1240
  209.6 1.2 constant_dynamic-update-slice_fusion.refs_5_
  210.8 2.4 convolution_convert_fusion.part
  213.2 45.6 %shard_map.399 = (f32[128,2048]{1,0:T(8,128)S(1)}, bf16[1024,2048]{1,0:T(8,128)(2,1)}) custom-call(bf16[1024,2048]{1,0:T(8,128)(2,1)S(1)} %convolution_convert_fusion.part, f32[128,2048]{1,0:T(8,128)S(1)} %get-tuple-element.239.x_ref, f32[1,2048]{1,0:T(1,128)S(1)} %bitcast.77), custom_call_target="tpu_custom_call" | custom-call | bytes 175000000 | tf_op jit(solution)/shard_map/pallas_call | solution.py:243
  259.8 13.9 %all-gather.11.cloned.1.call-done.w_ref = bf16[2048,1152]{1,0:T(8,128)(2,1)} async-done(((bf16[512,1152]{1,0:T(8,128)(2,1)}), bf16[2048,1152]{1,0:T(8,128)(2,1)}) %all-gather.11.cloned.1.call-update) | async-done | bytes 4718608 | tf_op jit(solution)/shard_map/all_gather | solution.py:1341
  273.7 16.9 %shard_map.400 = (bf16[1024,1152]{1,0:T(8,128)(2,1)}, bf16[1024,2048]{1,0:T(8,128)(2,1)}, bf16[1024,2048]{1,0:T(8,128)(2,1)}) custom-call(bf16[1024,2048]{1,0:T(8,128)(2,1)} %get-tuple-element.143.second_ref.refs_0_, bf16[1024,2048]{1,0:T(8,128)(2,1)} %get-tuple-element.144.low_ref.refs_1_, bf16[2048,1152]{1,0:T(8,128)(2,1)} %all-gather.11.cloned.1.call-done.w_ref), custom_call_target="tpu_custom_call" | custom-call | flops 2000000000 | bytes 40000000 | tf_op jit(solution)/shard_map/pallas_call | solution.py:1240
  290.6 10.5 %shard_map.401 = bf16[2048,1152]{1,0:T(8,128)(2,1)} custom-call(bf16[1024,2048]{1,0:T(8,128)(2,1)} %get-tuple-element.143.second_ref.refs_0_, bf16[1024,2048]{1,0:T(8,128)(2,1)} %get-tuple-element.144.low_ref.refs_1_, bf16[1024,1152]{1,0:T(8,128)(2,1)} %get-tuple-element.147.refs_2_.refs_3_, bf16[1024,1152]{1,0:T(8,128)(2,1)} %get-tuple-element.147.refs_2_.refs_3_), custom_call_target="tpu_custom_call" | custom-call | flops 2000000000 | bytes 40000000 | tf_op jit(solution)/shard_map/pallas_call | solution.py:1240
  301.1 9.6 %all-gather.9.cloned.1.call-done.w_ref = bf16[2048,384]{1,0:T(8,128)(2,1)} async-done(((bf16[512,384]{1,0:T(8,128)(2,1)}), bf16[2048,384]{1,0:T(8,128)(2,1)}) %all-gather.9.cloned.1.call-update) | async-done | bytes 1572880 | tf_op jit(solution)/shard_map/all_gather | solution.py:1341
  311.0 11.0 %shard_map.402 = (bf16[1024,384]{1,0:T(8,128)(2,1)}, bf16[1024,2048]{1,0:T(8,128)(2,1)S(1)}, bf16[1024,2048]{1,0:T(8,128)(2,1)S(1)}) custom-call(bf16[1024,2048]{1,0:T(8,128)(2,1)} %get-tuple-element.143.second_ref.refs_0_, bf16[1024,2048]{1,0:T(8,128)(2,1)} %get-tuple-element.144.low_ref.refs_1_, bf16[2048,384]{1,0:T(8,128)(2,1)} %all-gather.9.cloned.1.call-done.w_ref, ...), custom_call_target="tpu_custom_call" | custom-call | flops 2000000000 | bytes 40000000 | tf_op jit(solution)/shard_map/pallas_call | solution.py:1240
  322.0 47.2 %shard_map.403 = (f32[128,2048]{1,0:T(8,128)S(1)}, f32[8,2048]{1,0:T(8,128)S(1)}, bf16[1024,2048]{1,0:T(8,128)(2,1)}) custom-call(bf16[1024,2048]{1,0:T(8,128)(2,1)S(1)} %get-tuple-element.152.part, f32[128,2048]{1,0:T(8,128)S(1)} %copy-done.5, f32[128,2048]{1,0:T(8,128)S(1)} %get-tuple-element.251.cot, f32[1,2048]{1,0:T(1,128)S(1)} %bitcast.78), custom_call_target="tpu_custom_call" | custom-call | bytes 175000000 | tf_op jit(solution)/shard_map/pallas_call | solution.py:243
  370.3 10.3 %shard_map.405 = bf16[2048,896]{1,0:T(8,128)(2,1)} custom-call(bf16[1024,2048]{1,0:T(8,128)(2,1)} %get-tuple-element.143.second_ref.refs_0_, bf16[1024,2048]{1,0:T(8,128)(2,1)} %get-tuple-element.144.low_ref.refs_1_, bf16[1024,2048]{1,0:T(8,128)(2,1)} %get-tuple-element.155.refs_2_, bf16[1024,384]{1,0:T(8,128)(2,1)} %get-tuple-element.161.refs_3_.refs_4_, ...), custom_call_target="tpu_custom_call" | custom-call | flops 2000000000 | bytes 40000000 | tf_op jit(solution)/shard_map/pallas_call | solution.py:1240
  380.6 6.5 %fusion.9.d_ref = f32[1024,512]{1,0:T(8,128)} fusion(bf16[1024,2048]{1,0:T(8,128)(2,1)} %get-tuple-element.155.refs_2_, bf16[2048,1024]{1,0:T(8,128)(2,1)} %all-gather.7.cloned.1.call-done.wz_ref), kind=kOutput, calls=%fused_computation.12 | convolution fusion | flops 2147483648 | bytes 8388608 | tf_op jit(solution)/shard_map/dot_general | solution.py:1253
  387.1 9.7 %shard_map.404 = (bf16[1024,384]{1,0:T(8,128)(2,1)}, f32[1024,384]{1,0:T(8,128)}, f32[8,384,256]{2,1,0:T(8,128)}, f32[8,8,128]{2,1,0:T(8,128)S(1)}, bf16[384,256]{1,0:T(8,128)(2,1)}, /*index=5*/f32[8,384]{1,0:T(8,128)S(1)}) custom-call(s32[1]{0:T(128)} %bitcast.1.base_ref, f32[1024,128]{1,0:T(8,128)} %fusion.6.raw_ref, bf16[1024,512]{1,0:T(8,128)(2,1)} %bitcast.82, ...), custom_call_target="tpu_custom_call" | custom-call | flops 2000000000 | bytes 40000000 | tf_op jit(solution)/shard_map/pallas_call | solution.py:1240
  397.1 9.7 %shard_map.406 = (bf16[1024,128]{1,0:T(8,128)(2,1)}, bf16[4,4,64,1024]{3,2,1,0:T(8,128)(2,1)}) custom-call(s32[1]{0:T(128)} %bitcast.1.base_ref, s32[4]{0:T(128)S(1)} %slice_reduce_fusion.5.first_ref, bf16[1024,128]{1,0:T(8,128)(2,1)} %get-tuple-element.166.query_ref, s32[1024,1]{1,0:T(8,128)S(1)} %copy.78.starts_ref, f32[1024,128]{1,0:T(8,128)} %pad_maximum_fusion.cos_ref, ...), custom_call_target="tpu_custom_call" | custom-call | flops 2000000000 | bytes 40000000 | tf_op jit(solution)/shard_map/pallas_call | solution.py:1240
  406.9 1.0 constant_dynamic-update-slice_fusion.2.dz_ref
  407.9 1.0 copy-done.20
  408.9 6.0 convolution_convert_fusion.2
  414.9 2.2 copy-done.3
  417.1 1.6 copy-done.7
  418.7 52.5 %shard_map.407 = (bf16[3,384,256]{2,1,0:T(8,128)(2,1)}, f32[3,8,128]{2,1,0:T(8,128)}, bf16[256,1024]{1,0:T(8,128)(2,1)S(1)}, f32[128,2048]{1,0:T(8,128)S(1)}) custom-call(bf16[384,256]{1,0:T(8,128)(2,1)} %get-tuple-element.170.state, f32[8,128]{1,0:T(8,128)S(1)} %get-tuple-element.136.factor, bf16[1024,1024]{1,0:T(8,128)(2,1)S(1)} %bitcast.74, ...), custom_call_target="tpu_custom_call" | custom-call | bytes 157500000 | tf_op jit(solution)/shard_map/pallas_call | solution.py:243
  474.9 2.1 fusion.12.after_ref
  477.0 17.9 %shard_map.408 = (f32[1024,384]{1,0:T(8,128)}, bf16[512,1024]{1,0:T(8,128)(2,1)}, bf16[1024,128]{1,0:T(8,128)(2,1)}, f32[8,128]{1,0:T(8,128)S(1)}) custom-call(s32[1]{0:T(128)} %bitcast.1.base_ref, f32[1024,128]{1,0:T(8,128)} %fusion.6.raw_ref, bf16[1024,512]{1,0:T(8,128)(2,1)} %bitcast.83, s32[1024,1]{1,0:T(8,128)S(1)} %copy.78.starts_ref, ...), custom_call_target="tpu_custom_call" | custom-call | flops 2000000000 | bytes 40000000 | tf_op jit(solution)/shard_map/pallas_call | solution.py:1240
  495.0 1.2 copy-done.12
  496.2 29.4 %shard_map.409 = (f32[64,1024]{1,0:T(8,128)S(1)}, f32[64,128]{1,0:T(8,128)S(1)}, f32[16,384]{1,0:T(8,128)S(1)}, f32[64,1024]{1,0:T(8,128)S(1)}, bf16[4,128,1152]...) custom-call(bf16[512,1024]{1,0:T(8,128)(2,1)S(1)} %copy-done.12, bf16[4,64,1024]{2,1,0:T(8,128)(2,1)S(1)} %bitcast.76, ...), custom_call_target="tpu_custom_call" | custom-call | bytes 105000000 | tf_op jit(solution)/shard_map/pallas_call | solution.py:243
  525.6 2.9 shard_map.410
  528.5 7.2 %shard_map.411 = (bf16[1024,512]{1,0:T(8,128)(2,1)}, f32[8,512]{1,0:T(8,128)S(1)}) custom-call(s32[1]{0:T(128)} %bitcast.1.base_ref, f32[1040,512]{1,0:T(8,128)} %fusion.26.pa_ref, f32[1024,384]{1,0:T(8,128)} %get-tuple-element.190.gx.gx_ref, f32[16,384]{1,0:T(8,128)S(1)} %get-tuple-element.191.rim_x, f32[64,1024]{1,0:T(8,128)S(1)} %get-tuple-element.192.g_bc, ...), custom_call_target="tpu_custom_call" | custom-call | flops 2000000000 | bytes 40000000 | tf_op jit(solution)/shard_map/pallas_call | solution.py:1240
  535.7 5.0 convolution_convert_fusion.1
  541.5 2.9 fusion
  544.6 9.1 %shard_map.412.part = bf16[1024,2048]{1,0:T(8,128)(2,1)S(1)} custom-call(bf16[1024,512]{1,0:T(8,128)(2,1)} %get-tuple-element.195.da_ref, bf16[1024,512]{1,0:T(8,128)(2,1)} %copy-done.20, bf16[1024,128]{1,0:T(8,128)(2,1)} %get-tuple-element.196.raw_ref, bf16[2048,512]{1,0:T(8,128)(2,1)} %all-gather.5.cloned.1.call-done.wa_ref, ...), custom_call_target="tpu_custom_call" | custom-call | flops 2000000000 | bytes 40000000 | tf_op jit(solution)/shard_map/pallas_call | solution.py:1240
  553.7 34.1 %shard_map.413 = (f32[256,2048]{1,0:T(8,128)}, f32[256,2048]{1,0:T(8,128)}, f32[16,512]{1,0:T(8,128)S(1)}, bf16[4,128,512]{2,1,0:T(8,128)(2,1)}, bf16[4,128,512]{2,1,0:T(8,128)(2,1)}) custom-call(bf16[1024,2048]{1,0:T(8,128)(2,1)S(1)} %shard_map.412.part, f32[128,2048]{1,0:T(8,128)S(1)} %get-tuple-element.239.x_ref, f32[128,2048]{1,0:T(8,128)S(1)} %copy-done.9, ...), custom_call_target="tpu_custom_call" | custom-call | bytes 140000000 | tf_op jit(solution)/shard_map/pallas_call | solution.py:243
  588.2 17.9 %shard_map.414 = (bf16[4,128,384]{2,1,0:T(8,128)(2,1)}, bf16[8,128,128]{2,1,0:T(8,128)(2,1)}, f32[128,512]{1,0:T(8,128)}, f32[4,16,128]{2,1,0:T(8,128)}) custom-call(bf16[512,512]{1,0:T(8,128)(2,1)} %reduce-scatter.11.cloned.1.call-done.sum_a, f32[16,512]{1,0:T(8,128)S(1)} %get-tuple-element.208.small, f32[4,4,16,128]{3,2,1,0:T(8,128)S(1)} %bitcast.75), custom_call_target="tpu_custom_call" | custom-call | bytes 70000000 | tf_op jit(solution)/shard_map/pallas_call | solution.py:243
  614.5 5.1 shard_map.415
  (162 shorter events, 28.6 us)
Async XLA Ops:
  7.2 0.9 copy-start
  7.2 30.5 %copy-start.25 = (bf16[128,24]{0,1:T(8,128)(2,1)S(1)}, bf16[128,24]{0,1:T(8,128)(2,1)}, u32[]{:S(2)}) copy-start(bf16[128,24]{0,1:T(8,128)(2,1)} %param.30) | copy-start | bytes 18436
  7.2 68.3 %all-gather.5.cloned.1.call-start = ((), (), s32[]{:S(2)}) async-start(), calls=%async_computation.4 | async-start | bytes 2621440 | tf_op jit(solution)/shard_map/all_gather | solution.py:1341
  22.1 18.2 %copy-start.15 = (f32[2048]{0:T(1024)S(1)}, f32[2048]{0:T(1024)}, u32[]{:S(2)}) copy-start(f32[2048]{0:T(1024)} %param.25) | copy-start | bytes 24580
  22.2 162.1 %all-gather.7.cloned.1.call-start = ((), (), s32[]{:S(2)}) async-start(), calls=%async_computation.5 | async-start | bytes 5242880 | tf_op jit(solution)/shard_map/all_gather | solution.py:1341
  37.6 2.9 copy-start.26
  37.6 236.1 %all-gather.11.cloned.1.call-start = ((), (), s32[]{:S(2)}) async-start(), calls=%async_computation.7 | async-start | bytes 5898240 | tf_op jit(solution)/shard_map/all_gather | solution.py:1341
  73.5 0.6 copy-start.23
  82.1 31.8 %copy-start.24 = (bf16[4,4,16,128]{3,2,1,0:T(8,128)(2,1)S(1)}, bf16[4,4,16,128]{3,2,1,0:T(8,128)(2,1)}, u32[]{:S(2)}) copy-start(bf16[4,4,16,128]{3,2,1,0:T(8,128)(2,1)} %get-tuple-element.126) | copy-start | bytes 196612
  82.1 31.9 %copy-start.27 = (f32[24]{0:T(128)S(1)}, f32[24]{0:T(128)}, u32[]{:S(2)}) copy-start(f32[24]{0:T(128)} %param.42) | copy-start | bytes 292
  82.1 32.0 %copy-start.28 = (f32[24]{0:T(128)S(1)}, f32[24]{0:T(128)}, u32[]{:S(2)}) copy-start(f32[24]{0:T(128)} %param.41) | copy-start | bytes 292
  82.1 32.1 %copy-start.29 = (f32[24]{0:T(128)S(1)}, f32[24]{0:T(128)}, u32[]{:S(2)}) copy-start(f32[24]{0:T(128)} %param.43) | copy-start | bytes 292
  113.8 196.9 %all-gather.9.cloned.1.call-start = ((), (), s32[]{:S(2)}) async-start(), calls=%async_computation.6 | async-start | bytes 1966080 | tf_op jit(solution)/shard_map/all_gather | solution.py:1341
  181.9 215.1 %reduce-scatter.5.cloned.1.call-start = ((), (), s32[]{:S(2)}) async-start(), calls=%async_computation.8 | async-start | bytes 5898240 | tf_op jit(solution)/shard_map/reduce_scatter | solution.py:1373
  202.0 8.7 %copy-start.18 = (bf16[2048,1024]{1,0:T(8,128)(2,1)S(1)}, bf16[2048,1024]{1,0:T(8,128)(2,1)}, u32[]{:S(2)}) copy-start(bf16[2048,1024]{1,0:T(8,128)(2,1)} %all-gather.7.cloned.1.call-done.wz_ref) | copy-start | bytes 12582916
  209.6 3.6 copy-start.16
  210.7 2.4 copy-start.19
  210.8 2.4 copy-start.14
  258.8 1.0 copy-start.4
  310.7 184.2 %reduce-scatter.7.cloned.1.call-start = ((), (), s32[]{:S(2)}) async-start(), calls=%async_computation.9 | async-start | bytes 4587520 | tf_op jit(solution)/shard_map/reduce_scatter | solution.py:1373
  311.0 11.0 %copy-start.5 = (f32[128,2048]{1,0:T(8,128)S(1)}, f32[128,2048]{1,0:T(8,128)}, u32[]{:S(2)}) copy-start(f32[128,2048]{1,0:T(8,128)} %copy-done.4) | copy-start | bytes 3145732
  322.0 47.2 %copy-start.2 = (bf16[1024,2048]{1,0:T(8,128)(2,1)}, bf16[1024,2048]{1,0:T(8,128)(2,1)S(1)}, u32[]{:S(2)}) copy-start(bf16[1024,2048]{1,0:T(8,128)(2,1)S(1)} %get-tuple-element.172.part) | copy-start | bytes 12582916
  369.3 1.0 copy-start.8
  387.1 10.0 %copy-start.17 = (f32[1024,1]{1,0:T(8,128)S(1)}, f32[1024,1]{1,0:T(8,128)}, u32[]{:S(2)}) copy-start(f32[1024,1]{1,0:T(8,128)} %copy-done.16) | copy-start | bytes 12292
  397.0 143.6 %reduce-scatter.9.cloned.1.call-start = ((), (), s32[]{:S(2)}) async-start(), calls=%async_computation.10 | async-start | bytes 2621440 | tf_op jit(solution)/shard_map/reduce_scatter | solution.py:1373
  397.1 9.7 %copy-start.22 = (bf16[1024,384]{1,0:T(8,128)(2,1)S(1)}, bf16[1024,384]{1,0:T(8,128)(2,1)}, u32[]{:S(2)}) copy-start(bf16[1024,384]{1,0:T(8,128)(2,1)} %get-tuple-element.165) | copy-start | bytes 2359300
  407.9 1.0 copy-start.20
  408.9 6.0 copy-start.6
  414.9 2.2 copy-start.3
  417.1 1.6 copy-start.7
  471.2 1.0 copy-start.10
  472.2 115.9 %reduce-scatter.11.cloned.1.call-start = ((), (), s32[]{:S(2)}) async-start(), calls=%async_computation.11 | async-start | bytes 2621440 | tf_op jit(solution)/shard_map/reduce_scatter | solution.py:1373
  477.0 17.9 %copy-start.13 = (f32[64,1024]{1,0:T(8,128)S(1)}, f32[64,1024]{1,0:T(8,128)}, u32[]{:S(2)}) copy-start(f32[64,1024]{1,0:T(8,128)} %get-tuple-element.182.d_silu_bc) | copy-start | bytes 786436
  495.0 1.2 copy-start.12
  496.2 39.5 %slice-start = ((s8[4259840]{0:T(1024)(128)(4,1)}), s8[4194304]{0:T(1024)(128)(4,1)S(1)}, s32[]{:S(2)}) async-start(s8[4259840]{0:T(1024)(128)(4,1)} %bitcast.84), calls=%async_computation.12 | async-start | bytes 8388608
  525.6 10.1 %slice-start.1 = ((s8[4259840]{0:T(1024)(128)(4,1)}), s8[65536]{0:T(1024)(128)(4,1)S(1)}, s32[]{:S(2)}) async-start(s8[4259840]{0:T(1024)(128)(4,1)} %bitcast.84), calls=%async_computation.13 | async-start | bytes 131072
  535.7 5.8 copy-start.21
  544.6 9.1 %copy-start.9 = (f32[128,2048]{1,0:T(8,128)S(1)}, f32[128,2048]{1,0:T(8,128)}, u32[]{:S(2)}) copy-start(f32[128,2048]{1,0:T(8,128)} %copy-done.8) | copy-start | bytes 3145732
  544.6 9.1 %copy-start.11 = (f32[128,2048]{1,0:T(8,128)S(1)}, f32[128,2048]{1,0:T(8,128)}, u32[]{:S(2)}) copy-start(f32[128,2048]{1,0:T(8,128)} %copy-done.10) | copy-start | bytes 3145732
  606.1 13.4 %copy-start.1 = (bf16[128,512]{1,0:T(8,128)(2,1)S(1)}, bf16[128,512]{1,0:T(8,128)(2,1)}, u32[]{:S(2)}) copy-start(bf16[128,512]{1,0:T(8,128)(2,1)} %param.29) | copy-start | bytes 393220
Sparse Core Ops, SparseCore 0:
  22.3 52.6 all-gather.4
  76.6 96.6 all-gather.6
  174.8 98.8 all-gather.10
  275.1 35.5 all-gather.8
  312.9 84.1 reduce-scatter.4
  399.2 81.8 reduce-scatter.6
  484.0 56.5 reduce-scatter.8
  543.5 44.5 reduce-scatter.10
